TPU v7x, 32 devices: a whole 2x2x4 slice. The times are simulated.
32 devices in a mesh: expert: 4 (over y, x), wide: 8 (over z, core).
Axes of the slice: x: 2, y: 2, z: 4, core: 2. Of those that a mesh axis runs over, the one named last changes fastest.
Arguments:
- tokens: bfloat16 [4096, 2048], P(('expert', 'wide')), may hold values from -6 to 6
- out_grad: bfloat16 [4096, 2048], P(('expert', 'wide')), may hold values from -6 to 6
- routes: int32 [4096, 2], P(('expert', 'wide')), may hold values from 0 to 3, all different within a row; in each aligned block of 128 rows (0 to 127, 128 to 255, ...) at most 128 rows name the same one
- gate_prob: float32 [4096, 2], P(('expert', 'wide')), may hold values from 0.1 to 1
- w_gate: bfloat16 [4, 2048, 768], P('expert', 'wide'), may hold values from -0.125 to 0.125
- w_up: bfloat16 [4, 2048, 768], P('expert', 'wide'), may hold values from -0.125 to 0.125
- w_down: bfloat16 [4, 2048, 768], P('expert', 'wide'), may hold values from -0.21875 to 0.21875
Outputs:
- grad_input: bfloat16 [4096, 2048], P(('expert', 'wide'))
- grad_gate: float32 [4, 2048, 768], P('expert', 'wide')
- grad_up: float32 [4, 2048, 768], P('expert', 'wide')
- grad_down: float32 [4, 2048, 768], P('expert', 'wide')
Inputs may be any that keep to these rules, and one draw needn't show every extreme that they name: `routes`: each row names 2 different experts; the 128 rows of one device name one expert at most 128 times, and in every draw some device names some expert exactly 128 times.
All inputs are finite; a program needn't handle non-finite values.
Results may differ from a plain program's by a relative error of at most 0.017.
Values may be sent and summed in bfloat16 or wider, within the bound.
No kernel may reach another device: no remote copies, remote signals or barrier semaphores. Data moves between devices by JAX's collectives and lax.ppermute only.
A program may use at most 128 MiB of HBM per device.

v0:
```python
import jax
import jax.numpy as jnp
from jax import lax
from jax.experimental import pallas as pl
from jax.experimental.pallas import tpu as pltpu
from jax.sharding import PartitionSpec as P

LANES = 128
F32 = jnp.float32
BF16 = jnp.bfloat16


def swish_backward(gate_pre, up_pre, hidden_grad):
    squash = jax.nn.sigmoid(gate_pre)
    active = gate_pre * squash
    hidden = (active * up_pre).astype(BF16)
    gate_act = (hidden_grad * up_pre * squash * (1.0 + gate_pre * (1.0 - squash))).astype(BF16)
    up_act = (hidden_grad * active).astype(BF16)
    return (hidden, gate_act, up_act)


def dot(a, b):
    return jnp.dot(a, b, preferred_element_type=F32)


def dot_tn(a, b):
    return lax.dot_general(a, b, (((0,), (0,)), ((), ())), preferred_element_type=F32)


def dot_nt(a, b):
    return lax.dot_general(a, b, (((1,), (1,)), ((), ())), preferred_element_type=F32)


def add(a, b):
    return (a.astype(F32) + b.astype(F32)).astype(BF16)


def slot_plan(tokens, out_grad, routes, gate_prob, w_gate, w_up, w_down):
    experts = lax.axis_size("expert")
    tok_count, top_count = routes.shape
    capacity = min(tok_count, 2 * tok_count * top_count // experts)
    slot_count = experts * capacity
    model_width = tokens.shape[1]
    hidden_units = w_gate.shape[2]
    flat_routes = routes.reshape(-1)
    order = jnp.arange(tok_count * top_count, dtype=jnp.int32)
    same = flat_routes[:, None] == flat_routes[None, :]
    before = jnp.sum((same & (order[None, :] < order[:, None])).astype(jnp.int32), axis=1)
    positions = flat_routes * capacity + before
    chosen = (positions[None, :] == jnp.arange(slot_count, dtype=jnp.int32)[:, None]).reshape(
        slot_count, tok_count, top_count
    )
    picker = jnp.sum(chosen.astype(F32), axis=2)
    slot_gate = jnp.sum(jnp.where(chosen, gate_prob[None, :, :], 0.0), axis=(1, 2))
    picker_half = picker.astype(BF16)
    sent_rows = dot(picker_half, tokens).astype(BF16)
    sent_grad = (dot(picker_half, out_grad) * slot_gate[:, None]).astype(BF16)

    def exchange(rows):
        return lax.all_to_all(
            rows.reshape(experts, capacity, model_width),
            "expert",
            split_axis=0,
            concat_axis=0,
            tiled=True,
        ).reshape(slot_count, model_width)

    rows_in = exchange(sent_rows)
    grad_in = exchange(sent_grad)
    full_gate, full_up, full_down = (
        lax.all_gather(w, "wide", axis=1, tiled=True)[0] for w in (w_gate, w_up, w_down)
    )
    hidden, gate_act, up_act = swish_backward(
        dot(rows_in, full_gate), dot(rows_in, full_up), dot(grad_in, full_down)
    )
    merged = jnp.concatenate((gate_act, up_act), axis=1)
    input_grad = dot_nt(merged, jnp.concatenate((full_gate, full_up), axis=1)).astype(BF16)
    parts = jnp.concatenate((dot_tn(rows_in, merged), dot_tn(grad_in, hidden)), axis=1)
    summed = lax.psum_scatter(
        parts.astype(BF16), "wide", scatter_dimension=0, tiled=True
    ).astype(F32)
    grads = tuple(
        summed[:, i * hidden_units : (i + 1) * hidden_units][None] for i in range(3)
    )
    grad_input = dot_tn(picker_half, exchange(input_grad)).astype(BF16)
    return (grad_input,) + grads


VMEM = pl.BlockSpec(memory_space=pltpu.VMEM)
SMEM = pl.BlockSpec(memory_space=pltpu.SMEM)
ANY = pl.BlockSpec(memory_space=pl.ANY)
LIMIT = 40 << 20


def call(body, ins, outs, operands, scratch=(), flops=0, limit=LIMIT):
    moved = sum(a.size * a.dtype.itemsize for a in operands)
    moved += sum(o.size * o.dtype.itemsize for o in outs)
    return pl.pallas_call(
        body,
        out_shape=outs,
        in_specs=ins,
        out_specs=[VMEM] * len(outs),
        scratch_shapes=list(scratch),
        cost_estimate=pl.CostEstimate(flops=flops, bytes_accessed=moved, transcendentals=0),
        compiler_params=pltpu.CompilerParams(vmem_limit_bytes=limit),
    )(*operands)


def half_of(ref, side, half, i, step):
    return ref[:, pl.ds(pl.multiple_of(side * half + i * step, step), step)]


def pack_kernel(chunks, step, at, gate, up, down, *outs):
    half = chunks * step
    c = at[1]
    for side, group in ((c, outs[:chunks]), (1 - c, outs[chunks:])):
        for i, out in enumerate(group):
            for m, ref in enumerate((gate, up, down)):
                out[:, m * step : (m + 1) * step] = half_of(ref, side, half, i, step)


def combine_kernel(chunks, at, *refs):
    kept, given, outs = refs[:chunks], refs[chunks : 2 * chunks], refs[2 * chunks :]
    feats = kept[0].shape[0]
    c = at[1]
    for a, b, out in zip(kept, given, outs):
        out[pl.ds(pl.multiple_of(c * feats, feats), feats), :] = a[...]
        out[pl.ds(pl.multiple_of((1 - c) * feats, feats), feats), :] = b[...]


def scale_kernel(experts, at, *refs):
    pieces, out = refs[:-1], refs[-1]
    rows, width = pieces[0].shape[0], out.shape[1]
    lane = lax.broadcasted_iota(jnp.int32, (rows, LANES), 1)
    ours = (lax.rem(lane, experts) == at[2]) & (lane < 3 * experts)
    for p, ref in enumerate(pieces):
        terms = jnp.where(ours, ref[:, width:].astype(F32), 0.0)
        gate = jnp.sum(terms, axis=1, keepdims=True)
        out[p * rows : (p + 1) * rows, :] = (gate * ref[:, :width].astype(F32)).astype(BF16)


def chunk_kernel(line, n_pieces, at, *refs):
    pieces, refs = refs[:n_pieces], refs[n_pieces:]
    scaled, own = refs[0], refs[1]
    ups, downs = refs[2 : 1 + line], refs[1 + line : 2 * line]
    outs = refs[2 * line : 2 * line + line + 2]
    parts, merged, both = outs[:line], outs[line], outs[line + 1]
    x, g, w, hid, xsem, gsem, wsem = refs[2 * line + line + 2 :]
    z = at[0]
    depth, step = own.shape[0], own.shape[1] // 3
    rows = x.shape[0] // n_pieces
    block = x.shape[0] // 4

    def shard(k):
        f = lax.rem(z - k + line, line)
        return w.at[pl.ds(pl.multiple_of(f * depth, depth), depth), :]

    pltpu.make_async_copy(own, shard(0), wsem.at[0]).start()
    for k in range(1, line):

        @pl.when(z >= k)
        def _(k=k):
            pltpu.make_async_copy(ups[k - 1], shard(k), wsem.at[k]).start()

        @pl.when(z < k)
        def _(k=k):
            pltpu.make_async_copy(downs[line - k - 1], shard(k), wsem.at[k]).start()

    x_copies = [
        pltpu.make_async_copy(ref, x.at[pl.ds(p * rows, rows), :], xsem.at[p])
        for p, ref in enumerate(pieces)
    ]
    g_copies = [
        pltpu.make_async_copy(
            scaled.at[pl.ds(r * block, block), :], g.at[pl.ds(r * block, block), :], gsem.at[r]
        )
        for r in range(4)
    ]
    for r in range(4):
        for p in range(r * n_pieces // 4, (r + 1) * n_pieces // 4):
            x_copies[p].start()
        g_copies[r].start()
    for k in range(line):
        pltpu.make_async_copy(own, shard(k), wsem.at[k]).wait()

    for r in range(4):
        for p in range(r * n_pieces // 4, (r + 1) * n_pieces // 4):
            x_copies[p].wait()
        g_copies[r].wait()
        here = slice(r * block, (r + 1) * block)
        pre = dot(x[here, :], w[:, : 2 * step])
        back = dot(g[here, :], w[:, 2 * step :])
        h, a, b = swish_backward(pre[:, :step], pre[:, step:], back)
        hid[here, :] = h
        merged[here, :step] = a
        merged[here, step:] = b

    for k in range(line):
        f = lax.rem(z - k + line, line)
        cols = pl.ds(pl.multiple_of(f * depth, depth), depth)
        parts[k][:, : 2 * step] = dot_tn(x[:, cols], merged[...]).astype(BF16)
        parts[k][:, 2 * step :] = dot_tn(g[:, cols], hid[...]).astype(BF16)
    both[...] = w[:, : 2 * step]


def route_kernel(chunks, *refs):
    merged, both = refs[:chunks], refs[chunks : 2 * chunks]
    keep, give = refs[2 * chunks :]
    rows, width = keep.shape
    tile = width // 8

    for out, first in ((give, rows), (keep, 0)):

        @pl.loop(0, 8)
        def _(t, out=out, first=first):
            cols = pl.ds(pl.multiple_of(t * tile, tile), tile)
            total = None
            for m, b in zip(merged, both):
                part = dot_nt(m[first : first + rows, :], b[cols, :])
                total = part if total is None else total + part
            out[:, cols] = total.astype(BF16)


def dense_plan(tokens, out_grad, routes, gate_prob, w_gate, w_up, w_down):
    experts = lax.axis_size("expert")
    wide = lax.axis_size("wide")
    line = wide // 2
    rows, width = tokens.shape
    feats = w_gate.shape[1]
    half = w_gate.shape[2] // 2
    step = LANES
    chunks = half // step
    mine = lax.axis_index("expert")
    place = lax.axis_index("wide")
    z, c = place // 2, place % 2
    at = jnp.stack((z, c, mine)).astype(jnp.int32)
    shape = jax.ShapeDtypeStruct

    def twin(a):
        return lax.ppermute(a, "wide", [(i, i ^ 1) for i in range(wide)])

    def along(a, hops):
        return lax.ppermute(
            a, "wide", [(2 * s + i, 2 * t + i) for s, t in hops for i in range(2)]
        )

    def flip(a, bit):
        return lax.ppermute(a, "expert", [(e, e ^ bit) for e in range(experts)])

    cut = [shape((feats, 3 * step), BF16)] * (2 * chunks)
    packed = call(
        lambda *r: pack_kernel(chunks, step, *r),
        [SMEM] + [VMEM] * 3,
        cut,
        (at, w_gate[0], w_up[0], w_down[0]),
    )
    given = [twin(a) for a in packed[chunks:]]
    shards = call(
        lambda *r: combine_kernel(chunks, *r),
        [SMEM] + [VMEM] * (2 * chunks),
        [shape((2 * feats, 3 * step), BF16)] * chunks,
        (at, *packed[:chunks], *given),
    )

    named = jnp.arange(experts, dtype=jnp.int32)[None, :]
    gates = sum(
        jnp.where(routes[:, k : k + 1] == named, gate_prob[:, k : k + 1], 0.0)
        for k in range(routes.shape[1])
    )
    high = lax.reduce_precision(gates, 8, 7)
    middle = lax.reduce_precision(gates - high, 8, 7)
    terms = jnp.concatenate((high, middle, gates - high - middle), axis=1).astype(BF16)
    terms = jnp.pad(terms, ((0, 0), (0, LANES - terms.shape[1])))
    graded = jnp.concatenate((out_grad, terms), axis=1)

    t = [tokens, flip(tokens, 1), flip(tokens, 2)]
    t.append(flip(t[1], 2))
    g = [graded, flip(graded, 1), flip(graded, 2)]
    g.append(flip(g[2], 1))
    t += [twin(a) for a in t]
    g += [twin(a) for a in g]
    count = len(t) * rows
    [scaled] = call(
        lambda *r: scale_kernel(experts, *r),
        [SMEM] + [VMEM] * len(g),
        [shape((count, width), BF16)],
        (at, *g),
    )

    def gather(own):
        ups, downs = [own], [own]
        for s in range(1, line):
            ups.append(along(ups[-1], [(i, i + 1) for i in range(s - 1, line - 1)]))
            downs.append(along(downs[-1], [(i, i - 1) for i in range(1, line - s + 1)]))
        return (own, *ups[1:], *downs[1:])

    def scatter(parts):
        up = down = None
        for s in range(1, line):
            a, b = parts[s], parts[line - s]
            if up is not None:
                a, b = add(a, up), add(b, down)
            up = along(a, [(i, i + 1) for i in range(s)])
            down = along(b, [(i, i - 1) for i in range(line - s, line)])
        return parts[0].astype(F32) + up.astype(F32) + down.astype(F32)

    merged, both, sums = [], [], []
    for i in range(chunks):
        got = call(
            lambda *r: chunk_kernel(line, len(t), *r),
            [SMEM] + [ANY] * (len(t) + 2 * line),
            [shape((2 * feats, 3 * step), BF16)] * line
            + [shape((count, 2 * step), BF16), shape((width, 2 * step), BF16)],
            (at, *t, scaled, *gather(shards[i])),
            (
                pltpu.VMEM((count, width), BF16),
                pltpu.VMEM((count, width), BF16),
                pltpu.VMEM((width, 3 * step), BF16),
                pltpu.VMEM((count, step), BF16),
                pltpu.SemaphoreType.DMA((len(t),)),
                pltpu.SemaphoreType.DMA((4,)),
                pltpu.SemaphoreType.DMA((line,)),
            ),
            flops=12 * count * width * step,
        )
        merged.append(got[line])
        both.append(got[line + 1])
        sums.append(scatter(got[:line]))

    block = experts * rows
    keep, give = call(
        lambda *r: route_kernel(chunks, *r),
        [VMEM] * (2 * chunks),
        [shape((block, width), BF16)] * 2,
        (*merged, *both),
        flops=4 * count * width * step * chunks,
    )
    ret = keep.astype(F32) + twin(give).astype(F32)
    ret = ret.reshape(experts, rows, width)
    left, right = ret[:, :, : width // 2], ret[:, :, width // 2 :]
    left = left[:2] + flip(left[2:].astype(BF16), 2).astype(F32)
    odd = flip(jnp.stack((right[1], right[3])).astype(BF16), 1).astype(F32)
    left = left[0] + flip(left[1].astype(BF16), 1).astype(F32)
    right = right[0] + odd[0] + flip((right[2] + odd[1]).astype(BF16), 2).astype(F32)
    grad_input = jnp.concatenate((left, right), axis=1).astype(BF16)

    own = [lax.dynamic_slice_in_dim(s, c * feats, feats, 0) for s in sums]
    other = [twin(lax.dynamic_slice_in_dim(s, (1 - c) * feats, feats, 0)) for s in sums]

    def grad_of(j):
        cols = slice(j * step, (j + 1) * step)
        a = jnp.concatenate([s[:, cols] for s in own], axis=1)
        b = jnp.concatenate([s[:, cols] for s in other], axis=1)
        first = jnp.concatenate((a, b), axis=1)
        return jnp.where(c == 0, first, jnp.concatenate((b, a), axis=1))[None]

    return (grad_input, grad_of(0), grad_of(1), grad_of(2))


def solution(mesh):
    experts, wide = mesh.shape["expert"], mesh.shape["wide"]
    split = P(("expert", "wide"), None)
    weight = P("expert", "wide", None)

    def on_device(tokens, out_grad, routes, *rest):
        dense = experts == 4 and wide % 2 == 0 and 2 * routes.shape[1] >= experts
        dense = dense and rest[1].shape[2] % (2 * LANES) == 0
        return (dense_plan if dense else slot_plan)(tokens, out_grad, routes, *rest)

    return jax.shard_map(
        on_device,
        mesh=mesh,
        in_specs=(split,) * 4 + (weight,) * 3,
        out_specs=(split, weight, weight, weight),
        check_vma=False,
    )
```

profile of v0, /device:TPU:0, one launch (start us, length us, event | category | flops | bytes accessed | tf_op | source)
XLA Modules:
  0.0 228.8 jit_solution(4793802503171448810)
XLA Ops:
  0.6 3.0 %collective-permute-start = (bf16[128,2048]{1,0:T(8,128)(2,1)}, bf16[128,2048]{1,0:T(8,128)(2,1)}, u32[]{:S(2)}, u32[]{:S(2)}) collective-permute-start(bf16[128,2048]{1,0:T(8,128)(2,1)} %r_1_.5), channel_id=1, source_target_pairs={{0,8},{8,0},{16,24},{24,16},{1,9},{9,1},{17,25},{25,17},{2,10},{10... | collective-permute-start | bytes 1572872 | tf_op jit(solution)/shard_map/ppermute | solution.py:248
  3.6 1.5 collective-permute-start.1
  5.2 1.0 copy-done.4
  6.2 1.0 copy-done.5
  7.2 1.0 copy-done.6
  11.8 1.1 fusion.7.r_1_
  13.6 2.6 %collective-permute-done.r_2_ = bf16[128,2048]{1,0:T(8,128)(2,1)} collective-permute-done((bf16[128,2048]{1,0:T(8,128)(2,1)}, bf16[128,2048]{1,0:T(8,128)(2,1)}, u32[]{:S(2)}, u32[]{:S(2)}) %collective-permute-start) | collective-permute-done | bytes 524320 | tf_op jit(solution)/shard_map/ppermute | solution.py:248
  16.8 1.9 collective-permute-done.1.r_3_
  18.8 3.5 %collective-permute-start.29 = (bf16[512,384]{1,0:T(8,128)(2,1)S(1)}, bf16[512,384]{1,0:T(8,128)(2,1)S(1)}, u32[]{:S(2)}, u32[]{:S(2)}) collective-permute-start(bf16[512,384]{1,0:T(8,128)(2,1)S(1)} %get-tuple-element.43.r_10_), channel_id=1, source_target_pairs={{0,2},{1,3},{2,4},{3,5},{4,6},{5,7},{8,10},{9,11},{10,12},{11,13},... | collective-permute-start | bytes 1179656 | tf_op jit(solution)/shard_map/ppermute | solution.py:243
  22.3 1.3 collective-permute-start.32
  24.4 4.8 %collective-permute-done.8.r_3_ = bf16[128,2176]{1,0:T(8,128)(2,1)S(1)} collective-permute-done((bf16[128,2176]{1,0:T(8,128)(2,1)S(1)}, bf16[128,2176]{1,0:T(8,128)(2,1)S(1)}, u32[]{:S(2)}, u32[]{:S(2)}) %collective-permute-start.8) | collective-permute-done | bytes 557088 | tf_op jit(solution)/shard_map/ppermute | solution.py:248
  29.2 3.5 %collective-permute-start.23 = (bf16[512,384]{1,0:T(8,128)(2,1)S(1)}, bf16[512,384]{1,0:T(8,128)(2,1)S(1)}, u32[]{:S(2)}, u32[]{:S(2)}) collective-permute-start(bf16[512,384]{1,0:T(8,128)(2,1)S(1)} %get-tuple-element.41.r_10_), channel_id=1, source_target_pairs={{0,2},{1,3},{2,4},{3,5},{4,6},{5,7},{8,10},{9,11},{10,12},{11,13},... | collective-permute-start | bytes 1179656 | tf_op jit(solution)/shard_map/ppermute | solution.py:243
  32.7 1.3 collective-permute-start.26
  34.7 4.6 %collective-permute-start.17 = (bf16[512,384]{1,0:T(8,128)(2,1)S(1)}, bf16[512,384]{1,0:T(8,128)(2,1)S(1)}, u32[]{:S(2)}, u32[]{:S(2)}) collective-permute-start(bf16[512,384]{1,0:T(8,128)(2,1)S(1)} %get-tuple-element.39.r_10_), channel_id=1, source_target_pairs={{0,2},{1,3},{2,4},{3,5},{4,6},{5,7},{8,10},{9,11},{10,12},{11,13},... | collective-permute-start | bytes 1179656 | tf_op jit(solution)/shard_map/ppermute | solution.py:243
  39.3 1.3 collective-permute-start.20
  41.4 1.4 collective-permute-start.30
  43.6 1.3 collective-permute-start.33
  46.2 1.4 collective-permute-start.24
  48.4 1.3 collective-permute-start.27
  50.5 4.2 %collective-permute-done.20.r_14_ = bf16[512,384]{1,0:T(8,128)(2,1)S(1)} collective-permute-done((bf16[512,384]{1,0:T(8,128)(2,1)S(1)}, bf16[512,384]{1,0:T(8,128)(2,1)S(1)}, u32[]{:S(2)}, u32[]{:S(2)}) %collective-permute-start.20) | collective-permute-done | bytes 393248 | tf_op jit(solution)/shard_map/ppermute | solution.py:243
  56.1 1.3 collective-permute-start.21
  58.1 5.0 %collective-permute-done.33.r_15_ = bf16[512,384]{1,0:T(8,128)(2,1)} collective-permute-done((bf16[512,384]{1,0:T(8,128)(2,1)S(1)}, bf16[512,384]{1,0:T(8,128)(2,1)}, u32[]{:S(2)}, u32[]{:S(2)}) %collective-permute-start.33) | collective-permute-done | bytes 393248 | tf_op jit(solution)/shard_map/ppermute | solution.py:243
  63.7 1.5 collective-permute-start.2
  65.3 6.4 %collective-permute-done.27.r_15_ = bf16[512,384]{1,0:T(8,128)(2,1)} collective-permute-done((bf16[512,384]{1,0:T(8,128)(2,1)S(1)}, bf16[512,384]{1,0:T(8,128)(2,1)}, u32[]{:S(2)}, u32[]{:S(2)}) %collective-permute-start.27) | collective-permute-done | bytes 393248 | tf_op jit(solution)/shard_map/ppermute | solution.py:243
  72.1 5.5 %collective-permute-done.21.r_15_ = bf16[512,384]{1,0:T(8,128)(2,1)S(1)} collective-permute-done((bf16[512,384]{1,0:T(8,128)(2,1)S(1)}, bf16[512,384]{1,0:T(8,128)(2,1)S(1)}, u32[]{:S(2)}, u32[]{:S(2)}) %collective-permute-start.21) | collective-permute-done | bytes 393248 | tf_op jit(solution)/shard_map/ppermute | solution.py:243
  80.6 1.4 collective-permute-start.31
  82.0 1.3 collective-permute-start.34
  84.1 1.4 collective-permute-start.25
  86.3 1.3 collective-permute-start.28
  87.6 1.0 copy-done.1
  88.7 1.1 copy-done.3
  89.8 1.3 shard_map.102.r_9_
  92.0 4.2 %collective-permute-done.34.r_16_ = bf16[512,384]{1,0:T(8,128)(2,1)} collective-permute-done((bf16[512,384]{1,0:T(8,128)(2,1)}, bf16[512,384]{1,0:T(8,128)(2,1)}, u32[]{:S(2)}, u32[]{:S(2)}) %collective-permute-start.34) | collective-permute-done | bytes 393248 | tf_op jit(solution)/shard_map/ppermute | solution.py:243
  96.2 1.3 collective-permute-start.22
  97.5 7.7 %shard_map.107 = (bf16[512,384]{1,0:T(8,128)(2,1)S(1)}, bf16[512,384]{1,0:T(8,128)(2,1)S(1)}, bf16[512,384]{1,0:T(8,128)(2,1)S(1)}, bf16[512,384]{1,0:T(8,128)(2...) custom-call(s32[3]{0:T(128)S(1)} %pad_add_fusion.r_0_, bf16[128,2048]{1,0:T(8,128)(2,1)S(1)} %copy-done.7, ...), custom_call_target="tpu_custom_call" | custom-call | flops 3221225472 | bytes 14286860 | tf_op jit(solution)/shard_map/pallas_call | solution.py:98
  105.2 4.8 %collective-permute-start.52 = (bf16[512,384]{1,0:T(8,128)(2,1)S(1)}, bf16[512,384]{1,0:T(8,128)(2,1)S(1)}, u32[]{:S(2)}, u32[]{:S(2)}) collective-permute-start(bf16[512,384]{1,0:T(8,128)(2,1)S(1)} %get-tuple-element.61), channel_id=1, source_target_pairs={{0,2},{1,3},{8,10},{9,11},{16,18},{17,19},{24,26},{25,27}} | collective-permute-start | bytes 1179656 | tf_op jit(solution)/shard_map/ppermute | solution.py:243
  110.9 7.8 %shard_map.106 = (bf16[512,384]{1,0:T(8,128)(2,1)S(1)}, bf16[512,384]{1,0:T(8,128)(2,1)S(1)}, bf16[512,384]{1,0:T(8,128)(2,1)S(1)}, bf16[512,384]{1,0:T(8,128)(2...) custom-call(s32[3]{0:T(128)S(1)} %pad_add_fusion.r_0_, bf16[128,2048]{1,0:T(8,128)(2,1)S(1)} %copy-done.7, ...), custom_call_target="tpu_custom_call" | custom-call | flops 3221225472 | bytes 14286860 | tf_op jit(solution)/shard_map/pallas_call | solution.py:98
  118.8 1.5 collective-permute-start.46
  121.1 8.0 %shard_map.105 = (bf16[512,384]{1,0:T(8,128)(2,1)S(1)}, bf16[512,384]{1,0:T(8,128)(2,1)S(1)}, bf16[512,384]{1,0:T(8,128)(2,1)S(1)}, bf16[512,384]{1,0:T(8,128)(2...) custom-call(s32[3]{0:T(128)S(1)} %pad_add_fusion.r_0_, bf16[128,2048]{1,0:T(8,128)(2,1)S(1)} %copy-done.7, ...), custom_call_target="tpu_custom_call" | custom-call | flops 3221225472 | bytes 14286860 | tf_op jit(solution)/shard_map/pallas_call | solution.py:98
  129.1 1.4 collective-permute-start.40
  130.4 6.5 %shard_map.108 = (bf16[512,2048]{1,0:T(8,128)(2,1)S(1)}, bf16[512,2048]{1,0:T(8,128)(2,1)S(1)}) custom-call(bf16[1024,256]{1,0:T(8,128)(2,1)S(1)} %get-tuple-element.40.r_0_, bf16[1024,256]{1,0:T(8,128)(2,1)S(1)} %get-tuple-element.42.r_1_, bf16[1024,256]{1,0:T(8,128)(2,1)S(1)} %get-tuple-element.44.r_2_, bf16[2048,256]{1,0:T(8,128)(2,1)S(1)} %get-tuple-element.45.r_3_, ...), custom_call_target="tpu_custom_call" | custom-call | flops 3221225472 | bytes 8912896 | tf_op jit(solution)/shard_map/pallas_call | solution.py:98
  137.0 0.9 collective-permute-start.43
  138.2 1.3 collective-permute-start.53
  140.4 3.8 %collective-permute-start.47 = (bf16[512,384]{1,0:T(8,128)(2,1)S(1)}, bf16[512,384]{1,0:T(8,128)(2,1)S(1)}, u32[]{:S(2)}, u32[]{:S(2)}) collective-permute-start(bf16[512,384]{1,0:T(8,128)(2,1)S(1)} %get-tuple-element.102), channel_id=1, source_target_pairs={{0,2},{1,3},{2,4},{3,5},{8,10},{9,11},{10,12},{11,13},{16,18},{17,... | collective-permute-start | bytes 1179656 | tf_op jit(solution)/shard_map/ppermute | solution.py:243
  145.2 3.8 %collective-permute-done.53 = bf16[512,384]{1,0:T(8,128)(2,1)S(1)} collective-permute-done((bf16[512,384]{1,0:T(8,128)(2,1)S(1)}, bf16[512,384]{1,0:T(8,128)(2,1)S(1)}, u32[]{:S(2)}, u32[]{:S(2)}) %collective-permute-start.53) | collective-permute-done | bytes 393248 | tf_op jit(solution)/shard_map/ppermute | solution.py:243
  149.0 4.4 %collective-permute-start.41 = (bf16[512,384]{1,0:T(8,128)(2,1)S(1)}, bf16[512,384]{1,0:T(8,128)(2,1)S(1)}, u32[]{:S(2)}, u32[]{:S(2)}) collective-permute-start(bf16[512,384]{1,0:T(8,128)(2,1)S(1)} %get-tuple-element.104), channel_id=1, source_target_pairs={{0,2},{1,3},{2,4},{3,5},{8,10},{9,11},{10,12},{11,13},{16,18},{17,... | collective-permute-start | bytes 1179656 | tf_op jit(solution)/shard_map/ppermute | solution.py:243
  154.3 3.1 %collective-permute-done.47 = bf16[512,384]{1,0:T(8,128)(2,1)S(1)} collective-permute-done((bf16[512,384]{1,0:T(8,128)(2,1)S(1)}, bf16[512,384]{1,0:T(8,128)(2,1)S(1)}, u32[]{:S(2)}, u32[]{:S(2)}) %collective-permute-start.47) | collective-permute-done | bytes 393248 | tf_op jit(solution)/shard_map/ppermute | solution.py:243
  157.4 4.4 %collective-permute-start.54 = (bf16[512,384]{1,0:T(8,128)(2,1)S(1)}, bf16[512,384]{1,0:T(8,128)(2,1)S(1)}, u32[]{:S(2)}, u32[]{:S(2)}) collective-permute-start(bf16[512,384]{1,0:T(8,128)(2,1)S(1)} %add_convert_fusion.1), channel_id=1, source_target_pairs={{0,2},{1,3},{2,4},{3,5},{4,6},{5,7},{8,10},{9,11},{10,12},{11,13},... | collective-permute-start | bytes 1179656 | tf_op jit(solution)/shard_map/ppermute | solution.py:243
  161.9 3.6 %collective-permute-start.48 = (bf16[512,384]{1,0:T(8,128)(2,1)S(1)}, bf16[512,384]{1,0:T(8,128)(2,1)S(1)}, u32[]{:S(2)}, u32[]{:S(2)}) collective-permute-start(bf16[512,384]{1,0:T(8,128)(2,1)S(1)} %add_convert_fusion.3), channel_id=1, source_target_pairs={{0,2},{1,3},{2,4},{3,5},{4,6},{5,7},{8,10},{9,11},{10,12},{11,13},... | collective-permute-start | bytes 1179656 | tf_op jit(solution)/shard_map/ppermute | solution.py:243
  165.8 1.3 collective-permute-start.51
  167.2 1.3 collective-permute-start.57
  168.6 13.8 %collective-permute-done.48 = bf16[512,384]{1,0:T(8,128)(2,1)S(1)} collective-permute-done((bf16[512,384]{1,0:T(8,128)(2,1)S(1)}, bf16[512,384]{1,0:T(8,128)(2,1)S(1)}, u32[]{:S(2)}, u32[]{:S(2)}) %collective-permute-start.48) | collective-permute-done | bytes 393248 | tf_op jit(solution)/shard_map/ppermute | solution.py:243
  182.5 4.4 %collective-permute-start.42 = (bf16[512,384]{1,0:T(8,128)(2,1)S(1)}, bf16[512,384]{1,0:T(8,128)(2,1)S(1)}, u32[]{:S(2)}, u32[]{:S(2)}) collective-permute-start(bf16[512,384]{1,0:T(8,128)(2,1)S(1)} %add_convert_fusion.5), channel_id=1, source_target_pairs={{0,2},{1,3},{2,4},{3,5},{4,6},{5,7},{8,10},{9,11},{10,12},{11,13},... | collective-permute-start | bytes 1179656 | tf_op jit(solution)/shard_map/ppermute | solution.py:243
  186.9 1.3 collective-permute-start.45
  188.4 6.9 %collective-permute-done.42 = bf16[512,384]{1,0:T(8,128)(2,1)S(1)} collective-permute-done((bf16[512,384]{1,0:T(8,128)(2,1)S(1)}, bf16[512,384]{1,0:T(8,128)(2,1)S(1)}, u32[]{:S(2)}, u32[]{:S(2)}) %collective-permute-start.42) | collective-permute-done | bytes 393248 | tf_op jit(solution)/shard_map/ppermute | solution.py:243
  195.3 4.1 %collective-permute-done.45 = bf16[512,384]{1,0:T(8,128)(2,1)S(1)} collective-permute-done((bf16[512,384]{1,0:T(8,128)(2,1)S(1)}, bf16[512,384]{1,0:T(8,128)(2,1)S(1)}, u32[]{:S(2)}, u32[]{:S(2)}) %collective-permute-start.45) | collective-permute-done | bytes 393248 | tf_op jit(solution)/shard_map/ppermute | solution.py:243
  200.4 1.0 collective-permute-done.58
  203.5 1.6 collective-permute-start.36
  205.1 1.3 broadcast_select_fusion
  207.1 10.5 %collective-permute-done.36 = bf16[2,128,1024]{2,1,0:T(8,128)(2,1)S(1)} collective-permute-done((bf16[2,128,1024]{2,1,0:T(8,128)(2,1)S(1)}, bf16[2,128,1024]{2,1,0:T(8,128)(2,1)S(1)}, u32[]{:S(2)}, u32[]{:S(2)}) %collective-permute-start.36) | collective-permute-done | bytes 524320 | tf_op jit(solution)/shard_map/ppermute | solution.py:248
  218.4 2.3 %collective-permute-done.38 = bf16[2,128,1024]{2,1,0:T(8,128)(2,1)S(1)} collective-permute-done((bf16[2,128,1024]{2,1,0:T(8,128)(2,1)S(1)}, bf16[2,128,1024]{2,1,0:T(8,128)(2,1)S(1)}, u32[]{:S(2)}, u32[]{:S(2)}) %collective-permute-start.38) | collective-permute-done | bytes 524320 | tf_op jit(solution)/shard_map/ppermute | solution.py:248
  221.1 1.0 broadcast_select_fusion.2
  222.1 3.9 %collective-permute-done.37 = bf16[128,1024]{1,0:T(8,128)(2,1)S(1)} collective-permute-done((bf16[128,1024]{1,0:T(8,128)(2,1)S(1)}, bf16[128,1024]{1,0:T(8,128)(2,1)S(1)}, u32[]{:S(2)}, u32[]{:S(2)}) %collective-permute-start.37) | collective-permute-done | bytes 262176 | tf_op jit(solution)/shard_map/ppermute | solution.py:248
  226.0 1.8 collective-permute-done.39
  (178 shorter events, 30.6 us)
Async XLA Ops:
  0.6 15.6 %collective-permute-start = (bf16[128,2048]{1,0:T(8,128)(2,1)}, bf16[128,2048]{1,0:T(8,128)(2,1)}, u32[]{:S(2)}, u32[]{:S(2)}) collective-permute-start(bf16[128,2048]{1,0:T(8,128)(2,1)} %r_1_.5), channel_id=1, source_target_pairs={{0,8},{8,0},{16,24},{24,16},{1,9},{9,1},{17,25},{25,17},{2,10},{10... | collective-permute-start | bytes 1572872 | tf_op jit(solution)/shard_map/ppermute | solution.py:248
  3.6 15.2 %collective-permute-start.1 = (bf16[128,2048]{1,0:T(8,128)(2,1)}, bf16[128,2048]{1,0:T(8,128)(2,1)}, u32[]{:S(2)}, u32[]{:S(2)}) collective-permute-start(bf16[128,2048]{1,0:T(8,128)(2,1)} %r_1_.5), channel_id=1, source_target_pairs={{0,16},{8,24},{16,0},{24,8},{1,17},{9,25},{17,1},{25,9},{2,18},{10... | collective-permute-start | bytes 1572872 | tf_op jit(solution)/shard_map/ppermute | solution.py:248
  5.2 17.1 %collective-permute-start.3 = (bf16[128,2048]{1,0:T(8,128)(2,1)}, bf16[128,2048]{1,0:T(8,128)(2,1)}, u32[]{:S(2)}, u32[]{:S(2)}) collective-permute-start(bf16[128,2048]{1,0:T(8,128)(2,1)} %r_1_.5), channel_id=1, source_target_pairs={{0,1},{1,0},{2,3},{3,2},{4,5},{5,4},{6,7},{7,6},{8,9},{9,8},{10,11... | collective-permute-start | bytes 1572872 | tf_op jit(solution)/shard_map/ppermute | solution.py:240
  9.0 2.3 %collective-permute-start.14 = (bf16[256,384]{1,0:T(8,128)(2,1)S(1)}, bf16[256,384]{1,0:T(8,128)(2,1)S(1)}, u32[]{:S(2)}, u32[]{:S(2)}) collective-permute-start(bf16[256,384]{1,0:T(8,128)(2,1)S(1)} %get-tuple-element.36), channel_id=1, source_target_pairs={{0,1},{1,0},{2,3},{3,2},{4,5},{5,4},{6,7},{7,6},{8,9},{9,8},{10,11... | collective-permute-start | bytes 589832 | tf_op jit(solution)/shard_map/ppermute | solution.py:240
  9.6 3.3 %collective-permute-start.15 = (bf16[256,384]{1,0:T(8,128)(2,1)S(1)}, bf16[256,384]{1,0:T(8,128)(2,1)S(1)}, u32[]{:S(2)}, u32[]{:S(2)}) collective-permute-start(bf16[256,384]{1,0:T(8,128)(2,1)S(1)} %get-tuple-element.37), channel_id=1, source_target_pairs={{0,1},{1,0},{2,3},{3,2},{4,5},{5,4},{6,7},{7,6},{8,9},{9,8},{10,11... | collective-permute-start | bytes 589832 | tf_op jit(solution)/shard_map/ppermute | solution.py:240
  11.3 2.2 collective-permute-start.16
  12.9 16.3 %collective-permute-start.8 = (bf16[128,2176]{1,0:T(8,128)(2,1)S(1)}, bf16[128,2176]{1,0:T(8,128)(2,1)S(1)}, u32[]{:S(2)}, u32[]{:S(2)}) collective-permute-start(bf16[128,2176]{1,0:T(8,128)(2,1)S(1)} %fusion.7.r_1_), channel_id=1, source_target_pairs={{0,16},{8,24},{16,0},{24,8},{1,17},{9,25},{17,1},{25,9},{2,18},{10... | collective-permute-start | bytes 1671176 | tf_op jit(solution)/shard_map/ppermute | solution.py:248
  13.5 19.2 %collective-permute-start.7 = (bf16[128,2176]{1,0:T(8,128)(2,1)S(1)}, bf16[128,2176]{1,0:T(8,128)(2,1)S(1)}, u32[]{:S(2)}, u32[]{:S(2)}) collective-permute-start(bf16[128,2176]{1,0:T(8,128)(2,1)S(1)} %fusion.7.r_1_), channel_id=1, source_target_pairs={{0,8},{8,0},{16,24},{24,16},{1,9},{9,1},{17,25},{25,17},{2,10},{10... | collective-permute-start | bytes 1671176 | tf_op jit(solution)/shard_map/ppermute | solution.py:248
  16.2 18.5 %collective-permute-start.10 = (bf16[128,2176]{1,0:T(8,128)(2,1)S(1)}, bf16[128,2176]{1,0:T(8,128)(2,1)S(1)}, u32[]{:S(2)}, u32[]{:S(2)}) collective-permute-start(bf16[128,2176]{1,0:T(8,128)(2,1)S(1)} %fusion.7.r_1_), channel_id=1, source_target_pairs={{0,1},{1,0},{2,3},{3,2},{4,5},{5,4},{6,7},{7,6},{8,9},{9,8},{10,11... | collective-permute-start | bytes 1671176 | tf_op jit(solution)/shard_map/ppermute | solution.py:240
  18.8 20.5 %collective-permute-start.29 = (bf16[512,384]{1,0:T(8,128)(2,1)S(1)}, bf16[512,384]{1,0:T(8,128)(2,1)S(1)}, u32[]{:S(2)}, u32[]{:S(2)}) collective-permute-start(bf16[512,384]{1,0:T(8,128)(2,1)S(1)} %get-tuple-element.43.r_10_), channel_id=1, source_target_pairs={{0,2},{1,3},{2,4},{3,5},{4,6},{5,7},{8,10},{9,11},{10,12},{11,13},... | collective-permute-start | bytes 1179656 | tf_op jit(solution)/shard_map/ppermute | solution.py:243
  22.3 19.1 %collective-permute-start.32 = (bf16[512,384]{1,0:T(8,128)(2,1)S(1)}, bf16[512,384]{1,0:T(8,128)(2,1)S(1)}, u32[]{:S(2)}, u32[]{:S(2)}) collective-permute-start(bf16[512,384]{1,0:T(8,128)(2,1)S(1)} %get-tuple-element.43.r_10_), channel_id=1, source_target_pairs={{2,0},{3,1},{4,2},{5,3},{6,4},{7,5},{10,8},{11,9},{12,10},{13,11},... | collective-permute-start | bytes 1179656 | tf_op jit(solution)/shard_map/ppermute | solution.py:243
  29.2 14.4 %collective-permute-start.23 = (bf16[512,384]{1,0:T(8,128)(2,1)S(1)}, bf16[512,384]{1,0:T(8,128)(2,1)S(1)}, u32[]{:S(2)}, u32[]{:S(2)}) collective-permute-start(bf16[512,384]{1,0:T(8,128)(2,1)S(1)} %get-tuple-element.41.r_10_), channel_id=1, source_target_pairs={{0,2},{1,3},{2,4},{3,5},{4,6},{5,7},{8,10},{9,11},{10,12},{11,13},... | collective-permute-start | bytes 1179656 | tf_op jit(solution)/shard_map/ppermute | solution.py:243
  32.7 13.6 %collective-permute-start.26 = (bf16[512,384]{1,0:T(8,128)(2,1)S(1)}, bf16[512,384]{1,0:T(8,128)(2,1)S(1)}, u32[]{:S(2)}, u32[]{:S(2)}) collective-permute-start(bf16[512,384]{1,0:T(8,128)(2,1)S(1)} %get-tuple-element.41.r_10_), channel_id=1, source_target_pairs={{2,0},{3,1},{4,2},{5,3},{6,4},{7,5},{10,8},{11,9},{12,10},{13,11},... | collective-permute-start | bytes 1179656 | tf_op jit(solution)/shard_map/ppermute | solution.py:243
  34.7 13.7 %collective-permute-start.17 = (bf16[512,384]{1,0:T(8,128)(2,1)S(1)}, bf16[512,384]{1,0:T(8,128)(2,1)S(1)}, u32[]{:S(2)}, u32[]{:S(2)}) collective-permute-start(bf16[512,384]{1,0:T(8,128)(2,1)S(1)} %get-tuple-element.39.r_10_), channel_id=1, source_target_pairs={{0,2},{1,3},{2,4},{3,5},{4,6},{5,7},{8,10},{9,11},{10,12},{11,13},... | collective-permute-start | bytes 1179656 | tf_op jit(solution)/shard_map/ppermute | solution.py:243
  39.3 15.3 %collective-permute-start.20 = (bf16[512,384]{1,0:T(8,128)(2,1)S(1)}, bf16[512,384]{1,0:T(8,128)(2,1)S(1)}, u32[]{:S(2)}, u32[]{:S(2)}) collective-permute-start(bf16[512,384]{1,0:T(8,128)(2,1)S(1)} %get-tuple-element.39.r_10_), channel_id=1, source_target_pairs={{2,0},{3,1},{4,2},{5,3},{6,4},{7,5},{10,8},{11,9},{12,10},{13,11},... | collective-permute-start | bytes 1179656 | tf_op jit(solution)/shard_map/ppermute | solution.py:243
  41.4 14.7 %collective-permute-start.30 = (bf16[512,384]{1,0:T(8,128)(2,1)S(1)}, bf16[512,384]{1,0:T(8,128)(2,1)}, u32[]{:S(2)}, u32[]{:S(2)}) collective-permute-start(bf16[512,384]{1,0:T(8,128)(2,1)S(1)} %collective-permute-done.29.r_11_), channel_id=1, source_target_pairs={{2,4},{3,5},{4,6},{5,7},{10,12},{11,13},{12,14},{13,15},{18,20},{1... | collective-permute-start | bytes 1179656 | tf_op jit(solution)/shard_map/ppermute | solution.py:243
  43.6 19.6 %collective-permute-start.33 = (bf16[512,384]{1,0:T(8,128)(2,1)S(1)}, bf16[512,384]{1,0:T(8,128)(2,1)}, u32[]{:S(2)}, u32[]{:S(2)}) collective-permute-start(bf16[512,384]{1,0:T(8,128)(2,1)S(1)} %collective-permute-done.32.r_14_), channel_id=1, source_target_pairs={{2,0},{3,1},{4,2},{5,3},{10,8},{11,9},{12,10},{13,11},{18,16},{19,... | collective-permute-start | bytes 1179656 | tf_op jit(solution)/shard_map/ppermute | solution.py:243
  46.2 17.5 %collective-permute-start.24 = (bf16[512,384]{1,0:T(8,128)(2,1)S(1)}, bf16[512,384]{1,0:T(8,128)(2,1)}, u32[]{:S(2)}, u32[]{:S(2)}) collective-permute-start(bf16[512,384]{1,0:T(8,128)(2,1)S(1)} %collective-permute-done.23.r_11_), channel_id=1, source_target_pairs={{2,4},{3,5},{4,6},{5,7},{10,12},{11,13},{12,14},{13,15},{18,20},{1... | collective-permute-start | bytes 1179656 | tf_op jit(solution)/shard_map/ppermute | solution.py:243
  48.4 23.2 %collective-permute-start.27 = (bf16[512,384]{1,0:T(8,128)(2,1)S(1)}, bf16[512,384]{1,0:T(8,128)(2,1)}, u32[]{:S(2)}, u32[]{:S(2)}) collective-permute-start(bf16[512,384]{1,0:T(8,128)(2,1)S(1)} %collective-permute-done.26.r_14_), channel_id=1, source_target_pairs={{2,0},{3,1},{4,2},{5,3},{10,8},{11,9},{12,10},{13,11},{18,16},{19,... | collective-permute-start | bytes 1179656 | tf_op jit(solution)/shard_map/ppermute | solution.py:243
  54.7 17.0 %collective-permute-start.18 = (bf16[512,384]{1,0:T(8,128)(2,1)S(1)}, bf16[512,384]{1,0:T(8,128)(2,1)S(1)}, u32[]{:S(2)}, u32[]{:S(2)}) collective-permute-start(bf16[512,384]{1,0:T(8,128)(2,1)S(1)} %collective-permute-done.17.r_11_), channel_id=1, source_target_pairs={{2,4},{3,5},{4,6},{5,7},{10,12},{11,13},{12,14},{13,15},{18,20},{1... | collective-permute-start | bytes 1179656 | tf_op jit(solution)/shard_map/ppermute | solution.py:243
  56.1 21.6 %collective-permute-start.21 = (bf16[512,384]{1,0:T(8,128)(2,1)S(1)}, bf16[512,384]{1,0:T(8,128)(2,1)S(1)}, u32[]{:S(2)}, u32[]{:S(2)}) collective-permute-start(bf16[512,384]{1,0:T(8,128)(2,1)S(1)} %collective-permute-done.20.r_14_), channel_id=1, source_target_pairs={{2,0},{3,1},{4,2},{5,3},{10,8},{11,9},{12,10},{13,11},{18,16},{19,... | collective-permute-start | bytes 1179656 | tf_op jit(solution)/shard_map/ppermute | solution.py:243
  63.2 15.0 %collective-permute-start.9 = (bf16[128,2176]{1,0:T(8,128)(2,1)S(1)}, bf16[128,2176]{1,0:T(8,128)(2,1)S(1)}, u32[]{:S(2)}, u32[]{:S(2)}) collective-permute-start(bf16[128,2176]{1,0:T(8,128)(2,1)S(1)} %collective-permute-done.8.r_3_), channel_id=1, source_target_pairs={{0,8},{8,0},{16,24},{24,16},{1,9},{9,1},{17,25},{25,17},{2,10},{10... | collective-permute-start | bytes 1671176 | tf_op jit(solution)/shard_map/ppermute | solution.py:248
  63.7 13.9 %collective-permute-start.2 = (bf16[128,2048]{1,0:T(8,128)(2,1)}, bf16[128,2048]{1,0:T(8,128)(2,1)}, u32[]{:S(2)}, u32[]{:S(2)}) collective-permute-start(bf16[128,2048]{1,0:T(8,128)(2,1)} %collective-permute-done.r_2_), channel_id=1, source_target_pairs={{0,16},{8,24},{16,0},{24,8},{1,17},{9,25},{17,1},{25,9},{2,18},{10... | collective-permute-start | bytes 1572872 | tf_op jit(solution)/shard_map/ppermute | solution.py:248
  71.6 6.6 %collective-permute-start.4 = (bf16[128,2048]{1,0:T(8,128)(2,1)}, bf16[128,2048]{1,0:T(8,128)(2,1)S(1)}, u32[]{:S(2)}, u32[]{:S(2)}) collective-permute-start(bf16[128,2048]{1,0:T(8,128)(2,1)} %collective-permute-done.r_2_), channel_id=1, source_target_pairs={{0,1},{1,0},{2,3},{3,2},{4,5},{5,4},{6,7},{7,6},{8,9},{9,8},{10,11... | collective-permute-start | bytes 1572872 | tf_op jit(solution)/shard_map/ppermute | solution.py:240
  71.6 10.4 %collective-permute-start.12 = (bf16[128,2176]{1,0:T(8,128)(2,1)S(1)}, bf16[128,2176]{1,0:T(8,128)(2,1)S(1)}, u32[]{:S(2)}, u32[]{:S(2)}) collective-permute-start(bf16[128,2176]{1,0:T(8,128)(2,1)S(1)} %collective-permute-done.8.r_3_), channel_id=1, source_target_pairs={{0,1},{1,0},{2,3},{3,2},{4,5},{5,4},{6,7},{7,6},{8,9},{9,8},{10,11... | collective-permute-start | bytes 1671176 | tf_op jit(solution)/shard_map/ppermute | solution.py:240
  77.7 2.1 collective-permute-start.5
  77.7 5.6 %collective-permute-start.11 = (bf16[128,2176]{1,0:T(8,128)(2,1)S(1)}, bf16[128,2176]{1,0:T(8,128)(2,1)S(1)}, u32[]{:S(2)}, u32[]{:S(2)}) collective-permute-start(bf16[128,2176]{1,0:T(8,128)(2,1)S(1)} %collective-permute-done.7.r_2_), channel_id=1, source_target_pairs={{0,1},{1,0},{2,3},{3,2},{4,5},{5,4},{6,7},{7,6},{8,9},{9,8},{10,11... | collective-permute-start | bytes 1671176 | tf_op jit(solution)/shard_map/ppermute | solution.py:240
  78.2 7.3 %collective-permute-start.13 = (bf16[128,2176]{1,0:T(8,128)(2,1)S(1)}, bf16[128,2176]{1,0:T(8,128)(2,1)S(1)}, u32[]{:S(2)}, u32[]{:S(2)}) collective-permute-start(bf16[128,2176]{1,0:T(8,128)(2,1)S(1)} %collective-permute-done.9.r_4_), channel_id=1, source_target_pairs={{0,1},{1,0},{2,3},{3,2},{4,5},{5,4},{6,7},{7,6},{8,9},{9,8},{10,11... | collective-permute-start | bytes 1671176 | tf_op jit(solution)/shard_map/ppermute | solution.py:240
  79.1 18.4 %collective-permute-start.6 = (bf16[128,2048]{1,0:T(8,128)(2,1)}, bf16[128,2048]{1,0:T(8,128)(2,1)}, u32[]{:S(2)}, u32[]{:S(2)}) collective-permute-start(bf16[128,2048]{1,0:T(8,128)(2,1)} %collective-permute-done.2.r_4_), channel_id=1, source_target_pairs={{0,1},{1,0},{2,3},{3,2},{4,5},{5,4},{6,7},{7,6},{8,9},{9,8},{10,11... | collective-permute-start | bytes 1572872 | tf_op jit(solution)/shard_map/ppermute | solution.py:240
  80.6 10.6 %collective-permute-start.31 = (bf16[512,384]{1,0:T(8,128)(2,1)}, bf16[512,384]{1,0:T(8,128)(2,1)}, u32[]{:S(2)}, u32[]{:S(2)}) collective-permute-start(bf16[512,384]{1,0:T(8,128)(2,1)} %collective-permute-done.30.r_12_), channel_id=1, source_target_pairs={{4,6},{5,7},{12,14},{13,15},{20,22},{21,23},{28,30},{29,31}} | collective-permute-start | bytes 1179656 | tf_op jit(solution)/shard_map/ppermute | solution.py:243
  82.0 14.2 %collective-permute-start.34 = (bf16[512,384]{1,0:T(8,128)(2,1)}, bf16[512,384]{1,0:T(8,128)(2,1)}, u32[]{:S(2)}, u32[]{:S(2)}) collective-permute-start(bf16[512,384]{1,0:T(8,128)(2,1)} %collective-permute-done.33.r_15_), channel_id=1, source_target_pairs={{2,0},{3,1},{10,8},{11,9},{18,16},{19,17},{26,24},{27,25}} | collective-permute-start | bytes 1179656 | tf_op jit(solution)/shard_map/ppermute | solution.py:243
  84.1 25.9 %collective-permute-start.25 = (bf16[512,384]{1,0:T(8,128)(2,1)}, bf16[512,384]{1,0:T(8,128)(2,1)}, u32[]{:S(2)}, u32[]{:S(2)}) collective-permute-start(bf16[512,384]{1,0:T(8,128)(2,1)} %collective-permute-done.24.r_12_), channel_id=1, source_target_pairs={{4,6},{5,7},{12,14},{13,15},{20,22},{21,23},{28,30},{29,31}} | collective-permute-start | bytes 1179656 | tf_op jit(solution)/shard_map/ppermute | solution.py:243
  86.3 24.6 %collective-permute-start.28 = (bf16[512,384]{1,0:T(8,128)(2,1)}, bf16[512,384]{1,0:T(8,128)(2,1)}, u32[]{:S(2)}, u32[]{:S(2)}) collective-permute-start(bf16[512,384]{1,0:T(8,128)(2,1)} %collective-permute-done.27.r_15_), channel_id=1, source_target_pairs={{2,0},{3,1},{10,8},{11,9},{18,16},{19,17},{26,24},{27,25}} | collective-permute-start | bytes 1179656 | tf_op jit(solution)/shard_map/ppermute | solution.py:243
  91.1 19.8 %copy-start.15 = (bf16[512,384]{1,0:T(8,128)(2,1)S(1)}, bf16[512,384]{1,0:T(8,128)(2,1)}, u32[]{:S(2)}) copy-start(bf16[512,384]{1,0:T(8,128)(2,1)} %copy-done.14) | copy-start | bytes 1179652
  91.1 19.8 %copy-start.23 = (bf16[512,384]{1,0:T(8,128)(2,1)S(1)}, bf16[512,384]{1,0:T(8,128)(2,1)}, u32[]{:S(2)}) copy-start(bf16[512,384]{1,0:T(8,128)(2,1)} %copy-done.22) | copy-start | bytes 1179652
  91.1 19.8 %copy-start.25 = (bf16[512,384]{1,0:T(8,128)(2,1)S(1)}, bf16[512,384]{1,0:T(8,128)(2,1)}, u32[]{:S(2)}) copy-start(bf16[512,384]{1,0:T(8,128)(2,1)} %copy-done.24) | copy-start | bytes 1179652
  91.2 29.1 %collective-permute-start.19 = (bf16[512,384]{1,0:T(8,128)(2,1)S(1)}, bf16[512,384]{1,0:T(8,128)(2,1)S(1)}, u32[]{:S(2)}, u32[]{:S(2)}) collective-permute-start(bf16[512,384]{1,0:T(8,128)(2,1)S(1)} %copy-done.31), channel_id=1, source_target_pairs={{4,6},{5,7},{12,14},{13,15},{20,22},{21,23},{28,30},{29,31}} | collective-permute-start | bytes 1179656 | tf_op jit(solution)/shard_map/ppermute | solution.py:243
  96.2 24.8 %collective-permute-start.22 = (bf16[512,384]{1,0:T(8,128)(2,1)S(1)}, bf16[512,384]{1,0:T(8,128)(2,1)S(1)}, u32[]{:S(2)}, u32[]{:S(2)}) collective-permute-start(bf16[512,384]{1,0:T(8,128)(2,1)S(1)} %copy-done.33), channel_id=1, source_target_pairs={{2,0},{3,1},{10,8},{11,9},{18,16},{19,17},{26,24},{27,25}} | collective-permute-start | bytes 1179656 | tf_op jit(solution)/shard_map/ppermute | solution.py:243
  105.2 31.7 %collective-permute-start.52 = (bf16[512,384]{1,0:T(8,128)(2,1)S(1)}, bf16[512,384]{1,0:T(8,128)(2,1)S(1)}, u32[]{:S(2)}, u32[]{:S(2)}) collective-permute-start(bf16[512,384]{1,0:T(8,128)(2,1)S(1)} %get-tuple-element.61), channel_id=1, source_target_pairs={{0,2},{1,3},{8,10},{9,11},{16,18},{17,19},{24,26},{25,27}} | collective-permute-start | bytes 1179656 | tf_op jit(solution)/shard_map/ppermute | solution.py:243
  110.1 27.8 %collective-permute-start.55 = (bf16[512,384]{1,0:T(8,128)(2,1)S(1)}, bf16[512,384]{1,0:T(8,128)(2,1)S(1)}, u32[]{:S(2)}, u32[]{:S(2)}) collective-permute-start(bf16[512,384]{1,0:T(8,128)(2,1)S(1)} %get-tuple-element.59), channel_id=1, source_target_pairs={{6,4},{7,5},{14,12},{15,13},{22,20},{23,21},{30,28},{31,29}} | collective-permute-start | bytes 1179656 | tf_op jit(solution)/shard_map/ppermute | solution.py:243
  118.8 19.4 %collective-permute-start.46 = (bf16[512,384]{1,0:T(8,128)(2,1)S(1)}, bf16[512,384]{1,0:T(8,128)(2,1)S(1)}, u32[]{:S(2)}, u32[]{:S(2)}) collective-permute-start(bf16[512,384]{1,0:T(8,128)(2,1)S(1)} %get-tuple-element.57), channel_id=1, source_target_pairs={{0,2},{1,3},{8,10},{9,11},{16,18},{17,19},{24,26},{25,27}} | collective-permute-start | bytes 1179656 | tf_op jit(solution)/shard_map/ppermute | solution.py:243
  120.3 19.2 %collective-permute-start.49 = (bf16[512,384]{1,0:T(8,128)(2,1)S(1)}, bf16[512,384]{1,0:T(8,128)(2,1)S(1)}, u32[]{:S(2)}, u32[]{:S(2)}) collective-permute-start(bf16[512,384]{1,0:T(8,128)(2,1)S(1)} %get-tuple-element.55), channel_id=1, source_target_pairs={{6,4},{7,5},{14,12},{15,13},{22,20},{23,21},{30,28},{31,29}} | collective-permute-start | bytes 1179656 | tf_op jit(solution)/shard_map/ppermute | solution.py:243
  129.1 11.3 %collective-permute-start.40 = (bf16[512,384]{1,0:T(8,128)(2,1)S(1)}, bf16[512,384]{1,0:T(8,128)(2,1)S(1)}, u32[]{:S(2)}, u32[]{:S(2)}) collective-permute-start(bf16[512,384]{1,0:T(8,128)(2,1)S(1)} %get-tuple-element.53), channel_id=1, source_target_pairs={{0,2},{1,3},{8,10},{9,11},{16,18},{17,19},{24,26},{25,27}} | collective-permute-start | bytes 1179656 | tf_op jit(solution)/shard_map/ppermute | solution.py:243
  137.0 7.3 %collective-permute-start.43 = (bf16[512,384]{1,0:T(8,128)(2,1)S(1)}, bf16[512,384]{1,0:T(8,128)(2,1)S(1)}, u32[]{:S(2)}, u32[]{:S(2)}) collective-permute-start(bf16[512,384]{1,0:T(8,128)(2,1)S(1)} %get-tuple-element.51), channel_id=1, source_target_pairs={{6,4},{7,5},{14,12},{15,13},{22,20},{23,21},{30,28},{31,29}} | collective-permute-start | bytes 1179656 | tf_op jit(solution)/shard_map/ppermute | solution.py:243
  137.9 64.5 %collective-permute-start.35 = (bf16[512,2048]{1,0:T(8,128)(2,1)S(1)}, bf16[512,2048]{1,0:T(8,128)(2,1)S(1)}, u32[]{:S(2)}, u32[]{:S(2)}) collective-permute-start(bf16[512,2048]{1,0:T(8,128)(2,1)S(1)} %get-tuple-element.49), channel_id=1, source_target_pairs={{0,1},{1,0},{2,3},{3,2},{4,5},{5,4},{6,7},{7,6},{8,9},{9,8},{10,11... | collective-permute-start | bytes 6291464 | tf_op jit(solution)/shard_map/ppermute | solution.py:240
  138.2 10.8 %collective-permute-start.53 = (bf16[512,384]{1,0:T(8,128)(2,1)S(1)}, bf16[512,384]{1,0:T(8,128)(2,1)S(1)}, u32[]{:S(2)}, u32[]{:S(2)}) collective-permute-start(bf16[512,384]{1,0:T(8,128)(2,1)S(1)} %get-tuple-element.100), channel_id=1, source_target_pairs={{0,2},{1,3},{2,4},{3,5},{8,10},{9,11},{10,12},{11,13},{16,18},{17,... | collective-permute-start | bytes 1179656 | tf_op jit(solution)/shard_map/ppermute | solution.py:243
  139.5 14.0 %collective-permute-start.56 = (bf16[512,384]{1,0:T(8,128)(2,1)S(1)}, bf16[512,384]{1,0:T(8,128)(2,1)S(1)}, u32[]{:S(2)}, u32[]{:S(2)}) collective-permute-start(bf16[512,384]{1,0:T(8,128)(2,1)S(1)} %get-tuple-element.101), channel_id=1, source_target_pairs={{4,2},{5,3},{6,4},{7,5},{12,10},{13,11},{14,12},{15,13},{20,18},{2... | collective-permute-start | bytes 1179656 | tf_op jit(solution)/shard_map/ppermute | solution.py:243
  140.4 17.0 %collective-permute-start.47 = (bf16[512,384]{1,0:T(8,128)(2,1)S(1)}, bf16[512,384]{1,0:T(8,128)(2,1)S(1)}, u32[]{:S(2)}, u32[]{:S(2)}) collective-permute-start(bf16[512,384]{1,0:T(8,128)(2,1)S(1)} %get-tuple-element.102), channel_id=1, source_target_pairs={{0,2},{1,3},{2,4},{3,5},{8,10},{9,11},{10,12},{11,13},{16,18},{17,... | collective-permute-start | bytes 1179656 | tf_op jit(solution)/shard_map/ppermute | solution.py:243
  144.3 17.6 %collective-permute-start.50 = (bf16[512,384]{1,0:T(8,128)(2,1)S(1)}, bf16[512,384]{1,0:T(8,128)(2,1)S(1)}, u32[]{:S(2)}, u32[]{:S(2)}) collective-permute-start(bf16[512,384]{1,0:T(8,128)(2,1)S(1)} %get-tuple-element.103), channel_id=1, source_target_pairs={{4,2},{5,3},{6,4},{7,5},{12,10},{13,11},{14,12},{15,13},{20,18},{2... | collective-permute-start | bytes 1179656 | tf_op jit(solution)/shard_map/ppermute | solution.py:243
  149.0 16.9 %collective-permute-start.41 = (bf16[512,384]{1,0:T(8,128)(2,1)S(1)}, bf16[512,384]{1,0:T(8,128)(2,1)S(1)}, u32[]{:S(2)}, u32[]{:S(2)}) collective-permute-start(bf16[512,384]{1,0:T(8,128)(2,1)S(1)} %get-tuple-element.104), channel_id=1, source_target_pairs={{0,2},{1,3},{2,4},{3,5},{8,10},{9,11},{10,12},{11,13},{16,18},{17,... | collective-permute-start | bytes 1179656 | tf_op jit(solution)/shard_map/ppermute | solution.py:243
  153.5 13.7 %collective-permute-start.44 = (bf16[512,384]{1,0:T(8,128)(2,1)S(1)}, bf16[512,384]{1,0:T(8,128)(2,1)S(1)}, u32[]{:S(2)}, u32[]{:S(2)}) collective-permute-start(bf16[512,384]{1,0:T(8,128)(2,1)S(1)} %get-tuple-element.105), channel_id=1, source_target_pairs={{4,2},{5,3},{6,4},{7,5},{12,10},{13,11},{14,12},{15,13},{20,18},{2... | collective-permute-start | bytes 1179656 | tf_op jit(solution)/shard_map/ppermute | solution.py:243
  157.4 42.3 %collective-permute-start.54 = (bf16[512,384]{1,0:T(8,128)(2,1)S(1)}, bf16[512,384]{1,0:T(8,128)(2,1)S(1)}, u32[]{:S(2)}, u32[]{:S(2)}) collective-permute-start(bf16[512,384]{1,0:T(8,128)(2,1)S(1)} %add_convert_fusion.1), channel_id=1, source_target_pairs={{0,2},{1,3},{2,4},{3,5},{4,6},{5,7},{8,10},{9,11},{10,12},{11,13},... | collective-permute-start | bytes 1179656 | tf_op jit(solution)/shard_map/ppermute | solution.py:243
  161.9 20.6 %collective-permute-start.48 = (bf16[512,384]{1,0:T(8,128)(2,1)S(1)}, bf16[512,384]{1,0:T(8,128)(2,1)S(1)}, u32[]{:S(2)}, u32[]{:S(2)}) collective-permute-start(bf16[512,384]{1,0:T(8,128)(2,1)S(1)} %add_convert_fusion.3), channel_id=1, source_target_pairs={{0,2},{1,3},{2,4},{3,5},{4,6},{5,7},{8,10},{9,11},{10,12},{11,13},... | collective-permute-start | bytes 1179656 | tf_op jit(solution)/shard_map/ppermute | solution.py:243
  165.8 21.1 %collective-permute-start.51 = (bf16[512,384]{1,0:T(8,128)(2,1)S(1)}, bf16[512,384]{1,0:T(8,128)(2,1)S(1)}, u32[]{:S(2)}, u32[]{:S(2)}) collective-permute-start(bf16[512,384]{1,0:T(8,128)(2,1)S(1)} %add_convert_fusion.2), channel_id=1, source_target_pairs={{2,0},{3,1},{4,2},{5,3},{6,4},{7,5},{10,8},{11,9},{12,10},{13,11},... | collective-permute-start | bytes 1179656 | tf_op jit(solution)/shard_map/ppermute | solution.py:243
  167.2 32.5 %collective-permute-start.57 = (bf16[512,384]{1,0:T(8,128)(2,1)S(1)}, bf16[512,384]{1,0:T(8,128)(2,1)S(1)}, u32[]{:S(2)}, u32[]{:S(2)}) collective-permute-start(bf16[512,384]{1,0:T(8,128)(2,1)S(1)} %add_convert_fusion), channel_id=1, source_target_pairs={{2,0},{3,1},{4,2},{5,3},{6,4},{7,5},{10,8},{11,9},{12,10},{13,11},... | collective-permute-start | bytes 1179656 | tf_op jit(solution)/shard_map/ppermute | solution.py:243
  182.5 12.8 %collective-permute-start.42 = (bf16[512,384]{1,0:T(8,128)(2,1)S(1)}, bf16[512,384]{1,0:T(8,128)(2,1)S(1)}, u32[]{:S(2)}, u32[]{:S(2)}) collective-permute-start(bf16[512,384]{1,0:T(8,128)(2,1)S(1)} %add_convert_fusion.5), channel_id=1, source_target_pairs={{0,2},{1,3},{2,4},{3,5},{4,6},{5,7},{8,10},{9,11},{10,12},{11,13},... | collective-permute-start | bytes 1179656 | tf_op jit(solution)/shard_map/ppermute | solution.py:243
  186.9 12.6 %collective-permute-start.45 = (bf16[512,384]{1,0:T(8,128)(2,1)S(1)}, bf16[512,384]{1,0:T(8,128)(2,1)S(1)}, u32[]{:S(2)}, u32[]{:S(2)}) collective-permute-start(bf16[512,384]{1,0:T(8,128)(2,1)S(1)} %add_convert_fusion.4), channel_id=1, source_target_pairs={{2,0},{3,1},{4,2},{5,3},{6,4},{7,5},{10,8},{11,9},{12,10},{13,11},... | collective-permute-start | bytes 1179656 | tf_op jit(solution)/shard_map/ppermute | solution.py:243
  195.3 6.2 %collective-permute-start.59 = (f32[256,384]{1,0:T(8,128)S(1)}, f32[256,384]{1,0:T(8,128)S(1)}, u32[]{:S(2)}, u32[]{:S(2)}) collective-permute-start(f32[256,384]{1,0:T(8,128)S(1)} %constant_dynamic-slice_fusion.1), channel_id=1, source_target_pairs={{0,1},{1,0},{2,3},{3,2},{4,5},{5,4},{6,7},{7,6},{8,9},{9,8},{10,11... | collective-permute-start | bytes 1179656 | tf_op jit(solution)/shard_map/ppermute | solution.py:240
  199.6 1.8 collective-permute-start.58
  199.9 2.1 collective-permute-start.60
  203.5 14.1 %collective-permute-start.36 = (bf16[2,128,1024]{2,1,0:T(8,128)(2,1)S(1)}, bf16[2,128,1024]{2,1,0:T(8,128)(2,1)S(1)}, u32[]{:S(2)}, u32[]{:S(2)}) collective-permute-start(bf16[2,128,1024]{2,1,0:T(8,128)(2,1)S(1)} %slice.141), channel_id=1, source_target_pairs={{0,16},{8,24},{16,0},{24,8},{1,17},{9,25},{17,1},{25,9},{2,18},{10... | collective-permute-start | bytes 1572872 | tf_op jit(solution)/shard_map/ppermute | solution.py:248
  206.5 14.2 %collective-permute-start.38 = (bf16[2,128,1024]{2,1,0:T(8,128)(2,1)S(1)}, bf16[2,128,1024]{2,1,0:T(8,128)(2,1)S(1)}, u32[]{:S(2)}, u32[]{:S(2)}) collective-permute-start(bf16[2,128,1024]{2,1,0:T(8,128)(2,1)S(1)} %pad_maximum_fusion), channel_id=1, source_target_pairs={{0,8},{8,0},{16,24},{24,16},{1,9},{9,1},{17,25},{25,17},{2,10},{10... | collective-permute-start | bytes 1572872 | tf_op jit(solution)/shard_map/ppermute | solution.py:248
  217.8 8.1 %collective-permute-start.37 = (bf16[128,1024]{1,0:T(8,128)(2,1)S(1)}, bf16[128,1024]{1,0:T(8,128)(2,1)S(1)}, u32[]{:S(2)}, u32[]{:S(2)}) collective-permute-start(bf16[128,1024]{1,0:T(8,128)(2,1)S(1)} %fusion.14), channel_id=1, source_target_pairs={{0,8},{8,0},{16,24},{24,16},{1,9},{9,1},{17,25},{25,17},{2,10},{10... | collective-permute-start | bytes 786440 | tf_op jit(solution)/shard_map/ppermute | solution.py:248
  220.9 6.9 %collective-permute-start.39 = (bf16[128,1024]{1,0:T(8,128)(2,1)S(1)}, bf16[128,1024]{1,0:T(8,128)(2,1)S(1)}, u32[]{:S(2)}, u32[]{:S(2)}) collective-permute-start(bf16[128,1024]{1,0:T(8,128)(2,1)S(1)} %fusion.15), channel_id=1, source_target_pairs={{0,16},{8,24},{16,0},{24,8},{1,17},{9,25},{17,1},{25,9},{2,18},{10... | collective-permute-start | bytes 786440 | tf_op jit(solution)/shard_map/ppermute | solution.py:248
  (31 other events, 116.3 us)
where the time goes:
time: 230 us; the launch traced here: 229 us
  waiting for transfers between devices  87.6 us (38%)
  starting transfers between devices  81.8 us (36%)
  Pallas kernels  32.7 us (14%)
  local copies, waits for them, and re-layouts  17.5 us (8%)
  other arithmetic  7.53 us (3%)
    ppermute x36, starting transfers between devices, along(): lax.ppermute(a, 'wide', [(2 * s + i, 2 * t + i) for s, t in hops for i in...  68.2 us
    ppermute x36, waiting for transfers between devices, along(): lax.ppermute(a, 'wide', [(2 * s + i, 2 * t + i) for s, t in hops for i in...  57.9 us
    pallas_call x7, Pallas kernels, call(): pl.pallas_call(body, out_shape=outs, in_specs=ins, out_specs=[VMEM] * len...  32.7 us
    ppermute x10, waiting for transfers between devices, flip(): return lax.ppermute(a, 'expert', [(e, e ^ bit) for e in range(experts)])  27.9 us
    unnamed x75, local copies, waits for them, and re-layouts  15.5 us
    ppermute x10, starting transfers between devices, flip(): return lax.ppermute(a, 'expert', [(e, e ^ bit) for e in range(experts)])  10.2 us
  transfers between devices with their start and end apart: 61, of which 22 were waited for; matrix products, arithmetic and copies ran while one was open for 3% of the time, Pallas kernels for 14%

commit v1 on v0

--- a/solution.py
+++ b/solution.py
@@ -1,6 +1,8 @@
 import jax
 import jax.numpy as jnp
 from jax import lax
+from jax.experimental import pallas as pl
+from jax.experimental.pallas import tpu as pltpu
 from jax.experimental import pallas as pl
 from jax.experimental.pallas import tpu as pltpu
 from jax.sharding import PartitionSpec as P
@@ -236,6 +238,9 @@
     at = jnp.stack((z, c, mine)).astype(jnp.int32)
     shape = jax.ShapeDtypeStruct
 
+    def after(a, *b):
+        return lax.optimization_barrier((a, *b))[0]
+
     def twin(a):
         return lax.ppermute(a, "wide", [(i, i ^ 1) for i in range(wide)])
 
@@ -273,12 +278,13 @@
     terms = jnp.pad(terms, ((0, 0), (0, LANES - terms.shape[1])))
     graded = jnp.concatenate((out_grad, terms), axis=1)
 
-    t = [tokens, flip(tokens, 1), flip(tokens, 2)]
-    t.append(flip(t[1], 2))
-    g = [graded, flip(graded, 1), flip(graded, 2)]
-    g.append(flip(g[2], 1))
-    t += [twin(a) for a in t]
-    g += [twin(a) for a in g]
+    with jax.named_scope("rows"):
+        t = [tokens, *(after(flip(tokens, bit), *shards) for bit in (1, 2))]
+        g = [graded, *(after(flip(graded, bit), *shards) for bit in (1, 2))]
+        t.append(flip(t[1], 2))
+        g.append(flip(g[2], 1))
+        t += [twin(a) for a in t]
+        g += [twin(a) for a in g]
     count = len(t) * rows
     [scaled] = call(
         lambda *r: scale_kernel(experts, *r),
@@ -287,31 +293,37 @@
         (at, *g),
     )
 
-    def gather(own):
+    def gather(own, before):
+        own = after(own, *before)
         ups, downs = [own], [own]
         for s in range(1, line):
-            ups.append(along(ups[-1], [(i, i + 1) for i in range(s - 1, line - 1)]))
-            downs.append(along(downs[-1], [(i, i - 1) for i in range(1, line - s + 1)]))
-        return (own, *ups[1:], *downs[1:])
-
-    def scatter(parts):
+            with jax.named_scope(f"gather_step_{s}"):
+                ups.append(along(ups[-1], [(i, i + 1) for i in range(s - 1, line - 1)]))
+                downs.append(along(downs[-1], [(i, i - 1) for i in range(1, line - s + 1)]))
+        return (own, *ups[1:], *downs[1:]), (ups[line - 2], downs[line - 2])
+
+    def scatter(parts, waits):
         up = down = None
         for s in range(1, line):
             a, b = parts[s], parts[line - s]
             if up is not None:
                 a, b = add(a, up), add(b, down)
-            up = along(a, [(i, i + 1) for i in range(s)])
-            down = along(b, [(i, i - 1) for i in range(line - s, line)])
+            if waits:
+                a, b = after(a, waits[s - 1]), after(b, waits[s - 1])
+            with jax.named_scope(f"scatter_step_{s}"):
+                up = along(a, [(i, i + 1) for i in range(s)])
+                down = along(b, [(i, i - 1) for i in range(line - s, line)])
         return parts[0].astype(F32) + up.astype(F32) + down.astype(F32)
 
-    merged, both, sums = [], [], []
+    merged, both, sums, before = [], [], [], ()
     for i in range(chunks):
+        loaded, before = gather(shards[i], before)
         got = call(
             lambda *r: chunk_kernel(line, len(t), *r),
             [SMEM] + [ANY] * (len(t) + 2 * line),
             [shape((2 * feats, 3 * step), BF16)] * line
             + [shape((count, 2 * step), BF16), shape((width, 2 * step), BF16)],
-            (at, *t, scaled, *gather(shards[i])),
+            (at, *t, scaled, *loaded),
             (
                 pltpu.VMEM((count, width), BF16),
                 pltpu.VMEM((count, width), BF16),
@@ -325,7 +337,8 @@
         )
         merged.append(got[line])
         both.append(got[line + 1])
-        sums.append(scatter(got[:line]))
+        if i < chunks - 1:
+            sums.append(scatter(got[:line], ()))
 
     block = experts * rows
     keep, give = call(
@@ -335,14 +348,20 @@
         (*merged, *both),
         flops=4 * count * width * step * chunks,
     )
-    ret = keep.astype(F32) + twin(give).astype(F32)
-    ret = ret.reshape(experts, rows, width)
-    left, right = ret[:, :, : width // 2], ret[:, :, width // 2 :]
-    left = left[:2] + flip(left[2:].astype(BF16), 2).astype(F32)
-    odd = flip(jnp.stack((right[1], right[3])).astype(BF16), 1).astype(F32)
-    left = left[0] + flip(left[1].astype(BF16), 1).astype(F32)
-    right = right[0] + odd[0] + flip((right[2] + odd[1]).astype(BF16), 2).astype(F32)
-    grad_input = jnp.concatenate((left, right), axis=1).astype(BF16)
+    with jax.named_scope("back"):
+        other = twin(give)
+        ret = keep.astype(F32) + other.astype(F32)
+        ret = ret.reshape(experts, rows, width)
+        left, right = ret[:, :, : width // 2], ret[:, :, width // 2 :]
+        far = flip(left[2:].astype(BF16), 2)
+        odd = flip(jnp.stack((right[1], right[3])).astype(BF16), 1)
+        left = left[:2] + far.astype(F32)
+        near = flip(left[1].astype(BF16), 1)
+        last = flip((right[2] + odd[1].astype(F32)).astype(BF16), 2)
+        left = left[0] + near.astype(F32)
+        right = right[0] + odd[0].astype(F32) + last.astype(F32)
+        grad_input = jnp.concatenate((left, right), axis=1).astype(BF16)
+    sums.append(scatter(got[:line], (got[0], other, odd)))
 
     own = [lax.dynamic_slice_in_dim(s, c * feats, feats, 0) for s in sums]
     other = [twin(lax.dynamic_slice_in_dim(s, (1 - c) * feats, feats, 0)) for s in sums]

time: 230 us -> 237 us (1.030)
  starting transfers between devices: 81.8 us -> 88.7 us
    ppermute x10, waiting for transfers between devices: 27.9 us -> 13.6 us  [flip(): return lax.ppermute(a, 'expert', [(e, e ^ bit) for e in range(experts)])]
    ppermute x36, waiting for transfers between devices: 57.9 us -> 71.7 us  [along(): lax.ppermute(a, 'wide', [(2 * s + i, 2 * t + i) for s, t in hops for i in...]
    ppermute x36, starting transfers between devices: 68.2 us -> 76.6 us  [along(): lax.ppermute(a, 'wide', [(2 * s + i, 2 * t + i) for s, t in hops for i in...]
    unnamed x75 -> x63, local copies, waits for them, and re-layouts: 15.5 us -> 16.3 us
  transfers between devices with their start and end apart: 61 -> 61, of which waited for: 22 -> 22; matrix products, arithmetic and copies ran while one was open for 3% -> 3% of each run, Pallas kernels for 14% -> 13%
where the time goes in v1:
time: 237 us; the launch traced here: 235 us
  starting transfers between devices  88.7 us (37%)
  waiting for transfers between devices  85.8 us (36%)
  Pallas kernels  31.7 us (13%)
  local copies, waits for them, and re-layouts  18.2 us (8%)
  other arithmetic  9.12 us (4%)
    ppermute x36, starting transfers between devices, along(): lax.ppermute(a, 'wide', [(2 * s + i, 2 * t + i) for s, t in hops for i in...  76.6 us
    ppermute x36, waiting for transfers between devices, along(): lax.ppermute(a, 'wide', [(2 * s + i, 2 * t + i) for s, t in hops for i in...  71.7 us
    pallas_call x7, Pallas kernels, call(): pl.pallas_call(body, out_shape=outs, in_specs=ins, out_specs=[VMEM] * len...  31.7 us
    unnamed x63, local copies, waits for them, and re-layouts  16.3 us
    ppermute x10, waiting for transfers between devices, flip(): return lax.ppermute(a, 'expert', [(e, e ^ bit) for e in range(experts)])  13.6 us
    ppermute x10, starting transfers between devices, flip(): return lax.ppermute(a, 'expert', [(e, e ^ bit) for e in range(experts)])  10 us
  transfers between devices with their start and end apart: 61, of which 22 were waited for; matrix products, arithmetic and copies ran while one was open for 3% of the time, Pallas kernels for 13%

profile of v1, /device:TPU:0, one launch (start us, length us, event | category | flops | bytes accessed | tf_op | source)
XLA Modules:
  0.0 235.2 jit_solution(860038101532695288)
XLA Ops:
  0.6 3.0 %collective-permute-start = (bf16[128,2048]{1,0:T(8,128)(2,1)}, bf16[128,2048]{1,0:T(8,128)(2,1)S(1)}, u32[]{:S(2)}, u32[]{:S(2)}) collective-permute-start(bf16[128,2048]{1,0:T(8,128)(2,1)} %r_1_.5), channel_id=1, source_target_pairs={{0,8},{8,0},{16,24},{24,16},{1,9},{9,1},{17,25},{25,17},{2,10},{10... | collective-permute-start | bytes 1572872 | tf_op jit(solution)/shard_map/rows/ppermute | solution.py:253
  3.6 1.5 collective-permute-start.4
  5.2 1.0 copy-done.2
  6.2 1.0 copy-done.3
  7.2 1.0 copy-done.4
  12.0 3.5 %collective-permute-start.17 = (bf16[512,384]{1,0:T(8,128)(2,1)S(1)}, bf16[512,384]{1,0:T(8,128)(2,1)S(1)}, u32[]{:S(2)}, u32[]{:S(2)}) collective-permute-start(bf16[512,384]{1,0:T(8,128)(2,1)S(1)} %get-tuple-element.51.r_10_), channel_id=1, source_target_pairs={{0,2},{1,3},{2,4},{3,5},{4,6},{5,7},{8,10},{9,11},{10,12},{11,13},... | collective-permute-start | bytes 1179656 | tf_op jit(solution)/shard_map/gather_step_1/ppermute | solution.py:248
  15.5 1.3 collective-permute-start.20
  16.8 1.1 fusion.7.r_1_
  18.5 6.0 %collective-permute-done.17.r_11_ = bf16[512,384]{1,0:T(8,128)(2,1)S(1)} collective-permute-done((bf16[512,384]{1,0:T(8,128)(2,1)S(1)}, bf16[512,384]{1,0:T(8,128)(2,1)S(1)}, u32[]{:S(2)}, u32[]{:S(2)}) %collective-permute-start.17) | collective-permute-done | bytes 393248 | tf_op jit(solution)/shard_map/gather_step_1/ppermute | solution.py:248
  25.1 3.5 %collective-permute-done.20.r_14_ = bf16[512,384]{1,0:T(8,128)(2,1)S(1)} collective-permute-done((bf16[512,384]{1,0:T(8,128)(2,1)S(1)}, bf16[512,384]{1,0:T(8,128)(2,1)S(1)}, u32[]{:S(2)}, u32[]{:S(2)}) %collective-permute-start.20) | collective-permute-done | bytes 393248 | tf_op jit(solution)/shard_map/gather_step_1/ppermute | solution.py:248
  28.6 1.3 collective-permute-start.21
  30.5 2.2 collective-permute-done.11.r_3_
  33.2 7.8 %collective-permute-done.21.r_15_ = bf16[512,384]{1,0:T(8,128)(2,1)S(1)} collective-permute-done((bf16[512,384]{1,0:T(8,128)(2,1)S(1)}, bf16[512,384]{1,0:T(8,128)(2,1)S(1)}, u32[]{:S(2)}, u32[]{:S(2)}) %collective-permute-start.21) | collective-permute-done | bytes 393248 | tf_op jit(solution)/shard_map/gather_step_2/ppermute | solution.py:248
  41.5 3.7 %collective-permute-start.23 = (bf16[512,384]{1,0:T(8,128)(2,1)S(1)}, bf16[512,384]{1,0:T(8,128)(2,1)S(1)}, u32[]{:S(2)}, u32[]{:S(2)}) collective-permute-start(bf16[512,384]{1,0:T(8,128)(2,1)S(1)} %get-tuple-element.59.r_10_), channel_id=1, source_target_pairs={{0,2},{1,3},{2,4},{3,5},{4,6},{5,7},{8,10},{9,11},{10,12},{11,13},... | collective-permute-start | bytes 1179656 | tf_op jit(solution)/shard_map/gather_step_1/ppermute | solution.py:248
  45.5 1.3 collective-permute-start.26
  46.9 6.5 %collective-permute-done.5.r_4_ = bf16[128,2048]{1,0:T(8,128)(2,1)S(1)} collective-permute-done((bf16[128,2048]{1,0:T(8,128)(2,1)S(1)}, bf16[128,2048]{1,0:T(8,128)(2,1)S(1)}, u32[]{:S(2)}, u32[]{:S(2)}) %collective-permute-start.5) | collective-permute-done | bytes 524320 | tf_op jit(solution)/shard_map/rows/ppermute | solution.py:253
  53.4 2.3 collective-permute-done.12.r_4_
  55.8 1.5 collective-permute-start.24
  57.2 1.3 collective-permute-start.27
  60.3 14.0 %collective-permute-done.27.r_15_ = bf16[512,384]{1,0:T(8,128)(2,1)} collective-permute-done((bf16[512,384]{1,0:T(8,128)(2,1)S(1)}, bf16[512,384]{1,0:T(8,128)(2,1)}, u32[]{:S(2)}, u32[]{:S(2)}) %collective-permute-start.27) | collective-permute-done | bytes 393248 | tf_op jit(solution)/shard_map/gather_step_2/ppermute | solution.py:248
  74.3 1.3 collective-permute-start.22
  75.6 1.3 shard_map.104.r_9_
  76.9 5.4 %collective-permute-start.29 = (bf16[512,384]{1,0:T(8,128)(2,1)S(1)}, bf16[512,384]{1,0:T(8,128)(2,1)}, u32[]{:S(2)}, u32[]{:S(2)}) collective-permute-start(bf16[512,384]{1,0:T(8,128)(2,1)S(1)} %get-tuple-element.61.r_10_), channel_id=1, source_target_pairs={{0,2},{1,3},{2,4},{3,5},{4,6},{5,7},{8,10},{9,11},{10,12},{11,13},... | collective-permute-start | bytes 1179656 | tf_op jit(solution)/shard_map/gather_step_1/ppermute | solution.py:248
  82.3 1.3 collective-permute-start.32
  83.6 4.2 %collective-permute-done.22.r_16_ = bf16[512,384]{1,0:T(8,128)(2,1)S(1)} collective-permute-done((bf16[512,384]{1,0:T(8,128)(2,1)S(1)}, bf16[512,384]{1,0:T(8,128)(2,1)S(1)}, u32[]{:S(2)}, u32[]{:S(2)}) %collective-permute-start.22) | collective-permute-done | bytes 393248 | tf_op jit(solution)/shard_map/gather_step_3/ppermute | solution.py:248
  87.8 7.5 %shard_map.105 = (bf16[512,384]{1,0:T(8,128)(2,1)S(1)}, bf16[512,384]{1,0:T(8,128)(2,1)S(1)}, bf16[512,384]{1,0:T(8,128)(2,1)S(1)}, bf16[512,384]{1,0:T(8,128)(2...) custom-call(s32[3]{0:T(128)S(1)} %pad_add_fusion.r_0_, bf16[128,2048]{1,0:T(8,128)(2,1)S(1)} %copy-done.5, ...), custom_call_target="tpu_custom_call" | custom-call | flops 3221225472 | bytes 14286860 | tf_op jit(solution)/shard_map/pallas_call | solution.py:100
  97.1 1.5 collective-permute-start.40
  98.6 1.4 collective-permute-start.30
  100.1 1.3 collective-permute-start.33
  101.4 1.4 collective-permute-start.43
  102.8 1.4 collective-permute-start.25
  105.9 1.3 collective-permute-start.28
  107.9 6.1 %collective-permute-done.33.r_15_ = bf16[512,384]{1,0:T(8,128)(2,1)} collective-permute-done((bf16[512,384]{1,0:T(8,128)(2,1)}, bf16[512,384]{1,0:T(8,128)(2,1)}, u32[]{:S(2)}, u32[]{:S(2)}) %collective-permute-start.33) | collective-permute-done | bytes 393248 | tf_op jit(solution)/shard_map/gather_step_2/ppermute | solution.py:248
  114.0 1.3 collective-permute-start.34
  115.3 1.3 fusion.1
  117.4 5.2 %collective-permute-start.41 = (bf16[512,384]{1,0:T(8,128)(2,1)S(1)}, bf16[512,384]{1,0:T(8,128)(2,1)S(1)}, u32[]{:S(2)}, u32[]{:S(2)}) collective-permute-start(bf16[512,384]{1,0:T(8,128)(2,1)S(1)} %get-tuple-element.128), channel_id=1, source_target_pairs={{0,2},{1,3},{2,4},{3,5},{8,10},{9,11},{10,12},{11,13},{16,18},{17,... | collective-permute-start | bytes 1179656 | tf_op jit(solution)/shard_map/scatter_step_2/ppermute | solution.py:248
  122.6 2.2 copy-done.1
  124.8 1.0 copy-done.7
  125.8 1.0 copy-done.9
  126.9 1.0 copy-done.12
  127.9 1.0 copy-done.14
  128.9 1.0 copy-done.16
  133.0 7.4 %shard_map.106 = (bf16[512,384]{1,0:T(8,128)(2,1)S(1)}, bf16[512,384]{1,0:T(8,128)(2,1)S(1)}, bf16[512,384]{1,0:T(8,128)(2,1)S(1)}, bf16[512,384]{1,0:T(8,128)(2...) custom-call(s32[3]{0:T(128)S(1)} %pad_add_fusion.r_0_, bf16[128,2048]{1,0:T(8,128)(2,1)S(1)} %copy-done.5, ...), custom_call_target="tpu_custom_call" | custom-call | flops 3221225472 | bytes 14286860 | tf_op jit(solution)/shard_map/pallas_call | solution.py:100
  140.4 4.7 %collective-permute-start.46 = (bf16[512,384]{1,0:T(8,128)(2,1)S(1)}, bf16[512,384]{1,0:T(8,128)(2,1)S(1)}, u32[]{:S(2)}, u32[]{:S(2)}) collective-permute-start(bf16[512,384]{1,0:T(8,128)(2,1)S(1)} %get-tuple-element.75), channel_id=1, source_target_pairs={{0,2},{1,3},{8,10},{9,11},{16,18},{17,19},{24,26},{25,27}} | collective-permute-start | bytes 1179656 | tf_op jit(solution)/shard_map/scatter_step_1/ppermute | solution.py:248
  146.0 7.6 %shard_map.107 = (bf16[512,384]{1,0:T(8,128)(2,1)S(1)}, bf16[512,384]{1,0:T(8,128)(2,1)S(1)}, bf16[512,384]{1,0:T(8,128)(2,1)S(1)}, bf16[512,384]{1,0:T(8,128)(2...) custom-call(s32[3]{0:T(128)S(1)} %pad_add_fusion.r_0_, bf16[128,2048]{1,0:T(8,128)(2,1)S(1)} %copy-done.5, ...), custom_call_target="tpu_custom_call" | custom-call | flops 3221225472 | bytes 14286860 | tf_op jit(solution)/shard_map/pallas_call | solution.py:100
  153.6 6.5 %shard_map.108 = (bf16[512,2048]{1,0:T(8,128)(2,1)S(1)}, bf16[512,2048]{1,0:T(8,128)(2,1)S(1)}) custom-call(bf16[1024,256]{1,0:T(8,128)(2,1)S(1)} %copy-done.26, bf16[1024,256]{1,0:T(8,128)(2,1)S(1)} %get-tuple-element.60.r_1_, bf16[1024,256]{1,0:T(8,128)(2,1)S(1)} %get-tuple-element.62.r_2_, bf16[2048,256]{1,0:T(8,128)(2,1)S(1)} %copy-done.24, ...), custom_call_target="tpu_custom_call" | custom-call | flops 3221225472 | bytes 8912896 | tf_op jit(solution)/shard_map/pallas_call | solution.py:100
  161.2 1.3 collective-permute-start.45
  162.5 4.6 %collective-permute-start.47 = (bf16[512,384]{1,0:T(8,128)(2,1)S(1)}, bf16[512,384]{1,0:T(8,128)(2,1)S(1)}, u32[]{:S(2)}, u32[]{:S(2)}) collective-permute-start(bf16[512,384]{1,0:T(8,128)(2,1)S(1)} %get-tuple-element.126), channel_id=1, source_target_pairs={{0,2},{1,3},{2,4},{3,5},{8,10},{9,11},{10,12},{11,13},{16,18},{17,... | collective-permute-start | bytes 1179656 | tf_op jit(solution)/shard_map/scatter_step_2/ppermute | solution.py:248
  167.2 2.5 %collective-permute-start.42 = (bf16[512,384]{1,0:T(8,128)(2,1)S(1)}, bf16[512,384]{1,0:T(8,128)(2,1)S(1)}, u32[]{:S(2)}, u32[]{:S(2)}) collective-permute-start(bf16[512,384]{1,0:T(8,128)(2,1)S(1)} %add_convert_fusion.5), channel_id=1, source_target_pairs={{0,2},{1,3},{2,4},{3,5},{4,6},{5,7},{8,10},{9,11},{10,12},{11,13},... | collective-permute-start | bytes 1179656 | tf_op jit(solution)/shard_map/scatter_step_3/ppermute | solution.py:248
  169.8 1.3 collective-permute-start.51
  171.1 5.4 %collective-permute-done.47 = bf16[512,384]{1,0:T(8,128)(2,1)S(1)} collective-permute-done((bf16[512,384]{1,0:T(8,128)(2,1)S(1)}, bf16[512,384]{1,0:T(8,128)(2,1)S(1)}, u32[]{:S(2)}, u32[]{:S(2)}) %collective-permute-start.47) | collective-permute-done | bytes 393248 | tf_op jit(solution)/shard_map/scatter_step_2/ppermute | solution.py:248
  176.6 4.4 %collective-permute-start.48 = (bf16[512,384]{1,0:T(8,128)(2,1)S(1)}, bf16[512,384]{1,0:T(8,128)(2,1)S(1)}, u32[]{:S(2)}, u32[]{:S(2)}) collective-permute-start(bf16[512,384]{1,0:T(8,128)(2,1)S(1)} %add_convert_fusion.3), channel_id=1, source_target_pairs={{0,2},{1,3},{2,4},{3,5},{4,6},{5,7},{8,10},{9,11},{10,12},{11,13},... | collective-permute-start | bytes 1179656 | tf_op jit(solution)/shard_map/scatter_step_3/ppermute | solution.py:248
  181.0 3.9 %collective-permute-done.42 = bf16[512,384]{1,0:T(8,128)(2,1)S(1)} collective-permute-done((bf16[512,384]{1,0:T(8,128)(2,1)S(1)}, bf16[512,384]{1,0:T(8,128)(2,1)S(1)}, u32[]{:S(2)}, u32[]{:S(2)}) %collective-permute-start.42) | collective-permute-done | bytes 393248 | tf_op jit(solution)/shard_map/scatter_step_3/ppermute | solution.py:248
  185.2 4.4 %collective-permute-start.52 = (bf16[512,384]{1,0:T(8,128)(2,1)S(1)}, bf16[512,384]{1,0:T(8,128)(2,1)S(1)}, u32[]{:S(2)}, u32[]{:S(2)}) collective-permute-start(bf16[512,384]{1,0:T(8,128)(2,1)S(1)} %get-tuple-element.80), channel_id=1, source_target_pairs={{0,2},{1,3},{8,10},{9,11},{16,18},{17,19},{24,26},{25,27}} | collective-permute-start | bytes 1179656 | tf_op jit(solution)/shard_map/scatter_step_1/ppermute | solution.py:248
  190.4 3.0 %collective-permute-done.48 = bf16[512,384]{1,0:T(8,128)(2,1)S(1)} collective-permute-done((bf16[512,384]{1,0:T(8,128)(2,1)S(1)}, bf16[512,384]{1,0:T(8,128)(2,1)S(1)}, u32[]{:S(2)}, u32[]{:S(2)}) %collective-permute-start.48) | collective-permute-done | bytes 393248 | tf_op jit(solution)/shard_map/scatter_step_3/ppermute | solution.py:248
  193.6 7.4 %collective-permute-done.52 = bf16[512,384]{1,0:T(8,128)(2,1)S(1)} collective-permute-done((bf16[512,384]{1,0:T(8,128)(2,1)S(1)}, bf16[512,384]{1,0:T(8,128)(2,1)S(1)}, u32[]{:S(2)}, u32[]{:S(2)}) %collective-permute-start.52) | collective-permute-done | bytes 393248 | tf_op jit(solution)/shard_map/scatter_step_1/ppermute | solution.py:248
  203.7 5.0 %collective-permute-start.53 = (bf16[512,384]{1,0:T(8,128)(2,1)S(1)}, bf16[512,384]{1,0:T(8,128)(2,1)S(1)}, u32[]{:S(2)}, u32[]{:S(2)}) collective-permute-start(bf16[512,384]{1,0:T(8,128)(2,1)S(1)} %get-tuple-element.81), channel_id=1, source_target_pairs={{0,2},{1,3},{2,4},{3,5},{8,10},{9,11},{10,12},{11,13},{16,18},{17,... | collective-permute-start | bytes 1179656 | tf_op jit(solution)/shard_map/scatter_step_2/ppermute | solution.py:248
  209.5 6.9 %collective-permute-done.53 = bf16[512,384]{1,0:T(8,128)(2,1)S(1)} collective-permute-done((bf16[512,384]{1,0:T(8,128)(2,1)S(1)}, bf16[512,384]{1,0:T(8,128)(2,1)S(1)}, u32[]{:S(2)}, u32[]{:S(2)}) %collective-permute-start.53) | collective-permute-done | bytes 393248 | tf_op jit(solution)/shard_map/scatter_step_2/ppermute | solution.py:248
  217.2 1.3 collective-permute-start.57
  218.5 5.0 %collective-permute-start.54 = (bf16[512,384]{1,0:T(8,128)(2,1)S(1)}, bf16[512,384]{1,0:T(8,128)(2,1)S(1)}, u32[]{:S(2)}, u32[]{:S(2)}) collective-permute-start(bf16[512,384]{1,0:T(8,128)(2,1)S(1)} %get-tuple-element.82), channel_id=1, source_target_pairs={{0,2},{1,3},{2,4},{3,5},{4,6},{5,7},{8,10},{9,11},{10,12},{11,13},... | collective-permute-start | bytes 1179656 | tf_op jit(solution)/shard_map/scatter_step_3/ppermute | solution.py:248
  224.0 1.6 collective-permute-start.37
  225.6 1.6 collective-permute-done.39
  227.3 1.4 collective-permute-done.57
  228.7 1.2 collective-permute-done.54
  (165 shorter events, 30.1 us)
Async XLA Ops:
  0.6 29.3 %collective-permute-start = (bf16[128,2048]{1,0:T(8,128)(2,1)}, bf16[128,2048]{1,0:T(8,128)(2,1)S(1)}, u32[]{:S(2)}, u32[]{:S(2)}) collective-permute-start(bf16[128,2048]{1,0:T(8,128)(2,1)} %r_1_.5), channel_id=1, source_target_pairs={{0,8},{8,0},{16,24},{24,16},{1,9},{9,1},{17,25},{25,17},{2,10},{10... | collective-permute-start | bytes 1572872 | tf_op jit(solution)/shard_map/rows/ppermute | solution.py:253
  3.6 26.9 %collective-permute-start.4 = (bf16[128,2048]{1,0:T(8,128)(2,1)}, bf16[128,2048]{1,0:T(8,128)(2,1)S(1)}, u32[]{:S(2)}, u32[]{:S(2)}) collective-permute-start(bf16[128,2048]{1,0:T(8,128)(2,1)} %r_1_.5), channel_id=1, source_target_pairs={{0,16},{8,24},{16,0},{24,8},{1,17},{9,25},{17,1},{25,9},{2,18},{10... | collective-permute-start | bytes 1572872 | tf_op jit(solution)/shard_map/rows/ppermute | solution.py:253
  9.0 2.3 collective-permute-start.1
  9.1 2.3 collective-permute-start.2
  9.6 1.8 collective-permute-start.3
  12.0 64.9 %copy-start.17 = (bf16[512,384]{1,0:T(8,128)(2,1)}, bf16[512,384]{1,0:T(8,128)(2,1)S(1)}, u32[]{:S(2)}) copy-start(bf16[512,384]{1,0:T(8,128)(2,1)S(1)} %get-tuple-element.59.r_10_) | copy-start | bytes 1179652
  12.0 12.5 %collective-permute-start.17 = (bf16[512,384]{1,0:T(8,128)(2,1)S(1)}, bf16[512,384]{1,0:T(8,128)(2,1)S(1)}, u32[]{:S(2)}, u32[]{:S(2)}) collective-permute-start(bf16[512,384]{1,0:T(8,128)(2,1)S(1)} %get-tuple-element.51.r_10_), channel_id=1, source_target_pairs={{0,2},{1,3},{2,4},{3,5},{4,6},{5,7},{8,10},{9,11},{10,12},{11,13},... | collective-permute-start | bytes 1179656 | tf_op jit(solution)/shard_map/gather_step_1/ppermute | solution.py:248
  15.5 13.1 %collective-permute-start.20 = (bf16[512,384]{1,0:T(8,128)(2,1)S(1)}, bf16[512,384]{1,0:T(8,128)(2,1)S(1)}, u32[]{:S(2)}, u32[]{:S(2)}) collective-permute-start(bf16[512,384]{1,0:T(8,128)(2,1)S(1)} %get-tuple-element.51.r_10_), channel_id=1, source_target_pairs={{2,0},{3,1},{4,2},{5,3},{6,4},{7,5},{10,8},{11,9},{12,10},{13,11},... | collective-permute-start | bytes 1179656 | tf_op jit(solution)/shard_map/gather_step_1/ppermute | solution.py:248
  17.9 14.8 %collective-permute-start.11 = (bf16[128,2176]{1,0:T(8,128)(2,1)S(1)}, bf16[128,2176]{1,0:T(8,128)(2,1)S(1)}, u32[]{:S(2)}, u32[]{:S(2)}) collective-permute-start(bf16[128,2176]{1,0:T(8,128)(2,1)S(1)} %fusion.7.r_1_), channel_id=1, source_target_pairs={{0,16},{8,24},{16,0},{24,8},{1,17},{9,25},{17,1},{25,9},{2,18},{10... | collective-permute-start | bytes 1671176 | tf_op jit(solution)/shard_map/rows/ppermute | solution.py:253
  24.5 8.2 %collective-permute-start.18 = (bf16[512,384]{1,0:T(8,128)(2,1)S(1)}, bf16[512,384]{1,0:T(8,128)(2,1)S(1)}, u32[]{:S(2)}, u32[]{:S(2)}) collective-permute-start(bf16[512,384]{1,0:T(8,128)(2,1)S(1)} %collective-permute-done.17.r_11_), channel_id=1, source_target_pairs={{2,4},{3,5},{4,6},{5,7},{10,12},{11,13},{12,14},{13,15},{18,20},{1... | collective-permute-start | bytes 1179656 | tf_op jit(solution)/shard_map/gather_step_2/ppermute | solution.py:248
  28.6 12.4 %collective-permute-start.21 = (bf16[512,384]{1,0:T(8,128)(2,1)S(1)}, bf16[512,384]{1,0:T(8,128)(2,1)S(1)}, u32[]{:S(2)}, u32[]{:S(2)}) collective-permute-start(bf16[512,384]{1,0:T(8,128)(2,1)S(1)} %collective-permute-done.20.r_14_), channel_id=1, source_target_pairs={{2,0},{3,1},{4,2},{5,3},{10,8},{11,9},{12,10},{13,11},{18,16},{19,... | collective-permute-start | bytes 1179656 | tf_op jit(solution)/shard_map/gather_step_2/ppermute | solution.py:248
  29.9 15.6 %collective-permute-start.10 = (bf16[128,2176]{1,0:T(8,128)(2,1)S(1)}, bf16[128,2176]{1,0:T(8,128)(2,1)S(1)}, u32[]{:S(2)}, u32[]{:S(2)}) collective-permute-start(bf16[128,2176]{1,0:T(8,128)(2,1)S(1)} %fusion.7.r_1_), channel_id=1, source_target_pairs={{0,8},{8,0},{16,24},{24,16},{1,9},{9,1},{17,25},{25,17},{2,10},{10... | collective-permute-start | bytes 1671176 | tf_op jit(solution)/shard_map/rows/ppermute | solution.py:253
  30.5 11.0 %collective-permute-start.6 = (bf16[128,2048]{1,0:T(8,128)(2,1)S(1)}, bf16[128,2048]{1,0:T(8,128)(2,1)S(1)}, u32[]{:S(2)}, u32[]{:S(2)}) collective-permute-start(bf16[128,2048]{1,0:T(8,128)(2,1)S(1)} %copy-done.5), channel_id=1, source_target_pairs={{0,1},{1,0},{2,3},{3,2},{4,5},{5,4},{6,7},{7,6},{8,9},{9,8},{10,11... | collective-permute-start | bytes 1572872 | tf_op jit(solution)/shard_map/rows/ppermute | solution.py:245
  32.7 14.1 %collective-permute-start.13 = (bf16[128,2176]{1,0:T(8,128)(2,1)S(1)}, bf16[128,2176]{1,0:T(8,128)(2,1)S(1)}, u32[]{:S(2)}, u32[]{:S(2)}) collective-permute-start(bf16[128,2176]{1,0:T(8,128)(2,1)S(1)} %fusion.7.r_1_), channel_id=1, source_target_pairs={{0,1},{1,0},{2,3},{3,2},{4,5},{5,4},{6,7},{7,6},{8,9},{9,8},{10,11... | collective-permute-start | bytes 1671176 | tf_op jit(solution)/shard_map/rows/ppermute | solution.py:245
  32.7 23.1 %collective-permute-start.12 = (bf16[128,2176]{1,0:T(8,128)(2,1)S(1)}, bf16[128,2176]{1,0:T(8,128)(2,1)S(1)}, u32[]{:S(2)}, u32[]{:S(2)}) collective-permute-start(bf16[128,2176]{1,0:T(8,128)(2,1)S(1)} %collective-permute-done.11.r_3_), channel_id=1, source_target_pairs={{0,8},{8,0},{16,24},{24,16},{1,9},{9,1},{17,25},{25,17},{2,10},{10... | collective-permute-start | bytes 1671176 | tf_op jit(solution)/shard_map/rows/ppermute | solution.py:253
  41.0 12.4 %collective-permute-start.5 = (bf16[128,2048]{1,0:T(8,128)(2,1)S(1)}, bf16[128,2048]{1,0:T(8,128)(2,1)S(1)}, u32[]{:S(2)}, u32[]{:S(2)}) collective-permute-start(bf16[128,2048]{1,0:T(8,128)(2,1)S(1)} %collective-permute-done.r_2_), channel_id=1, source_target_pairs={{0,16},{8,24},{16,0},{24,8},{1,17},{9,25},{17,1},{25,9},{2,18},{10... | collective-permute-start | bytes 1572872 | tf_op jit(solution)/shard_map/rows/ppermute | solution.py:253
  41.5 46.3 %copy-start.6 = (bf16[128,2048]{1,0:T(8,128)(2,1)}, bf16[128,2048]{1,0:T(8,128)(2,1)S(1)}, u32[]{:S(2)}) copy-start(bf16[128,2048]{1,0:T(8,128)(2,1)S(1)} %collective-permute-done.6.r_5_) | copy-start | bytes 1572868
  41.5 14.2 %collective-permute-start.23 = (bf16[512,384]{1,0:T(8,128)(2,1)S(1)}, bf16[512,384]{1,0:T(8,128)(2,1)S(1)}, u32[]{:S(2)}, u32[]{:S(2)}) collective-permute-start(bf16[512,384]{1,0:T(8,128)(2,1)S(1)} %get-tuple-element.59.r_10_), channel_id=1, source_target_pairs={{0,2},{1,3},{2,4},{3,5},{4,6},{5,7},{8,10},{9,11},{10,12},{11,13},... | collective-permute-start | bytes 1179656 | tf_op jit(solution)/shard_map/gather_step_1/ppermute | solution.py:248
  45.5 11.7 %collective-permute-start.26 = (bf16[512,384]{1,0:T(8,128)(2,1)S(1)}, bf16[512,384]{1,0:T(8,128)(2,1)S(1)}, u32[]{:S(2)}, u32[]{:S(2)}) collective-permute-start(bf16[512,384]{1,0:T(8,128)(2,1)S(1)} %get-tuple-element.59.r_10_), channel_id=1, source_target_pairs={{2,0},{3,1},{4,2},{5,3},{6,4},{7,5},{10,8},{11,9},{12,10},{13,11},... | collective-permute-start | bytes 1179656 | tf_op jit(solution)/shard_map/gather_step_1/ppermute | solution.py:248
  46.8 11.7 %collective-permute-start.14 = (bf16[128,2176]{1,0:T(8,128)(2,1)S(1)}, bf16[128,2176]{1,0:T(8,128)(2,1)S(1)}, u32[]{:S(2)}, u32[]{:S(2)}) collective-permute-start(bf16[128,2176]{1,0:T(8,128)(2,1)S(1)} %collective-permute-done.10.r_2_), channel_id=1, source_target_pairs={{0,1},{1,0},{2,3},{3,2},{4,5},{5,4},{6,7},{7,6},{8,9},{9,8},{10,11... | collective-permute-start | bytes 1671176 | tf_op jit(solution)/shard_map/rows/ppermute | solution.py:245
  53.4 34.3 %copy-start.8 = (bf16[128,2048]{1,0:T(8,128)(2,1)}, bf16[128,2048]{1,0:T(8,128)(2,1)S(1)}, u32[]{:S(2)}) copy-start(bf16[128,2048]{1,0:T(8,128)(2,1)S(1)} %collective-permute-done.5.r_4_) | copy-start | bytes 1572868
  53.4 5.7 %collective-permute-start.15 = (bf16[128,2176]{1,0:T(8,128)(2,1)S(1)}, bf16[128,2176]{1,0:T(8,128)(2,1)S(1)}, u32[]{:S(2)}, u32[]{:S(2)}) collective-permute-start(bf16[128,2176]{1,0:T(8,128)(2,1)S(1)} %collective-permute-done.11.r_3_), channel_id=1, source_target_pairs={{0,1},{1,0},{2,3},{3,2},{4,5},{5,4},{6,7},{7,6},{8,9},{9,8},{10,11... | collective-permute-start | bytes 1671176 | tf_op jit(solution)/shard_map/rows/ppermute | solution.py:245
  55.8 3.4 %collective-permute-start.16 = (bf16[128,2176]{1,0:T(8,128)(2,1)S(1)}, bf16[128,2176]{1,0:T(8,128)(2,1)S(1)}, u32[]{:S(2)}, u32[]{:S(2)}) collective-permute-start(bf16[128,2176]{1,0:T(8,128)(2,1)S(1)} %collective-permute-done.12.r_4_), channel_id=1, source_target_pairs={{0,1},{1,0},{2,3},{3,2},{4,5},{5,4},{6,7},{7,6},{8,9},{9,8},{10,11... | collective-permute-start | bytes 1671176 | tf_op jit(solution)/shard_map/rows/ppermute | solution.py:245
  55.8 3.8 %collective-permute-start.24 = (bf16[512,384]{1,0:T(8,128)(2,1)S(1)}, bf16[512,384]{1,0:T(8,128)(2,1)}, u32[]{:S(2)}, u32[]{:S(2)}) collective-permute-start(bf16[512,384]{1,0:T(8,128)(2,1)S(1)} %collective-permute-done.23.r_11_), channel_id=1, source_target_pairs={{2,4},{3,5},{4,6},{5,7},{10,12},{11,13},{12,14},{13,15},{18,20},{1... | collective-permute-start | bytes 1179656 | tf_op jit(solution)/shard_map/gather_step_2/ppermute | solution.py:248
  57.2 17.0 %collective-permute-start.27 = (bf16[512,384]{1,0:T(8,128)(2,1)S(1)}, bf16[512,384]{1,0:T(8,128)(2,1)}, u32[]{:S(2)}, u32[]{:S(2)}) collective-permute-start(bf16[512,384]{1,0:T(8,128)(2,1)S(1)} %collective-permute-done.26.r_14_), channel_id=1, source_target_pairs={{2,0},{3,1},{4,2},{5,3},{10,8},{11,9},{12,10},{13,11},{18,16},{19,... | collective-permute-start | bytes 1179656 | tf_op jit(solution)/shard_map/gather_step_2/ppermute | solution.py:248
  58.5 18.4 %collective-permute-start.7 = (bf16[128,2048]{1,0:T(8,128)(2,1)S(1)}, bf16[128,2048]{1,0:T(8,128)(2,1)S(1)}, u32[]{:S(2)}, u32[]{:S(2)}) collective-permute-start(bf16[128,2048]{1,0:T(8,128)(2,1)S(1)} %collective-permute-done.r_2_), channel_id=1, source_target_pairs={{0,1},{1,0},{2,3},{3,2},{4,5},{5,4},{6,7},{7,6},{8,9},{9,8},{10,11... | collective-permute-start | bytes 1572872 | tf_op jit(solution)/shard_map/rows/ppermute | solution.py:245
  59.1 23.2 %collective-permute-start.8 = (bf16[128,2048]{1,0:T(8,128)(2,1)S(1)}, bf16[128,2048]{1,0:T(8,128)(2,1)S(1)}, u32[]{:S(2)}, u32[]{:S(2)}) collective-permute-start(bf16[128,2048]{1,0:T(8,128)(2,1)S(1)} %collective-permute-done.4.r_3_), channel_id=1, source_target_pairs={{0,1},{1,0},{2,3},{3,2},{4,5},{5,4},{6,7},{7,6},{8,9},{9,8},{10,11... | collective-permute-start | bytes 1572872 | tf_op jit(solution)/shard_map/rows/ppermute | solution.py:245
  59.2 28.6 %collective-permute-start.9 = (bf16[128,2048]{1,0:T(8,128)(2,1)S(1)}, bf16[128,2048]{1,0:T(8,128)(2,1)S(1)}, u32[]{:S(2)}, u32[]{:S(2)}) collective-permute-start(bf16[128,2048]{1,0:T(8,128)(2,1)S(1)} %collective-permute-done.5.r_4_), channel_id=1, source_target_pairs={{0,1},{1,0},{2,3},{3,2},{4,5},{5,4},{6,7},{7,6},{8,9},{9,8},{10,11... | collective-permute-start | bytes 1572872 | tf_op jit(solution)/shard_map/rows/ppermute | solution.py:245
  59.6 24.0 %collective-permute-start.19 = (bf16[512,384]{1,0:T(8,128)(2,1)S(1)}, bf16[512,384]{1,0:T(8,128)(2,1)S(1)}, u32[]{:S(2)}, u32[]{:S(2)}) collective-permute-start(bf16[512,384]{1,0:T(8,128)(2,1)S(1)} %collective-permute-done.18.r_12_), channel_id=1, source_target_pairs={{4,6},{5,7},{12,14},{13,15},{20,22},{21,23},{28,30},{29,31}} | collective-permute-start | bytes 1179656 | tf_op jit(solution)/shard_map/gather_step_3/ppermute | solution.py:248
  74.3 13.5 %collective-permute-start.22 = (bf16[512,384]{1,0:T(8,128)(2,1)S(1)}, bf16[512,384]{1,0:T(8,128)(2,1)S(1)}, u32[]{:S(2)}, u32[]{:S(2)}) collective-permute-start(bf16[512,384]{1,0:T(8,128)(2,1)S(1)} %collective-permute-done.21.r_15_), channel_id=1, source_target_pairs={{2,0},{3,1},{10,8},{11,9},{18,16},{19,17},{26,24},{27,25}} | collective-permute-start | bytes 1179656 | tf_op jit(solution)/shard_map/gather_step_3/ppermute | solution.py:248
  76.9 21.7 %collective-permute-start.29 = (bf16[512,384]{1,0:T(8,128)(2,1)S(1)}, bf16[512,384]{1,0:T(8,128)(2,1)}, u32[]{:S(2)}, u32[]{:S(2)}) collective-permute-start(bf16[512,384]{1,0:T(8,128)(2,1)S(1)} %get-tuple-element.61.r_10_), channel_id=1, source_target_pairs={{0,2},{1,3},{2,4},{3,5},{4,6},{5,7},{8,10},{9,11},{10,12},{11,13},... | collective-permute-start | bytes 1179656 | tf_op jit(solution)/shard_map/gather_step_1/ppermute | solution.py:248
  82.3 17.8 %collective-permute-start.32 = (bf16[512,384]{1,0:T(8,128)(2,1)S(1)}, bf16[512,384]{1,0:T(8,128)(2,1)}, u32[]{:S(2)}, u32[]{:S(2)}) collective-permute-start(bf16[512,384]{1,0:T(8,128)(2,1)S(1)} %get-tuple-element.61.r_10_), channel_id=1, source_target_pairs={{2,0},{3,1},{4,2},{5,3},{6,4},{7,5},{10,8},{11,9},{12,10},{13,11},... | collective-permute-start | bytes 1179656 | tf_op jit(solution)/shard_map/gather_step_1/ppermute | solution.py:248
  97.1 8.0 %collective-permute-start.40 = (bf16[512,384]{1,0:T(8,128)(2,1)S(1)}, bf16[512,384]{1,0:T(8,128)(2,1)S(1)}, u32[]{:S(2)}, u32[]{:S(2)}) collective-permute-start(bf16[512,384]{1,0:T(8,128)(2,1)S(1)} %get-tuple-element.71), channel_id=1, source_target_pairs={{0,2},{1,3},{8,10},{9,11},{16,18},{17,19},{24,26},{25,27}} | collective-permute-start | bytes 1179656 | tf_op jit(solution)/shard_map/scatter_step_1/ppermute | solution.py:248
  98.6 8.6 %collective-permute-start.30 = (bf16[512,384]{1,0:T(8,128)(2,1)}, bf16[512,384]{1,0:T(8,128)(2,1)}, u32[]{:S(2)}, u32[]{:S(2)}) collective-permute-start(bf16[512,384]{1,0:T(8,128)(2,1)} %collective-permute-done.29.r_11_), channel_id=1, source_target_pairs={{2,4},{3,5},{4,6},{5,7},{10,12},{11,13},{12,14},{13,15},{18,20},{1... | collective-permute-start | bytes 1179656 | tf_op jit(solution)/shard_map/gather_step_2/ppermute | solution.py:248
  100.1 14.0 %collective-permute-start.33 = (bf16[512,384]{1,0:T(8,128)(2,1)}, bf16[512,384]{1,0:T(8,128)(2,1)}, u32[]{:S(2)}, u32[]{:S(2)}) collective-permute-start(bf16[512,384]{1,0:T(8,128)(2,1)} %collective-permute-done.32.r_14_), channel_id=1, source_target_pairs={{2,0},{3,1},{4,2},{5,3},{10,8},{11,9},{12,10},{13,11},{18,16},{19,... | collective-permute-start | bytes 1179656 | tf_op jit(solution)/shard_map/gather_step_2/ppermute | solution.py:248
  101.4 14.0 %collective-permute-start.43 = (bf16[512,384]{1,0:T(8,128)(2,1)S(1)}, bf16[512,384]{1,0:T(8,128)(2,1)}, u32[]{:S(2)}, u32[]{:S(2)}) collective-permute-start(bf16[512,384]{1,0:T(8,128)(2,1)S(1)} %get-tuple-element.69), channel_id=1, source_target_pairs={{6,4},{7,5},{14,12},{15,13},{22,20},{23,21},{30,28},{31,29}} | collective-permute-start | bytes 1179656 | tf_op jit(solution)/shard_map/scatter_step_1/ppermute | solution.py:248
  102.8 14.6 %collective-permute-start.25 = (bf16[512,384]{1,0:T(8,128)(2,1)}, bf16[512,384]{1,0:T(8,128)(2,1)}, u32[]{:S(2)}, u32[]{:S(2)}) collective-permute-start(bf16[512,384]{1,0:T(8,128)(2,1)} %collective-permute-done.24.r_12_), channel_id=1, source_target_pairs={{4,6},{5,7},{12,14},{13,15},{20,22},{21,23},{28,30},{29,31}} | collective-permute-start | bytes 1179656 | tf_op jit(solution)/shard_map/gather_step_3/ppermute | solution.py:248
  105.9 16.7 %collective-permute-start.28 = (bf16[512,384]{1,0:T(8,128)(2,1)}, bf16[512,384]{1,0:T(8,128)(2,1)}, u32[]{:S(2)}, u32[]{:S(2)}) collective-permute-start(bf16[512,384]{1,0:T(8,128)(2,1)} %collective-permute-done.27.r_15_), channel_id=1, source_target_pairs={{2,0},{3,1},{10,8},{11,9},{18,16},{19,17},{26,24},{27,25}} | collective-permute-start | bytes 1179656 | tf_op jit(solution)/shard_map/gather_step_3/ppermute | solution.py:248
  107.2 37.9 %collective-permute-start.31 = (bf16[512,384]{1,0:T(8,128)(2,1)}, bf16[512,384]{1,0:T(8,128)(2,1)S(1)}, u32[]{:S(2)}, u32[]{:S(2)}) collective-permute-start(bf16[512,384]{1,0:T(8,128)(2,1)} %collective-permute-done.30.r_12_), channel_id=1, source_target_pairs={{4,6},{5,7},{12,14},{13,15},{20,22},{21,23},{28,30},{29,31}} | collective-permute-start | bytes 1179656 | tf_op jit(solution)/shard_map/gather_step_3/ppermute | solution.py:248
  114.0 31.9 %collective-permute-start.34 = (bf16[512,384]{1,0:T(8,128)(2,1)}, bf16[512,384]{1,0:T(8,128)(2,1)S(1)}, u32[]{:S(2)}, u32[]{:S(2)}) collective-permute-start(bf16[512,384]{1,0:T(8,128)(2,1)} %collective-permute-done.33.r_15_), channel_id=1, source_target_pairs={{2,0},{3,1},{10,8},{11,9},{18,16},{19,17},{26,24},{27,25}} | collective-permute-start | bytes 1179656 | tf_op jit(solution)/shard_map/gather_step_3/ppermute | solution.py:248
  116.7 44.4 %collective-permute-start.44 = (bf16[512,384]{1,0:T(8,128)(2,1)S(1)}, bf16[512,384]{1,0:T(8,128)(2,1)S(1)}, u32[]{:S(2)}, u32[]{:S(2)}) collective-permute-start(bf16[512,384]{1,0:T(8,128)(2,1)S(1)} %get-tuple-element.129), channel_id=1, source_target_pairs={{4,2},{5,3},{6,4},{7,5},{12,10},{13,11},{14,12},{15,13},{20,18},{2... | collective-permute-start | bytes 1179656 | tf_op jit(solution)/shard_map/scatter_step_2/ppermute | solution.py:248
  117.4 49.7 %collective-permute-start.41 = (bf16[512,384]{1,0:T(8,128)(2,1)S(1)}, bf16[512,384]{1,0:T(8,128)(2,1)S(1)}, u32[]{:S(2)}, u32[]{:S(2)}) collective-permute-start(bf16[512,384]{1,0:T(8,128)(2,1)S(1)} %get-tuple-element.128), channel_id=1, source_target_pairs={{0,2},{1,3},{2,4},{3,5},{8,10},{9,11},{10,12},{11,13},{16,18},{17,... | collective-permute-start | bytes 1179656 | tf_op jit(solution)/shard_map/scatter_step_2/ppermute | solution.py:248
  140.4 19.8 %collective-permute-start.46 = (bf16[512,384]{1,0:T(8,128)(2,1)S(1)}, bf16[512,384]{1,0:T(8,128)(2,1)S(1)}, u32[]{:S(2)}, u32[]{:S(2)}) collective-permute-start(bf16[512,384]{1,0:T(8,128)(2,1)S(1)} %get-tuple-element.75), channel_id=1, source_target_pairs={{0,2},{1,3},{8,10},{9,11},{16,18},{17,19},{24,26},{25,27}} | collective-permute-start | bytes 1179656 | tf_op jit(solution)/shard_map/scatter_step_1/ppermute | solution.py:248
  145.1 15.1 %collective-permute-start.49 = (bf16[512,384]{1,0:T(8,128)(2,1)S(1)}, bf16[512,384]{1,0:T(8,128)(2,1)S(1)}, u32[]{:S(2)}, u32[]{:S(2)}) collective-permute-start(bf16[512,384]{1,0:T(8,128)(2,1)S(1)} %get-tuple-element.73), channel_id=1, source_target_pairs={{6,4},{7,5},{14,12},{15,13},{22,20},{23,21},{30,28},{31,29}} | collective-permute-start | bytes 1179656 | tf_op jit(solution)/shard_map/scatter_step_1/ppermute | solution.py:248
  160.1 41.1 %collective-permute-start.35 = (bf16[512,2048]{1,0:T(8,128)(2,1)S(1)}, bf16[512,2048]{1,0:T(8,128)(2,1)S(1)}, u32[]{:S(2)}, u32[]{:S(2)}) collective-permute-start(bf16[512,2048]{1,0:T(8,128)(2,1)S(1)} %get-tuple-element.67), channel_id=1, source_target_pairs={{0,1},{1,0},{2,3},{3,2},{4,5},{5,4},{6,7},{7,6},{8,9},{9,8},{10,11... | collective-permute-start | bytes 6291464 | tf_op jit(solution)/shard_map/back/ppermute | solution.py:245
  160.4 9.3 %collective-permute-start.50 = (bf16[512,384]{1,0:T(8,128)(2,1)S(1)}, bf16[512,384]{1,0:T(8,128)(2,1)S(1)}, u32[]{:S(2)}, u32[]{:S(2)}) collective-permute-start(bf16[512,384]{1,0:T(8,128)(2,1)S(1)} %get-tuple-element.127), channel_id=1, source_target_pairs={{4,2},{5,3},{6,4},{7,5},{12,10},{13,11},{14,12},{15,13},{20,18},{2... | collective-permute-start | bytes 1179656 | tf_op jit(solution)/shard_map/scatter_step_2/ppermute | solution.py:248
  161.2 19.8 %collective-permute-start.45 = (bf16[512,384]{1,0:T(8,128)(2,1)S(1)}, bf16[512,384]{1,0:T(8,128)(2,1)S(1)}, u32[]{:S(2)}, u32[]{:S(2)}) collective-permute-start(bf16[512,384]{1,0:T(8,128)(2,1)S(1)} %add_convert_fusion.4), channel_id=1, source_target_pairs={{2,0},{3,1},{4,2},{5,3},{6,4},{7,5},{10,8},{11,9},{12,10},{13,11},... | collective-permute-start | bytes 1179656 | tf_op jit(solution)/shard_map/scatter_step_3/ppermute | solution.py:248
  162.5 14.0 %collective-permute-start.47 = (bf16[512,384]{1,0:T(8,128)(2,1)S(1)}, bf16[512,384]{1,0:T(8,128)(2,1)S(1)}, u32[]{:S(2)}, u32[]{:S(2)}) collective-permute-start(bf16[512,384]{1,0:T(8,128)(2,1)S(1)} %get-tuple-element.126), channel_id=1, source_target_pairs={{0,2},{1,3},{2,4},{3,5},{8,10},{9,11},{10,12},{11,13},{16,18},{17,... | collective-permute-start | bytes 1179656 | tf_op jit(solution)/shard_map/scatter_step_2/ppermute | solution.py:248
  167.2 17.7 %collective-permute-start.42 = (bf16[512,384]{1,0:T(8,128)(2,1)S(1)}, bf16[512,384]{1,0:T(8,128)(2,1)S(1)}, u32[]{:S(2)}, u32[]{:S(2)}) collective-permute-start(bf16[512,384]{1,0:T(8,128)(2,1)S(1)} %add_convert_fusion.5), channel_id=1, source_target_pairs={{0,2},{1,3},{2,4},{3,5},{4,6},{5,7},{8,10},{9,11},{10,12},{11,13},... | collective-permute-start | bytes 1179656 | tf_op jit(solution)/shard_map/scatter_step_3/ppermute | solution.py:248
  169.8 19.8 %collective-permute-start.51 = (bf16[512,384]{1,0:T(8,128)(2,1)S(1)}, bf16[512,384]{1,0:T(8,128)(2,1)S(1)}, u32[]{:S(2)}, u32[]{:S(2)}) collective-permute-start(bf16[512,384]{1,0:T(8,128)(2,1)S(1)} %add_convert_fusion.2), channel_id=1, source_target_pairs={{2,0},{3,1},{4,2},{5,3},{6,4},{7,5},{10,8},{11,9},{12,10},{13,11},... | collective-permute-start | bytes 1179656 | tf_op jit(solution)/shard_map/scatter_step_3/ppermute | solution.py:248
  176.6 16.8 %collective-permute-start.48 = (bf16[512,384]{1,0:T(8,128)(2,1)S(1)}, bf16[512,384]{1,0:T(8,128)(2,1)S(1)}, u32[]{:S(2)}, u32[]{:S(2)}) collective-permute-start(bf16[512,384]{1,0:T(8,128)(2,1)S(1)} %add_convert_fusion.3), channel_id=1, source_target_pairs={{0,2},{1,3},{2,4},{3,5},{4,6},{5,7},{8,10},{9,11},{10,12},{11,13},... | collective-permute-start | bytes 1179656 | tf_op jit(solution)/shard_map/scatter_step_3/ppermute | solution.py:248
  185.2 23.6 %collective-permute-start.58 = (f32[256,384]{1,0:T(8,128)S(1)}, f32[256,384]{1,0:T(8,128)S(1)}, u32[]{:S(2)}, u32[]{:S(2)}) collective-permute-start(f32[256,384]{1,0:T(8,128)S(1)} %constant_dynamic-slice_fusion.2), channel_id=1, source_target_pairs={{0,1},{1,0},{2,3},{3,2},{4,5},{5,4},{6,7},{7,6},{8,9},{9,8},{10,11... | collective-permute-start | bytes 1179656 | tf_op jit(solution)/shard_map/ppermute | solution.py:245
  185.2 15.8 %collective-permute-start.52 = (bf16[512,384]{1,0:T(8,128)(2,1)S(1)}, bf16[512,384]{1,0:T(8,128)(2,1)S(1)}, u32[]{:S(2)}, u32[]{:S(2)}) collective-permute-start(bf16[512,384]{1,0:T(8,128)(2,1)S(1)} %get-tuple-element.80), channel_id=1, source_target_pairs={{0,2},{1,3},{8,10},{9,11},{16,18},{17,19},{24,26},{25,27}} | collective-permute-start | bytes 1179656 | tf_op jit(solution)/shard_map/scatter_step_1/ppermute | solution.py:248
  189.7 11.4 %collective-permute-start.55 = (bf16[512,384]{1,0:T(8,128)(2,1)S(1)}, bf16[512,384]{1,0:T(8,128)(2,1)S(1)}, u32[]{:S(2)}, u32[]{:S(2)}) collective-permute-start(bf16[512,384]{1,0:T(8,128)(2,1)S(1)} %get-tuple-element.83), channel_id=1, source_target_pairs={{6,4},{7,5},{14,12},{15,13},{22,20},{23,21},{30,28},{31,29}} | collective-permute-start | bytes 1179656 | tf_op jit(solution)/shard_map/scatter_step_1/ppermute | solution.py:248
  193.6 15.2 %collective-permute-start.59 = (f32[256,384]{1,0:T(8,128)S(1)}, f32[256,384]{1,0:T(8,128)S(1)}, u32[]{:S(2)}, u32[]{:S(2)}) collective-permute-start(f32[256,384]{1,0:T(8,128)S(1)} %constant_dynamic-slice_fusion.1), channel_id=1, source_target_pairs={{0,1},{1,0},{2,3},{3,2},{4,5},{5,4},{6,7},{7,6},{8,9},{9,8},{10,11... | collective-permute-start | bytes 1179656 | tf_op jit(solution)/shard_map/ppermute | solution.py:245
  202.4 14.1 %collective-permute-start.38 = (bf16[2,128,1024]{2,1,0:T(8,128)(2,1)S(1)}, bf16[2,128,1024]{2,1,0:T(8,128)(2,1)S(1)}, u32[]{:S(2)}, u32[]{:S(2)}) collective-permute-start(bf16[2,128,1024]{2,1,0:T(8,128)(2,1)S(1)} %pad_maximum_fusion), channel_id=1, source_target_pairs={{0,8},{8,0},{16,24},{24,16},{1,9},{9,1},{17,25},{25,17},{2,10},{10... | collective-permute-start | bytes 1572872 | tf_op jit(solution)/shard_map/back/ppermute | solution.py:253
  203.0 6.4 %collective-permute-start.56 = (bf16[512,384]{1,0:T(8,128)(2,1)S(1)}, bf16[512,384]{1,0:T(8,128)(2,1)S(1)}, u32[]{:S(2)}, u32[]{:S(2)}) collective-permute-start(bf16[512,384]{1,0:T(8,128)(2,1)S(1)} %get-tuple-element.84), channel_id=1, source_target_pairs={{4,2},{5,3},{6,4},{7,5},{12,10},{13,11},{14,12},{15,13},{20,18},{2... | collective-permute-start | bytes 1179656 | tf_op jit(solution)/shard_map/scatter_step_2/ppermute | solution.py:248
  203.7 12.6 %collective-permute-start.53 = (bf16[512,384]{1,0:T(8,128)(2,1)S(1)}, bf16[512,384]{1,0:T(8,128)(2,1)S(1)}, u32[]{:S(2)}, u32[]{:S(2)}) collective-permute-start(bf16[512,384]{1,0:T(8,128)(2,1)S(1)} %get-tuple-element.81), channel_id=1, source_target_pairs={{0,2},{1,3},{2,4},{3,5},{8,10},{9,11},{10,12},{11,13},{16,18},{17,... | collective-permute-start | bytes 1179656 | tf_op jit(solution)/shard_map/scatter_step_2/ppermute | solution.py:248
  208.9 14.9 %collective-permute-start.36 = (bf16[2,128,1024]{2,1,0:T(8,128)(2,1)S(1)}, bf16[2,128,1024]{2,1,0:T(8,128)(2,1)S(1)}, u32[]{:S(2)}, u32[]{:S(2)}) collective-permute-start(bf16[2,128,1024]{2,1,0:T(8,128)(2,1)S(1)} %slice.141), channel_id=1, source_target_pairs={{0,16},{8,24},{16,0},{24,8},{1,17},{9,25},{17,1},{25,9},{2,18},{10... | collective-permute-start | bytes 1572872 | tf_op jit(solution)/shard_map/back/ppermute | solution.py:253
  216.6 10.6 %collective-permute-start.39 = (bf16[128,1024]{1,0:T(8,128)(2,1)S(1)}, bf16[128,1024]{1,0:T(8,128)(2,1)S(1)}, u32[]{:S(2)}, u32[]{:S(2)}) collective-permute-start(bf16[128,1024]{1,0:T(8,128)(2,1)S(1)} %fusion.15), channel_id=1, source_target_pairs={{0,16},{8,24},{16,0},{24,8},{1,17},{9,25},{17,1},{25,9},{2,18},{10... | collective-permute-start | bytes 786440 | tf_op jit(solution)/shard_map/back/ppermute | solution.py:253
  217.2 11.5 %collective-permute-start.57 = (bf16[512,384]{1,0:T(8,128)(2,1)S(1)}, bf16[512,384]{1,0:T(8,128)(2,1)S(1)}, u32[]{:S(2)}, u32[]{:S(2)}) collective-permute-start(bf16[512,384]{1,0:T(8,128)(2,1)S(1)} %get-tuple-element.85), channel_id=1, source_target_pairs={{2,0},{3,1},{4,2},{5,3},{6,4},{7,5},{10,8},{11,9},{12,10},{13,11},... | collective-permute-start | bytes 1179656 | tf_op jit(solution)/shard_map/scatter_step_3/ppermute | solution.py:248
  218.5 11.4 %collective-permute-start.54 = (bf16[512,384]{1,0:T(8,128)(2,1)S(1)}, bf16[512,384]{1,0:T(8,128)(2,1)S(1)}, u32[]{:S(2)}, u32[]{:S(2)}) collective-permute-start(bf16[512,384]{1,0:T(8,128)(2,1)S(1)} %get-tuple-element.82), channel_id=1, source_target_pairs={{0,2},{1,3},{2,4},{3,5},{4,6},{5,7},{8,10},{9,11},{10,12},{11,13},... | collective-permute-start | bytes 1179656 | tf_op jit(solution)/shard_map/scatter_step_3/ppermute | solution.py:248
  224.0 6.4 %collective-permute-start.37 = (bf16[128,1024]{1,0:T(8,128)(2,1)S(1)}, bf16[128,1024]{1,0:T(8,128)(2,1)S(1)}, u32[]{:S(2)}, u32[]{:S(2)}) collective-permute-start(bf16[128,1024]{1,0:T(8,128)(2,1)S(1)} %fusion.14), channel_id=1, source_target_pairs={{0,8},{8,0},{16,24},{24,16},{1,9},{9,1},{17,25},{25,17},{2,10},{10... | collective-permute-start | bytes 786440 | tf_op jit(solution)/shard_map/back/ppermute | solution.py:253
  230.1 1.8 collective-permute-start.60
  (25 other events, 166.3 us)

commit v2 on v1

v2 whole, which is shorter than its diff:
```python
import jax
import jax.numpy as jnp
from jax import lax
from jax.experimental import pallas as pl
from jax.experimental.pallas import tpu as pltpu
from jax.experimental import pallas as pl
from jax.experimental.pallas import tpu as pltpu
from jax.experimental import pallas as pl
from jax.experimental.pallas import tpu as pltpu
from jax.experimental import pallas as pl
from jax.experimental.pallas import tpu as pltpu
from jax.sharding import PartitionSpec as P

LANES = 128
F32 = jnp.float32
BF16 = jnp.bfloat16


def swish_backward(gate_pre, up_pre, hidden_grad):
    squash = jax.nn.sigmoid(gate_pre)
    active = gate_pre * squash
    hidden = (active * up_pre).astype(BF16)
    gate_act = (hidden_grad * up_pre * squash * (1.0 + gate_pre * (1.0 - squash))).astype(BF16)
    up_act = (hidden_grad * active).astype(BF16)
    return (hidden, gate_act, up_act)


def dot(a, b):
    return jnp.dot(a, b, preferred_element_type=F32)


def dot_tn(a, b):
    return lax.dot_general(a, b, (((0,), (0,)), ((), ())), preferred_element_type=F32)


def dot_nt(a, b):
    return lax.dot_general(a, b, (((1,), (1,)), ((), ())), preferred_element_type=F32)


def add(a, b):
    return (a.astype(F32) + b.astype(F32)).astype(BF16)


def slot_plan(tokens, out_grad, routes, gate_prob, w_gate, w_up, w_down):
    experts = lax.axis_size("expert")
    tok_count, top_count = routes.shape
    capacity = min(tok_count, 2 * tok_count * top_count // experts)
    slot_count = experts * capacity
    model_width = tokens.shape[1]
    hidden_units = w_gate.shape[2]
    flat_routes = routes.reshape(-1)
    order = jnp.arange(tok_count * top_count, dtype=jnp.int32)
    same = flat_routes[:, None] == flat_routes[None, :]
    before = jnp.sum((same & (order[None, :] < order[:, None])).astype(jnp.int32), axis=1)
    positions = flat_routes * capacity + before
    chosen = (positions[None, :] == jnp.arange(slot_count, dtype=jnp.int32)[:, None]).reshape(
        slot_count, tok_count, top_count
    )
    picker = jnp.sum(chosen.astype(F32), axis=2)
    slot_gate = jnp.sum(jnp.where(chosen, gate_prob[None, :, :], 0.0), axis=(1, 2))
    picker_half = picker.astype(BF16)
    sent_rows = dot(picker_half, tokens).astype(BF16)
    sent_grad = (dot(picker_half, out_grad) * slot_gate[:, None]).astype(BF16)

    def exchange(rows):
        return lax.all_to_all(
            rows.reshape(experts, capacity, model_width),
            "expert",
            split_axis=0,
            concat_axis=0,
            tiled=True,
        ).reshape(slot_count, model_width)

    rows_in = exchange(sent_rows)
    grad_in = exchange(sent_grad)
    full_gate, full_up, full_down = (
        lax.all_gather(w, "wide", axis=1, tiled=True)[0] for w in (w_gate, w_up, w_down)
    )
    hidden, gate_act, up_act = swish_backward(
        dot(rows_in, full_gate), dot(rows_in, full_up), dot(grad_in, full_down)
    )
    merged = jnp.concatenate((gate_act, up_act), axis=1)
    input_grad = dot_nt(merged, jnp.concatenate((full_gate, full_up), axis=1)).astype(BF16)
    parts = jnp.concatenate((dot_tn(rows_in, merged), dot_tn(grad_in, hidden)), axis=1)
    summed = lax.psum_scatter(
        parts.astype(BF16), "wide", scatter_dimension=0, tiled=True
    ).astype(F32)
    grads = tuple(
        summed[:, i * hidden_units : (i + 1) * hidden_units][None] for i in range(3)
    )
    grad_input = dot_tn(picker_half, exchange(input_grad)).astype(BF16)
    return (grad_input,) + grads


VMEM = pl.BlockSpec(memory_space=pltpu.VMEM)
SMEM = pl.BlockSpec(memory_space=pltpu.SMEM)
ANY = pl.BlockSpec(memory_space=pl.ANY)
LIMIT = 28 << 20


def call(body, ins, outs, operands, scratch=(), flops=0, limit=LIMIT):
    moved = sum(a.size * a.dtype.itemsize for a in (*operands, *outs))
    return pl.pallas_call(
        body,
        out_shape=outs,
        in_specs=ins,
        out_specs=[VMEM] * len(outs),
        scratch_shapes=list(scratch),
        cost_estimate=pl.CostEstimate(flops=flops, bytes_accessed=moved, transcendentals=0),
        compiler_params=pltpu.CompilerParams(vmem_limit_bytes=limit),
    )(*operands)


def pack_kernel(step, gate, up, down, *outs):
    for i, out in enumerate(outs):
        for m, ref in enumerate((gate, up, down)):
            out[:, m * step : (m + 1) * step] = ref[:, i * step : (i + 1) * step]


def scale_kernel(experts, at, *refs):
    pieces, out = refs[:-1], refs[-1]
    rows, width = pieces[0].shape[0], out.shape[1]
    lane = lax.broadcasted_iota(jnp.int32, (rows, LANES), 1)
    ours = (lax.rem(lane, experts) == at[2]) & (lane < 3 * experts)
    for p, ref in enumerate(pieces):
        terms = jnp.where(ours, ref[:, width:].astype(F32), 0.0)
        gate = jnp.sum(terms, axis=1, keepdims=True)
        out[p * rows : (p + 1) * rows, :] = (gate * ref[:, :width].astype(F32)).astype(BF16)


def chunk_kernel(line, n_pieces, whole, at, *refs):
    pieces, scaled, refs = refs[:n_pieces], refs[n_pieces], refs[n_pieces + 1 :]
    n_weights = 1 if whole else 2 * (2 * line - 1)
    weights, refs = refs[:n_weights], refs[n_weights:]
    mine, theirs, merged, both = refs[:line], refs[line], refs[line + 1], refs[line + 2]
    x, g, w, hid, xsem, gsem, wsem = refs[line + 3 :]
    z, c = at[0], at[1]
    feats = w.shape[0] // (2 * line)
    step = w.shape[1] // 3
    rows = x.shape[0] // n_pieces
    parts = 2 * line
    blocks = 2
    block = x.shape[0] // blocks

    def rows_of(f):
        return pl.ds(pl.multiple_of(f * feats, feats), feats)

    def owner(k, side):
        return lax.rem(z - k + line, line) * 2 + (c if side == 0 else 1 - c)

    if whole:
        for f in range(parts):
            here = pl.ds(f * feats, feats)
            pltpu.make_async_copy(weights[0].at[here, :], w.at[here, :], wsem.at[f]).start()
    else:
        for side in range(2):
            own, *rest = weights[side * (2 * line - 1) : (side + 1) * (2 * line - 1)]
            ups, downs = rest[: line - 1], rest[line - 1 :]
            sem = wsem.at[side * line]
            pltpu.make_async_copy(own, w.at[rows_of(owner(0, side)), :], sem).start()
            for k in range(1, line):
                to = w.at[rows_of(owner(k, side)), :]
                sem = wsem.at[side * line + k]

                @pl.when(z >= k)
                def _(k=k, to=to, sem=sem, ups=ups):
                    pltpu.make_async_copy(ups[k - 1], to, sem).start()

                @pl.when(z < k)
                def _(k=k, to=to, sem=sem, downs=downs):
                    pltpu.make_async_copy(downs[line - k - 1], to, sem).start()

    x_copies = [
        pltpu.make_async_copy(ref, x.at[pl.ds(p * rows, rows), :], xsem.at[p])
        for p, ref in enumerate(pieces)
    ]
    g_copies = []
    for r in range(blocks):
        here = pl.ds(r * block, block)
        g_copies.append(pltpu.make_async_copy(scaled.at[here, :], g.at[here, :], gsem.at[r]))
    for r in range(blocks):
        for p in range(r * n_pieces // blocks, (r + 1) * n_pieces // blocks):
            x_copies[p].start()
        g_copies[r].start()
    for f in range(parts):
        part = w.at[pl.ds(f * feats, feats), :]
        pltpu.make_async_copy(part, part, wsem.at[f]).wait()

    for r in range(blocks):
        for p in range(r * n_pieces // blocks, (r + 1) * n_pieces // blocks):
            x_copies[p].wait()
        g_copies[r].wait()
        here = slice(r * block, (r + 1) * block)
        pre = dot(x[here, :], w[:, : 2 * step])
        back = dot(g[here, :], w[:, 2 * step :])
        h, a, b = swish_backward(pre[:, :step], pre[:, step:], back)
        hid[here, :] = h
        merged[here, :step] = a
        merged[here, step:] = b

    for side in (1, 0):
        for k in range(line):
            cols = rows_of(owner(k, side))
            out = theirs.at[k] if side else mine[k]
            out[:, : 2 * step] = dot_tn(x[:, cols], merged[...]).astype(BF16)
            out[:, 2 * step :] = dot_tn(g[:, cols], hid[...]).astype(BF16)
    both[...] = w[:, : 2 * step]


def route_kernel(chunks, rows, *refs):
    merged, both = refs[:chunks], refs[chunks : 2 * chunks]
    far, odd, left, right = refs[2 * chunks :]
    width = far.shape[1]
    tile = width // 4

    def emit(out, blocks, first):
        @pl.loop(0, 4)
        def _(t):
            cols = pl.ds(pl.multiple_of(t * tile, tile), tile)
            for n, b in enumerate(blocks):
                here = slice(b * rows, (b + 1) * rows)
                total = None
                for m, w in zip(merged, both):
                    wide_cols = pl.ds(pl.multiple_of(first + t * tile, tile), tile)
                    part = dot_nt(m[here, :], w[wide_cols, :])
                    total = part if total is None else total + part
                out[n * rows : (n + 1) * rows, cols] = total.astype(out.dtype)

    emit(far, (2, 3), 0)
    emit(odd, (1, 3), width)
    emit(left, (0, 1), 0)
    emit(right, (0, 2), width)


def dense_plan(tokens, out_grad, routes, gate_prob, w_gate, w_up, w_down):
    experts = lax.axis_size("expert")
    wide = lax.axis_size("wide")
    line = wide // 2
    rows, width = tokens.shape
    feats = w_gate.shape[1]
    step = 2 * LANES
    chunks = w_gate.shape[2] // step
    count = experts * rows
    mine = lax.axis_index("expert")
    place = lax.axis_index("wide")
    z, c = place // 2, place % 2
    at = jnp.stack((z, c, mine)).astype(jnp.int32)
    shape = jax.ShapeDtypeStruct

    def after(a, *b):
        return lax.optimization_barrier((a, *b))[0]

    def twin(a):
        return lax.ppermute(a, "wide", [(i, i ^ 1) for i in range(wide)])

    def along(a, hops):
        return lax.ppermute(
            a, "wide", [(2 * s + i, 2 * t + i) for s, t in hops for i in range(2)]
        )

    def flip(a, bit):
        return lax.ppermute(a, "expert", [(e, e ^ bit) for e in range(experts)])

    own = call(
        lambda *r: pack_kernel(step, *r),
        [VMEM] * 3,
        [shape((feats, 3 * step), BF16)] * chunks,
        (w_gate[0], w_up[0], w_down[0]),
    )
    whole = [lax.all_gather(a, "wide", axis=0, tiled=True) for a in own[1:]]

    def gather(a):
        ups, downs = [a], [a]
        for s in range(1, line):
            with jax.named_scope(f"gather_step_{s}"):
                ups.append(along(ups[-1], [(i, i + 1) for i in range(s - 1, line - 1)]))
                downs.append(along(downs[-1], [(i, i - 1) for i in range(1, line - s + 1)]))
        held = (a, *ups[1:], *downs[1:])
        return held + tuple(twin(p) for p in held)

    first = gather(own[0])

    named = jnp.arange(experts, dtype=jnp.int32)[None, :]
    gates = sum(
        jnp.where(routes[:, k : k + 1] == named, gate_prob[:, k : k + 1], 0.0)
        for k in range(routes.shape[1])
    )
    high = lax.reduce_precision(gates, 8, 7)
    middle = lax.reduce_precision(gates - high, 8, 7)
    terms = jnp.concatenate((high, middle, gates - high - middle), axis=1).astype(BF16)
    terms = jnp.pad(terms, ((0, 0), (0, LANES - terms.shape[1])))
    graded = jnp.concatenate((out_grad, terms), axis=1)
    with jax.named_scope("rows"):
        t = [tokens, flip(tokens, 1), flip(tokens, 2)]
        g = [graded, flip(graded, 1), flip(graded, 2)]
        t.append(flip(t[1], 2))
        g.append(flip(g[2], 1))
    [scaled] = call(
        lambda *r: scale_kernel(experts, *r),
        [SMEM] + [VMEM] * len(g),
        [shape((count, width), BF16)],
        (at, *g),
    )

    def scatter(parts, swapped, begin, last):
        def block(k, *more):
            total = parts[k].astype(F32)
            for m in (swapped[k], *more):
                total = total + m.astype(F32)
            return total.astype(BF16)

        with jax.named_scope("scatter_step_1"):
            a = jnp.where(z == 0, block(1), block(line - 1))
            up = down = along(after(a, *begin), [(0, 1), (line - 1, line - 2)])
            marks = [up]
        for s in range(2, line):
            if s == 2 and line == 4:
                a = b = block(2, up)
            elif s == 2:
                a = block(2, jnp.where(z == 1, up, 0))
                b = block(line - 2, jnp.where(z == line - 2, down, 0))
            else:
                a, b = block(s, up), block(line - s, down)
            if s == line - 1:
                a, b = after(a, *last), after(b, *last)
            with jax.named_scope(f"scatter_step_{s}"):
                up = along(a, [(i, i + 1) for i in range(s)])
                down = along(b, [(i, i - 1) for i in range(line - s, line)])
            marks.append(up)
        total = parts[0].astype(F32) + swapped[0].astype(F32)
        return total + up.astype(F32) + down.astype(F32), marks

    merged, both, sums, marks = [], [], [], ()
    for i in range(chunks):
        weights = first if i == 0 else (whole[i - 1],)
        got = call(
            lambda *r, i=i: chunk_kernel(line, len(t), i > 0, *r),
            [SMEM] + [ANY] * (len(t) + 1 + len(weights)),
            [shape((feats, 3 * step), BF16)] * line
            + [
                shape((line, feats, 3 * step), BF16),
                shape((count, 2 * step), BF16),
                shape((width, 2 * step), BF16),
            ],
            (at, *t, after(scaled, *marks[:1]), *weights),
            (
                pltpu.VMEM((count, width), BF16),
                pltpu.VMEM((count, width), BF16),
                pltpu.VMEM((width, 3 * step), BF16),
                pltpu.VMEM((count, step), BF16),
                pltpu.SemaphoreType.DMA((len(t),)),
                pltpu.SemaphoreType.DMA((2,)),
                pltpu.SemaphoreType.DMA((2 * line,)),
            ),
            flops=12 * count * width * step,
        )
        merged.append(got[line + 1])
        both.append(got[line + 2])
        swapped = twin(got[line])
        if i < chunks - 1:
            total, marks = scatter(got[:line], swapped, marks[1:2], ())
            sums.append(total)

    far, odd, left, right = call(
        lambda *r: route_kernel(chunks, rows, *r),
        [VMEM] * (2 * chunks),
        [shape((2 * rows, width // 2), BF16)] * 2 + [shape((2 * rows, width // 2), F32)] * 2,
        (*merged, *both),
        flops=4 * count * width * step * chunks,
    )
    with jax.named_scope("back"):
        far, odd = flip(far, 2), flip(odd, 1)
        left, right = left + far.astype(F32), right + odd.astype(F32)
        halfway = (left, right)
        near = flip(left[rows:].astype(BF16), 1)
        last = flip(right[rows:].astype(BF16), 2)
        left, right = left[:rows] + near.astype(F32), right[:rows] + last.astype(F32)
        grad_input = jnp.concatenate((left, right), axis=1).astype(BF16)
    sums.append(scatter(got[:line], swapped, marks[1:2], halfway)[0])

    def grad_of(j):
        cols = slice(j * step, (j + 1) * step)
        return jnp.concatenate([s[:, cols] for s in sums], axis=1)[None]

    return (grad_input, grad_of(0), grad_of(1), grad_of(2))


def solution(mesh):
    experts, wide = mesh.shape["expert"], mesh.shape["wide"]
    split = P(("expert", "wide"), None)
    weight = P("expert", "wide", None)

    def on_device(tokens, out_grad, routes, *rest):
        dense = experts == 4 and wide % 2 == 0 and 2 * routes.shape[1] >= experts
        dense = dense and rest[1].shape[2] % (2 * LANES) == 0
        return (dense_plan if dense else slot_plan)(tokens, out_grad, routes, *rest)

    return jax.shard_map(
        on_device,
        mesh=mesh,
        in_specs=(split,) * 4 + (weight,) * 3,
        out_specs=(split, weight, weight, weight),
        check_vma=False,
    )
```

time: 237 us -> 246 us (1.038)
  starting transfers between devices: 88.7 us -> 75.1 us
  between operations: 1.6 us -> 14.8 us
  other arithmetic: 9.12 us -> 13.8 us
  Pallas kernels: 31.7 us -> 36 us
  local copies, waits for them, and re-layouts: 18.2 us -> 21.7 us
  waiting for transfers between devices: 85.8 us -> 83.3 us
    ppermute x36 -> x21, starting transfers between devices: 76.6 us -> 59.5 us  [along(): lax.ppermute(a, 'wide', [(2 * s + i, 2 * t + i) for s, t in hops for i in...]
    ppermute x36 -> x21, waiting for transfers between devices: 71.7 us -> 65.3 us  [along(): lax.ppermute(a, 'wide', [(2 * s + i, 2 * t + i) for s, t in hops for i in...]
    unnamed x63 -> x94, local copies, waits for them, and re-layouts: 16.3 us -> 21.3 us
    convert_element_type x9 -> x6, other arithmetic: 2.33 us -> 6.62 us  [block(): return total.astype(BF16)]
    pallas_call x7 -> x6, Pallas kernels: 31.7 us -> 36 us  [call(): pl.pallas_call(body, out_shape=outs, in_specs=ins, out_specs=[VMEM] * len...]
    ppermute x10, starting transfers between devices: 10 us -> 14.2 us  [flip(): return lax.ppermute(a, 'expert', [(e, e ^ bit) for e in range(experts)])]
    ppermute x15 -> x10, waiting for transfers between devices: 0.54 us -> 3.47 us  [twin(): return lax.ppermute(a, 'wide', [(i, i ^ 1) for i in range(wide)])]
  transfers between devices with their start and end apart: 61 -> 43, of which waited for: 22 -> 15; matrix products, arithmetic and copies ran while one was open for 3% -> 5% of each run, Pallas kernels for 13% -> 14%
where the time goes in v2:
time: 246 us; the launch traced here: 245 us
  waiting for transfers between devices  83.3 us (34%)
  starting transfers between devices  75.1 us (31%)
  Pallas kernels  36 us (15%)
  local copies, waits for them, and re-layouts  21.7 us (9%)
  between operations  14.8 us (6%)
  other arithmetic  13.8 us (6%)
    ppermute x21, waiting for transfers between devices, along(): lax.ppermute(a, 'wide', [(2 * s + i, 2 * t + i) for s, t in hops for i in...  65.3 us
    ppermute x21, starting transfers between devices, along(): lax.ppermute(a, 'wide', [(2 * s + i, 2 * t + i) for s, t in hops for i in...  59.5 us
    pallas_call x6, Pallas kernels, call(): pl.pallas_call(body, out_shape=outs, in_specs=ins, out_specs=[VMEM] * len...  36 us
    unnamed x94, local copies, waits for them, and re-layouts  21.3 us
    ppermute x10, waiting for transfers between devices, flip(): return lax.ppermute(a, 'expert', [(e, e ^ bit) for e in range(experts)])  14.4 us
    ppermute x10, starting transfers between devices, flip(): return lax.ppermute(a, 'expert', [(e, e ^ bit) for e in range(experts)])  14.2 us
    convert_element_type x6, other arithmetic, block(): return total.astype(BF16)  6.62 us
  transfers between devices with their start and end apart: 43, of which 15 were waited for; matrix products, arithmetic and copies ran while one was open for 5% of the time, Pallas kernels for 14%

profile of v2, /device:TPU:0, one launch (start us, length us, event | category | flops | bytes accessed | tf_op | source)
XLA Modules:
  0.0 244.7 jit_solution(386056616204534028)
XLA Ops:
  7.2 1.0 copy-done.10
  8.2 1.0 copy-done.11
  9.2 1.0 copy-done.12
  10.2 1.0 shard_map.103
  11.3 5.7 %collective-permute-start.6 = (bf16[256,768]{1,0:T(8,128)(2,1)S(1)}, bf16[256,768]{1,0:T(8,128)(2,1)}, u32[]{:S(2)}, u32[]{:S(2)}) collective-permute-start(bf16[256,768]{1,0:T(8,128)(2,1)S(1)} %get-tuple-element.38.r_6_), channel_id=1, source_target_pairs={{0,2},{1,3},{2,4},{3,5},{4,6},{5,7},{8,10},{9,11},{10,12},{11,13},... | collective-permute-start | bytes 1179656 | tf_op jit(solution)/shard_map/gather_step_1/ppermute | solution.py:257
  17.0 1.3 collective-permute-start.9
  18.4 1.6 collective-permute-start
  20.2 1.6 collective-permute-start.4
  21.8 6.2 %collective-permute-done.6.r_7_ = bf16[256,768]{1,0:T(8,128)(2,1)} collective-permute-done((bf16[256,768]{1,0:T(8,128)(2,1)S(1)}, bf16[256,768]{1,0:T(8,128)(2,1)}, u32[]{:S(2)}, u32[]{:S(2)}) %collective-permute-start.6) | collective-permute-done | bytes 393248 | tf_op jit(solution)/shard_map/gather_step_1/ppermute | solution.py:257
  28.0 1.3 collective-permute-start.1
  29.2 13.2 %collective-permute-done.9.r_10_ = bf16[256,768]{1,0:T(8,128)(2,1)} collective-permute-done((bf16[256,768]{1,0:T(8,128)(2,1)S(1)}, bf16[256,768]{1,0:T(8,128)(2,1)}, u32[]{:S(2)}, u32[]{:S(2)}) %collective-permute-start.9) | collective-permute-done | bytes 393248 | tf_op jit(solution)/shard_map/gather_step_1/ppermute | solution.py:257
  42.5 1.5 collective-permute-start.3
  44.7 1.5 collective-permute-start.7
  46.2 1.3 collective-permute-start.10
  48.9 7.0 %collective-permute-done.3.r_2_ = bf16[128,2176]{1,0:T(8,128)(2,1)S(1)} collective-permute-done((bf16[128,2176]{1,0:T(8,128)(2,1)S(1)}, bf16[128,2176]{1,0:T(8,128)(2,1)S(1)}, u32[]{:S(2)}, u32[]{:S(2)}) %collective-permute-start.3) | collective-permute-done | bytes 557088 | tf_op jit(solution)/shard_map/rows/ppermute | solution.py:262
  56.7 1.4 collective-permute-start.8
  58.2 5.1 %collective-permute-done.10.r_11_ = bf16[256,768]{1,0:T(8,128)(2,1)} collective-permute-done((bf16[256,768]{1,0:T(8,128)(2,1)}, bf16[256,768]{1,0:T(8,128)(2,1)}, u32[]{:S(2)}, u32[]{:S(2)}) %collective-permute-start.10) | collective-permute-done | bytes 393248 | tf_op jit(solution)/shard_map/gather_step_2/ppermute | solution.py:257
  63.3 1.3 collective-permute-start.11
  64.6 1.6 collective-permute-start.2
  68.3 6.4 %collective-permute-done.11.r_12_ = bf16[256,768]{1,0:T(8,128)(2,1)} collective-permute-done((bf16[256,768]{1,0:T(8,128)(2,1)}, bf16[256,768]{1,0:T(8,128)(2,1)}, u32[]{:S(2)}, u32[]{:S(2)}) %collective-permute-start.11) | collective-permute-done | bytes 393248 | tf_op jit(solution)/shard_map/gather_step_3/ppermute | solution.py:257
  74.8 1.1 copy-done.3
  75.8 1.1 copy-done.5
  78.6 8.3 %shard_map.104 = (bf16[256,768]{1,0:T(8,128)(2,1)S(1)}, bf16[256,768]{1,0:T(8,128)(2,1)S(1)}, bf16[256,768]{1,0:T(8,128)(2,1)S(1)}, bf16[256,768]{1,0:T(8,128)(2...) custom-call(s32[3]{0:T(128)S(1)} %pad_add_fusion.r_0_, ...), custom_call_target="tpu_custom_call" | custom-call | flops 3221225472 | bytes 15466508 | tf_op jit(solution)/shard_map/pallas_call | solution.py:103
  88.4 1.4 copy-done.34
  91.2 3.4 %collective-permute-done.19 = bf16[4,256,768]{2,1,0:T(8,128)(2,1)} collective-permute-done((bf16[4,256,768]{2,1,0:T(8,128)(2,1)}, bf16[4,256,768]{2,1,0:T(8,128)(2,1)}, u32[]{:S(2)}, u32[]{:S(2)}) %collective-permute-start.19) | collective-permute-done | bytes 1572896 | tf_op jit(solution)/shard_map/ppermute | solution.py:254
  94.6 1.3 fusion.24
  95.9 4.0 %collective-permute-start.20 = (bf16[256,768]{1,0:T(8,128)(2,1)S(1)}, bf16[256,768]{1,0:T(8,128)(2,1)}, u32[]{:S(2)}, u32[]{:S(2)}) collective-permute-start(bf16[256,768]{1,0:T(8,128)(2,1)S(1)} %fusion.24), channel_id=1, source_target_pairs={{0,2},{1,3},{6,4},{7,5},{8,10},{9,11},{14,12},{15,13},{16,18},{17,... | collective-permute-start | bytes 1179656 | tf_op jit(solution)/shard_map/scatter_step_1/ppermute | solution.py:257
  99.9 8.3 %collective-permute-done.20 = bf16[256,768]{1,0:T(8,128)(2,1)} collective-permute-done((bf16[256,768]{1,0:T(8,128)(2,1)S(1)}, bf16[256,768]{1,0:T(8,128)(2,1)}, u32[]{:S(2)}, u32[]{:S(2)}) %collective-permute-start.20) | collective-permute-done | bytes 393248 | tf_op jit(solution)/shard_map/scatter_step_1/ppermute | solution.py:257
  108.2 1.9 copy-done.16
  110.1 1.0 copy-done.20
  111.2 1.0 copy-done.24
  112.2 7.8 %shard_map.105 = (bf16[256,768]{1,0:T(8,128)(2,1)S(1)}, bf16[256,768]{1,0:T(8,128)(2,1)S(1)}, bf16[256,768]{1,0:T(8,128)(2,1)S(1)}, bf16[256,768]{1,0:T(8,128)(2...) custom-call(s32[3]{0:T(128)S(1)} %pad_add_fusion.r_0_, ...), custom_call_target="tpu_custom_call" | custom-call | flops 3221225472 | bytes 13107212 | tf_op jit(solution)/shard_map/pallas_call | solution.py:103
  120.1 2.3 fusion.12
  122.4 4.5 %collective-permute-start.22 = (bf16[256,768]{1,0:T(8,128)(2,1)S(1)}, bf16[256,768]{1,0:T(8,128)(2,1)S(1)}, u32[]{:S(2)}, u32[]{:S(2)}) collective-permute-start(bf16[256,768]{1,0:T(8,128)(2,1)S(1)} %fusion.12), channel_id=1, source_target_pairs={{0,2},{1,3},{2,4},{3,5},{8,10},{9,11},{10,12},{11,13},{16,18},{17,... | collective-permute-start | bytes 1179656 | tf_op jit(solution)/shard_map/scatter_step_2/ppermute | solution.py:257
  127.9 7.3 %collective-permute-done.22 = bf16[256,768]{1,0:T(8,128)(2,1)S(1)} collective-permute-done((bf16[256,768]{1,0:T(8,128)(2,1)S(1)}, bf16[256,768]{1,0:T(8,128)(2,1)S(1)}, u32[]{:S(2)}, u32[]{:S(2)}) %collective-permute-start.22) | collective-permute-done | bytes 393248 | tf_op jit(solution)/shard_map/scatter_step_2/ppermute | solution.py:257
  135.3 5.4 %collective-permute-start.23 = (bf16[256,768]{1,0:T(8,128)(2,1)S(1)}, bf16[256,768]{1,0:T(8,128)(2,1)}, u32[]{:S(2)}, u32[]{:S(2)}) collective-permute-start(bf16[256,768]{1,0:T(8,128)(2,1)S(1)} %fusion.23), channel_id=1, source_target_pairs={{0,2},{1,3},{6,4},{7,5},{8,10},{9,11},{14,12},{15,13},{16,18},{17,... | collective-permute-start | bytes 1179656 | tf_op jit(solution)/shard_map/scatter_step_1/ppermute | solution.py:257
  140.7 2.4 add_convert_fusion.5
  143.0 4.1 %collective-permute-start.28 = (bf16[256,768]{1,0:T(8,128)(2,1)}, bf16[256,768]{1,0:T(8,128)(2,1)}, u32[]{:S(2)}, u32[]{:S(2)}) collective-permute-start(bf16[256,768]{1,0:T(8,128)(2,1)} %get-tuple-element.72), channel_id=1, source_target_pairs={{0,2},{1,3},{2,4},{3,5},{4,6},{5,7},{8,10},{9,11},{10,12},{11,13},... | collective-permute-start | bytes 1179656 | tf_op jit(solution)/shard_map/scatter_step_3/ppermute | solution.py:257
  147.2 1.4 collective-permute-start.30
  149.5 1.9 copy-done.17
  151.4 1.0 copy-done.21
  152.4 1.0 copy-done.25
  153.5 7.8 %shard_map.106 = (bf16[256,768]{1,0:T(8,128)(2,1)S(1)}, bf16[256,768]{1,0:T(8,128)(2,1)S(1)}, bf16[256,768]{1,0:T(8,128)(2,1)S(1)}, bf16[256,768]{1,0:T(8,128)(2...) custom-call(s32[3]{0:T(128)S(1)} %pad_add_fusion.r_0_, ...), custom_call_target="tpu_custom_call" | custom-call | flops 3221225472 | bytes 13107212 | tf_op jit(solution)/shard_map/pallas_call | solution.py:103
  161.5 1.6 fusion.10
  163.0 1.2 fusion.6
  164.2 4.5 %collective-permute-start.31 = (bf16[256,768]{1,0:T(8,128)(2,1)S(1)}, bf16[256,768]{1,0:T(8,128)(2,1)S(1)}, u32[]{:S(2)}, u32[]{:S(2)}) collective-permute-start(bf16[256,768]{1,0:T(8,128)(2,1)S(1)} %fusion.6), channel_id=1, source_target_pairs={{0,2},{1,3},{2,4},{3,5},{8,10},{9,11},{10,12},{11,13},{16,18},{17,... | collective-permute-start | bytes 1179656 | tf_op jit(solution)/shard_map/scatter_step_2/ppermute | solution.py:257
  169.5 10.2 %shard_map.107 = (bf16[256,1024]{1,0:T(8,128)(2,1)S(1)}, bf16[256,1024]{1,0:T(8,128)(2,1)S(1)}, f32[256,1024]{1,0:T(8,128)S(1)}, f32[256,1024]{1,0:T(8,128)S(1)}) custom-call(bf16[512,512]{1,0:T(8,128)(2,1)S(1)} %copy-done.39, bf16[512,512]{1,0:T(8,128)(2,1)S(1)} %copy-done.41, bf16[512,512]{1,0:T(8,128)(2,1)S(1)} %get-tuple-element.53.r_2_, ...), custom_call_target="tpu_custom_call" | custom-call | flops 3221225472 | bytes 11010048 | tf_op jit(solution)/shard_map/pallas_call | solution.py:103
  179.6 1.5 collective-permute-start.24
  181.2 1.5 collective-permute-start.26
  183.1 3.1 %collective-permute-start.32 = (bf16[256,768]{1,0:T(8,128)(2,1)S(1)}, bf16[256,768]{1,0:T(8,128)(2,1)S(1)}, u32[]{:S(2)}, u32[]{:S(2)}) collective-permute-start(bf16[256,768]{1,0:T(8,128)(2,1)S(1)} %get-tuple-element.74), channel_id=1, source_target_pairs={{0,2},{1,3},{2,4},{3,5},{4,6},{5,7},{8,10},{9,11},{10,12},{11,13},... | collective-permute-start | bytes 1179656 | tf_op jit(solution)/shard_map/scatter_step_3/ppermute | solution.py:257
  186.2 1.3 collective-permute-start.34
  187.5 6.3 %collective-permute-done.24 = bf16[256,1024]{1,0:T(8,128)(2,1)S(1)} collective-permute-done((bf16[256,1024]{1,0:T(8,128)(2,1)S(1)}, bf16[256,1024]{1,0:T(8,128)(2,1)S(1)}, u32[]{:S(2)}, u32[]{:S(2)}) %collective-permute-start.24) | collective-permute-done | bytes 524320 | tf_op jit(solution)/shard_map/back/ppermute | solution.py:262
  193.9 1.5 collective-permute-start.25
  195.7 3.1 %collective-permute-start.36 = (bf16[256,768]{1,0:T(8,128)(2,1)S(1)}, bf16[256,768]{1,0:T(8,128)(2,1)S(1)}, u32[]{:S(2)}, u32[]{:S(2)}) collective-permute-start(bf16[256,768]{1,0:T(8,128)(2,1)S(1)} %fusion.22), channel_id=1, source_target_pairs={{0,2},{1,3},{6,4},{7,5},{8,10},{9,11},{14,12},{15,13},{16,18},{17,... | collective-permute-start | bytes 1179656 | tf_op jit(solution)/shard_map/scatter_step_1/ppermute | solution.py:257
  199.0 1.5 collective-permute-start.27
  200.5 1.1 collective-permute-done.25
  201.6 4.7 %collective-permute-done.36 = bf16[256,768]{1,0:T(8,128)(2,1)S(1)} collective-permute-done((bf16[256,768]{1,0:T(8,128)(2,1)S(1)}, bf16[256,768]{1,0:T(8,128)(2,1)S(1)}, u32[]{:S(2)}, u32[]{:S(2)}) %collective-permute-start.36) | collective-permute-done | bytes 393248 | tf_op jit(solution)/shard_map/scatter_step_1/ppermute | solution.py:257
  206.5 4.4 %collective-permute-start.37 = (bf16[256,768]{1,0:T(8,128)(2,1)S(1)}, bf16[256,768]{1,0:T(8,128)(2,1)S(1)}, u32[]{:S(2)}, u32[]{:S(2)}) collective-permute-start(bf16[256,768]{1,0:T(8,128)(2,1)S(1)} %fusion.2), channel_id=1, source_target_pairs={{0,2},{1,3},{2,4},{3,5},{8,10},{9,11},{10,12},{11,13},{16,18},{17,... | collective-permute-start | bytes 1179656 | tf_op jit(solution)/shard_map/scatter_step_2/ppermute | solution.py:257
  211.9 5.7 %collective-permute-done.37 = bf16[256,768]{1,0:T(8,128)(2,1)S(1)} collective-permute-done((bf16[256,768]{1,0:T(8,128)(2,1)S(1)}, bf16[256,768]{1,0:T(8,128)(2,1)S(1)}, u32[]{:S(2)}, u32[]{:S(2)}) %collective-permute-start.37) | collective-permute-done | bytes 393248 | tf_op jit(solution)/shard_map/scatter_step_2/ppermute | solution.py:257
  217.9 7.8 %collective-permute-start.38 = (bf16[256,768]{1,0:T(8,128)(2,1)S(1)}, bf16[256,768]{1,0:T(8,128)(2,1)S(1)}, u32[]{:S(2)}, u32[]{:S(2)}) collective-permute-start(bf16[256,768]{1,0:T(8,128)(2,1)S(1)} %get-tuple-element.70), channel_id=1, source_target_pairs={{0,2},{1,3},{2,4},{3,5},{4,6},{5,7},{8,10},{9,11},{10,12},{11,13},... | collective-permute-start | bytes 1179656 | tf_op jit(solution)/shard_map/scatter_step_3/ppermute | solution.py:257
  225.7 1.3 collective-permute-start.40
  227.9 3.1 %collective-permute-done.38 = bf16[256,768]{1,0:T(8,128)(2,1)S(1)} collective-permute-done((bf16[256,768]{1,0:T(8,128)(2,1)S(1)}, bf16[256,768]{1,0:T(8,128)(2,1)S(1)}, u32[]{:S(2)}, u32[]{:S(2)}) %collective-permute-start.38) | collective-permute-done | bytes 393248 | tf_op jit(solution)/shard_map/scatter_step_3/ppermute | solution.py:257
  231.0 4.4 %collective-permute-done.40 = bf16[256,768]{1,0:T(8,128)(2,1)S(1)} collective-permute-done((bf16[256,768]{1,0:T(8,128)(2,1)S(1)}, bf16[256,768]{1,0:T(8,128)(2,1)S(1)}, u32[]{:S(2)}, u32[]{:S(2)}) %collective-permute-start.40) | collective-permute-done | bytes 393248 | tf_op jit(solution)/shard_map/scatter_step_3/ppermute | solution.py:257
  236.6 1.2 maximum_bitcast_fusion
  (155 shorter events, 17.2 us)
Async XLA Ops:
  7.2 12.8 %copy-start.45 = (s32[128,2]{0,1:T(2,128)S(1)}, s32[128,2]{0,1:T(2,128)}, u32[]{:S(2)}) copy-start(s32[128,2]{0,1:T(2,128)} %param.9) | copy-start | bytes 3076
  7.2 12.8 %copy-start.46 = (f32[128,2]{0,1:T(2,128)S(1)}, f32[128,2]{0,1:T(2,128)}, u32[]{:S(2)}) copy-start(f32[128,2]{0,1:T(2,128)} %param.10) | copy-start | bytes 3076
  7.2 101.1 %all-gather.3.cloned.1.call-start = ((), (), s32[]{:S(2)}) async-start(), calls=%async_computation | async-start | bytes 3538944 | tf_op jit(solution)/shard_map/all_gather | solution.py:270
  10.2 8.1 %copy-start.18 = (bf16[128,2048]{1,0:T(8,128)(2,1)S(1)}, bf16[128,2048]{1,0:T(8,128)(2,1)}, u32[]{:S(2)}) copy-start(bf16[128,2048]{1,0:T(8,128)(2,1)} %r_1_.5) | copy-start | bytes 1572868
  10.2 9.9 %copy-start.44 = (bf16[128,2048]{1,0:T(8,128)(2,1)S(1)}, bf16[128,2048]{1,0:T(8,128)(2,1)}, u32[]{:S(2)}) copy-start(bf16[128,2048]{1,0:T(8,128)(2,1)} %param.8) | copy-start | bytes 1572868
  11.2 63.5 %copy-start.26 = (bf16[256,768]{1,0:T(8,128)(2,1)}, bf16[256,768]{1,0:T(8,128)(2,1)S(1)}, u32[]{:S(2)}) copy-start(bf16[256,768]{1,0:T(8,128)(2,1)S(1)} %get-tuple-element.38.r_6_) | copy-start | bytes 1179652
  11.2 138.3 %all-gather.5.cloned.1.call-start = ((), (), s32[]{:S(2)}) async-start(), calls=%async_computation.1 | async-start | bytes 3538944 | tf_op jit(solution)/shard_map/all_gather | solution.py:270
  11.3 16.7 %collective-permute-start.6 = (bf16[256,768]{1,0:T(8,128)(2,1)S(1)}, bf16[256,768]{1,0:T(8,128)(2,1)}, u32[]{:S(2)}, u32[]{:S(2)}) collective-permute-start(bf16[256,768]{1,0:T(8,128)(2,1)S(1)} %get-tuple-element.38.r_6_), channel_id=1, source_target_pairs={{0,2},{1,3},{2,4},{3,5},{4,6},{5,7},{8,10},{9,11},{10,12},{11,13},... | collective-permute-start | bytes 1179656 | tf_op jit(solution)/shard_map/gather_step_1/ppermute | solution.py:257
  17.0 25.5 %collective-permute-start.9 = (bf16[256,768]{1,0:T(8,128)(2,1)S(1)}, bf16[256,768]{1,0:T(8,128)(2,1)}, u32[]{:S(2)}, u32[]{:S(2)}) collective-permute-start(bf16[256,768]{1,0:T(8,128)(2,1)S(1)} %get-tuple-element.38.r_6_), channel_id=1, source_target_pairs={{2,0},{3,1},{4,2},{5,3},{6,4},{7,5},{10,8},{11,9},{12,10},{13,11},... | collective-permute-start | bytes 1179656 | tf_op jit(solution)/shard_map/gather_step_1/ppermute | solution.py:257
  18.3 25.7 %collective-permute-start.12 = (bf16[256,768]{1,0:T(8,128)(2,1)S(1)}, bf16[256,768]{1,0:T(8,128)(2,1)S(1)}, u32[]{:S(2)}, u32[]{:S(2)}) collective-permute-start(bf16[256,768]{1,0:T(8,128)(2,1)S(1)} %get-tuple-element.38.r_6_), channel_id=1, source_target_pairs={{0,1},{1,0},{2,3},{3,2},{4,5},{5,4},{6,7},{7,6},{8,9},{9,8},{10,11... | collective-permute-start | bytes 1179656 | tf_op jit(solution)/shard_map/ppermute | solution.py:254
  18.4 27.8 %collective-permute-start = (bf16[128,2048]{1,0:T(8,128)(2,1)S(1)}, bf16[128,2048]{1,0:T(8,128)(2,1)}, u32[]{:S(2)}, u32[]{:S(2)}) collective-permute-start(bf16[128,2048]{1,0:T(8,128)(2,1)S(1)} %copy-done.18), channel_id=1, source_target_pairs={{0,8},{8,0},{16,24},{24,16},{1,9},{9,1},{17,25},{25,17},{2,10},{10... | collective-permute-start | bytes 1572872 | tf_op jit(solution)/shard_map/rows/ppermute | solution.py:262
  20.2 27.3 %collective-permute-start.4 = (bf16[128,2176]{1,0:T(8,128)(2,1)S(1)}, bf16[128,2176]{1,0:T(8,128)(2,1)S(1)}, u32[]{:S(2)}, u32[]{:S(2)}) collective-permute-start(bf16[128,2176]{1,0:T(8,128)(2,1)S(1)} %fusion.19.r_1_), channel_id=1, source_target_pairs={{0,16},{8,24},{16,0},{24,8},{1,17},{9,25},{17,1},{25,9},{2,18},{10... | collective-permute-start | bytes 1671176 | tf_op jit(solution)/shard_map/rows/ppermute | solution.py:262
  28.0 20.1 %collective-permute-start.1 = (bf16[128,2048]{1,0:T(8,128)(2,1)S(1)}, bf16[128,2048]{1,0:T(8,128)(2,1)S(1)}, u32[]{:S(2)}, u32[]{:S(2)}) collective-permute-start(bf16[128,2048]{1,0:T(8,128)(2,1)S(1)} %copy-done.18), channel_id=1, source_target_pairs={{0,16},{8,24},{16,0},{24,8},{1,17},{9,25},{17,1},{25,9},{2,18},{10... | collective-permute-start | bytes 1572872 | tf_op jit(solution)/shard_map/rows/ppermute | solution.py:262
  42.5 13.5 %collective-permute-start.3 = (bf16[128,2176]{1,0:T(8,128)(2,1)S(1)}, bf16[128,2176]{1,0:T(8,128)(2,1)S(1)}, u32[]{:S(2)}, u32[]{:S(2)}) collective-permute-start(bf16[128,2176]{1,0:T(8,128)(2,1)S(1)} %fusion.19.r_1_), channel_id=1, source_target_pairs={{0,8},{8,0},{16,24},{24,16},{1,9},{9,1},{17,25},{25,17},{2,10},{10... | collective-permute-start | bytes 1671176 | tf_op jit(solution)/shard_map/rows/ppermute | solution.py:262
  44.7 12.0 %collective-permute-start.7 = (bf16[256,768]{1,0:T(8,128)(2,1)}, bf16[256,768]{1,0:T(8,128)(2,1)}, u32[]{:S(2)}, u32[]{:S(2)}) collective-permute-start(bf16[256,768]{1,0:T(8,128)(2,1)} %collective-permute-done.6.r_7_), channel_id=1, source_target_pairs={{2,4},{3,5},{4,6},{5,7},{10,12},{11,13},{12,14},{13,15},{18,20},{1... | collective-permute-start | bytes 1179656 | tf_op jit(solution)/shard_map/gather_step_2/ppermute | solution.py:257
  46.2 17.1 %collective-permute-start.10 = (bf16[256,768]{1,0:T(8,128)(2,1)}, bf16[256,768]{1,0:T(8,128)(2,1)}, u32[]{:S(2)}, u32[]{:S(2)}) collective-permute-start(bf16[256,768]{1,0:T(8,128)(2,1)} %collective-permute-done.9.r_10_), channel_id=1, source_target_pairs={{2,0},{3,1},{4,2},{5,3},{10,8},{11,9},{12,10},{13,11},{18,16},{19,... | collective-permute-start | bytes 1179656 | tf_op jit(solution)/shard_map/gather_step_2/ppermute | solution.py:257
  47.5 19.5 %collective-permute-start.5 = (bf16[128,2176]{1,0:T(8,128)(2,1)S(1)}, bf16[128,2176]{1,0:T(8,128)(2,1)S(1)}, u32[]{:S(2)}, u32[]{:S(2)}) collective-permute-start(bf16[128,2176]{1,0:T(8,128)(2,1)S(1)} %collective-permute-done.4.r_3_), channel_id=1, source_target_pairs={{0,8},{8,0},{16,24},{24,16},{1,9},{9,1},{17,25},{25,17},{2,10},{10... | collective-permute-start | bytes 1671176 | tf_op jit(solution)/shard_map/rows/ppermute | solution.py:262
  48.9 15.7 %collective-permute-start.13 = (bf16[256,768]{1,0:T(8,128)(2,1)}, bf16[256,768]{1,0:T(8,128)(2,1)S(1)}, u32[]{:S(2)}, u32[]{:S(2)}) collective-permute-start(bf16[256,768]{1,0:T(8,128)(2,1)} %collective-permute-done.6.r_7_), channel_id=1, source_target_pairs={{0,1},{1,0},{2,3},{3,2},{4,5},{5,4},{6,7},{7,6},{8,9},{9,8},{10,11... | collective-permute-start | bytes 1179656 | tf_op jit(solution)/shard_map/ppermute | solution.py:254
  56.7 9.5 %collective-permute-start.16 = (bf16[256,768]{1,0:T(8,128)(2,1)}, bf16[256,768]{1,0:T(8,128)(2,1)S(1)}, u32[]{:S(2)}, u32[]{:S(2)}) collective-permute-start(bf16[256,768]{1,0:T(8,128)(2,1)} %collective-permute-done.9.r_10_), channel_id=1, source_target_pairs={{0,1},{1,0},{2,3},{3,2},{4,5},{5,4},{6,7},{7,6},{8,9},{9,8},{10,11... | collective-permute-start | bytes 1179656 | tf_op jit(solution)/shard_map/ppermute | solution.py:254
  56.7 11.5 %collective-permute-start.8 = (bf16[256,768]{1,0:T(8,128)(2,1)}, bf16[256,768]{1,0:T(8,128)(2,1)}, u32[]{:S(2)}, u32[]{:S(2)}) collective-permute-start(bf16[256,768]{1,0:T(8,128)(2,1)} %collective-permute-done.7.r_8_), channel_id=1, source_target_pairs={{4,6},{5,7},{12,14},{13,15},{20,22},{21,23},{28,30},{29,31}} | collective-permute-start | bytes 1179656 | tf_op jit(solution)/shard_map/gather_step_3/ppermute | solution.py:257
  63.3 11.4 %collective-permute-start.11 = (bf16[256,768]{1,0:T(8,128)(2,1)}, bf16[256,768]{1,0:T(8,128)(2,1)}, u32[]{:S(2)}, u32[]{:S(2)}) collective-permute-start(bf16[256,768]{1,0:T(8,128)(2,1)} %collective-permute-done.10.r_11_), channel_id=1, source_target_pairs={{2,0},{3,1},{10,8},{11,9},{18,16},{19,17},{26,24},{27,25}} | collective-permute-start | bytes 1179656 | tf_op jit(solution)/shard_map/gather_step_3/ppermute | solution.py:257
  64.6 10.1 %copy-start.30 = (bf16[256,768]{1,0:T(8,128)(2,1)}, bf16[256,768]{1,0:T(8,128)(2,1)S(1)}, u32[]{:S(2)}) copy-start(bf16[256,768]{1,0:T(8,128)(2,1)S(1)} %collective-permute-done.13.r_14_) | copy-start | bytes 1179652
  64.6 13.3 %collective-permute-start.2 = (bf16[128,2048]{1,0:T(8,128)(2,1)}, bf16[128,2048]{1,0:T(8,128)(2,1)}, u32[]{:S(2)}, u32[]{:S(2)}) collective-permute-start(bf16[128,2048]{1,0:T(8,128)(2,1)} %collective-permute-done.r_2_), channel_id=1, source_target_pairs={{0,16},{8,24},{16,0},{24,8},{1,17},{9,25},{17,1},{25,9},{2,18},{10... | collective-permute-start | bytes 1572872 | tf_op jit(solution)/shard_map/rows/ppermute | solution.py:262
  66.9 11.0 %collective-permute-start.14 = (bf16[256,768]{1,0:T(8,128)(2,1)}, bf16[256,768]{1,0:T(8,128)(2,1)}, u32[]{:S(2)}, u32[]{:S(2)}) collective-permute-start(bf16[256,768]{1,0:T(8,128)(2,1)} %collective-permute-done.7.r_8_), channel_id=1, source_target_pairs={{0,1},{1,0},{2,3},{3,2},{4,5},{5,4},{6,7},{7,6},{8,9},{9,8},{10,11... | collective-permute-start | bytes 1179656 | tf_op jit(solution)/shard_map/ppermute | solution.py:254
  67.8 10.2 %collective-permute-start.17 = (bf16[256,768]{1,0:T(8,128)(2,1)}, bf16[256,768]{1,0:T(8,128)(2,1)}, u32[]{:S(2)}, u32[]{:S(2)}) collective-permute-start(bf16[256,768]{1,0:T(8,128)(2,1)} %collective-permute-done.10.r_11_), channel_id=1, source_target_pairs={{0,1},{1,0},{2,3},{3,2},{4,5},{5,4},{6,7},{7,6},{8,9},{9,8},{10,11... | collective-permute-start | bytes 1179656 | tf_op jit(solution)/shard_map/ppermute | solution.py:254
  68.3 9.7 %collective-permute-start.15 = (bf16[256,768]{1,0:T(8,128)(2,1)}, bf16[256,768]{1,0:T(8,128)(2,1)}, u32[]{:S(2)}, u32[]{:S(2)}) collective-permute-start(bf16[256,768]{1,0:T(8,128)(2,1)} %collective-permute-done.8.r_9_), channel_id=1, source_target_pairs={{0,1},{1,0},{2,3},{3,2},{4,5},{5,4},{6,7},{7,6},{8,9},{9,8},{10,11... | collective-permute-start | bytes 1179656 | tf_op jit(solution)/shard_map/ppermute | solution.py:254
  74.7 3.2 %collective-permute-start.18 = (bf16[256,768]{1,0:T(8,128)(2,1)}, bf16[256,768]{1,0:T(8,128)(2,1)}, u32[]{:S(2)}, u32[]{:S(2)}) collective-permute-start(bf16[256,768]{1,0:T(8,128)(2,1)} %collective-permute-done.11.r_12_), channel_id=1, source_target_pairs={{0,1},{1,0},{2,3},{3,2},{4,5},{5,4},{6,7},{7,6},{8,9},{9,8},{10,11... | collective-permute-start | bytes 1179656 | tf_op jit(solution)/shard_map/ppermute | solution.py:254
  90.6 17.7 %copy-start = (bf16[256,768]{1,0:T(8,128)(2,1)}, bf16[256,768]{1,0:T(8,128)(2,1)S(1)}, u32[]{:S(2)}) copy-start(bf16[256,768]{1,0:T(8,128)(2,1)S(1)} %get-tuple-element.42) | copy-start | bytes 1179652
  90.6 4.0 %collective-permute-start.19 = (bf16[4,256,768]{2,1,0:T(8,128)(2,1)}, bf16[4,256,768]{2,1,0:T(8,128)(2,1)}, u32[]{:S(2)}, u32[]{:S(2)}) collective-permute-start(bf16[4,256,768]{2,1,0:T(8,128)(2,1)} %get-tuple-element.41), channel_id=1, source_target_pairs={{0,1},{1,0},{2,3},{3,2},{4,5},{5,4},{6,7},{7,6},{8,9},{9,8},{10,11... | collective-permute-start | bytes 4718600 | tf_op jit(solution)/shard_map/ppermute | solution.py:254
  95.9 12.3 %collective-permute-start.20 = (bf16[256,768]{1,0:T(8,128)(2,1)S(1)}, bf16[256,768]{1,0:T(8,128)(2,1)}, u32[]{:S(2)}, u32[]{:S(2)}) collective-permute-start(bf16[256,768]{1,0:T(8,128)(2,1)S(1)} %fusion.24), channel_id=1, source_target_pairs={{0,2},{1,3},{6,4},{7,5},{8,10},{9,11},{14,12},{15,13},{16,18},{17,... | collective-permute-start | bytes 1179656 | tf_op jit(solution)/shard_map/scatter_step_1/ppermute | solution.py:257
  108.2 1.9 copy-start.16
  120.0 7.9 %copy-start.6 = (bf16[256,768]{1,0:T(8,128)(2,1)}, bf16[256,768]{1,0:T(8,128)(2,1)S(1)}, u32[]{:S(2)}) copy-start(bf16[256,768]{1,0:T(8,128)(2,1)S(1)} %get-tuple-element.62) | copy-start | bytes 1179652
  120.0 7.9 %copy-start.13 = (bf16[256,768]{1,0:T(8,128)(2,1)}, bf16[256,768]{1,0:T(8,128)(2,1)S(1)}, u32[]{:S(2)}) copy-start(bf16[256,768]{1,0:T(8,128)(2,1)S(1)} %get-tuple-element.63) | copy-start | bytes 1179652
  120.0 7.9 %copy-start.36 = (bf16[2048,512]{1,0:T(8,128)(2,1)}, bf16[2048,512]{1,0:T(8,128)(2,1)S(1)}, u32[]{:S(2)}) copy-start(bf16[2048,512]{1,0:T(8,128)(2,1)S(1)} %get-tuple-element.55.r_4_) | copy-start | bytes 6291460
  120.0 7.9 %copy-start.40 = (bf16[512,512]{1,0:T(8,128)(2,1)}, bf16[512,512]{1,0:T(8,128)(2,1)S(1)}, u32[]{:S(2)}) copy-start(bf16[512,512]{1,0:T(8,128)(2,1)S(1)} %get-tuple-element.45.r_1_) | copy-start | bytes 1572868
  120.0 7.6 %collective-permute-start.21 = (bf16[4,256,768]{2,1,0:T(8,128)(2,1)S(1)}, bf16[4,256,768]{2,1,0:T(8,128)(2,1)S(1)}, u32[]{:S(2)}, u32[]{:S(2)}) collective-permute-start(bf16[4,256,768]{2,1,0:T(8,128)(2,1)S(1)} %get-tuple-element.47), channel_id=1, source_target_pairs={{0,1},{1,0},{2,3},{3,2},{4,5},{5,4},{6,7},{7,6},{8,9},{9,8},{10,11... | collective-permute-start | bytes 4718600 | tf_op jit(solution)/shard_map/ppermute | solution.py:254
  120.1 20.6 %copy-start.1 = (bf16[256,768]{1,0:T(8,128)(2,1)S(1)}, bf16[256,768]{1,0:T(8,128)(2,1)}, u32[]{:S(2)}) copy-start(bf16[256,768]{1,0:T(8,128)(2,1)} %copy-done) | copy-start | bytes 1179652
  122.4 12.8 %collective-permute-start.22 = (bf16[256,768]{1,0:T(8,128)(2,1)S(1)}, bf16[256,768]{1,0:T(8,128)(2,1)S(1)}, u32[]{:S(2)}, u32[]{:S(2)}) collective-permute-start(bf16[256,768]{1,0:T(8,128)(2,1)S(1)} %fusion.12), channel_id=1, source_target_pairs={{0,2},{1,3},{2,4},{3,5},{8,10},{9,11},{10,12},{11,13},{16,18},{17,... | collective-permute-start | bytes 1179656 | tf_op jit(solution)/shard_map/scatter_step_2/ppermute | solution.py:257
  127.0 13.7 %collective-permute-start.29 = (bf16[256,768]{1,0:T(8,128)(2,1)S(1)}, bf16[256,768]{1,0:T(8,128)(2,1)S(1)}, u32[]{:S(2)}, u32[]{:S(2)}) collective-permute-start(bf16[256,768]{1,0:T(8,128)(2,1)S(1)} %fusion.12), channel_id=1, source_target_pairs={{4,2},{5,3},{6,4},{7,5},{12,10},{13,11},{14,12},{15,13},{20,18},{2... | collective-permute-start | bytes 1179656 | tf_op jit(solution)/shard_map/scatter_step_2/ppermute | solution.py:257
  127.7 7.6 %copy-start.42 = (bf16[4,256,768]{2,1,0:T(8,128)(2,1)}, bf16[4,256,768]{2,1,0:T(8,128)(2,1)S(1)}, u32[]{:S(2)}) copy-start(bf16[4,256,768]{2,1,0:T(8,128)(2,1)S(1)} %collective-permute-done.21) | copy-start | bytes 4718596
  135.3 14.2 %collective-permute-start.23 = (bf16[256,768]{1,0:T(8,128)(2,1)S(1)}, bf16[256,768]{1,0:T(8,128)(2,1)}, u32[]{:S(2)}, u32[]{:S(2)}) collective-permute-start(bf16[256,768]{1,0:T(8,128)(2,1)S(1)} %fusion.23), channel_id=1, source_target_pairs={{0,2},{1,3},{6,4},{7,5},{8,10},{9,11},{14,12},{15,13},{16,18},{17,... | collective-permute-start | bytes 1179656 | tf_op jit(solution)/shard_map/scatter_step_1/ppermute | solution.py:257
  143.0 18.3 %collective-permute-start.28 = (bf16[256,768]{1,0:T(8,128)(2,1)}, bf16[256,768]{1,0:T(8,128)(2,1)}, u32[]{:S(2)}, u32[]{:S(2)}) collective-permute-start(bf16[256,768]{1,0:T(8,128)(2,1)} %get-tuple-element.72), channel_id=1, source_target_pairs={{0,2},{1,3},{2,4},{3,5},{4,6},{5,7},{8,10},{9,11},{10,12},{11,13},... | collective-permute-start | bytes 1179656 | tf_op jit(solution)/shard_map/scatter_step_3/ppermute | solution.py:257
  147.2 14.2 %copy-start.9 = (bf16[256,768]{1,0:T(8,128)(2,1)S(1)}, bf16[256,768]{1,0:T(8,128)(2,1)}, u32[]{:S(2)}) copy-start(bf16[256,768]{1,0:T(8,128)(2,1)} %copy-done.8) | copy-start | bytes 1179652
  147.2 14.2 %collective-permute-start.30 = (bf16[256,768]{1,0:T(8,128)(2,1)}, bf16[256,768]{1,0:T(8,128)(2,1)}, u32[]{:S(2)}, u32[]{:S(2)}) collective-permute-start(bf16[256,768]{1,0:T(8,128)(2,1)} %get-tuple-element.73), channel_id=1, source_target_pairs={{2,0},{3,1},{4,2},{5,3},{6,4},{7,5},{10,8},{11,9},{12,10},{13,11},... | collective-permute-start | bytes 1179656 | tf_op jit(solution)/shard_map/scatter_step_3/ppermute | solution.py:257
  153.5 9.6 %copy-start.43 = (bf16[4,256,768]{2,1,0:T(8,128)(2,1)S(1)}, bf16[4,256,768]{2,1,0:T(8,128)(2,1)}, u32[]{:S(2)}) copy-start(bf16[4,256,768]{2,1,0:T(8,128)(2,1)} %copy-done.42) | copy-start | bytes 4718596
  153.5 16.0 %copy-start.37 = (bf16[2048,512]{1,0:T(8,128)(2,1)S(1)}, bf16[2048,512]{1,0:T(8,128)(2,1)}, u32[]{:S(2)}) copy-start(bf16[2048,512]{1,0:T(8,128)(2,1)} %copy-done.36) | copy-start | bytes 6291460
  161.3 34.1 %collective-permute-start.35 = (bf16[4,256,768]{2,1,0:T(8,128)(2,1)S(1)}, bf16[4,256,768]{2,1,0:T(8,128)(2,1)S(1)}, u32[]{:S(2)}, u32[]{:S(2)}) collective-permute-start(bf16[4,256,768]{2,1,0:T(8,128)(2,1)S(1)} %get-tuple-element.65), channel_id=1, source_target_pairs={{0,1},{1,0},{2,3},{3,2},{4,5},{5,4},{6,7},{7,6},{8,9},{9,8},{10,11... | collective-permute-start | bytes 4718600 | tf_op jit(solution)/shard_map/ppermute | solution.py:254
  161.4 8.0 %copy-start.35 = (bf16[2048,512]{1,0:T(8,128)(2,1)S(1)}, bf16[2048,512]{1,0:T(8,128)(2,1)}, u32[]{:S(2)}) copy-start(bf16[2048,512]{1,0:T(8,128)(2,1)} %copy-done.34) | copy-start | bytes 6291460
  161.4 8.0 %copy-start.39 = (bf16[512,512]{1,0:T(8,128)(2,1)S(1)}, bf16[512,512]{1,0:T(8,128)(2,1)}, u32[]{:S(2)}) copy-start(bf16[512,512]{1,0:T(8,128)(2,1)} %copy-done.38) | copy-start | bytes 1572868
  161.4 8.0 %copy-start.41 = (bf16[512,512]{1,0:T(8,128)(2,1)S(1)}, bf16[512,512]{1,0:T(8,128)(2,1)}, u32[]{:S(2)}) copy-start(bf16[512,512]{1,0:T(8,128)(2,1)} %copy-done.40) | copy-start | bytes 1572868
  164.2 18.6 %collective-permute-start.31 = (bf16[256,768]{1,0:T(8,128)(2,1)S(1)}, bf16[256,768]{1,0:T(8,128)(2,1)S(1)}, u32[]{:S(2)}, u32[]{:S(2)}) collective-permute-start(bf16[256,768]{1,0:T(8,128)(2,1)S(1)} %fusion.6), channel_id=1, source_target_pairs={{0,2},{1,3},{2,4},{3,5},{8,10},{9,11},{10,12},{11,13},{16,18},{17,... | collective-permute-start | bytes 1179656 | tf_op jit(solution)/shard_map/scatter_step_2/ppermute | solution.py:257
  168.7 14.0 %collective-permute-start.33 = (bf16[256,768]{1,0:T(8,128)(2,1)S(1)}, bf16[256,768]{1,0:T(8,128)(2,1)S(1)}, u32[]{:S(2)}, u32[]{:S(2)}) collective-permute-start(bf16[256,768]{1,0:T(8,128)(2,1)S(1)} %fusion.6), channel_id=1, source_target_pairs={{4,2},{5,3},{6,4},{7,5},{12,10},{13,11},{14,12},{15,13},{20,18},{2... | collective-permute-start | bytes 1179656 | tf_op jit(solution)/shard_map/scatter_step_2/ppermute | solution.py:257
  179.6 14.1 %collective-permute-start.24 = (bf16[256,1024]{1,0:T(8,128)(2,1)S(1)}, bf16[256,1024]{1,0:T(8,128)(2,1)S(1)}, u32[]{:S(2)}, u32[]{:S(2)}) collective-permute-start(bf16[256,1024]{1,0:T(8,128)(2,1)S(1)} %get-tuple-element.58), channel_id=1, source_target_pairs={{0,16},{8,24},{16,0},{24,8},{1,17},{9,25},{17,1},{25,9},{2,18},{10... | collective-permute-start | bytes 1572872 | tf_op jit(solution)/shard_map/back/ppermute | solution.py:262
  181.2 17.5 %collective-permute-start.26 = (bf16[256,1024]{1,0:T(8,128)(2,1)S(1)}, bf16[256,1024]{1,0:T(8,128)(2,1)S(1)}, u32[]{:S(2)}, u32[]{:S(2)}) collective-permute-start(bf16[256,1024]{1,0:T(8,128)(2,1)S(1)} %get-tuple-element.60), channel_id=1, source_target_pairs={{0,8},{8,0},{16,24},{24,16},{1,9},{9,1},{17,25},{25,17},{2,10},{10... | collective-permute-start | bytes 1572872 | tf_op jit(solution)/shard_map/back/ppermute | solution.py:262
  183.1 28.7 %collective-permute-start.32 = (bf16[256,768]{1,0:T(8,128)(2,1)S(1)}, bf16[256,768]{1,0:T(8,128)(2,1)S(1)}, u32[]{:S(2)}, u32[]{:S(2)}) collective-permute-start(bf16[256,768]{1,0:T(8,128)(2,1)S(1)} %get-tuple-element.74), channel_id=1, source_target_pairs={{0,2},{1,3},{2,4},{3,5},{4,6},{5,7},{8,10},{9,11},{10,12},{11,13},... | collective-permute-start | bytes 1179656 | tf_op jit(solution)/shard_map/scatter_step_3/ppermute | solution.py:257
  186.2 25.6 %collective-permute-start.34 = (bf16[256,768]{1,0:T(8,128)(2,1)S(1)}, bf16[256,768]{1,0:T(8,128)(2,1)S(1)}, u32[]{:S(2)}, u32[]{:S(2)}) collective-permute-start(bf16[256,768]{1,0:T(8,128)(2,1)S(1)} %get-tuple-element.75), channel_id=1, source_target_pairs={{2,0},{3,1},{4,2},{5,3},{6,4},{7,5},{10,8},{11,9},{12,10},{13,11},... | collective-permute-start | bytes 1179656 | tf_op jit(solution)/shard_map/scatter_step_3/ppermute | solution.py:257
  193.9 7.7 %collective-permute-start.25 = (bf16[128,1024]{1,0:T(8,128)(2,1)S(1)}, bf16[128,1024]{1,0:T(8,128)(2,1)S(1)}, u32[]{:S(2)}, u32[]{:S(2)}) collective-permute-start(bf16[128,1024]{1,0:T(8,128)(2,1)S(1)} %slice.210), channel_id=1, source_target_pairs={{0,8},{8,0},{16,24},{24,16},{1,9},{9,1},{17,25},{25,17},{2,10},{10... | collective-permute-start | bytes 786440 | tf_op jit(solution)/shard_map/back/ppermute | solution.py:262
  195.7 10.7 %collective-permute-start.36 = (bf16[256,768]{1,0:T(8,128)(2,1)S(1)}, bf16[256,768]{1,0:T(8,128)(2,1)S(1)}, u32[]{:S(2)}, u32[]{:S(2)}) collective-permute-start(bf16[256,768]{1,0:T(8,128)(2,1)S(1)} %fusion.22), channel_id=1, source_target_pairs={{0,2},{1,3},{6,4},{7,5},{8,10},{9,11},{14,12},{15,13},{16,18},{17,... | collective-permute-start | bytes 1179656 | tf_op jit(solution)/shard_map/scatter_step_1/ppermute | solution.py:257
  199.0 12.7 %collective-permute-start.27 = (bf16[128,1024]{1,0:T(8,128)(2,1)S(1)}, bf16[128,1024]{1,0:T(8,128)(2,1)S(1)}, u32[]{:S(2)}, u32[]{:S(2)}) collective-permute-start(bf16[128,1024]{1,0:T(8,128)(2,1)S(1)} %slice.209), channel_id=1, source_target_pairs={{0,16},{8,24},{16,0},{24,8},{1,17},{9,25},{17,1},{25,9},{2,18},{10... | collective-permute-start | bytes 786440 | tf_op jit(solution)/shard_map/back/ppermute | solution.py:262
  201.6 10.1 %copy-start.7 = (bf16[256,768]{1,0:T(8,128)(2,1)S(1)}, bf16[256,768]{1,0:T(8,128)(2,1)}, u32[]{:S(2)}) copy-start(bf16[256,768]{1,0:T(8,128)(2,1)} %copy-done.6) | copy-start | bytes 1179652
  206.5 11.1 %collective-permute-start.37 = (bf16[256,768]{1,0:T(8,128)(2,1)S(1)}, bf16[256,768]{1,0:T(8,128)(2,1)S(1)}, u32[]{:S(2)}, u32[]{:S(2)}) collective-permute-start(bf16[256,768]{1,0:T(8,128)(2,1)S(1)} %fusion.2), channel_id=1, source_target_pairs={{0,2},{1,3},{2,4},{3,5},{8,10},{9,11},{10,12},{11,13},{16,18},{17,... | collective-permute-start | bytes 1179656 | tf_op jit(solution)/shard_map/scatter_step_2/ppermute | solution.py:257
  210.9 6.7 %collective-permute-start.39 = (bf16[256,768]{1,0:T(8,128)(2,1)S(1)}, bf16[256,768]{1,0:T(8,128)(2,1)S(1)}, u32[]{:S(2)}, u32[]{:S(2)}) collective-permute-start(bf16[256,768]{1,0:T(8,128)(2,1)S(1)} %fusion.2), channel_id=1, source_target_pairs={{4,2},{5,3},{6,4},{7,5},{12,10},{13,11},{14,12},{15,13},{20,18},{2... | collective-permute-start | bytes 1179656 | tf_op jit(solution)/shard_map/scatter_step_2/ppermute | solution.py:257
  217.9 13.0 %collective-permute-start.38 = (bf16[256,768]{1,0:T(8,128)(2,1)S(1)}, bf16[256,768]{1,0:T(8,128)(2,1)S(1)}, u32[]{:S(2)}, u32[]{:S(2)}) collective-permute-start(bf16[256,768]{1,0:T(8,128)(2,1)S(1)} %get-tuple-element.70), channel_id=1, source_target_pairs={{0,2},{1,3},{2,4},{3,5},{4,6},{5,7},{8,10},{9,11},{10,12},{11,13},... | collective-permute-start | bytes 1179656 | tf_op jit(solution)/shard_map/scatter_step_3/ppermute | solution.py:257
  225.7 9.7 %collective-permute-start.40 = (bf16[256,768]{1,0:T(8,128)(2,1)S(1)}, bf16[256,768]{1,0:T(8,128)(2,1)S(1)}, u32[]{:S(2)}, u32[]{:S(2)}) collective-permute-start(bf16[256,768]{1,0:T(8,128)(2,1)S(1)} %get-tuple-element.71), channel_id=1, source_target_pairs={{2,0},{3,1},{4,2},{5,3},{6,4},{7,5},{10,8},{11,9},{12,10},{13,11},... | collective-permute-start | bytes 1179656 | tf_op jit(solution)/shard_map/scatter_step_3/ppermute | solution.py:257
  (26 other events, 28.6 us)
Sparse Core Ops, SparseCore 0:
  11.3 49.8 all-gather.2
  66.3 37.4 all-gather.4

commit v3 on v2

--- a/solution.py
+++ b/solution.py
@@ -1,6 +1,12 @@
 import jax
 import jax.numpy as jnp
 from jax import lax
+from jax.experimental import pallas as pl
+from jax.experimental.pallas import tpu as pltpu
+from jax.experimental import pallas as pl
+from jax.experimental.pallas import tpu as pltpu
+from jax.experimental import pallas as pl
+from jax.experimental.pallas import tpu as pltpu
 from jax.experimental import pallas as pl
 from jax.experimental.pallas import tpu as pltpu
 from jax.experimental import pallas as pl
@@ -94,7 +100,7 @@
 
 VMEM = pl.BlockSpec(memory_space=pltpu.VMEM)
 SMEM = pl.BlockSpec(memory_space=pltpu.SMEM)
-ANY = pl.BlockSpec(memory_space=pl.ANY)
+HBM = pl.BlockSpec(memory_space=pltpu.HBM)
 LIMIT = 28 << 20
 
 
@@ -269,17 +275,6 @@
     )
     whole = [lax.all_gather(a, "wide", axis=0, tiled=True) for a in own[1:]]
 
-    def gather(a):
-        ups, downs = [a], [a]
-        for s in range(1, line):
-            with jax.named_scope(f"gather_step_{s}"):
-                ups.append(along(ups[-1], [(i, i + 1) for i in range(s - 1, line - 1)]))
-                downs.append(along(downs[-1], [(i, i - 1) for i in range(1, line - s + 1)]))
-        held = (a, *ups[1:], *downs[1:])
-        return held + tuple(twin(p) for p in held)
-
-    first = gather(own[0])
-
     named = jnp.arange(experts, dtype=jnp.int32)[None, :]
     gates = sum(
         jnp.where(routes[:, k : k + 1] == named, gate_prob[:, k : k + 1], 0.0)
@@ -290,11 +285,25 @@
     terms = jnp.concatenate((high, middle, gates - high - middle), axis=1).astype(BF16)
     terms = jnp.pad(terms, ((0, 0), (0, LANES - terms.shape[1])))
     graded = jnp.concatenate((out_grad, terms), axis=1)
+    def hop(ups, downs, s):
+        with jax.named_scope(f"gather_step_{s}"):
+            ups.append(along(ups[-1], [(i, i + 1) for i in range(s - 1, line - 1)]))
+            downs.append(along(downs[-1], [(i, i - 1) for i in range(1, line - s + 1)]))
+
+    ups, downs = [own[0]], [own[0]]
     with jax.named_scope("rows"):
         t = [tokens, flip(tokens, 1), flip(tokens, 2)]
         g = [graded, flip(graded, 1), flip(graded, 2)]
-        t.append(flip(t[1], 2))
-        g.append(flip(g[2], 1))
+    hop(ups, downs, 1)
+    with jax.named_scope("rows"):
+        near = (t[1], t[2], g[1], g[2], ups[1], downs[1])
+        t.append(flip(after(t[1], *near), 2))
+        g.append(flip(after(g[2], *near), 1))
+    for s in range(2, line):
+        hop(ups, downs, s)
+    held = (own[0], *ups[1:], *downs[1:])
+    held += tuple(twin(p) for p in held)
+    g[0] = after(graded, ups[2], downs[2])
     [scaled] = call(
         lambda *r: scale_kernel(experts, *r),
         [SMEM] + [VMEM] * len(g),
@@ -326,23 +335,24 @@
             with jax.named_scope(f"scatter_step_{s}"):
                 up = along(a, [(i, i + 1) for i in range(s)])
                 down = along(b, [(i, i - 1) for i in range(line - s, line)])
-            marks.append(up)
+            marks += [a, up]
         total = parts[0].astype(F32) + swapped[0].astype(F32)
         return total + up.astype(F32) + down.astype(F32), marks
 
+    order = [1, 0, *range(2, chunks)]
     merged, both, sums, marks = [], [], [], ()
     for i in range(chunks):
-        weights = first if i == 0 else (whole[i - 1],)
+        weights = held if i == 1 else (whole[order[i] - 1],)
         got = call(
-            lambda *r, i=i: chunk_kernel(line, len(t), i > 0, *r),
-            [SMEM] + [ANY] * (len(t) + 1 + len(weights)),
+            lambda *r, i=i: chunk_kernel(line, len(t), i != 1, *r),
+            [SMEM] + [HBM] * (len(t) + 1 + len(weights)),
             [shape((feats, 3 * step), BF16)] * line
             + [
                 shape((line, feats, 3 * step), BF16),
                 shape((count, 2 * step), BF16),
                 shape((width, 2 * step), BF16),
             ],
-            (at, *t, after(scaled, *marks[:1]), *weights),
+            (at, *t, after(scaled, *marks[:2]), *weights),
             (
                 pltpu.VMEM((count, width), BF16),
                 pltpu.VMEM((count, width), BF16),
@@ -358,7 +368,7 @@
         both.append(got[line + 2])
         swapped = twin(got[line])
         if i < chunks - 1:
-            total, marks = scatter(got[:line], swapped, marks[1:2], ())
+            total, marks = scatter(got[:line], swapped, marks[2:3], ())
             sums.append(total)
 
     far, odd, left, right = call(
@@ -376,11 +386,11 @@
         last = flip(right[rows:].astype(BF16), 2)
         left, right = left[:rows] + near.astype(F32), right[:rows] + last.astype(F32)
         grad_input = jnp.concatenate((left, right), axis=1).astype(BF16)
-    sums.append(scatter(got[:line], swapped, marks[1:2], halfway)[0])
+    sums.append(scatter(got[:line], swapped, marks[2:3], halfway)[0])
 
     def grad_of(j):
         cols = slice(j * step, (j + 1) * step)
-        return jnp.concatenate([s[:, cols] for s in sums], axis=1)[None]
+        return jnp.concatenate([sums[order.index(i)][:, cols] for i in range(chunks)], axis=1)[None]
 
     return (grad_input, grad_of(0), grad_of(1), grad_of(2))
 
@@ -392,7 +402,7 @@
 
     def on_device(tokens, out_grad, routes, *rest):
         dense = experts == 4 and wide % 2 == 0 and 2 * routes.shape[1] >= experts
-        dense = dense and rest[1].shape[2] % (2 * LANES) == 0
+        dense = dense and wide > 4 and rest[1].shape[2] >= 4 * LANES and rest[1].shape[2] % (2 * LANES) == 0
         return (dense_plan if dense else slot_plan)(tokens, out_grad, routes, *rest)
 
     return jax.shard_map(

time: 246 us -> 244 us (level)
  waiting for transfers between devices: 83.3 us -> 93.7 us
  starting transfers between devices: 75.1 us -> 66.5 us
  local copies, waits for them, and re-layouts: 21.7 us -> 18.9 us
    ppermute x21, waiting for transfers between devices: 65.3 us -> 80.8 us  [along(): lax.ppermute(a, 'wide', [(2 * s + i, 2 * t + i) for s, t in hops for i in...]
    ppermute x10, starting transfers between devices: 14.2 us -> 9.6 us  [flip(): return lax.ppermute(a, 'expert', [(e, e ^ bit) for e in range(experts)])]
    ppermute x21, starting transfers between devices: 59.5 us -> 55.4 us  [along(): lax.ppermute(a, 'wide', [(2 * s + i, 2 * t + i) for s, t in hops for i in...]
    ppermute x10, waiting for transfers between devices: 14.4 us -> 11.2 us  [flip(): return lax.ppermute(a, 'expert', [(e, e ^ bit) for e in range(experts)])]
    unnamed x94 -> x78, local copies, waits for them, and re-layouts: 21.3 us -> 18.6 us
  transfers between devices with their start and end apart: 43 -> 43, of which waited for: 15 -> 15; matrix products, arithmetic and copies ran while one was open for 5% -> 4% of each run, Pallas kernels for 14% -> 14%
where the time goes in v3:
time: 244 us; the launch traced here: 243 us
  waiting for transfers between devices  93.7 us (38%)
  starting transfers between devices  66.5 us (27%)
  Pallas kernels  36.3 us (15%)
  local copies, waits for them, and re-layouts  18.9 us (8%)
  between operations  14.8 us (6%)
  other arithmetic  12.5 us (5%)
    ppermute x21, waiting for transfers between devices, along(): lax.ppermute(a, 'wide', [(2 * s + i, 2 * t + i) for s, t in hops for i in...  80.8 us
    ppermute x21, starting transfers between devices, along(): lax.ppermute(a, 'wide', [(2 * s + i, 2 * t + i) for s, t in hops for i in...  55.4 us
    pallas_call x6, Pallas kernels, call(): pl.pallas_call(body, out_shape=outs, in_specs=ins, out_specs=[VMEM] * len...  36.3 us
    unnamed x78, local copies, waits for them, and re-layouts  18.6 us
    ppermute x10, waiting for transfers between devices, flip(): return lax.ppermute(a, 'expert', [(e, e ^ bit) for e in range(experts)])  11.2 us
    ppermute x10, starting transfers between devices, flip(): return lax.ppermute(a, 'expert', [(e, e ^ bit) for e in range(experts)])  9.6 us
    convert_element_type x6, other arithmetic, block(): return total.astype(BF16)  5.21 us
  transfers between devices with their start and end apart: 43, of which 15 were waited for; matrix products, arithmetic and copies ran while one was open for 4% of the time, Pallas kernels for 14%

profile of v3, /device:TPU:0, one launch (start us, length us, event | category | flops | bytes accessed | tf_op | source)
XLA Modules:
  0.0 242.6 jit_solution(8597338772881073999)
XLA Ops:
  7.2 1.0 copy-done.10
  8.2 1.0 copy-done.11
  9.2 1.0 copy-done.12
  10.2 1.1 shard_map.102
  11.4 5.7 %collective-permute-start.4 = (bf16[256,768]{1,0:T(8,128)(2,1)}, bf16[256,768]{1,0:T(8,128)(2,1)}, u32[]{:S(2)}, u32[]{:S(2)}) collective-permute-start(bf16[256,768]{1,0:T(8,128)(2,1)} %get-tuple-element.41.r_6_), channel_id=1, source_target_pairs={{0,2},{1,3},{2,4},{3,5},{4,6},{5,7},{8,10},{9,11},{10,12},{11,13},... | collective-permute-start | bytes 1179656 | tf_op jit(solution)/shard_map/gather_step_1/ppermute | solution.py:263
  17.4 1.6 collective-permute-start.2
  19.0 1.5 collective-permute-start.3
  21.5 7.1 %collective-permute-done.4.r_7_ = bf16[256,768]{1,0:T(8,128)(2,1)} collective-permute-done((bf16[256,768]{1,0:T(8,128)(2,1)}, bf16[256,768]{1,0:T(8,128)(2,1)}, u32[]{:S(2)}, u32[]{:S(2)}) %collective-permute-start.4) | collective-permute-done | bytes 393248 | tf_op jit(solution)/shard_map/gather_step_1/ppermute | solution.py:263
  28.6 1.3 collective-permute-start.5
  29.9 28.3 %collective-permute-done.5.r_10_ = bf16[256,768]{1,0:T(8,128)(2,1)S(1)} collective-permute-done((bf16[256,768]{1,0:T(8,128)(2,1)}, bf16[256,768]{1,0:T(8,128)(2,1)S(1)}, u32[]{:S(2)}, u32[]{:S(2)}) %collective-permute-start.5) | collective-permute-done | bytes 393248 | tf_op jit(solution)/shard_map/gather_step_1/ppermute | solution.py:263
  58.3 0.8 copy-done.19
  59.1 1.5 collective-permute-start.9
  60.6 0.8 copy-done.2
  61.4 1.5 collective-permute-start.6
  62.8 1.4 collective-permute-start.7
  64.3 1.3 collective-permute-start.8
  65.7 9.0 %collective-permute-done.8.r_11_ = bf16[256,768]{1,0:T(8,128)(2,1)} collective-permute-done((bf16[256,768]{1,0:T(8,128)(2,1)S(1)}, bf16[256,768]{1,0:T(8,128)(2,1)}, u32[]{:S(2)}, u32[]{:S(2)}) %collective-permute-start.8) | collective-permute-done | bytes 393248 | tf_op jit(solution)/shard_map/gather_step_2/ppermute | solution.py:263
  75.5 1.1 copy-done.3
  76.5 1.1 copy-done.5
  77.6 1.0 shard_map.103.r_5_
  78.6 1.9 copy-done.14
  80.5 1.0 copy-done.16
  81.5 1.1 copy-done.20
  82.6 8.8 %shard_map.104 = (bf16[256,768]{1,0:T(8,128)(2,1)S(1)}, bf16[256,768]{1,0:T(8,128)(2,1)S(1)}, bf16[256,768]{1,0:T(8,128)(2,1)S(1)}, bf16[256,768]{1,0:T(8,128)(2...) custom-call(s32[3]{0:T(128)S(1)} %pad_add_fusion.r_0_, ...), custom_call_target="tpu_custom_call" | custom-call | flops 3221225472 | bytes 13107212 | tf_op jit(solution)/shard_map/pallas_call | solution.py:109
  92.1 1.4 copy-done.27
  94.8 0.8 collective-permute-start.12
  95.7 1.3 collective-permute-start.13
  97.0 1.1 collective-permute-done.10
  98.1 1.4 fusion.24
  99.5 3.9 %collective-permute-start.11 = (bf16[256,768]{1,0:T(8,128)(2,1)S(1)}, bf16[256,768]{1,0:T(8,128)(2,1)S(1)}, u32[]{:S(2)}, u32[]{:S(2)}) collective-permute-start(bf16[256,768]{1,0:T(8,128)(2,1)S(1)} %fusion.24), channel_id=1, source_target_pairs={{0,2},{1,3},{6,4},{7,5},{8,10},{9,11},{14,12},{15,13},{16,18},{17,... | collective-permute-start | bytes 1179656 | tf_op jit(solution)/shard_map/scatter_step_1/ppermute | solution.py:263
  104.1 6.8 %collective-permute-done.13.r_12_ = bf16[256,768]{1,0:T(8,128)(2,1)S(1)} collective-permute-done((bf16[256,768]{1,0:T(8,128)(2,1)}, bf16[256,768]{1,0:T(8,128)(2,1)S(1)}, u32[]{:S(2)}, u32[]{:S(2)}) %collective-permute-start.13) | collective-permute-done | bytes 393248 | tf_op jit(solution)/shard_map/gather_step_3/ppermute | solution.py:263
  110.9 1.1 collective-permute-done.11
  112.0 1.2 fusion.12
  113.8 7.4 %shard_map.105 = (bf16[256,768]{1,0:T(8,128)(2,1)S(1)}, bf16[256,768]{1,0:T(8,128)(2,1)S(1)}, bf16[256,768]{1,0:T(8,128)(2,1)S(1)}, bf16[256,768]{1,0:T(8,128)(2...) custom-call(s32[3]{0:T(128)S(1)} %pad_add_fusion.r_0_, ...), custom_call_target="tpu_custom_call" | custom-call | flops 3221225472 | bytes 15466508 | tf_op jit(solution)/shard_map/pallas_call | solution.py:109
  121.4 4.4 %collective-permute-start.22 = (bf16[256,768]{1,0:T(8,128)(2,1)S(1)}, bf16[256,768]{1,0:T(8,128)(2,1)S(1)}, u32[]{:S(2)}, u32[]{:S(2)}) collective-permute-start(bf16[256,768]{1,0:T(8,128)(2,1)S(1)} %fusion.12), channel_id=1, source_target_pairs={{0,2},{1,3},{2,4},{3,5},{8,10},{9,11},{10,12},{11,13},{16,18},{17,... | collective-permute-start | bytes 1179656 | tf_op jit(solution)/shard_map/scatter_step_2/ppermute | solution.py:263
  126.7 7.9 %collective-permute-done.22 = bf16[256,768]{1,0:T(8,128)(2,1)S(1)} collective-permute-done((bf16[256,768]{1,0:T(8,128)(2,1)S(1)}, bf16[256,768]{1,0:T(8,128)(2,1)S(1)}, u32[]{:S(2)}, u32[]{:S(2)}) %collective-permute-start.22) | collective-permute-done | bytes 393248 | tf_op jit(solution)/shard_map/scatter_step_2/ppermute | solution.py:263
  134.6 4.6 %collective-permute-start.23 = (bf16[256,768]{1,0:T(8,128)(2,1)S(1)}, bf16[256,768]{1,0:T(8,128)(2,1)S(1)}, u32[]{:S(2)}, u32[]{:S(2)}) collective-permute-start(bf16[256,768]{1,0:T(8,128)(2,1)S(1)} %fusion.23), channel_id=1, source_target_pairs={{0,2},{1,3},{6,4},{7,5},{8,10},{9,11},{14,12},{15,13},{16,18},{17,... | collective-permute-start | bytes 1179656 | tf_op jit(solution)/shard_map/scatter_step_1/ppermute | solution.py:263
  139.2 2.3 add_convert_fusion.3
  141.5 2.5 %collective-permute-start.32 = (bf16[256,768]{1,0:T(8,128)(2,1)}, bf16[256,768]{1,0:T(8,128)(2,1)}, u32[]{:S(2)}, u32[]{:S(2)}) collective-permute-start(bf16[256,768]{1,0:T(8,128)(2,1)} %get-tuple-element.80), channel_id=1, source_target_pairs={{0,2},{1,3},{2,4},{3,5},{4,6},{5,7},{8,10},{9,11},{10,12},{11,13},... | collective-permute-start | bytes 1179656 | tf_op jit(solution)/shard_map/scatter_step_3/ppermute | solution.py:263
  144.0 1.3 collective-permute-start.34
  145.3 3.4 %collective-permute-done.23 = bf16[256,768]{1,0:T(8,128)(2,1)S(1)} collective-permute-done((bf16[256,768]{1,0:T(8,128)(2,1)S(1)}, bf16[256,768]{1,0:T(8,128)(2,1)S(1)}, u32[]{:S(2)}, u32[]{:S(2)}) %collective-permute-start.23) | collective-permute-done | bytes 393248 | tf_op jit(solution)/shard_map/scatter_step_1/ppermute | solution.py:263
  148.7 0.9 fusion.10
  149.6 1.9 copy-done.13
  151.6 1.0 copy-done.18
  152.6 1.0 copy-done.22
  153.6 7.8 %shard_map.106 = (bf16[256,768]{1,0:T(8,128)(2,1)S(1)}, bf16[256,768]{1,0:T(8,128)(2,1)S(1)}, bf16[256,768]{1,0:T(8,128)(2,1)S(1)}, bf16[256,768]{1,0:T(8,128)(2...) custom-call(s32[3]{0:T(128)S(1)} %pad_add_fusion.r_0_, ...), custom_call_target="tpu_custom_call" | custom-call | flops 3221225472 | bytes 13107212 | tf_op jit(solution)/shard_map/pallas_call | solution.py:109
  161.5 1.5 fusion.6
  163.1 4.4 %collective-permute-start.28 = (bf16[256,768]{1,0:T(8,128)(2,1)S(1)}, bf16[256,768]{1,0:T(8,128)(2,1)S(1)}, u32[]{:S(2)}, u32[]{:S(2)}) collective-permute-start(bf16[256,768]{1,0:T(8,128)(2,1)S(1)} %copy-done.36), channel_id=1, source_target_pairs={{0,2},{1,3},{2,4},{3,5},{8,10},{9,11},{10,12},{11,13},{16,18},{17,... | collective-permute-start | bytes 1179656 | tf_op jit(solution)/shard_map/scatter_step_2/ppermute | solution.py:263
  168.3 10.2 %shard_map.107 = (bf16[256,1024]{1,0:T(8,128)(2,1)S(1)}, bf16[256,1024]{1,0:T(8,128)(2,1)S(1)}, f32[256,1024]{1,0:T(8,128)S(1)}, f32[256,1024]{1,0:T(8,128)S(1)}) custom-call(bf16[512,512]{1,0:T(8,128)(2,1)S(1)} %copy-done.32, bf16[512,512]{1,0:T(8,128)(2,1)S(1)} %copy-done.30, bf16[512,512]{1,0:T(8,128)(2,1)S(1)} %get-tuple-element.60.r_2_, ...), custom_call_target="tpu_custom_call" | custom-call | flops 3221225472 | bytes 11010048 | tf_op jit(solution)/shard_map/pallas_call | solution.py:109
  180.2 2.8 %collective-permute-start.29 = (bf16[256,768]{1,0:T(8,128)(2,1)S(1)}, bf16[256,768]{1,0:T(8,128)(2,1)S(1)}, u32[]{:S(2)}, u32[]{:S(2)}) collective-permute-start(bf16[256,768]{1,0:T(8,128)(2,1)S(1)} %get-tuple-element.78), channel_id=1, source_target_pairs={{0,2},{1,3},{2,4},{3,5},{4,6},{5,7},{8,10},{9,11},{10,12},{11,13},... | collective-permute-start | bytes 1179656 | tf_op jit(solution)/shard_map/scatter_step_3/ppermute | solution.py:263
  183.0 1.3 collective-permute-start.31
  184.3 8.1 %collective-permute-done.24 = bf16[256,1024]{1,0:T(8,128)(2,1)S(1)} collective-permute-done((bf16[256,1024]{1,0:T(8,128)(2,1)S(1)}, bf16[256,1024]{1,0:T(8,128)(2,1)S(1)}, u32[]{:S(2)}, u32[]{:S(2)}) %collective-permute-start.24) | collective-permute-done | bytes 524320 | tf_op jit(solution)/shard_map/back/ppermute | solution.py:268
  193.6 2.8 %collective-permute-start.36 = (bf16[256,768]{1,0:T(8,128)(2,1)S(1)}, bf16[256,768]{1,0:T(8,128)(2,1)S(1)}, u32[]{:S(2)}, u32[]{:S(2)}) collective-permute-start(bf16[256,768]{1,0:T(8,128)(2,1)S(1)} %fusion.22), channel_id=1, source_target_pairs={{0,2},{1,3},{6,4},{7,5},{8,10},{9,11},{14,12},{15,13},{16,18},{17,... | collective-permute-start | bytes 1179656 | tf_op jit(solution)/shard_map/scatter_step_1/ppermute | solution.py:263
  197.2 3.0 %collective-permute-done.25 = bf16[128,1024]{1,0:T(8,128)(2,1)S(1)} collective-permute-done((bf16[128,1024]{1,0:T(8,128)(2,1)S(1)}, bf16[128,1024]{1,0:T(8,128)(2,1)S(1)}, u32[]{:S(2)}, u32[]{:S(2)}) %collective-permute-start.25) | collective-permute-done | bytes 262176 | tf_op jit(solution)/shard_map/back/ppermute | solution.py:268
  200.2 3.9 %collective-permute-done.36 = bf16[256,768]{1,0:T(8,128)(2,1)S(1)} collective-permute-done((bf16[256,768]{1,0:T(8,128)(2,1)S(1)}, bf16[256,768]{1,0:T(8,128)(2,1)S(1)}, u32[]{:S(2)}, u32[]{:S(2)}) %collective-permute-start.36) | collective-permute-done | bytes 393248 | tf_op jit(solution)/shard_map/scatter_step_1/ppermute | solution.py:263
  204.3 4.4 %collective-permute-start.37 = (bf16[256,768]{1,0:T(8,128)(2,1)S(1)}, bf16[256,768]{1,0:T(8,128)(2,1)S(1)}, u32[]{:S(2)}, u32[]{:S(2)}) collective-permute-start(bf16[256,768]{1,0:T(8,128)(2,1)S(1)} %fusion.2), channel_id=1, source_target_pairs={{0,2},{1,3},{2,4},{3,5},{8,10},{9,11},{10,12},{11,13},{16,18},{17,... | collective-permute-start | bytes 1179656 | tf_op jit(solution)/shard_map/scatter_step_2/ppermute | solution.py:263
  209.7 5.8 %collective-permute-done.37 = bf16[256,768]{1,0:T(8,128)(2,1)S(1)} collective-permute-done((bf16[256,768]{1,0:T(8,128)(2,1)S(1)}, bf16[256,768]{1,0:T(8,128)(2,1)S(1)}, u32[]{:S(2)}, u32[]{:S(2)}) %collective-permute-start.37) | collective-permute-done | bytes 393248 | tf_op jit(solution)/shard_map/scatter_step_2/ppermute | solution.py:263
  215.9 7.8 %collective-permute-start.38 = (bf16[256,768]{1,0:T(8,128)(2,1)S(1)}, bf16[256,768]{1,0:T(8,128)(2,1)S(1)}, u32[]{:S(2)}, u32[]{:S(2)}) collective-permute-start(bf16[256,768]{1,0:T(8,128)(2,1)S(1)} %get-tuple-element.76), channel_id=1, source_target_pairs={{0,2},{1,3},{2,4},{3,5},{4,6},{5,7},{8,10},{9,11},{10,12},{11,13},... | collective-permute-start | bytes 1179656 | tf_op jit(solution)/shard_map/scatter_step_3/ppermute | solution.py:263
  223.7 1.3 collective-permute-start.40
  225.0 0.8 pad_maximum_fusion
  225.9 3.1 %collective-permute-done.38 = bf16[256,768]{1,0:T(8,128)(2,1)S(1)} collective-permute-done((bf16[256,768]{1,0:T(8,128)(2,1)S(1)}, bf16[256,768]{1,0:T(8,128)(2,1)S(1)}, u32[]{:S(2)}, u32[]{:S(2)}) %collective-permute-start.38) | collective-permute-done | bytes 393248 | tf_op jit(solution)/shard_map/scatter_step_3/ppermute | solution.py:263
  229.0 4.3 %collective-permute-done.40 = bf16[256,768]{1,0:T(8,128)(2,1)S(1)} collective-permute-done((bf16[256,768]{1,0:T(8,128)(2,1)S(1)}, bf16[256,768]{1,0:T(8,128)(2,1)S(1)}, u32[]{:S(2)}, u32[]{:S(2)}) %collective-permute-start.40) | collective-permute-done | bytes 393248 | tf_op jit(solution)/shard_map/scatter_step_3/ppermute | solution.py:263
  233.6 0.9 maximum_bitcast_fusion.2
  234.6 1.2 maximum_bitcast_fusion
  (139 shorter events, 12.8 us)
Async XLA Ops:
  7.2 10.0 %copy-start.37 = (s32[128,2]{0,1:T(2,128)S(1)}, s32[128,2]{0,1:T(2,128)}, u32[]{:S(2)}) copy-start(s32[128,2]{0,1:T(2,128)} %param.9) | copy-start | bytes 3076
  7.2 10.0 %copy-start.38 = (f32[128,2]{0,1:T(2,128)S(1)}, f32[128,2]{0,1:T(2,128)}, u32[]{:S(2)}) copy-start(f32[128,2]{0,1:T(2,128)} %param.10) | copy-start | bytes 3076
  7.2 71.4 %all-gather.3.cloned.1.call-start = ((), (), s32[]{:S(2)}) async-start(), calls=%async_computation | async-start | bytes 3538944 | tf_op jit(solution)/shard_map/all_gather | solution.py:276
  10.2 7.2 %copy-start.35 = (bf16[128,2048]{1,0:T(8,128)(2,1)S(1)}, bf16[128,2048]{1,0:T(8,128)(2,1)}, u32[]{:S(2)}) copy-start(bf16[128,2048]{1,0:T(8,128)(2,1)} %param.8) | copy-start | bytes 1572868
  10.2 10.3 %copy-start.15 = (bf16[128,2048]{1,0:T(8,128)(2,1)S(1)}, bf16[128,2048]{1,0:T(8,128)(2,1)}, u32[]{:S(2)}) copy-start(bf16[128,2048]{1,0:T(8,128)(2,1)} %r_1_.5) | copy-start | bytes 1572868
  11.4 138.2 %all-gather.5.cloned.1.call-start = ((), (), s32[]{:S(2)}) async-start(), calls=%async_computation.1 | async-start | bytes 3538944 | tf_op jit(solution)/shard_map/all_gather | solution.py:276
  11.4 17.2 %collective-permute-start.4 = (bf16[256,768]{1,0:T(8,128)(2,1)}, bf16[256,768]{1,0:T(8,128)(2,1)}, u32[]{:S(2)}, u32[]{:S(2)}) collective-permute-start(bf16[256,768]{1,0:T(8,128)(2,1)} %get-tuple-element.41.r_6_), channel_id=1, source_target_pairs={{0,2},{1,3},{2,4},{3,5},{4,6},{5,7},{8,10},{9,11},{10,12},{11,13},... | collective-permute-start | bytes 1179656 | tf_op jit(solution)/shard_map/gather_step_1/ppermute | solution.py:263
  17.4 41.7 %collective-permute-start.2 = (bf16[128,2176]{1,0:T(8,128)(2,1)S(1)}, bf16[128,2176]{1,0:T(8,128)(2,1)S(1)}, u32[]{:S(2)}, u32[]{:S(2)}) collective-permute-start(bf16[128,2176]{1,0:T(8,128)(2,1)S(1)} %fusion.19.r_1_), channel_id=1, source_target_pairs={{0,8},{8,0},{16,24},{24,16},{1,9},{9,1},{17,25},{25,17},{2,10},{10... | collective-permute-start | bytes 1671176 | tf_op jit(solution)/shard_map/rows/ppermute | solution.py:268
  19.0 40.1 %collective-permute-start.3 = (bf16[128,2176]{1,0:T(8,128)(2,1)S(1)}, bf16[128,2176]{1,0:T(8,128)(2,1)S(1)}, u32[]{:S(2)}, u32[]{:S(2)}) collective-permute-start(bf16[128,2176]{1,0:T(8,128)(2,1)S(1)} %fusion.19.r_1_), channel_id=1, source_target_pairs={{0,16},{8,24},{16,0},{24,8},{1,17},{9,25},{17,1},{25,9},{2,18},{10... | collective-permute-start | bytes 1671176 | tf_op jit(solution)/shard_map/rows/ppermute | solution.py:268
  20.5 37.8 %collective-permute-start = (bf16[128,2048]{1,0:T(8,128)(2,1)S(1)}, bf16[128,2048]{1,0:T(8,128)(2,1)}, u32[]{:S(2)}, u32[]{:S(2)}) collective-permute-start(bf16[128,2048]{1,0:T(8,128)(2,1)S(1)} %copy-done.15), channel_id=1, source_target_pairs={{0,8},{8,0},{16,24},{24,16},{1,9},{9,1},{17,25},{25,17},{2,10},{10... | collective-permute-start | bytes 1572872 | tf_op jit(solution)/shard_map/rows/ppermute | solution.py:268
  21.0 37.2 %collective-permute-start.1 = (bf16[128,2048]{1,0:T(8,128)(2,1)S(1)}, bf16[128,2048]{1,0:T(8,128)(2,1)S(1)}, u32[]{:S(2)}, u32[]{:S(2)}) collective-permute-start(bf16[128,2048]{1,0:T(8,128)(2,1)S(1)} %copy-done.15), channel_id=1, source_target_pairs={{0,16},{8,24},{16,0},{24,8},{1,17},{9,25},{17,1},{25,9},{2,18},{10... | collective-permute-start | bytes 1572872 | tf_op jit(solution)/shard_map/rows/ppermute | solution.py:268
  28.6 29.6 %collective-permute-start.5 = (bf16[256,768]{1,0:T(8,128)(2,1)}, bf16[256,768]{1,0:T(8,128)(2,1)S(1)}, u32[]{:S(2)}, u32[]{:S(2)}) collective-permute-start(bf16[256,768]{1,0:T(8,128)(2,1)} %get-tuple-element.41.r_6_), channel_id=1, source_target_pairs={{2,0},{3,1},{4,2},{5,3},{6,4},{7,5},{10,8},{11,9},{12,10},{13,11},... | collective-permute-start | bytes 1179656 | tf_op jit(solution)/shard_map/gather_step_1/ppermute | solution.py:263
  58.3 16.4 %copy-start.23 = (bf16[256,768]{1,0:T(8,128)(2,1)}, bf16[256,768]{1,0:T(8,128)(2,1)S(1)}, u32[]{:S(2)}) copy-start(bf16[256,768]{1,0:T(8,128)(2,1)S(1)} %collective-permute-done.5.r_10_) | copy-start | bytes 1179652
  59.1 15.6 %collective-permute-start.9 = (bf16[128,2176]{1,0:T(8,128)(2,1)S(1)}, bf16[128,2176]{1,0:T(8,128)(2,1)S(1)}, u32[]{:S(2)}, u32[]{:S(2)}) collective-permute-start(bf16[128,2176]{1,0:T(8,128)(2,1)S(1)} %collective-permute-done.3.r_3_), channel_id=1, source_target_pairs={{0,8},{8,0},{16,24},{24,16},{1,9},{9,1},{17,25},{25,17},{2,10},{10... | collective-permute-start | bytes 1671176 | tf_op jit(solution)/shard_map/rows/ppermute | solution.py:268
  61.4 17.2 %collective-permute-start.6 = (bf16[128,2048]{1,0:T(8,128)(2,1)}, bf16[128,2048]{1,0:T(8,128)(2,1)}, u32[]{:S(2)}, u32[]{:S(2)}) collective-permute-start(bf16[128,2048]{1,0:T(8,128)(2,1)} %collective-permute-done.r_2_), channel_id=1, source_target_pairs={{0,16},{8,24},{16,0},{24,8},{1,17},{9,25},{17,1},{25,9},{2,18},{10... | collective-permute-start | bytes 1572872 | tf_op jit(solution)/shard_map/rows/ppermute | solution.py:268
  62.8 2.8 %collective-permute-start.7 = (bf16[256,768]{1,0:T(8,128)(2,1)}, bf16[256,768]{1,0:T(8,128)(2,1)}, u32[]{:S(2)}, u32[]{:S(2)}) collective-permute-start(bf16[256,768]{1,0:T(8,128)(2,1)} %collective-permute-done.4.r_7_), channel_id=1, source_target_pairs={{2,4},{3,5},{4,6},{5,7},{10,12},{11,13},{12,14},{13,15},{18,20},{1... | collective-permute-start | bytes 1179656 | tf_op jit(solution)/shard_map/gather_step_2/ppermute | solution.py:263
  64.3 10.4 %collective-permute-start.8 = (bf16[256,768]{1,0:T(8,128)(2,1)S(1)}, bf16[256,768]{1,0:T(8,128)(2,1)}, u32[]{:S(2)}, u32[]{:S(2)}) collective-permute-start(bf16[256,768]{1,0:T(8,128)(2,1)S(1)} %collective-permute-done.5.r_10_), channel_id=1, source_target_pairs={{2,0},{3,1},{4,2},{5,3},{10,8},{11,9},{12,10},{13,11},{18,16},{19,... | collective-permute-start | bytes 1179656 | tf_op jit(solution)/shard_map/gather_step_2/ppermute | solution.py:263
  94.3 18.9 %copy-start = (bf16[256,768]{1,0:T(8,128)(2,1)}, bf16[256,768]{1,0:T(8,128)(2,1)S(1)}, u32[]{:S(2)}) copy-start(bf16[256,768]{1,0:T(8,128)(2,1)S(1)} %get-tuple-element.49) | copy-start | bytes 1179652
  94.3 3.8 %collective-permute-start.10 = (bf16[4,256,768]{2,1,0:T(8,128)(2,1)}, bf16[4,256,768]{2,1,0:T(8,128)(2,1)}, u32[]{:S(2)}, u32[]{:S(2)}) collective-permute-start(bf16[4,256,768]{2,1,0:T(8,128)(2,1)} %get-tuple-element.48), channel_id=1, source_target_pairs={{0,1},{1,0},{2,3},{3,2},{4,5},{5,4},{6,7},{7,6},{8,9},{9,8},{10,11... | collective-permute-start | bytes 4718600 | tf_op jit(solution)/shard_map/ppermute | solution.py:260
  94.3 9.1 %collective-permute-start.14 = (bf16[256,768]{1,0:T(8,128)(2,1)}, bf16[256,768]{1,0:T(8,128)(2,1)}, u32[]{:S(2)}, u32[]{:S(2)}) collective-permute-start(bf16[256,768]{1,0:T(8,128)(2,1)} %get-tuple-element.41.r_6_), channel_id=1, source_target_pairs={{0,1},{1,0},{2,3},{3,2},{4,5},{5,4},{6,7},{7,6},{8,9},{9,8},{10,11... | collective-permute-start | bytes 1179656 | tf_op jit(solution)/shard_map/ppermute | solution.py:260
  94.8 8.6 %copy-start.24 = (bf16[256,768]{1,0:T(8,128)(2,1)S(1)}, bf16[256,768]{1,0:T(8,128)(2,1)}, u32[]{:S(2)}) copy-start(bf16[256,768]{1,0:T(8,128)(2,1)} %copy-done.23) | copy-start | bytes 1179652
  94.8 8.7 %collective-permute-start.15 = (bf16[256,768]{1,0:T(8,128)(2,1)}, bf16[256,768]{1,0:T(8,128)(2,1)S(1)}, u32[]{:S(2)}, u32[]{:S(2)}) collective-permute-start(bf16[256,768]{1,0:T(8,128)(2,1)} %collective-permute-done.4.r_7_), channel_id=1, source_target_pairs={{0,1},{1,0},{2,3},{3,2},{4,5},{5,4},{6,7},{7,6},{8,9},{9,8},{10,11... | collective-permute-start | bytes 1179656 | tf_op jit(solution)/shard_map/ppermute | solution.py:260
  94.8 9.2 %collective-permute-start.12 = (bf16[256,768]{1,0:T(8,128)(2,1)}, bf16[256,768]{1,0:T(8,128)(2,1)S(1)}, u32[]{:S(2)}, u32[]{:S(2)}) collective-permute-start(bf16[256,768]{1,0:T(8,128)(2,1)} %collective-permute-done.7.r_8_), channel_id=1, source_target_pairs={{4,6},{5,7},{12,14},{13,15},{20,22},{21,23},{28,30},{29,31}} | collective-permute-start | bytes 1179656 | tf_op jit(solution)/shard_map/gather_step_3/ppermute | solution.py:263
  95.7 15.2 %collective-permute-start.13 = (bf16[256,768]{1,0:T(8,128)(2,1)}, bf16[256,768]{1,0:T(8,128)(2,1)S(1)}, u32[]{:S(2)}, u32[]{:S(2)}) collective-permute-start(bf16[256,768]{1,0:T(8,128)(2,1)} %collective-permute-done.8.r_11_), channel_id=1, source_target_pairs={{2,0},{3,1},{10,8},{11,9},{18,16},{19,17},{26,24},{27,25}} | collective-permute-start | bytes 1179656 | tf_op jit(solution)/shard_map/gather_step_3/ppermute | solution.py:263
  98.1 15.7 %copy-start.17 = (bf16[128,2048]{1,0:T(8,128)(2,1)S(1)}, bf16[128,2048]{1,0:T(8,128)(2,1)}, u32[]{:S(2)}) copy-start(bf16[128,2048]{1,0:T(8,128)(2,1)} %r_1_.5) | copy-start | bytes 1572868
  98.1 15.7 %copy-start.21 = (bf16[128,2048]{1,0:T(8,128)(2,1)S(1)}, bf16[128,2048]{1,0:T(8,128)(2,1)}, u32[]{:S(2)}) copy-start(bf16[128,2048]{1,0:T(8,128)(2,1)} %copy-done.19) | copy-start | bytes 1572868
  99.5 12.5 %collective-permute-start.11 = (bf16[256,768]{1,0:T(8,128)(2,1)S(1)}, bf16[256,768]{1,0:T(8,128)(2,1)S(1)}, u32[]{:S(2)}, u32[]{:S(2)}) collective-permute-start(bf16[256,768]{1,0:T(8,128)(2,1)S(1)} %fusion.24), channel_id=1, source_target_pairs={{0,2},{1,3},{6,4},{7,5},{8,10},{9,11},{14,12},{15,13},{16,18},{17,... | collective-permute-start | bytes 1179656 | tf_op jit(solution)/shard_map/scatter_step_1/ppermute | solution.py:263
  103.4 9.8 %collective-permute-start.18 = (bf16[256,768]{1,0:T(8,128)(2,1)S(1)}, bf16[256,768]{1,0:T(8,128)(2,1)S(1)}, u32[]{:S(2)}, u32[]{:S(2)}) collective-permute-start(bf16[256,768]{1,0:T(8,128)(2,1)S(1)} %copy-done.24), channel_id=1, source_target_pairs={{0,1},{1,0},{2,3},{3,2},{4,5},{5,4},{6,7},{7,6},{8,9},{9,8},{10,11... | collective-permute-start | bytes 1179656 | tf_op jit(solution)/shard_map/ppermute | solution.py:260
  103.5 9.7 %collective-permute-start.16 = (bf16[256,768]{1,0:T(8,128)(2,1)}, bf16[256,768]{1,0:T(8,128)(2,1)S(1)}, u32[]{:S(2)}, u32[]{:S(2)}) collective-permute-start(bf16[256,768]{1,0:T(8,128)(2,1)} %collective-permute-done.7.r_8_), channel_id=1, source_target_pairs={{0,1},{1,0},{2,3},{3,2},{4,5},{5,4},{6,7},{7,6},{8,9},{9,8},{10,11... | collective-permute-start | bytes 1179656 | tf_op jit(solution)/shard_map/ppermute | solution.py:260
  104.0 9.2 %collective-permute-start.19 = (bf16[256,768]{1,0:T(8,128)(2,1)}, bf16[256,768]{1,0:T(8,128)(2,1)S(1)}, u32[]{:S(2)}, u32[]{:S(2)}) collective-permute-start(bf16[256,768]{1,0:T(8,128)(2,1)} %collective-permute-done.8.r_11_), channel_id=1, source_target_pairs={{0,1},{1,0},{2,3},{3,2},{4,5},{5,4},{6,7},{7,6},{8,9},{9,8},{10,11... | collective-permute-start | bytes 1179656 | tf_op jit(solution)/shard_map/ppermute | solution.py:260
  110.9 2.3 collective-permute-start.17
  112.0 1.7 collective-permute-start.20
  121.2 20.4 %copy-start.6 = (bf16[256,768]{1,0:T(8,128)(2,1)}, bf16[256,768]{1,0:T(8,128)(2,1)S(1)}, u32[]{:S(2)}) copy-start(bf16[256,768]{1,0:T(8,128)(2,1)S(1)} %get-tuple-element.68) | copy-start | bytes 1179652
  121.2 20.4 %copy-start.25 = (bf16[2048,512]{1,0:T(8,128)(2,1)}, bf16[2048,512]{1,0:T(8,128)(2,1)S(1)}, u32[]{:S(2)}) copy-start(bf16[2048,512]{1,0:T(8,128)(2,1)S(1)} %get-tuple-element.62.r_4_) | copy-start | bytes 6291460
  121.2 20.3 %copy-start.29 = (bf16[512,512]{1,0:T(8,128)(2,1)}, bf16[512,512]{1,0:T(8,128)(2,1)S(1)}, u32[]{:S(2)}) copy-start(bf16[512,512]{1,0:T(8,128)(2,1)S(1)} %get-tuple-element.52.r_1_) | copy-start | bytes 1572868
  121.2 18.0 %copy-start.1 = (bf16[256,768]{1,0:T(8,128)(2,1)S(1)}, bf16[256,768]{1,0:T(8,128)(2,1)}, u32[]{:S(2)}) copy-start(bf16[256,768]{1,0:T(8,128)(2,1)} %copy-done) | copy-start | bytes 1179652
  121.2 5.3 %collective-permute-start.21 = (bf16[4,256,768]{2,1,0:T(8,128)(2,1)S(1)}, bf16[4,256,768]{2,1,0:T(8,128)(2,1)S(1)}, u32[]{:S(2)}, u32[]{:S(2)}) collective-permute-start(bf16[4,256,768]{2,1,0:T(8,128)(2,1)S(1)} %get-tuple-element.54), channel_id=1, source_target_pairs={{0,1},{1,0},{2,3},{3,2},{4,5},{5,4},{6,7},{7,6},{8,9},{9,8},{10,11... | collective-permute-start | bytes 4718600 | tf_op jit(solution)/shard_map/ppermute | solution.py:260
  121.4 13.2 %collective-permute-start.22 = (bf16[256,768]{1,0:T(8,128)(2,1)S(1)}, bf16[256,768]{1,0:T(8,128)(2,1)S(1)}, u32[]{:S(2)}, u32[]{:S(2)}) collective-permute-start(bf16[256,768]{1,0:T(8,128)(2,1)S(1)} %fusion.12), channel_id=1, source_target_pairs={{0,2},{1,3},{2,4},{3,5},{8,10},{9,11},{10,12},{11,13},{16,18},{17,... | collective-permute-start | bytes 1179656 | tf_op jit(solution)/shard_map/scatter_step_2/ppermute | solution.py:263
  125.8 13.4 %collective-permute-start.33 = (bf16[256,768]{1,0:T(8,128)(2,1)S(1)}, bf16[256,768]{1,0:T(8,128)(2,1)S(1)}, u32[]{:S(2)}, u32[]{:S(2)}) collective-permute-start(bf16[256,768]{1,0:T(8,128)(2,1)S(1)} %fusion.12), channel_id=1, source_target_pairs={{4,2},{5,3},{6,4},{7,5},{12,10},{13,11},{14,12},{15,13},{20,18},{2... | collective-permute-start | bytes 1179656 | tf_op jit(solution)/shard_map/scatter_step_2/ppermute | solution.py:263
  126.5 22.2 %copy-start.33 = (bf16[4,256,768]{2,1,0:T(8,128)(2,1)}, bf16[4,256,768]{2,1,0:T(8,128)(2,1)S(1)}, u32[]{:S(2)}) copy-start(bf16[4,256,768]{2,1,0:T(8,128)(2,1)S(1)} %collective-permute-done.21) | copy-start | bytes 4718596
  134.6 14.1 %collective-permute-start.23 = (bf16[256,768]{1,0:T(8,128)(2,1)S(1)}, bf16[256,768]{1,0:T(8,128)(2,1)S(1)}, u32[]{:S(2)}, u32[]{:S(2)}) collective-permute-start(bf16[256,768]{1,0:T(8,128)(2,1)S(1)} %fusion.23), channel_id=1, source_target_pairs={{0,2},{1,3},{6,4},{7,5},{8,10},{9,11},{14,12},{15,13},{16,18},{17,... | collective-permute-start | bytes 1179656 | tf_op jit(solution)/shard_map/scatter_step_1/ppermute | solution.py:263
  141.5 20.0 %collective-permute-start.32 = (bf16[256,768]{1,0:T(8,128)(2,1)}, bf16[256,768]{1,0:T(8,128)(2,1)}, u32[]{:S(2)}, u32[]{:S(2)}) collective-permute-start(bf16[256,768]{1,0:T(8,128)(2,1)} %get-tuple-element.80), channel_id=1, source_target_pairs={{0,2},{1,3},{2,4},{3,5},{4,6},{5,7},{8,10},{9,11},{10,12},{11,13},... | collective-permute-start | bytes 1179656 | tf_op jit(solution)/shard_map/scatter_step_3/ppermute | solution.py:263
  144.0 17.5 %collective-permute-start.34 = (bf16[256,768]{1,0:T(8,128)(2,1)}, bf16[256,768]{1,0:T(8,128)(2,1)}, u32[]{:S(2)}, u32[]{:S(2)}) collective-permute-start(bf16[256,768]{1,0:T(8,128)(2,1)} %get-tuple-element.81), channel_id=1, source_target_pairs={{2,0},{3,1},{4,2},{5,3},{6,4},{7,5},{10,8},{11,9},{12,10},{13,11},... | collective-permute-start | bytes 1179656 | tf_op jit(solution)/shard_map/scatter_step_3/ppermute | solution.py:263
  149.6 11.9 %copy-start.9 = (bf16[256,768]{1,0:T(8,128)(2,1)S(1)}, bf16[256,768]{1,0:T(8,128)(2,1)}, u32[]{:S(2)}) copy-start(bf16[256,768]{1,0:T(8,128)(2,1)} %copy-done.8) | copy-start | bytes 1179652
  153.6 9.5 %copy-start.36 = (bf16[256,768]{1,0:T(8,128)(2,1)S(1)}, bf16[256,768]{1,0:T(8,128)(2,1)}, u32[]{:S(2)}) copy-start(bf16[256,768]{1,0:T(8,128)(2,1)} %fusion.10) | copy-start | bytes 1179652
  153.6 14.6 %copy-start.28 = (bf16[2048,512]{1,0:T(8,128)(2,1)S(1)}, bf16[2048,512]{1,0:T(8,128)(2,1)}, u32[]{:S(2)}) copy-start(bf16[2048,512]{1,0:T(8,128)(2,1)} %copy-done.27) | copy-start | bytes 6291460
  153.6 14.6 %copy-start.30 = (bf16[512,512]{1,0:T(8,128)(2,1)S(1)}, bf16[512,512]{1,0:T(8,128)(2,1)}, u32[]{:S(2)}) copy-start(bf16[512,512]{1,0:T(8,128)(2,1)} %copy-done.29) | copy-start | bytes 1572868
  153.6 14.6 %copy-start.32 = (bf16[512,512]{1,0:T(8,128)(2,1)S(1)}, bf16[512,512]{1,0:T(8,128)(2,1)}, u32[]{:S(2)}) copy-start(bf16[512,512]{1,0:T(8,128)(2,1)} %copy-done.31) | copy-start | bytes 1572868
  161.4 6.8 %copy-start.26 = (bf16[2048,512]{1,0:T(8,128)(2,1)S(1)}, bf16[2048,512]{1,0:T(8,128)(2,1)}, u32[]{:S(2)}) copy-start(bf16[2048,512]{1,0:T(8,128)(2,1)} %copy-done.25) | copy-start | bytes 6291460
  161.4 31.9 %collective-permute-start.35 = (bf16[4,256,768]{2,1,0:T(8,128)(2,1)S(1)}, bf16[4,256,768]{2,1,0:T(8,128)(2,1)S(1)}, u32[]{:S(2)}, u32[]{:S(2)}) collective-permute-start(bf16[4,256,768]{2,1,0:T(8,128)(2,1)S(1)} %get-tuple-element.71), channel_id=1, source_target_pairs={{0,1},{1,0},{2,3},{3,2},{4,5},{5,4},{6,7},{7,6},{8,9},{9,8},{10,11... | collective-permute-start | bytes 4718600 | tf_op jit(solution)/shard_map/ppermute | solution.py:260
  163.1 16.7 %collective-permute-start.28 = (bf16[256,768]{1,0:T(8,128)(2,1)S(1)}, bf16[256,768]{1,0:T(8,128)(2,1)S(1)}, u32[]{:S(2)}, u32[]{:S(2)}) collective-permute-start(bf16[256,768]{1,0:T(8,128)(2,1)S(1)} %copy-done.36), channel_id=1, source_target_pairs={{0,2},{1,3},{2,4},{3,5},{8,10},{9,11},{10,12},{11,13},{16,18},{17,... | collective-permute-start | bytes 1179656 | tf_op jit(solution)/shard_map/scatter_step_2/ppermute | solution.py:263
  167.5 12.3 %collective-permute-start.30 = (bf16[256,768]{1,0:T(8,128)(2,1)S(1)}, bf16[256,768]{1,0:T(8,128)(2,1)S(1)}, u32[]{:S(2)}, u32[]{:S(2)}) collective-permute-start(bf16[256,768]{1,0:T(8,128)(2,1)S(1)} %copy-done.36), channel_id=1, source_target_pairs={{4,2},{5,3},{6,4},{7,5},{12,10},{13,11},{14,12},{15,13},{20,18},{2... | collective-permute-start | bytes 1179656 | tf_op jit(solution)/shard_map/scatter_step_2/ppermute | solution.py:263
  178.5 14.0 %collective-permute-start.24 = (bf16[256,1024]{1,0:T(8,128)(2,1)S(1)}, bf16[256,1024]{1,0:T(8,128)(2,1)S(1)}, u32[]{:S(2)}, u32[]{:S(2)}) collective-permute-start(bf16[256,1024]{1,0:T(8,128)(2,1)S(1)} %get-tuple-element.65), channel_id=1, source_target_pairs={{0,16},{8,24},{16,0},{24,8},{1,17},{9,25},{17,1},{25,9},{2,18},{10... | collective-permute-start | bytes 1572872 | tf_op jit(solution)/shard_map/back/ppermute | solution.py:268
  179.3 17.1 %collective-permute-start.26 = (bf16[256,1024]{1,0:T(8,128)(2,1)S(1)}, bf16[256,1024]{1,0:T(8,128)(2,1)S(1)}, u32[]{:S(2)}, u32[]{:S(2)}) collective-permute-start(bf16[256,1024]{1,0:T(8,128)(2,1)S(1)} %get-tuple-element.67), channel_id=1, source_target_pairs={{0,8},{8,0},{16,24},{24,16},{1,9},{9,1},{17,25},{25,17},{2,10},{10... | collective-permute-start | bytes 1572872 | tf_op jit(solution)/shard_map/back/ppermute | solution.py:268
  180.2 29.3 %collective-permute-start.29 = (bf16[256,768]{1,0:T(8,128)(2,1)S(1)}, bf16[256,768]{1,0:T(8,128)(2,1)S(1)}, u32[]{:S(2)}, u32[]{:S(2)}) collective-permute-start(bf16[256,768]{1,0:T(8,128)(2,1)S(1)} %get-tuple-element.78), channel_id=1, source_target_pairs={{0,2},{1,3},{2,4},{3,5},{4,6},{5,7},{8,10},{9,11},{10,12},{11,13},... | collective-permute-start | bytes 1179656 | tf_op jit(solution)/shard_map/scatter_step_3/ppermute | solution.py:263
  183.0 26.5 %collective-permute-start.31 = (bf16[256,768]{1,0:T(8,128)(2,1)S(1)}, bf16[256,768]{1,0:T(8,128)(2,1)S(1)}, u32[]{:S(2)}, u32[]{:S(2)}) collective-permute-start(bf16[256,768]{1,0:T(8,128)(2,1)S(1)} %get-tuple-element.79), channel_id=1, source_target_pairs={{2,0},{3,1},{4,2},{5,3},{6,4},{7,5},{10,8},{11,9},{12,10},{13,11},... | collective-permute-start | bytes 1179656 | tf_op jit(solution)/shard_map/scatter_step_3/ppermute | solution.py:263
  192.7 7.5 %collective-permute-start.25 = (bf16[128,1024]{1,0:T(8,128)(2,1)S(1)}, bf16[128,1024]{1,0:T(8,128)(2,1)S(1)}, u32[]{:S(2)}, u32[]{:S(2)}) collective-permute-start(bf16[128,1024]{1,0:T(8,128)(2,1)S(1)} %slice.210), channel_id=1, source_target_pairs={{0,8},{8,0},{16,24},{24,16},{1,9},{9,1},{17,25},{25,17},{2,10},{10... | collective-permute-start | bytes 786440 | tf_op jit(solution)/shard_map/back/ppermute | solution.py:268
  193.6 10.6 %collective-permute-start.36 = (bf16[256,768]{1,0:T(8,128)(2,1)S(1)}, bf16[256,768]{1,0:T(8,128)(2,1)S(1)}, u32[]{:S(2)}, u32[]{:S(2)}) collective-permute-start(bf16[256,768]{1,0:T(8,128)(2,1)S(1)} %fusion.22), channel_id=1, source_target_pairs={{0,2},{1,3},{6,4},{7,5},{8,10},{9,11},{14,12},{15,13},{16,18},{17,... | collective-permute-start | bytes 1179656 | tf_op jit(solution)/shard_map/scatter_step_1/ppermute | solution.py:263
  196.6 12.8 %collective-permute-start.27 = (bf16[128,1024]{1,0:T(8,128)(2,1)S(1)}, bf16[128,1024]{1,0:T(8,128)(2,1)S(1)}, u32[]{:S(2)}, u32[]{:S(2)}) collective-permute-start(bf16[128,1024]{1,0:T(8,128)(2,1)S(1)} %slice.209), channel_id=1, source_target_pairs={{0,16},{8,24},{16,0},{24,8},{1,17},{9,25},{17,1},{25,9},{2,18},{10... | collective-permute-start | bytes 786440 | tf_op jit(solution)/shard_map/back/ppermute | solution.py:268
  200.2 9.3 %copy-start.7 = (bf16[256,768]{1,0:T(8,128)(2,1)S(1)}, bf16[256,768]{1,0:T(8,128)(2,1)}, u32[]{:S(2)}) copy-start(bf16[256,768]{1,0:T(8,128)(2,1)} %copy-done.6) | copy-start | bytes 1179652
  204.3 11.3 %collective-permute-start.37 = (bf16[256,768]{1,0:T(8,128)(2,1)S(1)}, bf16[256,768]{1,0:T(8,128)(2,1)S(1)}, u32[]{:S(2)}, u32[]{:S(2)}) collective-permute-start(bf16[256,768]{1,0:T(8,128)(2,1)S(1)} %fusion.2), channel_id=1, source_target_pairs={{0,2},{1,3},{2,4},{3,5},{8,10},{9,11},{10,12},{11,13},{16,18},{17,... | collective-permute-start | bytes 1179656 | tf_op jit(solution)/shard_map/scatter_step_2/ppermute | solution.py:263
  208.7 6.8 %collective-permute-start.39 = (bf16[256,768]{1,0:T(8,128)(2,1)S(1)}, bf16[256,768]{1,0:T(8,128)(2,1)S(1)}, u32[]{:S(2)}, u32[]{:S(2)}) collective-permute-start(bf16[256,768]{1,0:T(8,128)(2,1)S(1)} %fusion.2), channel_id=1, source_target_pairs={{4,2},{5,3},{6,4},{7,5},{12,10},{13,11},{14,12},{15,13},{20,18},{2... | collective-permute-start | bytes 1179656 | tf_op jit(solution)/shard_map/scatter_step_2/ppermute | solution.py:263
  215.9 13.1 %collective-permute-start.38 = (bf16[256,768]{1,0:T(8,128)(2,1)S(1)}, bf16[256,768]{1,0:T(8,128)(2,1)S(1)}, u32[]{:S(2)}, u32[]{:S(2)}) collective-permute-start(bf16[256,768]{1,0:T(8,128)(2,1)S(1)} %get-tuple-element.76), channel_id=1, source_target_pairs={{0,2},{1,3},{2,4},{3,5},{4,6},{5,7},{8,10},{9,11},{10,12},{11,13},... | collective-permute-start | bytes 1179656 | tf_op jit(solution)/shard_map/scatter_step_3/ppermute | solution.py:263
  223.7 9.7 %collective-permute-start.40 = (bf16[256,768]{1,0:T(8,128)(2,1)S(1)}, bf16[256,768]{1,0:T(8,128)(2,1)S(1)}, u32[]{:S(2)}, u32[]{:S(2)}) collective-permute-start(bf16[256,768]{1,0:T(8,128)(2,1)S(1)} %get-tuple-element.77), channel_id=1, source_target_pairs={{2,0},{3,1},{4,2},{5,3},{6,4},{7,5},{10,8},{11,9},{12,10},{13,11},... | collective-permute-start | bytes 1179656 | tf_op jit(solution)/shard_map/scatter_step_3/ppermute | solution.py:263
  (18 other events, 19.9 us)
Sparse Core Ops, SparseCore 0:
  11.5 47.6 all-gather.2
  65.7 40.0 all-gather.4

commit v4 on v3

--- a/solution.py
+++ b/solution.py
@@ -1,6 +1,10 @@
 import jax
 import jax.numpy as jnp
 from jax import lax
+from jax.experimental import pallas as pl
+from jax.experimental.pallas import tpu as pltpu
+from jax.experimental import pallas as pl
+from jax.experimental.pallas import tpu as pltpu
 from jax.experimental import pallas as pl
 from jax.experimental.pallas import tpu as pltpu
 from jax.experimental import pallas as pl
@@ -101,7 +105,7 @@
 VMEM = pl.BlockSpec(memory_space=pltpu.VMEM)
 SMEM = pl.BlockSpec(memory_space=pltpu.SMEM)
 HBM = pl.BlockSpec(memory_space=pltpu.HBM)
-LIMIT = 28 << 20
+LIMIT = 58 << 20
 
 
 def call(body, ins, outs, operands, scratch=(), flops=0, limit=LIMIT):
@@ -117,10 +121,11 @@
     )(*operands)
 
 
-def pack_kernel(step, gate, up, down, *outs):
+def pack_kernel(step, first, gate, up, down, *outs):
     for i, out in enumerate(outs):
+        cols = slice((first + i) * step, (first + i + 1) * step)
         for m, ref in enumerate((gate, up, down)):
-            out[:, m * step : (m + 1) * step] = ref[:, i * step : (i + 1) * step]
+            out[:, m * step : (m + 1) * step] = ref[:, cols]
 
 
 def scale_kernel(experts, at, *refs):
@@ -134,10 +139,9 @@
         out[p * rows : (p + 1) * rows, :] = (gate * ref[:, :width].astype(F32)).astype(BF16)
 
 
-def chunk_kernel(line, n_pieces, whole, at, *refs):
-    pieces, scaled, refs = refs[:n_pieces], refs[n_pieces], refs[n_pieces + 1 :]
-    n_weights = 1 if whole else 2 * (2 * line - 1)
-    weights, refs = refs[:n_weights], refs[n_weights:]
+def chunk_kernel(line, n_pieces, at, *refs):
+    pieces, refs = refs[:n_pieces], refs[n_pieces:]
+    scaled, weights, refs = refs[0], refs[1], refs[2:]
     mine, theirs, merged, both = refs[:line], refs[line], refs[line + 1], refs[line + 2]
     x, g, w, hid, xsem, gsem, wsem = refs[line + 3 :]
     z, c = at[0], at[1]
@@ -154,28 +158,9 @@
     def owner(k, side):
         return lax.rem(z - k + line, line) * 2 + (c if side == 0 else 1 - c)
 
-    if whole:
-        for f in range(parts):
-            here = pl.ds(f * feats, feats)
-            pltpu.make_async_copy(weights[0].at[here, :], w.at[here, :], wsem.at[f]).start()
-    else:
-        for side in range(2):
-            own, *rest = weights[side * (2 * line - 1) : (side + 1) * (2 * line - 1)]
-            ups, downs = rest[: line - 1], rest[line - 1 :]
-            sem = wsem.at[side * line]
-            pltpu.make_async_copy(own, w.at[rows_of(owner(0, side)), :], sem).start()
-            for k in range(1, line):
-                to = w.at[rows_of(owner(k, side)), :]
-                sem = wsem.at[side * line + k]
-
-                @pl.when(z >= k)
-                def _(k=k, to=to, sem=sem, ups=ups):
-                    pltpu.make_async_copy(ups[k - 1], to, sem).start()
-
-                @pl.when(z < k)
-                def _(k=k, to=to, sem=sem, downs=downs):
-                    pltpu.make_async_copy(downs[line - k - 1], to, sem).start()
-
+    for f in range(parts):
+        here = pl.ds(f * feats, feats)
+        pltpu.make_async_copy(weights.at[here, :], w.at[here, :], wsem.at[f]).start()
     x_copies = [
         pltpu.make_async_copy(ref, x.at[pl.ds(p * rows, rows), :], xsem.at[p])
         for p, ref in enumerate(pieces)
@@ -219,23 +204,29 @@
     width = far.shape[1]
     tile = width // 4
 
-    def emit(out, blocks, first):
-        @pl.loop(0, 4)
-        def _(t):
-            cols = pl.ds(pl.multiple_of(t * tile, tile), tile)
-            for n, b in enumerate(blocks):
-                here = slice(b * rows, (b + 1) * rows)
-                total = None
-                for m, w in zip(merged, both):
-                    wide_cols = pl.ds(pl.multiple_of(first + t * tile, tile), tile)
-                    part = dot_nt(m[here, :], w[wide_cols, :])
-                    total = part if total is None else total + part
-                out[n * rows : (n + 1) * rows, cols] = total.astype(out.dtype)
-
-    emit(far, (2, 3), 0)
-    emit(odd, (1, 3), width)
-    emit(left, (0, 1), 0)
-    emit(right, (0, 2), width)
+    @pl.loop(0, 8)
+    def _(t):
+        cols = pl.ds(pl.multiple_of(t * tile, tile), tile)
+        total = None
+        for m, w in zip(merged, both):
+            part = dot_nt(m[...], w[cols, :])
+            total = part if total is None else total + part
+        blocks = [total[b * rows : (b + 1) * rows] for b in range(4)]
+
+        def emit(out, at, a, b):
+            here = pl.ds(pl.multiple_of(at * tile, tile), tile)
+            out[:rows, here] = blocks[a].astype(out.dtype)
+            out[rows:, here] = blocks[b].astype(out.dtype)
+
+        @pl.when(t < 4)
+        def _():
+            emit(far, t, 2, 3)
+            emit(left, t, 0, 1)
+
+        @pl.when(t >= 4)
+        def _():
+            emit(odd, t - 4, 1, 3)
+            emit(right, t - 4, 0, 2)
 
 
 def dense_plan(tokens, out_grad, routes, gate_prob, w_gate, w_up, w_down):
@@ -268,12 +259,12 @@
         return lax.ppermute(a, "expert", [(e, e ^ bit) for e in range(experts)])
 
     own = call(
-        lambda *r: pack_kernel(step, *r),
+        lambda *r: pack_kernel(step, 0, *r),
         [VMEM] * 3,
         [shape((feats, 3 * step), BF16)] * chunks,
         (w_gate[0], w_up[0], w_down[0]),
     )
-    whole = [lax.all_gather(a, "wide", axis=0, tiled=True) for a in own[1:]]
+    whole = [lax.all_gather(a, "wide", axis=0, tiled=True) for a in own]
 
     named = jnp.arange(experts, dtype=jnp.int32)[None, :]
     gates = sum(
@@ -285,25 +276,12 @@
     terms = jnp.concatenate((high, middle, gates - high - middle), axis=1).astype(BF16)
     terms = jnp.pad(terms, ((0, 0), (0, LANES - terms.shape[1])))
     graded = jnp.concatenate((out_grad, terms), axis=1)
-    def hop(ups, downs, s):
-        with jax.named_scope(f"gather_step_{s}"):
-            ups.append(along(ups[-1], [(i, i + 1) for i in range(s - 1, line - 1)]))
-            downs.append(along(downs[-1], [(i, i - 1) for i in range(1, line - s + 1)]))
-
-    ups, downs = [own[0]], [own[0]]
     with jax.named_scope("rows"):
         t = [tokens, flip(tokens, 1), flip(tokens, 2)]
         g = [graded, flip(graded, 1), flip(graded, 2)]
-    hop(ups, downs, 1)
-    with jax.named_scope("rows"):
-        near = (t[1], t[2], g[1], g[2], ups[1], downs[1])
+        near = (t[1], t[2], g[1], g[2])
         t.append(flip(after(t[1], *near), 2))
         g.append(flip(after(g[2], *near), 1))
-    for s in range(2, line):
-        hop(ups, downs, s)
-    held = (own[0], *ups[1:], *downs[1:])
-    held += tuple(twin(p) for p in held)
-    g[0] = after(graded, ups[2], downs[2])
     [scaled] = call(
         lambda *r: scale_kernel(experts, *r),
         [SMEM] + [VMEM] * len(g),
@@ -335,24 +313,22 @@
             with jax.named_scope(f"scatter_step_{s}"):
                 up = along(a, [(i, i + 1) for i in range(s)])
                 down = along(b, [(i, i - 1) for i in range(line - s, line)])
-            marks += [a, up]
+            marks += [a, b, up, down]
         total = parts[0].astype(F32) + swapped[0].astype(F32)
         return total + up.astype(F32) + down.astype(F32), marks
 
-    order = [1, 0, *range(2, chunks)]
-    merged, both, sums, marks = [], [], [], ()
+    merged, both, sums, marks, tie = [], [], [], (), ()
     for i in range(chunks):
-        weights = held if i == 1 else (whole[order[i] - 1],)
         got = call(
-            lambda *r, i=i: chunk_kernel(line, len(t), i != 1, *r),
-            [SMEM] + [HBM] * (len(t) + 1 + len(weights)),
+            lambda *r: chunk_kernel(line, len(t), *r),
+            [SMEM] + [HBM] * (len(t) + 2),
             [shape((feats, 3 * step), BF16)] * line
             + [
                 shape((line, feats, 3 * step), BF16),
                 shape((count, 2 * step), BF16),
                 shape((width, 2 * step), BF16),
             ],
-            (at, *t, after(scaled, *marks[:2]), *weights),
+            (at, *t, after(scaled, *tie), whole[i]),
             (
                 pltpu.VMEM((count, width), BF16),
                 pltpu.VMEM((count, width), BF16),
@@ -368,7 +344,8 @@
         both.append(got[line + 2])
         swapped = twin(got[line])
         if i < chunks - 1:
-            total, marks = scatter(got[:line], swapped, marks[2:3], ())
+            total, marks = scatter(got[:line], swapped, marks[3:5], ())
+            tie = marks[: 3 if i == 0 else 5]
             sums.append(total)
 
     far, odd, left, right = call(
@@ -386,11 +363,11 @@
         last = flip(right[rows:].astype(BF16), 2)
         left, right = left[:rows] + near.astype(F32), right[:rows] + last.astype(F32)
         grad_input = jnp.concatenate((left, right), axis=1).astype(BF16)
-    sums.append(scatter(got[:line], swapped, marks[2:3], halfway)[0])
+    sums.append(scatter(got[:line], swapped, marks[3:5], halfway)[0])
 
     def grad_of(j):
         cols = slice(j * step, (j + 1) * step)
-        return jnp.concatenate([sums[order.index(i)][:, cols] for i in range(chunks)], axis=1)[None]
+        return jnp.concatenate([a[:, cols] for a in sums], axis=1)[None]
 
     return (grad_input, grad_of(0), grad_of(1), grad_of(2))
 

time: 244 us -> 251 us (1.029)
  local copies, waits for them, and re-layouts: 18.9 us -> 2.9 us
  Pallas kernels: 36.3 us -> 45.7 us
  starting transfers between devices: 66.5 us -> 74.6 us
  waiting for transfers between devices: 93.7 us -> 98.5 us
    ppermute x10, waiting for transfers between devices: 11.2 us -> 40 us  [flip(): return lax.ppermute(a, 'expert', [(e, e ^ bit) for e in range(experts)])]
    ppermute x21 -> x15, waiting for transfers between devices: 80.8 us -> 54.2 us  [along(): lax.ppermute(a, 'wide', [(2 * s + i, 2 * t + i) for s, t in hops for i in...]
    unnamed x78 -> x50, local copies, waits for them, and re-layouts: 18.6 us -> 2.51 us
    pallas_call x6, Pallas kernels: 36.3 us -> 45.7 us  [call(): pl.pallas_call(body, out_shape=outs, in_specs=ins, out_specs=[VMEM] * len...]
    ppermute x21 -> x15, starting transfers between devices: 55.4 us -> 64.1 us  [along(): lax.ppermute(a, 'wide', [(2 * s + i, 2 * t + i) for s, t in hops for i in...]
  transfers between devices with their start and end apart: 43 -> 31, of which waited for: 15 -> 12; matrix products, arithmetic and copies ran while one was open for 4% -> 5% of each run, Pallas kernels for 14% -> 17%
where the time goes in v4:
time: 251 us; the launch traced here: 250 us
  waiting for transfers between devices  98.5 us (39%)
  starting transfers between devices  74.6 us (30%)
  Pallas kernels  45.7 us (18%)
  between operations  14.4 us (6%)
  other arithmetic  13.9 us (6%)
  local copies, waits for them, and re-layouts  2.9 us (1%)
    ppermute x15, starting transfers between devices, along(): lax.ppermute(a, 'wide', [(2 * s + i, 2 * t + i) for s, t in hops for i in...  64.1 us
    ppermute x15, waiting for transfers between devices, along(): lax.ppermute(a, 'wide', [(2 * s + i, 2 * t + i) for s, t in hops for i in...  54.2 us
    pallas_call x6, Pallas kernels, call(): pl.pallas_call(body, out_shape=outs, in_specs=ins, out_specs=[VMEM] * len...  45.7 us
    ppermute x10, waiting for transfers between devices, flip(): return lax.ppermute(a, 'expert', [(e, e ^ bit) for e in range(experts)])  40 us
    ppermute x10, starting transfers between devices, flip(): return lax.ppermute(a, 'expert', [(e, e ^ bit) for e in range(experts)])  10.2 us
  transfers between devices with their start and end apart: 31, of which 12 were waited for; matrix products, arithmetic and copies ran while one was open for 5% of the time, Pallas kernels for 17%

profile of v4, /device:TPU:0, one launch (start us, length us, event | category | flops | bytes accessed | tf_op | source)
XLA Modules:
  0.0 250.0 jit_solution(5082641729497663970)
XLA Ops:
  7.3 2.3 shard_map.103
  9.7 0.7 all-gather.6.cloned.1.call-update
  10.7 3.0 %collective-permute-start.2 = (bf16[128,2176]{1,0:T(8,128)(2,1)S(1)}, bf16[128,2176]{1,0:T(8,128)(2,1)S(1)}, u32[]{:S(2)}, u32[]{:S(2)}) collective-permute-start(bf16[128,2176]{1,0:T(8,128)(2,1)S(1)} %fusion.19.r_1_), channel_id=1, source_target_pairs={{0,8},{8,0},{16,24},{24,16},{1,9},{9,1},{17,25},{25,17},{2,10},{10... | collective-permute-start | bytes 1671176 | tf_op jit(solution)/shard_map/rows/ppermute | solution.py:259
  13.7 1.5 collective-permute-start.3
  15.2 0.5 collective-permute-start
  15.8 21.8 %collective-permute-done.r_2_ = bf16[128,2048]{1,0:T(8,128)(2,1)S(1)} collective-permute-done((bf16[128,2048]{1,0:T(8,128)(2,1)S(1)}, bf16[128,2048]{1,0:T(8,128)(2,1)S(1)}, u32[]{:S(2)}, u32[]{:S(2)}) %collective-permute-start) | collective-permute-done | bytes 524320 | tf_op jit(solution)/shard_map/rows/ppermute | solution.py:259
  37.5 1.5 collective-permute-done.1.r_3_
  39.0 0.8 copy-done.23
  39.8 0.4 collective-permute-start.5
  40.3 1.6 collective-permute-start.4
  41.9 0.6 pad_add_fusion.r_0_
  42.4 10.7 %collective-permute-done.5.r_4_ = bf16[128,2176]{1,0:T(8,128)(2,1)S(1)} collective-permute-done((bf16[128,2176]{1,0:T(8,128)(2,1)S(1)}, bf16[128,2176]{1,0:T(8,128)(2,1)S(1)}, u32[]{:S(2)}, u32[]{:S(2)}) %collective-permute-start.5) | collective-permute-done | bytes 557088 | tf_op jit(solution)/shard_map/rows/ppermute | solution.py:259
  53.1 0.8 copy-done.11
  54.0 3.3 %shard_map.102.r_5_ = bf16[512,2048]{1,0:T(8,128)(2,1)} custom-call(s32[3]{0:T(128)} %pad_add_fusion.r_0_, bf16[128,2176]{1,0:T(8,128)(2,1)} %copy-done, bf16[128,2176]{1,0:T(8,128)(2,1)} %copy-done.9, bf16[128,2176]{1,0:T(8,128)(2,1)} %copy-done.10, bf16[128,2176]{1,0:T(8,128)(2,1)} %copy-done.11), custom_call_target="tpu_custom_call" | custom-call | bytes 4325388 | tf_op jit(solution)/shard_map/pallas_call | solution.py:113
  57.4 0.8 copy-done.24
  58.1 10.1 %shard_map.104 = (bf16[256,768]{1,0:T(8,128)(2,1)}, bf16[256,768]{1,0:T(8,128)(2,1)}, bf16[256,768]{1,0:T(8,128)(2,1)}, bf16[256,768]{1,0:T(8,128)(2,1)}, bf16[4...) custom-call(s32[3]{0:T(128)} %pad_add_fusion.r_0_, bf16[128,2048]{1,0:T(8,128)(2,1)} %r_1_.5, ...), custom_call_target="tpu_custom_call" | custom-call | flops 3221225472 | bytes 13107212 | tf_op jit(solution)/shard_map/pallas_call | solution.py:113
  68.3 3.6 %collective-permute-done.6 = bf16[4,256,768]{2,1,0:T(8,128)(2,1)S(1)} collective-permute-done((bf16[4,256,768]{2,1,0:T(8,128)(2,1)}, bf16[4,256,768]{2,1,0:T(8,128)(2,1)S(1)}, u32[]{:S(2)}, u32[]{:S(2)}) %collective-permute-start.6) | collective-permute-done | bytes 1572896 | tf_op jit(solution)/shard_map/ppermute | solution.py:251
  71.9 1.3 fusion.24
  73.3 3.5 %collective-permute-start.7 = (bf16[256,768]{1,0:T(8,128)(2,1)S(1)}, bf16[256,768]{1,0:T(8,128)(2,1)S(1)}, u32[]{:S(2)}, u32[]{:S(2)}) collective-permute-start(bf16[256,768]{1,0:T(8,128)(2,1)S(1)} %fusion.24), channel_id=1, source_target_pairs={{0,2},{1,3},{6,4},{7,5},{8,10},{9,11},{14,12},{15,13},{16,18},{17,... | collective-permute-start | bytes 1179656 | tf_op jit(solution)/shard_map/scatter_step_1/ppermute | solution.py:254
  76.8 16.4 %collective-permute-done.7 = bf16[256,768]{1,0:T(8,128)(2,1)S(1)} collective-permute-done((bf16[256,768]{1,0:T(8,128)(2,1)S(1)}, bf16[256,768]{1,0:T(8,128)(2,1)S(1)}, u32[]{:S(2)}, u32[]{:S(2)}) %collective-permute-start.7) | collective-permute-done | bytes 393248 | tf_op jit(solution)/shard_map/scatter_step_1/ppermute | solution.py:254
  93.2 0.1 fusion.12
  93.3 9.9 %shard_map.105 = (bf16[256,768]{1,0:T(8,128)(2,1)}, bf16[256,768]{1,0:T(8,128)(2,1)}, bf16[256,768]{1,0:T(8,128)(2,1)}, bf16[256,768]{1,0:T(8,128)(2,1)}, bf16[4...) custom-call(s32[3]{0:T(128)} %pad_add_fusion.r_0_, bf16[128,2048]{1,0:T(8,128)(2,1)} %r_1_.5, ...), custom_call_target="tpu_custom_call" | custom-call | flops 3221225472 | bytes 13107212 | tf_op jit(solution)/shard_map/pallas_call | solution.py:113
  103.4 0.8 collective-permute-start.10
  104.2 7.1 %collective-permute-start.9 = (bf16[256,768]{1,0:T(8,128)(2,1)S(1)}, bf16[256,768]{1,0:T(8,128)(2,1)S(1)}, u32[]{:S(2)}, u32[]{:S(2)}) collective-permute-start(bf16[256,768]{1,0:T(8,128)(2,1)S(1)} %fusion.12), channel_id=1, source_target_pairs={{0,2},{1,3},{2,4},{3,5},{8,10},{9,11},{10,12},{11,13},{16,18},{17,... | collective-permute-start | bytes 1179656 | tf_op jit(solution)/shard_map/scatter_step_2/ppermute | solution.py:254
  111.3 1.4 fusion.23
  112.7 16.2 %collective-permute-done.9 = bf16[256,768]{1,0:T(8,128)(2,1)S(1)} collective-permute-done((bf16[256,768]{1,0:T(8,128)(2,1)S(1)}, bf16[256,768]{1,0:T(8,128)(2,1)S(1)}, u32[]{:S(2)}, u32[]{:S(2)}) %collective-permute-start.9) | collective-permute-done | bytes 393248 | tf_op jit(solution)/shard_map/scatter_step_2/ppermute | solution.py:254
  128.9 12.5 %collective-permute-start.11 = (bf16[256,768]{1,0:T(8,128)(2,1)S(1)}, bf16[256,768]{1,0:T(8,128)(2,1)S(1)}, u32[]{:S(2)}, u32[]{:S(2)}) collective-permute-start(bf16[256,768]{1,0:T(8,128)(2,1)S(1)} %fusion.23), channel_id=1, source_target_pairs={{0,2},{1,3},{6,4},{7,5},{8,10},{9,11},{14,12},{15,13},{16,18},{17,... | collective-permute-start | bytes 1179656 | tf_op jit(solution)/shard_map/scatter_step_1/ppermute | solution.py:254
  141.4 7.6 %collective-permute-done.11 = bf16[256,768]{1,0:T(8,128)(2,1)S(1)} collective-permute-done((bf16[256,768]{1,0:T(8,128)(2,1)S(1)}, bf16[256,768]{1,0:T(8,128)(2,1)S(1)}, u32[]{:S(2)}, u32[]{:S(2)}) %collective-permute-start.11) | collective-permute-done | bytes 393248 | tf_op jit(solution)/shard_map/scatter_step_1/ppermute | solution.py:254
  148.9 0.1 fusion.10
  149.1 5.1 %collective-permute-start.12 = (bf16[256,768]{1,0:T(8,128)(2,1)S(1)}, bf16[256,768]{1,0:T(8,128)(2,1)}, u32[]{:S(2)}, u32[]{:S(2)}) collective-permute-start(bf16[256,768]{1,0:T(8,128)(2,1)S(1)} %fusion.10), channel_id=1, source_target_pairs={{0,2},{1,3},{2,4},{3,5},{8,10},{9,11},{10,12},{11,13},{16,18},{17,... | collective-permute-start | bytes 1179656 | tf_op jit(solution)/shard_map/scatter_step_2/ppermute | solution.py:254
  154.2 1.4 collective-permute-start.13
  155.6 1.2 add_convert_fusion.5
  156.8 5.1 %collective-permute-start.18 = (bf16[256,768]{1,0:T(8,128)(2,1)}, bf16[256,768]{1,0:T(8,128)(2,1)}, u32[]{:S(2)}, u32[]{:S(2)}) collective-permute-start(bf16[256,768]{1,0:T(8,128)(2,1)} %get-tuple-element.76), channel_id=1, source_target_pairs={{0,2},{1,3},{2,4},{3,5},{4,6},{5,7},{8,10},{9,11},{10,12},{11,13},... | collective-permute-start | bytes 1179656 | tf_op jit(solution)/shard_map/scatter_step_3/ppermute | solution.py:254
  162.0 1.6 collective-permute-start.19
  163.6 9.8 %shard_map.106 = (bf16[256,768]{1,0:T(8,128)(2,1)}, bf16[256,768]{1,0:T(8,128)(2,1)}, bf16[256,768]{1,0:T(8,128)(2,1)}, bf16[256,768]{1,0:T(8,128)(2,1)}, bf16[4...) custom-call(s32[3]{0:T(128)} %pad_add_fusion.r_0_, bf16[128,2048]{1,0:T(8,128)(2,1)} %r_1_.5, ...), custom_call_target="tpu_custom_call" | custom-call | flops 3221225472 | bytes 13107212 | tf_op jit(solution)/shard_map/pallas_call | solution.py:113
  173.6 1.4 fusion.8
  174.9 2.2 add_convert_fusion.3
  177.1 7.9 %collective-permute-start.20 = (bf16[256,768]{1,0:T(8,128)(2,1)}, bf16[256,768]{1,0:T(8,128)(2,1)S(1)}, u32[]{:S(2)}, u32[]{:S(2)}) collective-permute-start(bf16[256,768]{1,0:T(8,128)(2,1)} %get-tuple-element.78), channel_id=1, source_target_pairs={{0,2},{1,3},{2,4},{3,5},{4,6},{5,7},{8,10},{9,11},{10,12},{11,13},... | collective-permute-start | bytes 1179656 | tf_op jit(solution)/shard_map/scatter_step_3/ppermute | solution.py:254
  185.0 1.3 collective-permute-start.21
  186.4 10.2 %shard_map.107 = (bf16[256,1024]{1,0:T(8,128)(2,1)}, bf16[256,1024]{1,0:T(8,128)(2,1)}, f32[256,1024]{1,0:T(8,128)}, f32[256,1024]{1,0:T(8,128)}) custom-call(bf16[512,512]{1,0:T(8,128)(2,1)} %get-tuple-element.43.r_0_, bf16[512,512]{1,0:T(8,128)(2,1)} %get-tuple-element.50.r_1_, bf16[512,512]{1,0:T(8,128)(2,1)} %get-tuple-element.58.r_2_, ...), custom_call_target="tpu_custom_call" | custom-call | flops 3221225472 | bytes 11010048 | tf_op jit(solution)/shard_map/pallas_call | solution.py:113
  196.6 1.4 collective-permute-start.14
  197.9 0.5 collective-permute-start.16
  198.5 1.2 fusion.6
  199.7 0.2 fusion.22
  199.9 4.7 %collective-permute-start.23 = (bf16[256,768]{1,0:T(8,128)(2,1)S(1)}, bf16[256,768]{1,0:T(8,128)(2,1)S(1)}, u32[]{:S(2)}, u32[]{:S(2)}) collective-permute-start(bf16[256,768]{1,0:T(8,128)(2,1)S(1)} %fusion.22), channel_id=1, source_target_pairs={{0,2},{1,3},{6,4},{7,5},{8,10},{9,11},{14,12},{15,13},{16,18},{17,... | collective-permute-start | bytes 1179656 | tf_op jit(solution)/shard_map/scatter_step_1/ppermute | solution.py:254
  204.7 6.1 %collective-permute-done.14 = bf16[256,1024]{1,0:T(8,128)(2,1)S(1)} collective-permute-done((bf16[256,1024]{1,0:T(8,128)(2,1)}, bf16[256,1024]{1,0:T(8,128)(2,1)S(1)}, u32[]{:S(2)}, u32[]{:S(2)}) %collective-permute-start.14) | collective-permute-done | bytes 524320 | tf_op jit(solution)/shard_map/back/ppermute | solution.py:259
  210.7 0.2 convert_add_fusion.1
  211.0 0.5 collective-permute-start.15
  211.4 1.0 collective-permute-done.23
  212.4 0.2 fusion.2
  212.6 4.4 %collective-permute-start.24 = (bf16[256,768]{1,0:T(8,128)(2,1)S(1)}, bf16[256,768]{1,0:T(8,128)(2,1)S(1)}, u32[]{:S(2)}, u32[]{:S(2)}) collective-permute-start(bf16[256,768]{1,0:T(8,128)(2,1)S(1)} %fusion.2), channel_id=1, source_target_pairs={{0,2},{1,3},{2,4},{3,5},{8,10},{9,11},{10,12},{11,13},{16,18},{17,... | collective-permute-start | bytes 1179656 | tf_op jit(solution)/shard_map/scatter_step_2/ppermute | solution.py:254
  217.0 0.7 collective-permute-start.26
  217.7 0.2 convert_add_fusion
  217.9 0.7 collective-permute-start.17
  218.7 5.2 %collective-permute-done.24 = bf16[256,768]{1,0:T(8,128)(2,1)S(1)} collective-permute-done((bf16[256,768]{1,0:T(8,128)(2,1)S(1)}, bf16[256,768]{1,0:T(8,128)(2,1)S(1)}, u32[]{:S(2)}, u32[]{:S(2)}) %collective-permute-start.24) | collective-permute-done | bytes 393248 | tf_op jit(solution)/shard_map/scatter_step_2/ppermute | solution.py:254
  223.9 0.3 add_convert_fusion.1
  224.2 6.7 %collective-permute-start.25 = (bf16[256,768]{1,0:T(8,128)(2,1)S(1)}, bf16[256,768]{1,0:T(8,128)(2,1)S(1)}, u32[]{:S(2)}, u32[]{:S(2)}) collective-permute-start(bf16[256,768]{1,0:T(8,128)(2,1)S(1)} %get-tuple-element.74), channel_id=1, source_target_pairs={{0,2},{1,3},{2,4},{3,5},{4,6},{5,7},{8,10},{9,11},{10,12},{11,13},... | collective-permute-start | bytes 1179656 | tf_op jit(solution)/shard_map/scatter_step_3/ppermute | solution.py:254
  230.9 1.3 collective-permute-start.27
  232.3 0.8 pad_maximum_fusion
  233.1 3.8 %collective-permute-done.25 = bf16[256,768]{1,0:T(8,128)(2,1)S(1)} collective-permute-done((bf16[256,768]{1,0:T(8,128)(2,1)S(1)}, bf16[256,768]{1,0:T(8,128)(2,1)S(1)}, u32[]{:S(2)}, u32[]{:S(2)}) %collective-permute-start.25) | collective-permute-done | bytes 393248 | tf_op jit(solution)/shard_map/scatter_step_3/ppermute | solution.py:254
  236.9 4.1 %collective-permute-done.27 = bf16[256,768]{1,0:T(8,128)(2,1)S(1)} collective-permute-done((bf16[256,768]{1,0:T(8,128)(2,1)S(1)}, bf16[256,768]{1,0:T(8,128)(2,1)S(1)}, u32[]{:S(2)}, u32[]{:S(2)}) %collective-permute-start.27) | collective-permute-done | bytes 393248 | tf_op jit(solution)/shard_map/scatter_step_3/ppermute | solution.py:254
  241.0 0.2 fusion.4
  241.3 0.9 maximum_bitcast_fusion.2
  242.2 1.2 maximum_bitcast_fusion
  (88 shorter events, 1.2 us)
Async XLA Ops:
  7.2 3.2 %copy-start.19 = (s32[128,2]{0,1:T(2,128)S(1)}, s32[128,2]{0,1:T(2,128)}, u32[]{:S(2)}) copy-start(s32[128,2]{0,1:T(2,128)} %param.9) | copy-start | bytes 3076
  7.2 3.3 %copy-start.20 = (f32[128,2]{0,1:T(2,128)S(1)}, f32[128,2]{0,1:T(2,128)}, u32[]{:S(2)}) copy-start(f32[128,2]{0,1:T(2,128)} %param.10) | copy-start | bytes 3076
  7.2 3.4 %copy-start.12 = (bf16[128,2048]{1,0:T(8,128)(2,1)S(1)}, bf16[128,2048]{1,0:T(8,128)(2,1)}, u32[]{:S(2)}) copy-start(bf16[128,2048]{1,0:T(8,128)(2,1)} %param.8) | copy-start | bytes 1572868
  7.2 50.1 %all-gather.4.cloned.1.call-start = ((), (), s32[]{:S(2)}) async-start(), calls=%async_computation | async-start | bytes 3538944 | tf_op jit(solution)/shard_map/all_gather | solution.py:267
  7.2 8.0 %copy-start.21 = (bf16[128,2048]{1,0:T(8,128)(2,1)S(1)}, bf16[128,2048]{1,0:T(8,128)(2,1)}, u32[]{:S(2)}) copy-start(bf16[128,2048]{1,0:T(8,128)(2,1)} %r_1_.5) | copy-start | bytes 1572868
  9.6 83.7 %all-gather.6.cloned.1.call-start = ((), (), s32[]{:S(2)}) async-start(), calls=%async_computation.1 | async-start | bytes 3538944 | tf_op jit(solution)/shard_map/all_gather | solution.py:267
  10.4 153.2 %all-gather.8.cloned.1.call-start = ((), (), s32[]{:S(2)}) async-start(), calls=%async_computation.2 | async-start | bytes 3538944 | tf_op jit(solution)/shard_map/all_gather | solution.py:267
  10.7 42.4 %copy-start = (bf16[128,2176]{1,0:T(8,128)(2,1)}, bf16[128,2176]{1,0:T(8,128)(2,1)S(1)}, u32[]{:S(2)}) copy-start(bf16[128,2176]{1,0:T(8,128)(2,1)S(1)} %fusion.19.r_1_) | copy-start | bytes 1671172
  10.7 28.3 %collective-permute-start.2 = (bf16[128,2176]{1,0:T(8,128)(2,1)S(1)}, bf16[128,2176]{1,0:T(8,128)(2,1)S(1)}, u32[]{:S(2)}, u32[]{:S(2)}) collective-permute-start(bf16[128,2176]{1,0:T(8,128)(2,1)S(1)} %fusion.19.r_1_), channel_id=1, source_target_pairs={{0,8},{8,0},{16,24},{24,16},{1,9},{9,1},{17,25},{25,17},{2,10},{10... | collective-permute-start | bytes 1671176 | tf_op jit(solution)/shard_map/rows/ppermute | solution.py:259
  13.7 26.1 %collective-permute-start.3 = (bf16[128,2176]{1,0:T(8,128)(2,1)S(1)}, bf16[128,2176]{1,0:T(8,128)(2,1)S(1)}, u32[]{:S(2)}, u32[]{:S(2)}) collective-permute-start(bf16[128,2176]{1,0:T(8,128)(2,1)S(1)} %fusion.19.r_1_), channel_id=1, source_target_pairs={{0,16},{8,24},{16,0},{24,8},{1,17},{9,25},{17,1},{25,9},{2,18},{10... | collective-permute-start | bytes 1671176 | tf_op jit(solution)/shard_map/rows/ppermute | solution.py:259
  15.2 22.3 %collective-permute-start = (bf16[128,2048]{1,0:T(8,128)(2,1)S(1)}, bf16[128,2048]{1,0:T(8,128)(2,1)S(1)}, u32[]{:S(2)}, u32[]{:S(2)}) collective-permute-start(bf16[128,2048]{1,0:T(8,128)(2,1)S(1)} %copy-done.21), channel_id=1, source_target_pairs={{0,8},{8,0},{16,24},{24,16},{1,9},{9,1},{17,25},{25,17},{2,10},{10... | collective-permute-start | bytes 1572872 | tf_op jit(solution)/shard_map/rows/ppermute | solution.py:259
  15.7 23.3 %collective-permute-start.1 = (bf16[128,2048]{1,0:T(8,128)(2,1)S(1)}, bf16[128,2048]{1,0:T(8,128)(2,1)S(1)}, u32[]{:S(2)}, u32[]{:S(2)}) collective-permute-start(bf16[128,2048]{1,0:T(8,128)(2,1)S(1)} %copy-done.21), channel_id=1, source_target_pairs={{0,16},{8,24},{16,0},{24,8},{1,17},{9,25},{17,1},{25,9},{2,18},{10... | collective-permute-start | bytes 1572872 | tf_op jit(solution)/shard_map/rows/ppermute | solution.py:259
  37.5 19.8 %copy-start.22 = (bf16[128,2048]{1,0:T(8,128)(2,1)}, bf16[128,2048]{1,0:T(8,128)(2,1)S(1)}, u32[]{:S(2)}) copy-start(bf16[128,2048]{1,0:T(8,128)(2,1)S(1)} %collective-permute-done.r_2_) | copy-start | bytes 1572868
  39.0 0.8 copy-start.23
  39.8 13.3 %copy-start.9 = (bf16[128,2176]{1,0:T(8,128)(2,1)}, bf16[128,2176]{1,0:T(8,128)(2,1)S(1)}, u32[]{:S(2)}) copy-start(bf16[128,2176]{1,0:T(8,128)(2,1)S(1)} %collective-permute-done.2.r_2_) | copy-start | bytes 1671172
  39.8 13.3 %copy-start.10 = (bf16[128,2176]{1,0:T(8,128)(2,1)}, bf16[128,2176]{1,0:T(8,128)(2,1)S(1)}, u32[]{:S(2)}) copy-start(bf16[128,2176]{1,0:T(8,128)(2,1)S(1)} %collective-permute-done.3.r_3_) | copy-start | bytes 1671172
  39.8 13.3 %collective-permute-start.5 = (bf16[128,2176]{1,0:T(8,128)(2,1)S(1)}, bf16[128,2176]{1,0:T(8,128)(2,1)S(1)}, u32[]{:S(2)}, u32[]{:S(2)}) collective-permute-start(bf16[128,2176]{1,0:T(8,128)(2,1)S(1)} %collective-permute-done.3.r_3_), channel_id=1, source_target_pairs={{0,8},{8,0},{16,24},{24,16},{1,9},{9,1},{17,25},{25,17},{2,10},{10... | collective-permute-start | bytes 1671176 | tf_op jit(solution)/shard_map/rows/ppermute | solution.py:259
  40.3 17.1 %collective-permute-start.4 = (bf16[128,2048]{1,0:T(8,128)(2,1)S(1)}, bf16[128,2048]{1,0:T(8,128)(2,1)S(1)}, u32[]{:S(2)}, u32[]{:S(2)}) collective-permute-start(bf16[128,2048]{1,0:T(8,128)(2,1)S(1)} %collective-permute-done.r_2_), channel_id=1, source_target_pairs={{0,16},{8,24},{16,0},{24,8},{1,17},{9,25},{17,1},{25,9},{2,18},{10... | collective-permute-start | bytes 1572872 | tf_op jit(solution)/shard_map/rows/ppermute | solution.py:259
  53.1 0.8 copy-start.11
  57.3 0.8 copy-start.24
  68.2 24.9 %copy-start.18 = (bf16[256,768]{1,0:T(8,128)(2,1)S(1)}, bf16[256,768]{1,0:T(8,128)(2,1)}, u32[]{:S(2)}) copy-start(bf16[256,768]{1,0:T(8,128)(2,1)} %get-tuple-element.47) | copy-start | bytes 1179652
  68.2 3.7 %collective-permute-start.6 = (bf16[4,256,768]{2,1,0:T(8,128)(2,1)}, bf16[4,256,768]{2,1,0:T(8,128)(2,1)S(1)}, u32[]{:S(2)}, u32[]{:S(2)}) collective-permute-start(bf16[4,256,768]{2,1,0:T(8,128)(2,1)} %get-tuple-element.45), channel_id=1, source_target_pairs={{0,1},{1,0},{2,3},{3,2},{4,5},{5,4},{6,7},{7,6},{8,9},{9,8},{10,11... | collective-permute-start | bytes 4718600 | tf_op jit(solution)/shard_map/ppermute | solution.py:251
  73.3 19.9 %collective-permute-start.7 = (bf16[256,768]{1,0:T(8,128)(2,1)S(1)}, bf16[256,768]{1,0:T(8,128)(2,1)S(1)}, u32[]{:S(2)}, u32[]{:S(2)}) collective-permute-start(bf16[256,768]{1,0:T(8,128)(2,1)S(1)} %fusion.24), channel_id=1, source_target_pairs={{0,2},{1,3},{6,4},{7,5},{8,10},{9,11},{14,12},{15,13},{16,18},{17,... | collective-permute-start | bytes 1179656 | tf_op jit(solution)/shard_map/scatter_step_1/ppermute | solution.py:254
  103.3 45.6 %copy-start.17 = (bf16[256,768]{1,0:T(8,128)(2,1)S(1)}, bf16[256,768]{1,0:T(8,128)(2,1)}, u32[]{:S(2)}) copy-start(bf16[256,768]{1,0:T(8,128)(2,1)} %get-tuple-element.55) | copy-start | bytes 1179652
  103.3 8.0 %collective-permute-start.8 = (bf16[4,256,768]{2,1,0:T(8,128)(2,1)}, bf16[4,256,768]{2,1,0:T(8,128)(2,1)S(1)}, u32[]{:S(2)}, u32[]{:S(2)}) collective-permute-start(bf16[4,256,768]{2,1,0:T(8,128)(2,1)} %get-tuple-element.52), channel_id=1, source_target_pairs={{0,1},{1,0},{2,3},{3,2},{4,5},{5,4},{6,7},{7,6},{8,9},{9,8},{10,11... | collective-permute-start | bytes 4718600 | tf_op jit(solution)/shard_map/ppermute | solution.py:251
  103.4 9.3 %collective-permute-start.10 = (bf16[256,768]{1,0:T(8,128)(2,1)S(1)}, bf16[256,768]{1,0:T(8,128)(2,1)S(1)}, u32[]{:S(2)}, u32[]{:S(2)}) collective-permute-start(bf16[256,768]{1,0:T(8,128)(2,1)S(1)} %fusion.12), channel_id=1, source_target_pairs={{4,2},{5,3},{6,4},{7,5},{12,10},{13,11},{14,12},{15,13},{20,18},{2... | collective-permute-start | bytes 1179656 | tf_op jit(solution)/shard_map/scatter_step_2/ppermute | solution.py:254
  104.2 24.7 %collective-permute-start.9 = (bf16[256,768]{1,0:T(8,128)(2,1)S(1)}, bf16[256,768]{1,0:T(8,128)(2,1)S(1)}, u32[]{:S(2)}, u32[]{:S(2)}) collective-permute-start(bf16[256,768]{1,0:T(8,128)(2,1)S(1)} %fusion.12), channel_id=1, source_target_pairs={{0,2},{1,3},{2,4},{3,5},{8,10},{9,11},{10,12},{11,13},{16,18},{17,... | collective-permute-start | bytes 1179656 | tf_op jit(solution)/shard_map/scatter_step_2/ppermute | solution.py:254
  111.3 44.4 %copy-start.5 = (bf16[256,768]{1,0:T(8,128)(2,1)S(1)}, bf16[256,768]{1,0:T(8,128)(2,1)}, u32[]{:S(2)}) copy-start(bf16[256,768]{1,0:T(8,128)(2,1)} %get-tuple-element.44) | copy-start | bytes 1179652
  111.3 44.3 %copy-start.6 = (bf16[256,768]{1,0:T(8,128)(2,1)S(1)}, bf16[256,768]{1,0:T(8,128)(2,1)}, u32[]{:S(2)}) copy-start(bf16[256,768]{1,0:T(8,128)(2,1)} %get-tuple-element.46) | copy-start | bytes 1179652
  128.9 20.0 %collective-permute-start.11 = (bf16[256,768]{1,0:T(8,128)(2,1)S(1)}, bf16[256,768]{1,0:T(8,128)(2,1)S(1)}, u32[]{:S(2)}, u32[]{:S(2)}) collective-permute-start(bf16[256,768]{1,0:T(8,128)(2,1)S(1)} %fusion.23), channel_id=1, source_target_pairs={{0,2},{1,3},{6,4},{7,5},{8,10},{9,11},{14,12},{15,13},{16,18},{17,... | collective-permute-start | bytes 1179656 | tf_op jit(solution)/shard_map/scatter_step_1/ppermute | solution.py:254
  149.1 14.5 %collective-permute-start.12 = (bf16[256,768]{1,0:T(8,128)(2,1)S(1)}, bf16[256,768]{1,0:T(8,128)(2,1)}, u32[]{:S(2)}, u32[]{:S(2)}) collective-permute-start(bf16[256,768]{1,0:T(8,128)(2,1)S(1)} %fusion.10), channel_id=1, source_target_pairs={{0,2},{1,3},{2,4},{3,5},{8,10},{9,11},{10,12},{11,13},{16,18},{17,... | collective-permute-start | bytes 1179656 | tf_op jit(solution)/shard_map/scatter_step_2/ppermute | solution.py:254
  154.2 9.4 %collective-permute-start.13 = (bf16[256,768]{1,0:T(8,128)(2,1)S(1)}, bf16[256,768]{1,0:T(8,128)(2,1)}, u32[]{:S(2)}, u32[]{:S(2)}) collective-permute-start(bf16[256,768]{1,0:T(8,128)(2,1)S(1)} %fusion.10), channel_id=1, source_target_pairs={{4,2},{5,3},{6,4},{7,5},{12,10},{13,11},{14,12},{15,13},{20,18},{2... | collective-permute-start | bytes 1179656 | tf_op jit(solution)/shard_map/scatter_step_2/ppermute | solution.py:254
  156.8 16.7 %collective-permute-start.18 = (bf16[256,768]{1,0:T(8,128)(2,1)}, bf16[256,768]{1,0:T(8,128)(2,1)}, u32[]{:S(2)}, u32[]{:S(2)}) collective-permute-start(bf16[256,768]{1,0:T(8,128)(2,1)} %get-tuple-element.76), channel_id=1, source_target_pairs={{0,2},{1,3},{2,4},{3,5},{4,6},{5,7},{8,10},{9,11},{10,12},{11,13},... | collective-permute-start | bytes 1179656 | tf_op jit(solution)/shard_map/scatter_step_3/ppermute | solution.py:254
  162.0 11.6 %copy-start.15 = (bf16[256,768]{1,0:T(8,128)(2,1)S(1)}, bf16[256,768]{1,0:T(8,128)(2,1)}, u32[]{:S(2)}) copy-start(bf16[256,768]{1,0:T(8,128)(2,1)} %get-tuple-element.66) | copy-start | bytes 1179652
  162.0 11.6 %collective-permute-start.19 = (bf16[256,768]{1,0:T(8,128)(2,1)}, bf16[256,768]{1,0:T(8,128)(2,1)}, u32[]{:S(2)}, u32[]{:S(2)}) collective-permute-start(bf16[256,768]{1,0:T(8,128)(2,1)} %get-tuple-element.77), channel_id=1, source_target_pairs={{2,0},{3,1},{4,2},{5,3},{6,4},{7,5},{10,8},{11,9},{12,10},{13,11},... | collective-permute-start | bytes 1179656 | tf_op jit(solution)/shard_map/scatter_step_3/ppermute | solution.py:254
  173.4 1.5 copy-start.3
  173.4 1.5 copy-start.4
  173.4 26.2 %collective-permute-start.22 = (bf16[4,256,768]{2,1,0:T(8,128)(2,1)}, bf16[4,256,768]{2,1,0:T(8,128)(2,1)S(1)}, u32[]{:S(2)}, u32[]{:S(2)}) collective-permute-start(bf16[4,256,768]{2,1,0:T(8,128)(2,1)} %get-tuple-element.69), channel_id=1, source_target_pairs={{0,1},{1,0},{2,3},{3,2},{4,5},{5,4},{6,7},{7,6},{8,9},{9,8},{10,11... | collective-permute-start | bytes 4718600 | tf_op jit(solution)/shard_map/ppermute | solution.py:251
  177.1 21.3 %collective-permute-start.20 = (bf16[256,768]{1,0:T(8,128)(2,1)}, bf16[256,768]{1,0:T(8,128)(2,1)S(1)}, u32[]{:S(2)}, u32[]{:S(2)}) collective-permute-start(bf16[256,768]{1,0:T(8,128)(2,1)} %get-tuple-element.78), channel_id=1, source_target_pairs={{0,2},{1,3},{2,4},{3,5},{4,6},{5,7},{8,10},{9,11},{10,12},{11,13},... | collective-permute-start | bytes 1179656 | tf_op jit(solution)/shard_map/scatter_step_3/ppermute | solution.py:254
  185.0 13.5 %collective-permute-start.21 = (bf16[256,768]{1,0:T(8,128)(2,1)S(1)}, bf16[256,768]{1,0:T(8,128)(2,1)}, u32[]{:S(2)}, u32[]{:S(2)}) collective-permute-start(bf16[256,768]{1,0:T(8,128)(2,1)S(1)} %get-tuple-element.79), channel_id=1, source_target_pairs={{2,0},{3,1},{4,2},{5,3},{6,4},{7,5},{10,8},{11,9},{12,10},{13,11},... | collective-permute-start | bytes 1179656 | tf_op jit(solution)/shard_map/scatter_step_3/ppermute | solution.py:254
  186.4 12.1 %copy-start.14 = (bf16[256,768]{1,0:T(8,128)(2,1)S(1)}, bf16[256,768]{1,0:T(8,128)(2,1)}, u32[]{:S(2)}) copy-start(bf16[256,768]{1,0:T(8,128)(2,1)} %get-tuple-element.67) | copy-start | bytes 1179652
  196.6 3.1 %copy-start.1 = (bf16[256,768]{1,0:T(8,128)(2,1)S(1)}, bf16[256,768]{1,0:T(8,128)(2,1)}, u32[]{:S(2)}) copy-start(bf16[256,768]{1,0:T(8,128)(2,1)} %get-tuple-element.72) | copy-start | bytes 1179652
  196.6 3.1 %copy-start.2 = (bf16[256,768]{1,0:T(8,128)(2,1)S(1)}, bf16[256,768]{1,0:T(8,128)(2,1)}, u32[]{:S(2)}) copy-start(bf16[256,768]{1,0:T(8,128)(2,1)} %get-tuple-element.70) | copy-start | bytes 1179652
  196.6 14.2 %collective-permute-start.14 = (bf16[256,1024]{1,0:T(8,128)(2,1)}, bf16[256,1024]{1,0:T(8,128)(2,1)S(1)}, u32[]{:S(2)}, u32[]{:S(2)}) collective-permute-start(bf16[256,1024]{1,0:T(8,128)(2,1)} %get-tuple-element.63), channel_id=1, source_target_pairs={{0,16},{8,24},{16,0},{24,8},{1,17},{9,25},{17,1},{25,9},{2,18},{10... | collective-permute-start | bytes 1572872 | tf_op jit(solution)/shard_map/back/ppermute | solution.py:259
  197.9 19.8 %collective-permute-start.16 = (bf16[256,1024]{1,0:T(8,128)(2,1)}, bf16[256,1024]{1,0:T(8,128)(2,1)S(1)}, u32[]{:S(2)}, u32[]{:S(2)}) collective-permute-start(bf16[256,1024]{1,0:T(8,128)(2,1)} %get-tuple-element.65), channel_id=1, source_target_pairs={{0,8},{8,0},{16,24},{24,16},{1,9},{9,1},{17,25},{25,17},{2,10},{10... | collective-permute-start | bytes 1572872 | tf_op jit(solution)/shard_map/back/ppermute | solution.py:259
  199.7 11.1 %copy-start.8 = (f32[256,1024]{1,0:T(8,128)S(1)}, f32[256,1024]{1,0:T(8,128)}, u32[]{:S(2)}) copy-start(f32[256,1024]{1,0:T(8,128)} %get-tuple-element.62) | copy-start | bytes 3145732
  199.9 12.5 %collective-permute-start.23 = (bf16[256,768]{1,0:T(8,128)(2,1)S(1)}, bf16[256,768]{1,0:T(8,128)(2,1)S(1)}, u32[]{:S(2)}, u32[]{:S(2)}) collective-permute-start(bf16[256,768]{1,0:T(8,128)(2,1)S(1)} %fusion.22), channel_id=1, source_target_pairs={{0,2},{1,3},{6,4},{7,5},{8,10},{9,11},{14,12},{15,13},{16,18},{17,... | collective-permute-start | bytes 1179656 | tf_op jit(solution)/shard_map/scatter_step_1/ppermute | solution.py:254
  210.7 1.7 copy-start.16
  210.9 6.8 %copy-start.7 = (f32[256,1024]{1,0:T(8,128)S(1)}, f32[256,1024]{1,0:T(8,128)}, u32[]{:S(2)}) copy-start(f32[256,1024]{1,0:T(8,128)} %get-tuple-element.64) | copy-start | bytes 3145732
  211.0 7.6 %collective-permute-start.15 = (bf16[128,1024]{1,0:T(8,128)(2,1)S(1)}, bf16[128,1024]{1,0:T(8,128)(2,1)S(1)}, u32[]{:S(2)}, u32[]{:S(2)}) collective-permute-start(bf16[128,1024]{1,0:T(8,128)(2,1)S(1)} %slice.210), channel_id=1, source_target_pairs={{0,8},{8,0},{16,24},{24,16},{1,9},{9,1},{17,25},{25,17},{2,10},{10... | collective-permute-start | bytes 786440 | tf_op jit(solution)/shard_map/back/ppermute | solution.py:259
  212.6 11.3 %collective-permute-start.24 = (bf16[256,768]{1,0:T(8,128)(2,1)S(1)}, bf16[256,768]{1,0:T(8,128)(2,1)S(1)}, u32[]{:S(2)}, u32[]{:S(2)}) collective-permute-start(bf16[256,768]{1,0:T(8,128)(2,1)S(1)} %fusion.2), channel_id=1, source_target_pairs={{0,2},{1,3},{2,4},{3,5},{8,10},{9,11},{10,12},{11,13},{16,18},{17,... | collective-permute-start | bytes 1179656 | tf_op jit(solution)/shard_map/scatter_step_2/ppermute | solution.py:254
  217.0 6.9 %collective-permute-start.26 = (bf16[256,768]{1,0:T(8,128)(2,1)S(1)}, bf16[256,768]{1,0:T(8,128)(2,1)S(1)}, u32[]{:S(2)}, u32[]{:S(2)}) collective-permute-start(bf16[256,768]{1,0:T(8,128)(2,1)S(1)} %fusion.2), channel_id=1, source_target_pairs={{4,2},{5,3},{6,4},{7,5},{12,10},{13,11},{14,12},{15,13},{20,18},{2... | collective-permute-start | bytes 1179656 | tf_op jit(solution)/shard_map/scatter_step_2/ppermute | solution.py:254
  217.9 14.3 %collective-permute-start.17 = (bf16[128,1024]{1,0:T(8,128)(2,1)S(1)}, bf16[128,1024]{1,0:T(8,128)(2,1)S(1)}, u32[]{:S(2)}, u32[]{:S(2)}) collective-permute-start(bf16[128,1024]{1,0:T(8,128)(2,1)S(1)} %slice.209), channel_id=1, source_target_pairs={{0,16},{8,24},{16,0},{24,8},{1,17},{9,25},{17,1},{25,9},{2,18},{10... | collective-permute-start | bytes 786440 | tf_op jit(solution)/shard_map/back/ppermute | solution.py:259
  224.2 16.8 %copy-start.13 = (bf16[256,768]{1,0:T(8,128)(2,1)S(1)}, bf16[256,768]{1,0:T(8,128)(2,1)}, u32[]{:S(2)}) copy-start(bf16[256,768]{1,0:T(8,128)(2,1)} %get-tuple-element.68) | copy-start | bytes 1179652
  224.2 12.7 %collective-permute-start.25 = (bf16[256,768]{1,0:T(8,128)(2,1)S(1)}, bf16[256,768]{1,0:T(8,128)(2,1)S(1)}, u32[]{:S(2)}, u32[]{:S(2)}) collective-permute-start(bf16[256,768]{1,0:T(8,128)(2,1)S(1)} %get-tuple-element.74), channel_id=1, source_target_pairs={{0,2},{1,3},{2,4},{3,5},{4,6},{5,7},{8,10},{9,11},{10,12},{11,13},... | collective-permute-start | bytes 1179656 | tf_op jit(solution)/shard_map/scatter_step_3/ppermute | solution.py:254
  230.9 10.1 %collective-permute-start.27 = (bf16[256,768]{1,0:T(8,128)(2,1)S(1)}, bf16[256,768]{1,0:T(8,128)(2,1)S(1)}, u32[]{:S(2)}, u32[]{:S(2)}) collective-permute-start(bf16[256,768]{1,0:T(8,128)(2,1)S(1)} %get-tuple-element.75), channel_id=1, source_target_pairs={{2,0},{3,1},{4,2},{5,3},{6,4},{7,5},{10,8},{11,9},{12,10},{13,11},... | collective-permute-start | bytes 1179656 | tf_op jit(solution)/shard_map/scatter_step_3/ppermute | solution.py:254
Sparse Core Ops, SparseCore 0:
  9.7 40.9 all-gather.3
  52.4 39.9 all-gather.5
  94.0 51.1 all-gather.7

commit v5 on v1

--- a/solution.py
+++ b/solution.py
@@ -293,31 +293,35 @@
         (at, *g),
     )
 
-    def gather(own, before):
-        own = after(own, *before)
+    def gather(own):
         ups, downs = [own], [own]
         for s in range(1, line):
             with jax.named_scope(f"gather_step_{s}"):
                 ups.append(along(ups[-1], [(i, i + 1) for i in range(s - 1, line - 1)]))
                 downs.append(along(downs[-1], [(i, i - 1) for i in range(1, line - s + 1)]))
-        return (own, *ups[1:], *downs[1:]), (ups[line - 2], downs[line - 2])
+        return (own, *ups[1:], *downs[1:])
 
     def scatter(parts, waits):
-        up = down = None
-        for s in range(1, line):
-            a, b = parts[s], parts[line - s]
-            if up is not None:
-                a, b = add(a, up), add(b, down)
-            if waits:
-                a, b = after(a, waits[s - 1]), after(b, waits[s - 1])
+        with jax.named_scope("scatter_step_1"):
+            a = jnp.where(z == 0, parts[1], parts[line - 1])
+            up = down = along(a, [(0, 1), (line - 1, line - 2)])
+        for s in range(2, line):
+            if s == 2 and line == 4:
+                a = b = add(parts[2], up)
+            elif s == 2:
+                a = add(parts[2], jnp.where(z == 1, up, 0))
+                b = add(parts[line - 2], jnp.where(z == line - 2, down, 0))
+            else:
+                a, b = add(parts[s], up), add(parts[line - s], down)
+            a, b = after(a, *waits[s - 2]), after(b, *waits[s - 2])
             with jax.named_scope(f"scatter_step_{s}"):
                 up = along(a, [(i, i + 1) for i in range(s)])
                 down = along(b, [(i, i - 1) for i in range(line - s, line)])
         return parts[0].astype(F32) + up.astype(F32) + down.astype(F32)
 
-    merged, both, sums, before = [], [], [], ()
+    merged, both, parts = [], [], []
     for i in range(chunks):
-        loaded, before = gather(shards[i], before)
+        loaded = gather(shards[i])
         got = call(
             lambda *r: chunk_kernel(line, len(t), *r),
             [SMEM] + [ANY] * (len(t) + 2 * line),
@@ -337,8 +341,7 @@
         )
         merged.append(got[line])
         both.append(got[line + 1])
-        if i < chunks - 1:
-            sums.append(scatter(got[:line], ()))
+        parts.append(got[:line])
 
     block = experts * rows
     keep, give = call(
@@ -361,7 +364,7 @@
         left = left[0] + near.astype(F32)
         right = right[0] + odd[0].astype(F32) + last.astype(F32)
         grad_input = jnp.concatenate((left, right), axis=1).astype(BF16)
-    sums.append(scatter(got[:line], (got[0], other, odd)))
+    sums = [scatter(p, ((other,), *(((odd, far),) * (line - 3)))) for p in parts]
 
     own = [lax.dynamic_slice_in_dim(s, c * feats, feats, 0) for s in sums]
     other = [twin(lax.dynamic_slice_in_dim(s, (1 - c) * feats, feats, 0)) for s in sums]
@@ -382,7 +385,7 @@
     weight = P("expert", "wide", None)
 
     def on_device(tokens, out_grad, routes, *rest):
-        dense = experts == 4 and wide % 2 == 0 and 2 * routes.shape[1] >= experts
+        dense = experts == 4 and wide % 2 == 0 and wide > 4 and 2 * routes.shape[1] >= experts
         dense = dense and rest[1].shape[2] % (2 * LANES) == 0
         return (dense_plan if dense else slot_plan)(tokens, out_grad, routes, *rest)
 

time: 237 us -> 240 us (1.013)
  waiting for transfers between devices: 85.8 us -> 95.3 us
  local copies, waits for them, and re-layouts: 18.2 us -> 10.8 us
    unnamed x63 -> x55, local copies, waits for them, and re-layouts: 16.3 us -> 8.84 us
    ppermute x36 -> x33, waiting for transfers between devices: 71.7 us -> 78.4 us  [along(): lax.ppermute(a, 'wide', [(2 * s + i, 2 * t + i) for s, t in hops for i in...]
    ppermute x36 -> x33, starting transfers between devices: 76.6 us -> 72.3 us  [along(): lax.ppermute(a, 'wide', [(2 * s + i, 2 * t + i) for s, t in hops for i in...]
    ppermute x10, starting transfers between devices: 10 us -> 13.7 us  [flip(): return lax.ppermute(a, 'expert', [(e, e ^ bit) for e in range(experts)])]
  transfers between devices with their start and end apart: 61 -> 58, of which waited for: 22 -> 25; matrix products, arithmetic and copies ran while one was open for 3% -> 4% of each run, Pallas kernels for 13% -> 8%
where the time goes in v5:
time: 240 us; the launch traced here: 238 us
  waiting for transfers between devices  95.3 us (40%)
  starting transfers between devices  88.6 us (37%)
  Pallas kernels  32.8 us (14%)
  local copies, waits for them, and re-layouts  10.8 us (4%)
  other arithmetic  8.91 us (4%)
    ppermute x33, waiting for transfers between devices, along(): lax.ppermute(a, 'wide', [(2 * s + i, 2 * t + i) for s, t in hops for i in...  78.4 us
    ppermute x33, starting transfers between devices, along(): lax.ppermute(a, 'wide', [(2 * s + i, 2 * t + i) for s, t in hops for i in...  72.3 us
    pallas_call x7, Pallas kernels, call(): pl.pallas_call(body, out_shape=outs, in_specs=ins, out_specs=[VMEM] * len...  32.8 us
    ppermute x10, waiting for transfers between devices, flip(): return lax.ppermute(a, 'expert', [(e, e ^ bit) for e in range(experts)])  15.4 us
    ppermute x10, starting transfers between devices, flip(): return lax.ppermute(a, 'expert', [(e, e ^ bit) for e in range(experts)])  13.7 us
    unnamed x55, local copies, waits for them, and re-layouts  8.84 us
  transfers between devices with their start and end apart: 58, of which 25 were waited for; matrix products, arithmetic and copies ran while one was open for 4% of the time, Pallas kernels for 8%

profile of v5, /device:TPU:0, one launch (start us, length us, event | category | flops | bytes accessed | tf_op | source)
XLA Modules:
  0.0 238.0 jit_solution(1102966500237513604)
XLA Ops:
  0.6 3.0 %collective-permute-start.4 = (bf16[128,2048]{1,0:T(8,128)(2,1)}, bf16[128,2048]{1,0:T(8,128)(2,1)S(1)}, u32[]{:S(2)}, u32[]{:S(2)}) collective-permute-start(bf16[128,2048]{1,0:T(8,128)(2,1)} %r_1_.5), channel_id=1, source_target_pairs={{0,16},{8,24},{16,0},{24,8},{1,17},{9,25},{17,1},{25,9},{2,18},{10... | collective-permute-start | bytes 1572872 | tf_op jit(solution)/shard_map/rows/ppermute | solution.py:253
  3.7 1.5 collective-permute-start
  5.2 1.0 copy-done.6
  6.2 1.0 copy-done.7
  7.2 1.0 copy-done.8
  11.8 1.1 fusion.1.r_1_
  13.6 2.7 %collective-permute-done.4.r_3_ = bf16[128,2048]{1,0:T(8,128)(2,1)S(1)} collective-permute-done((bf16[128,2048]{1,0:T(8,128)(2,1)}, bf16[128,2048]{1,0:T(8,128)(2,1)S(1)}, u32[]{:S(2)}, u32[]{:S(2)}) %collective-permute-start.4) | collective-permute-done | bytes 524320 | tf_op jit(solution)/shard_map/rows/ppermute | solution.py:253
  17.0 1.6 collective-permute-done.r_2_
  18.6 3.5 %collective-permute-start.29 = (bf16[512,384]{1,0:T(8,128)(2,1)S(1)}, bf16[512,384]{1,0:T(8,128)(2,1)S(1)}, u32[]{:S(2)}, u32[]{:S(2)}) collective-permute-start(bf16[512,384]{1,0:T(8,128)(2,1)S(1)} %get-tuple-element.54.r_10_), channel_id=1, source_target_pairs={{0,2},{1,3},{2,4},{3,5},{4,6},{5,7},{8,10},{9,11},{10,12},{11,13},... | collective-permute-start | bytes 1179656 | tf_op jit(solution)/shard_map/gather_step_1/ppermute | solution.py:248
  22.1 1.3 collective-permute-start.32
  23.4 4.4 %collective-permute-done.11.r_3_ = bf16[128,2176]{1,0:T(8,128)(2,1)S(1)} collective-permute-done((bf16[128,2176]{1,0:T(8,128)(2,1)S(1)}, bf16[128,2176]{1,0:T(8,128)(2,1)S(1)}, u32[]{:S(2)}, u32[]{:S(2)}) %collective-permute-start.11) | collective-permute-done | bytes 557088 | tf_op jit(solution)/shard_map/rows/ppermute | solution.py:253
  27.7 3.7 %collective-permute-start.23 = (bf16[512,384]{1,0:T(8,128)(2,1)S(1)}, bf16[512,384]{1,0:T(8,128)(2,1)S(1)}, u32[]{:S(2)}, u32[]{:S(2)}) collective-permute-start(bf16[512,384]{1,0:T(8,128)(2,1)S(1)} %get-tuple-element.53.r_10_), channel_id=1, source_target_pairs={{0,2},{1,3},{2,4},{3,5},{4,6},{5,7},{8,10},{9,11},{10,12},{11,13},... | collective-permute-start | bytes 1179656 | tf_op jit(solution)/shard_map/gather_step_1/ppermute | solution.py:248
  31.5 1.3 collective-permute-start.26
  32.8 4.7 %collective-permute-start.17 = (bf16[512,384]{1,0:T(8,128)(2,1)S(1)}, bf16[512,384]{1,0:T(8,128)(2,1)S(1)}, u32[]{:S(2)}, u32[]{:S(2)}) collective-permute-start(bf16[512,384]{1,0:T(8,128)(2,1)S(1)} %get-tuple-element.52.r_10_), channel_id=1, source_target_pairs={{0,2},{1,3},{2,4},{3,5},{4,6},{5,7},{8,10},{9,11},{10,12},{11,13},... | collective-permute-start | bytes 1179656 | tf_op jit(solution)/shard_map/gather_step_1/ppermute | solution.py:248
  37.5 1.3 collective-permute-start.20
  39.5 1.5 collective-permute-done.23.r_11_
  41.0 1.3 collective-permute-start.33
  42.3 3.2 %collective-permute-done.26.r_14_ = bf16[512,384]{1,0:T(8,128)(2,1)S(1)} collective-permute-done((bf16[512,384]{1,0:T(8,128)(2,1)S(1)}, bf16[512,384]{1,0:T(8,128)(2,1)S(1)}, u32[]{:S(2)}, u32[]{:S(2)}) %collective-permute-start.26) | collective-permute-done | bytes 393248 | tf_op jit(solution)/shard_map/gather_step_1/ppermute | solution.py:248
  46.1 1.9 collective-permute-done.17.r_11_
  48.0 1.3 collective-permute-start.27
  49.3 4.6 %collective-permute-done.20.r_14_ = bf16[512,384]{1,0:T(8,128)(2,1)S(1)} collective-permute-done((bf16[512,384]{1,0:T(8,128)(2,1)S(1)}, bf16[512,384]{1,0:T(8,128)(2,1)S(1)}, u32[]{:S(2)}, u32[]{:S(2)}) %collective-permute-start.20) | collective-permute-done | bytes 393248 | tf_op jit(solution)/shard_map/gather_step_1/ppermute | solution.py:248
  54.5 1.3 collective-permute-start.21
  55.8 6.4 %collective-permute-done.33.r_15_ = bf16[512,384]{1,0:T(8,128)(2,1)S(1)} collective-permute-done((bf16[512,384]{1,0:T(8,128)(2,1)S(1)}, bf16[512,384]{1,0:T(8,128)(2,1)S(1)}, u32[]{:S(2)}, u32[]{:S(2)}) %collective-permute-start.33) | collective-permute-done | bytes 393248 | tf_op jit(solution)/shard_map/gather_step_2/ppermute | solution.py:248
  62.3 1.5 collective-permute-start.12
  63.8 6.9 %collective-permute-done.27.r_15_ = bf16[512,384]{1,0:T(8,128)(2,1)S(1)} collective-permute-done((bf16[512,384]{1,0:T(8,128)(2,1)S(1)}, bf16[512,384]{1,0:T(8,128)(2,1)S(1)}, u32[]{:S(2)}, u32[]{:S(2)}) %collective-permute-start.27) | collective-permute-done | bytes 393248 | tf_op jit(solution)/shard_map/gather_step_2/ppermute | solution.py:248
  70.7 1.5 collective-permute-start.5
  72.2 5.2 %collective-permute-done.21.r_15_ = bf16[512,384]{1,0:T(8,128)(2,1)S(1)} collective-permute-done((bf16[512,384]{1,0:T(8,128)(2,1)S(1)}, bf16[512,384]{1,0:T(8,128)(2,1)S(1)}, u32[]{:S(2)}, u32[]{:S(2)}) %collective-permute-start.21) | collective-permute-done | bytes 393248 | tf_op jit(solution)/shard_map/gather_step_2/ppermute | solution.py:248
  78.0 3.2 %collective-permute-done.5.r_4_ = bf16[128,2048]{1,0:T(8,128)(2,1)S(1)} collective-permute-done((bf16[128,2048]{1,0:T(8,128)(2,1)S(1)}, bf16[128,2048]{1,0:T(8,128)(2,1)S(1)}, u32[]{:S(2)}, u32[]{:S(2)}) %collective-permute-start.5) | collective-permute-done | bytes 524320 | tf_op jit(solution)/shard_map/rows/ppermute | solution.py:253
  81.9 1.3 collective-permute-start.34
  83.9 1.3 collective-permute-start.28
  85.2 1.3 shard_map.104.r_9_
  87.3 8.5 %collective-permute-done.34.r_16_ = bf16[512,384]{1,0:T(8,128)(2,1)S(1)} collective-permute-done((bf16[512,384]{1,0:T(8,128)(2,1)S(1)}, bf16[512,384]{1,0:T(8,128)(2,1)S(1)}, u32[]{:S(2)}, u32[]{:S(2)}) %collective-permute-start.34) | collective-permute-done | bytes 393248 | tf_op jit(solution)/shard_map/gather_step_3/ppermute | solution.py:248
  95.7 1.3 collective-permute-start.22
  97.0 7.5 %shard_map.107 = (bf16[512,384]{1,0:T(8,128)(2,1)S(1)}, bf16[512,384]{1,0:T(8,128)(2,1)S(1)}, bf16[512,384]{1,0:T(8,128)(2,1)S(1)}, bf16[512,384]{1,0:T(8,128)(2...) custom-call(s32[3]{0:T(128)S(1)} %pad_add_fusion.r_0_, bf16[128,2048]{1,0:T(8,128)(2,1)S(1)} %copy-done.21, ...), custom_call_target="tpu_custom_call" | custom-call | flops 3221225472 | bytes 14286860 | tf_op jit(solution)/shard_map/pallas_call | solution.py:100
  106.8 7.7 %shard_map.106 = (bf16[512,384]{1,0:T(8,128)(2,1)S(1)}, bf16[512,384]{1,0:T(8,128)(2,1)S(1)}, bf16[512,384]{1,0:T(8,128)(2,1)S(1)}, bf16[512,384]{1,0:T(8,128)(2...) custom-call(s32[3]{0:T(128)S(1)} %pad_add_fusion.r_0_, bf16[128,2048]{1,0:T(8,128)(2,1)S(1)} %copy-done.21, ...), custom_call_target="tpu_custom_call" | custom-call | flops 3221225472 | bytes 14286860 | tf_op jit(solution)/shard_map/pallas_call | solution.py:100
  117.7 7.5 %shard_map.105 = (bf16[512,384]{1,0:T(8,128)(2,1)S(1)}, bf16[512,384]{1,0:T(8,128)(2,1)S(1)}, bf16[512,384]{1,0:T(8,128)(2,1)S(1)}, bf16[512,384]{1,0:T(8,128)(2...) custom-call(s32[3]{0:T(128)S(1)} %pad_add_fusion.r_0_, bf16[128,2048]{1,0:T(8,128)(2,1)S(1)} %copy-done.21, ...), custom_call_target="tpu_custom_call" | custom-call | flops 3221225472 | bytes 14286860 | tf_op jit(solution)/shard_map/pallas_call | solution.py:100
  125.3 7.4 %shard_map.108 = (bf16[512,2048]{1,0:T(8,128)(2,1)S(1)}, bf16[512,2048]{1,0:T(8,128)(2,1)}) custom-call(bf16[1024,256]{1,0:T(8,128)(2,1)S(1)} %get-tuple-element.59.r_0_, bf16[1024,256]{1,0:T(8,128)(2,1)S(1)} %get-tuple-element.60.r_1_, bf16[1024,256]{1,0:T(8,128)(2,1)S(1)} %get-tuple-element.61.r_2_, bf16[2048,256]{1,0:T(8,128)(2,1)S(1)} %get-tuple-element.62.r_3_, ...), custom_call_target="tpu_custom_call" | custom-call | flops 3221225472 | bytes 8912896 | tf_op jit(solution)/shard_map/pallas_call | solution.py:100
  132.9 5.9 %collective-permute-start.50 = (bf16[512,384]{1,0:T(8,128)(2,1)S(1)}, bf16[512,384]{1,0:T(8,128)(2,1)S(1)}, u32[]{:S(2)}, u32[]{:S(2)}) collective-permute-start(bf16[512,384]{1,0:T(8,128)(2,1)S(1)} %broadcast_select_fusion), channel_id=1, source_target_pairs={{0,2},{1,3},{6,4},{7,5},{8,10},{9,11},{14,12},{15,13},{16,18},{17,... | collective-permute-start | bytes 1179656 | tf_op jit(solution)/shard_map/scatter_step_1/ppermute | solution.py:248
  138.8 2.3 collective-permute-start.45
  141.2 1.3 collective-permute-start.40
  142.6 5.6 %collective-permute-done.50 = bf16[512,384]{1,0:T(8,128)(2,1)S(1)} collective-permute-done((bf16[512,384]{1,0:T(8,128)(2,1)S(1)}, bf16[512,384]{1,0:T(8,128)(2,1)S(1)}, u32[]{:S(2)}, u32[]{:S(2)}) %collective-permute-start.50) | collective-permute-done | bytes 393248 | tf_op jit(solution)/shard_map/scatter_step_1/ppermute | solution.py:248
  148.3 8.3 %collective-permute-done.45 = bf16[512,384]{1,0:T(8,128)(2,1)S(1)} collective-permute-done((bf16[512,384]{1,0:T(8,128)(2,1)S(1)}, bf16[512,384]{1,0:T(8,128)(2,1)S(1)}, u32[]{:S(2)}, u32[]{:S(2)}) %collective-permute-start.45) | collective-permute-done | bytes 393248 | tf_op jit(solution)/shard_map/scatter_step_1/ppermute | solution.py:248
  156.7 7.9 %collective-permute-done.40 = bf16[512,384]{1,0:T(8,128)(2,1)S(1)} collective-permute-done((bf16[512,384]{1,0:T(8,128)(2,1)S(1)}, bf16[512,384]{1,0:T(8,128)(2,1)S(1)}, u32[]{:S(2)}, u32[]{:S(2)}) %collective-permute-start.40) | collective-permute-done | bytes 393248 | tf_op jit(solution)/shard_map/scatter_step_1/ppermute | solution.py:248
  164.7 4.4 %collective-permute-start.51 = (bf16[512,384]{1,0:T(8,128)(2,1)S(1)}, bf16[512,384]{1,0:T(8,128)(2,1)S(1)}, u32[]{:S(2)}, u32[]{:S(2)}) collective-permute-start(bf16[512,384]{1,0:T(8,128)(2,1)S(1)} %add_convert_fusion.2), channel_id=1, source_target_pairs={{0,2},{1,3},{2,4},{3,5},{8,10},{9,11},{10,12},{11,13},{16,18},{17,... | collective-permute-start | bytes 1179656 | tf_op jit(solution)/shard_map/scatter_step_2/ppermute | solution.py:248
  169.8 2.3 convert_add_fusion
  172.6 5.4 %collective-permute-start.46 = (bf16[512,384]{1,0:T(8,128)(2,1)S(1)}, bf16[512,384]{1,0:T(8,128)(2,1)S(1)}, u32[]{:S(2)}, u32[]{:S(2)}) collective-permute-start(bf16[512,384]{1,0:T(8,128)(2,1)S(1)} %add_convert_fusion.5), channel_id=1, source_target_pairs={{0,2},{1,3},{2,4},{3,5},{8,10},{9,11},{10,12},{11,13},{16,18},{17,... | collective-permute-start | bytes 1179656 | tf_op jit(solution)/shard_map/scatter_step_2/ppermute | solution.py:248
  178.7 5.2 %collective-permute-start.41 = (bf16[512,384]{1,0:T(8,128)(2,1)S(1)}, bf16[512,384]{1,0:T(8,128)(2,1)S(1)}, u32[]{:S(2)}, u32[]{:S(2)}) collective-permute-start(bf16[512,384]{1,0:T(8,128)(2,1)S(1)} %add_convert_fusion.8), channel_id=1, source_target_pairs={{0,2},{1,3},{2,4},{3,5},{8,10},{9,11},{10,12},{11,13},{16,18},{17,... | collective-permute-start | bytes 1179656 | tf_op jit(solution)/shard_map/scatter_step_2/ppermute | solution.py:248
  184.8 1.6 collective-permute-start.38
  186.4 1.1 collective-permute-done.46
  187.5 1.5 collective-permute-start.36
  189.3 5.0 %collective-permute-done.41 = bf16[512,384]{1,0:T(8,128)(2,1)S(1)} collective-permute-done((bf16[512,384]{1,0:T(8,128)(2,1)S(1)}, bf16[512,384]{1,0:T(8,128)(2,1)S(1)}, u32[]{:S(2)}, u32[]{:S(2)}) %collective-permute-start.41) | collective-permute-done | bytes 393248 | tf_op jit(solution)/shard_map/scatter_step_2/ppermute | solution.py:248
  194.4 2.8 %collective-permute-done.38 = bf16[2,128,1024]{2,1,0:T(8,128)(2,1)S(1)} collective-permute-done((bf16[2,128,1024]{2,1,0:T(8,128)(2,1)S(1)}, bf16[2,128,1024]{2,1,0:T(8,128)(2,1)S(1)}, u32[]{:S(2)}, u32[]{:S(2)}) %collective-permute-start.38) | collective-permute-done | bytes 524320 | tf_op jit(solution)/shard_map/back/ppermute | solution.py:253
  197.3 1.6 collective-permute-start.39
  200.7 4.9 %collective-permute-start.52 = (bf16[512,384]{1,0:T(8,128)(2,1)S(1)}, bf16[512,384]{1,0:T(8,128)(2,1)S(1)}, u32[]{:S(2)}, u32[]{:S(2)}) collective-permute-start(bf16[512,384]{1,0:T(8,128)(2,1)S(1)} %add_convert_fusion.1), channel_id=1, source_target_pairs={{0,2},{1,3},{2,4},{3,5},{4,6},{5,7},{8,10},{9,11},{10,12},{11,13},... | collective-permute-start | bytes 1179656 | tf_op jit(solution)/shard_map/scatter_step_3/ppermute | solution.py:248
  205.6 1.3 collective-permute-start.54
  206.9 4.9 %collective-permute-start.47 = (bf16[512,384]{1,0:T(8,128)(2,1)S(1)}, bf16[512,384]{1,0:T(8,128)(2,1)S(1)}, u32[]{:S(2)}, u32[]{:S(2)}) collective-permute-start(bf16[512,384]{1,0:T(8,128)(2,1)S(1)} %add_convert_fusion.4), channel_id=1, source_target_pairs={{0,2},{1,3},{2,4},{3,5},{4,6},{5,7},{8,10},{9,11},{10,12},{11,13},... | collective-permute-start | bytes 1179656 | tf_op jit(solution)/shard_map/scatter_step_3/ppermute | solution.py:248
  211.8 1.3 collective-permute-start.49
  213.3 4.6 %collective-permute-start.42 = (bf16[512,384]{1,0:T(8,128)(2,1)S(1)}, bf16[512,384]{1,0:T(8,128)(2,1)S(1)}, u32[]{:S(2)}, u32[]{:S(2)}) collective-permute-start(bf16[512,384]{1,0:T(8,128)(2,1)S(1)} %add_convert_fusion.7), channel_id=1, source_target_pairs={{0,2},{1,3},{2,4},{3,5},{4,6},{5,7},{8,10},{9,11},{10,12},{11,13},... | collective-permute-start | bytes 1179656 | tf_op jit(solution)/shard_map/scatter_step_3/ppermute | solution.py:248
  218.7 3.3 %collective-permute-done.47 = bf16[512,384]{1,0:T(8,128)(2,1)S(1)} collective-permute-done((bf16[512,384]{1,0:T(8,128)(2,1)S(1)}, bf16[512,384]{1,0:T(8,128)(2,1)S(1)}, u32[]{:S(2)}, u32[]{:S(2)}) %collective-permute-start.47) | collective-permute-done | bytes 393248 | tf_op jit(solution)/shard_map/scatter_step_3/ppermute | solution.py:248
  222.0 1.3 collective-permute-start.44
  223.3 2.8 %collective-permute-done.49 = bf16[512,384]{1,0:T(8,128)(2,1)S(1)} collective-permute-done((bf16[512,384]{1,0:T(8,128)(2,1)S(1)}, bf16[512,384]{1,0:T(8,128)(2,1)S(1)}, u32[]{:S(2)}, u32[]{:S(2)}) %collective-permute-start.49) | collective-permute-done | bytes 393248 | tf_op jit(solution)/shard_map/scatter_step_3/ppermute | solution.py:248
  226.4 1.4 collective-permute-done.42
  227.8 5.0 %collective-permute-done.44 = bf16[512,384]{1,0:T(8,128)(2,1)S(1)} collective-permute-done((bf16[512,384]{1,0:T(8,128)(2,1)S(1)}, bf16[512,384]{1,0:T(8,128)(2,1)S(1)}, u32[]{:S(2)}, u32[]{:S(2)}) %collective-permute-start.44) | collective-permute-done | bytes 393248 | tf_op jit(solution)/shard_map/scatter_step_3/ppermute | solution.py:248
  236.7 1.3 broadcast_select_fusion.3
  (154 shorter events, 25.8 us)
Async XLA Ops:
  0.6 15.7 %collective-permute-start.4 = (bf16[128,2048]{1,0:T(8,128)(2,1)}, bf16[128,2048]{1,0:T(8,128)(2,1)S(1)}, u32[]{:S(2)}, u32[]{:S(2)}) collective-permute-start(bf16[128,2048]{1,0:T(8,128)(2,1)} %r_1_.5), channel_id=1, source_target_pairs={{0,16},{8,24},{16,0},{24,8},{1,17},{9,25},{17,1},{25,9},{2,18},{10... | collective-permute-start | bytes 1572872 | tf_op jit(solution)/shard_map/rows/ppermute | solution.py:253
  3.7 14.9 %collective-permute-start = (bf16[128,2048]{1,0:T(8,128)(2,1)}, bf16[128,2048]{1,0:T(8,128)(2,1)S(1)}, u32[]{:S(2)}, u32[]{:S(2)}) collective-permute-start(bf16[128,2048]{1,0:T(8,128)(2,1)} %r_1_.5), channel_id=1, source_target_pairs={{0,8},{8,0},{16,24},{24,16},{1,9},{9,1},{17,25},{25,17},{2,10},{10... | collective-permute-start | bytes 1572872 | tf_op jit(solution)/shard_map/rows/ppermute | solution.py:253
  5.2 16.9 %collective-permute-start.6 = (bf16[128,2048]{1,0:T(8,128)(2,1)}, bf16[128,2048]{1,0:T(8,128)(2,1)S(1)}, u32[]{:S(2)}, u32[]{:S(2)}) collective-permute-start(bf16[128,2048]{1,0:T(8,128)(2,1)} %r_1_.5), channel_id=1, source_target_pairs={{0,1},{1,0},{2,3},{3,2},{4,5},{5,4},{6,7},{7,6},{8,9},{9,8},{10,11... | collective-permute-start | bytes 1572872 | tf_op jit(solution)/shard_map/rows/ppermute | solution.py:245
  9.0 2.3 collective-permute-start.1
  9.6 3.3 %collective-permute-start.2 = (bf16[256,384]{1,0:T(8,128)(2,1)S(1)}, bf16[256,384]{1,0:T(8,128)(2,1)S(1)}, u32[]{:S(2)}, u32[]{:S(2)}) collective-permute-start(bf16[256,384]{1,0:T(8,128)(2,1)S(1)} %get-tuple-element.50), channel_id=1, source_target_pairs={{0,1},{1,0},{2,3},{3,2},{4,5},{5,4},{6,7},{7,6},{8,9},{9,8},{10,11... | collective-permute-start | bytes 589832 | tf_op jit(solution)/shard_map/ppermute | solution.py:245
  11.3 2.2 collective-permute-start.3
  12.9 14.8 %collective-permute-start.11 = (bf16[128,2176]{1,0:T(8,128)(2,1)S(1)}, bf16[128,2176]{1,0:T(8,128)(2,1)S(1)}, u32[]{:S(2)}, u32[]{:S(2)}) collective-permute-start(bf16[128,2176]{1,0:T(8,128)(2,1)S(1)} %fusion.1.r_1_), channel_id=1, source_target_pairs={{0,16},{8,24},{16,0},{24,8},{1,17},{9,25},{17,1},{25,9},{2,18},{10... | collective-permute-start | bytes 1671176 | tf_op jit(solution)/shard_map/rows/ppermute | solution.py:253
  13.5 18.0 %collective-permute-start.10 = (bf16[128,2176]{1,0:T(8,128)(2,1)S(1)}, bf16[128,2176]{1,0:T(8,128)(2,1)S(1)}, u32[]{:S(2)}, u32[]{:S(2)}) collective-permute-start(bf16[128,2176]{1,0:T(8,128)(2,1)S(1)} %fusion.1.r_1_), channel_id=1, source_target_pairs={{0,8},{8,0},{16,24},{24,16},{1,9},{9,1},{17,25},{25,17},{2,10},{10... | collective-permute-start | bytes 1671176 | tf_op jit(solution)/shard_map/rows/ppermute | solution.py:253
  16.3 16.5 %collective-permute-start.13 = (bf16[128,2176]{1,0:T(8,128)(2,1)S(1)}, bf16[128,2176]{1,0:T(8,128)(2,1)S(1)}, u32[]{:S(2)}, u32[]{:S(2)}) collective-permute-start(bf16[128,2176]{1,0:T(8,128)(2,1)S(1)} %fusion.1.r_1_), channel_id=1, source_target_pairs={{0,1},{1,0},{2,3},{3,2},{4,5},{5,4},{6,7},{7,6},{8,9},{9,8},{10,11... | collective-permute-start | bytes 1671176 | tf_op jit(solution)/shard_map/rows/ppermute | solution.py:245
  18.6 18.9 %collective-permute-start.29 = (bf16[512,384]{1,0:T(8,128)(2,1)S(1)}, bf16[512,384]{1,0:T(8,128)(2,1)S(1)}, u32[]{:S(2)}, u32[]{:S(2)}) collective-permute-start(bf16[512,384]{1,0:T(8,128)(2,1)S(1)} %get-tuple-element.54.r_10_), channel_id=1, source_target_pairs={{0,2},{1,3},{2,4},{3,5},{4,6},{5,7},{8,10},{9,11},{10,12},{11,13},... | collective-permute-start | bytes 1179656 | tf_op jit(solution)/shard_map/gather_step_1/ppermute | solution.py:248
  22.1 16.7 %collective-permute-start.32 = (bf16[512,384]{1,0:T(8,128)(2,1)S(1)}, bf16[512,384]{1,0:T(8,128)(2,1)S(1)}, u32[]{:S(2)}, u32[]{:S(2)}) collective-permute-start(bf16[512,384]{1,0:T(8,128)(2,1)S(1)} %get-tuple-element.54.r_10_), channel_id=1, source_target_pairs={{2,0},{3,1},{4,2},{5,3},{6,4},{7,5},{10,8},{11,9},{12,10},{13,11},... | collective-permute-start | bytes 1179656 | tf_op jit(solution)/shard_map/gather_step_1/ppermute | solution.py:248
  27.7 13.2 %collective-permute-start.23 = (bf16[512,384]{1,0:T(8,128)(2,1)S(1)}, bf16[512,384]{1,0:T(8,128)(2,1)S(1)}, u32[]{:S(2)}, u32[]{:S(2)}) collective-permute-start(bf16[512,384]{1,0:T(8,128)(2,1)S(1)} %get-tuple-element.53.r_10_), channel_id=1, source_target_pairs={{0,2},{1,3},{2,4},{3,5},{4,6},{5,7},{8,10},{9,11},{10,12},{11,13},... | collective-permute-start | bytes 1179656 | tf_op jit(solution)/shard_map/gather_step_1/ppermute | solution.py:248
  31.5 13.9 %collective-permute-start.26 = (bf16[512,384]{1,0:T(8,128)(2,1)S(1)}, bf16[512,384]{1,0:T(8,128)(2,1)S(1)}, u32[]{:S(2)}, u32[]{:S(2)}) collective-permute-start(bf16[512,384]{1,0:T(8,128)(2,1)S(1)} %get-tuple-element.53.r_10_), channel_id=1, source_target_pairs={{2,0},{3,1},{4,2},{5,3},{6,4},{7,5},{10,8},{11,9},{12,10},{13,11},... | collective-permute-start | bytes 1179656 | tf_op jit(solution)/shard_map/gather_step_1/ppermute | solution.py:248
  32.8 64.3 %copy-start.21 = (bf16[128,2048]{1,0:T(8,128)(2,1)S(1)}, bf16[128,2048]{1,0:T(8,128)(2,1)}, u32[]{:S(2)}) copy-start(bf16[128,2048]{1,0:T(8,128)(2,1)} %r_1_.5) | copy-start | bytes 1572868
  32.8 15.2 %collective-permute-start.17 = (bf16[512,384]{1,0:T(8,128)(2,1)S(1)}, bf16[512,384]{1,0:T(8,128)(2,1)S(1)}, u32[]{:S(2)}, u32[]{:S(2)}) collective-permute-start(bf16[512,384]{1,0:T(8,128)(2,1)S(1)} %get-tuple-element.52.r_10_), channel_id=1, source_target_pairs={{0,2},{1,3},{2,4},{3,5},{4,6},{5,7},{8,10},{9,11},{10,12},{11,13},... | collective-permute-start | bytes 1179656 | tf_op jit(solution)/shard_map/gather_step_1/ppermute | solution.py:248
  37.5 16.3 %collective-permute-start.20 = (bf16[512,384]{1,0:T(8,128)(2,1)S(1)}, bf16[512,384]{1,0:T(8,128)(2,1)S(1)}, u32[]{:S(2)}, u32[]{:S(2)}) collective-permute-start(bf16[512,384]{1,0:T(8,128)(2,1)S(1)} %get-tuple-element.52.r_10_), channel_id=1, source_target_pairs={{2,0},{3,1},{4,2},{5,3},{6,4},{7,5},{10,8},{11,9},{12,10},{13,11},... | collective-permute-start | bytes 1179656 | tf_op jit(solution)/shard_map/gather_step_1/ppermute | solution.py:248
  38.8 15.7 %collective-permute-start.30 = (bf16[512,384]{1,0:T(8,128)(2,1)S(1)}, bf16[512,384]{1,0:T(8,128)(2,1)S(1)}, u32[]{:S(2)}, u32[]{:S(2)}) collective-permute-start(bf16[512,384]{1,0:T(8,128)(2,1)S(1)} %collective-permute-done.29.r_11_), channel_id=1, source_target_pairs={{2,4},{3,5},{4,6},{5,7},{10,12},{11,13},{12,14},{13,15},{18,20},{1... | collective-permute-start | bytes 1179656 | tf_op jit(solution)/shard_map/gather_step_2/ppermute | solution.py:248
  41.0 21.3 %collective-permute-start.33 = (bf16[512,384]{1,0:T(8,128)(2,1)S(1)}, bf16[512,384]{1,0:T(8,128)(2,1)S(1)}, u32[]{:S(2)}, u32[]{:S(2)}) collective-permute-start(bf16[512,384]{1,0:T(8,128)(2,1)S(1)} %collective-permute-done.32.r_14_), channel_id=1, source_target_pairs={{2,0},{3,1},{4,2},{5,3},{10,8},{11,9},{12,10},{13,11},{18,16},{19,... | collective-permute-start | bytes 1179656 | tf_op jit(solution)/shard_map/gather_step_2/ppermute | solution.py:248
  45.4 18.3 %collective-permute-start.24 = (bf16[512,384]{1,0:T(8,128)(2,1)S(1)}, bf16[512,384]{1,0:T(8,128)(2,1)S(1)}, u32[]{:S(2)}, u32[]{:S(2)}) collective-permute-start(bf16[512,384]{1,0:T(8,128)(2,1)S(1)} %collective-permute-done.23.r_11_), channel_id=1, source_target_pairs={{2,4},{3,5},{4,6},{5,7},{10,12},{11,13},{12,14},{13,15},{18,20},{1... | collective-permute-start | bytes 1179656 | tf_op jit(solution)/shard_map/gather_step_2/ppermute | solution.py:248
  48.0 22.7 %collective-permute-start.27 = (bf16[512,384]{1,0:T(8,128)(2,1)S(1)}, bf16[512,384]{1,0:T(8,128)(2,1)S(1)}, u32[]{:S(2)}, u32[]{:S(2)}) collective-permute-start(bf16[512,384]{1,0:T(8,128)(2,1)S(1)} %collective-permute-done.26.r_14_), channel_id=1, source_target_pairs={{2,0},{3,1},{4,2},{5,3},{10,8},{11,9},{12,10},{13,11},{18,16},{19,... | collective-permute-start | bytes 1179656 | tf_op jit(solution)/shard_map/gather_step_2/ppermute | solution.py:248
  53.8 18.4 %collective-permute-start.18 = (bf16[512,384]{1,0:T(8,128)(2,1)S(1)}, bf16[512,384]{1,0:T(8,128)(2,1)S(1)}, u32[]{:S(2)}, u32[]{:S(2)}) collective-permute-start(bf16[512,384]{1,0:T(8,128)(2,1)S(1)} %collective-permute-done.17.r_11_), channel_id=1, source_target_pairs={{2,4},{3,5},{4,6},{5,7},{10,12},{11,13},{12,14},{13,15},{18,20},{1... | collective-permute-start | bytes 1179656 | tf_op jit(solution)/shard_map/gather_step_2/ppermute | solution.py:248
  54.5 22.9 %collective-permute-start.21 = (bf16[512,384]{1,0:T(8,128)(2,1)S(1)}, bf16[512,384]{1,0:T(8,128)(2,1)S(1)}, u32[]{:S(2)}, u32[]{:S(2)}) collective-permute-start(bf16[512,384]{1,0:T(8,128)(2,1)S(1)} %collective-permute-done.20.r_14_), channel_id=1, source_target_pairs={{2,0},{3,1},{4,2},{5,3},{10,8},{11,9},{12,10},{13,11},{18,16},{19,... | collective-permute-start | bytes 1179656 | tf_op jit(solution)/shard_map/gather_step_2/ppermute | solution.py:248
  62.3 15.7 %collective-permute-start.12 = (bf16[128,2176]{1,0:T(8,128)(2,1)S(1)}, bf16[128,2176]{1,0:T(8,128)(2,1)S(1)}, u32[]{:S(2)}, u32[]{:S(2)}) collective-permute-start(bf16[128,2176]{1,0:T(8,128)(2,1)S(1)} %collective-permute-done.11.r_3_), channel_id=1, source_target_pairs={{0,8},{8,0},{16,24},{24,16},{1,9},{9,1},{17,25},{25,17},{2,10},{10... | collective-permute-start | bytes 1671176 | tf_op jit(solution)/shard_map/rows/ppermute | solution.py:253
  63.8 13.7 %collective-permute-start.8 = (bf16[128,2048]{1,0:T(8,128)(2,1)S(1)}, bf16[128,2048]{1,0:T(8,128)(2,1)S(1)}, u32[]{:S(2)}, u32[]{:S(2)}) collective-permute-start(bf16[128,2048]{1,0:T(8,128)(2,1)S(1)} %collective-permute-done.4.r_3_), channel_id=1, source_target_pairs={{0,1},{1,0},{2,3},{3,2},{4,5},{5,4},{6,7},{7,6},{8,9},{9,8},{10,11... | collective-permute-start | bytes 1572872 | tf_op jit(solution)/shard_map/rows/ppermute | solution.py:245
  70.7 10.5 %collective-permute-start.5 = (bf16[128,2048]{1,0:T(8,128)(2,1)S(1)}, bf16[128,2048]{1,0:T(8,128)(2,1)S(1)}, u32[]{:S(2)}, u32[]{:S(2)}) collective-permute-start(bf16[128,2048]{1,0:T(8,128)(2,1)S(1)} %collective-permute-done.r_2_), channel_id=1, source_target_pairs={{0,16},{8,24},{16,0},{24,8},{1,17},{9,25},{17,1},{25,9},{2,18},{10... | collective-permute-start | bytes 1572872 | tf_op jit(solution)/shard_map/rows/ppermute | solution.py:253
  72.2 9.7 %collective-permute-start.15 = (bf16[128,2176]{1,0:T(8,128)(2,1)S(1)}, bf16[128,2176]{1,0:T(8,128)(2,1)S(1)}, u32[]{:S(2)}, u32[]{:S(2)}) collective-permute-start(bf16[128,2176]{1,0:T(8,128)(2,1)S(1)} %collective-permute-done.11.r_3_), channel_id=1, source_target_pairs={{0,1},{1,0},{2,3},{3,2},{4,5},{5,4},{6,7},{7,6},{8,9},{9,8},{10,11... | collective-permute-start | bytes 1671176 | tf_op jit(solution)/shard_map/rows/ppermute | solution.py:245
  77.4 3.8 %collective-permute-start.7 = (bf16[128,2048]{1,0:T(8,128)(2,1)S(1)}, bf16[128,2048]{1,0:T(8,128)(2,1)S(1)}, u32[]{:S(2)}, u32[]{:S(2)}) collective-permute-start(bf16[128,2048]{1,0:T(8,128)(2,1)S(1)} %collective-permute-done.r_2_), channel_id=1, source_target_pairs={{0,1},{1,0},{2,3},{3,2},{4,5},{5,4},{6,7},{7,6},{8,9},{9,8},{10,11... | collective-permute-start | bytes 1572872 | tf_op jit(solution)/shard_map/rows/ppermute | solution.py:245
  77.4 5.8 %collective-permute-start.14 = (bf16[128,2176]{1,0:T(8,128)(2,1)S(1)}, bf16[128,2176]{1,0:T(8,128)(2,1)S(1)}, u32[]{:S(2)}, u32[]{:S(2)}) collective-permute-start(bf16[128,2176]{1,0:T(8,128)(2,1)S(1)} %collective-permute-done.10.r_2_), channel_id=1, source_target_pairs={{0,1},{1,0},{2,3},{3,2},{4,5},{5,4},{6,7},{7,6},{8,9},{9,8},{10,11... | collective-permute-start | bytes 1671176 | tf_op jit(solution)/shard_map/rows/ppermute | solution.py:245
  77.9 6.0 %collective-permute-start.16 = (bf16[128,2176]{1,0:T(8,128)(2,1)S(1)}, bf16[128,2176]{1,0:T(8,128)(2,1)S(1)}, u32[]{:S(2)}, u32[]{:S(2)}) collective-permute-start(bf16[128,2176]{1,0:T(8,128)(2,1)S(1)} %collective-permute-done.12.r_4_), channel_id=1, source_target_pairs={{0,1},{1,0},{2,3},{3,2},{4,5},{5,4},{6,7},{7,6},{8,9},{9,8},{10,11... | collective-permute-start | bytes 1671176 | tf_op jit(solution)/shard_map/rows/ppermute | solution.py:245
  81.2 15.8 %collective-permute-start.9 = (bf16[128,2048]{1,0:T(8,128)(2,1)S(1)}, bf16[128,2048]{1,0:T(8,128)(2,1)S(1)}, u32[]{:S(2)}, u32[]{:S(2)}) collective-permute-start(bf16[128,2048]{1,0:T(8,128)(2,1)S(1)} %collective-permute-done.5.r_4_), channel_id=1, source_target_pairs={{0,1},{1,0},{2,3},{3,2},{4,5},{5,4},{6,7},{7,6},{8,9},{9,8},{10,11... | collective-permute-start | bytes 1572872 | tf_op jit(solution)/shard_map/rows/ppermute | solution.py:245
  81.2 5.3 %collective-permute-start.31 = (bf16[512,384]{1,0:T(8,128)(2,1)S(1)}, bf16[512,384]{1,0:T(8,128)(2,1)S(1)}, u32[]{:S(2)}, u32[]{:S(2)}) collective-permute-start(bf16[512,384]{1,0:T(8,128)(2,1)S(1)} %collective-permute-done.30.r_12_), channel_id=1, source_target_pairs={{4,6},{5,7},{12,14},{13,15},{20,22},{21,23},{28,30},{29,31}} | collective-permute-start | bytes 1179656 | tf_op jit(solution)/shard_map/gather_step_3/ppermute | solution.py:248
  81.9 13.8 %collective-permute-start.34 = (bf16[512,384]{1,0:T(8,128)(2,1)S(1)}, bf16[512,384]{1,0:T(8,128)(2,1)S(1)}, u32[]{:S(2)}, u32[]{:S(2)}) collective-permute-start(bf16[512,384]{1,0:T(8,128)(2,1)S(1)} %collective-permute-done.33.r_15_), channel_id=1, source_target_pairs={{2,0},{3,1},{10,8},{11,9},{18,16},{19,17},{26,24},{27,25}} | collective-permute-start | bytes 1179656 | tf_op jit(solution)/shard_map/gather_step_3/ppermute | solution.py:248
  83.2 23.6 %collective-permute-start.25 = (bf16[512,384]{1,0:T(8,128)(2,1)S(1)}, bf16[512,384]{1,0:T(8,128)(2,1)S(1)}, u32[]{:S(2)}, u32[]{:S(2)}) collective-permute-start(bf16[512,384]{1,0:T(8,128)(2,1)S(1)} %collective-permute-done.24.r_12_), channel_id=1, source_target_pairs={{4,6},{5,7},{12,14},{13,15},{20,22},{21,23},{28,30},{29,31}} | collective-permute-start | bytes 1179656 | tf_op jit(solution)/shard_map/gather_step_3/ppermute | solution.py:248
  83.9 22.9 %collective-permute-start.28 = (bf16[512,384]{1,0:T(8,128)(2,1)S(1)}, bf16[512,384]{1,0:T(8,128)(2,1)S(1)}, u32[]{:S(2)}, u32[]{:S(2)}) collective-permute-start(bf16[512,384]{1,0:T(8,128)(2,1)S(1)} %collective-permute-done.27.r_15_), channel_id=1, source_target_pairs={{2,0},{3,1},{10,8},{11,9},{18,16},{19,17},{26,24},{27,25}} | collective-permute-start | bytes 1179656 | tf_op jit(solution)/shard_map/gather_step_3/ppermute | solution.py:248
  86.6 31.1 %collective-permute-start.19 = (bf16[512,384]{1,0:T(8,128)(2,1)S(1)}, bf16[512,384]{1,0:T(8,128)(2,1)S(1)}, u32[]{:S(2)}, u32[]{:S(2)}) collective-permute-start(bf16[512,384]{1,0:T(8,128)(2,1)S(1)} %collective-permute-done.18.r_12_), channel_id=1, source_target_pairs={{4,6},{5,7},{12,14},{13,15},{20,22},{21,23},{28,30},{29,31}} | collective-permute-start | bytes 1179656 | tf_op jit(solution)/shard_map/gather_step_3/ppermute | solution.py:248
  95.7 22.0 %collective-permute-start.22 = (bf16[512,384]{1,0:T(8,128)(2,1)S(1)}, bf16[512,384]{1,0:T(8,128)(2,1)S(1)}, u32[]{:S(2)}, u32[]{:S(2)}) collective-permute-start(bf16[512,384]{1,0:T(8,128)(2,1)S(1)} %collective-permute-done.21.r_15_), channel_id=1, source_target_pairs={{2,0},{3,1},{10,8},{11,9},{18,16},{19,17},{26,24},{27,25}} | collective-permute-start | bytes 1179656 | tf_op jit(solution)/shard_map/gather_step_3/ppermute | solution.py:248
  132.7 32.0 %collective-permute-start.35 = (bf16[512,2048]{1,0:T(8,128)(2,1)}, bf16[512,2048]{1,0:T(8,128)(2,1)}, u32[]{:S(2)}, u32[]{:S(2)}) collective-permute-start(bf16[512,2048]{1,0:T(8,128)(2,1)} %get-tuple-element.66), channel_id=1, source_target_pairs={{0,1},{1,0},{2,3},{3,2},{4,5},{5,4},{6,7},{7,6},{8,9},{9,8},{10,11... | collective-permute-start | bytes 6291464 | tf_op jit(solution)/shard_map/back/ppermute | solution.py:245
  132.8 15.4 %copy-start.10 = (bf16[512,384]{1,0:T(8,128)(2,1)S(1)}, bf16[512,384]{1,0:T(8,128)(2,1)}, u32[]{:S(2)}) copy-start(bf16[512,384]{1,0:T(8,128)(2,1)} %copy-done.9) | copy-start | bytes 1179652
  132.8 23.8 %copy-start.12 = (bf16[512,384]{1,0:T(8,128)(2,1)S(1)}, bf16[512,384]{1,0:T(8,128)(2,1)}, u32[]{:S(2)}) copy-start(bf16[512,384]{1,0:T(8,128)(2,1)} %copy-done.11) | copy-start | bytes 1179652
  132.9 15.3 %collective-permute-start.50 = (bf16[512,384]{1,0:T(8,128)(2,1)S(1)}, bf16[512,384]{1,0:T(8,128)(2,1)S(1)}, u32[]{:S(2)}, u32[]{:S(2)}) collective-permute-start(bf16[512,384]{1,0:T(8,128)(2,1)S(1)} %broadcast_select_fusion), channel_id=1, source_target_pairs={{0,2},{1,3},{6,4},{7,5},{8,10},{9,11},{14,12},{15,13},{16,18},{17,... | collective-permute-start | bytes 1179656 | tf_op jit(solution)/shard_map/scatter_step_1/ppermute | solution.py:248
  138.8 25.8 %copy-start.14 = (bf16[512,384]{1,0:T(8,128)(2,1)S(1)}, bf16[512,384]{1,0:T(8,128)(2,1)}, u32[]{:S(2)}) copy-start(bf16[512,384]{1,0:T(8,128)(2,1)} %copy-done.13) | copy-start | bytes 1179652
  138.8 17.7 %collective-permute-start.45 = (bf16[512,384]{1,0:T(8,128)(2,1)S(1)}, bf16[512,384]{1,0:T(8,128)(2,1)S(1)}, u32[]{:S(2)}, u32[]{:S(2)}) collective-permute-start(bf16[512,384]{1,0:T(8,128)(2,1)S(1)} %broadcast_select_fusion.1), channel_id=1, source_target_pairs={{0,2},{1,3},{6,4},{7,5},{8,10},{9,11},{14,12},{15,13},{16,18},{17,... | collective-permute-start | bytes 1179656 | tf_op jit(solution)/shard_map/scatter_step_1/ppermute | solution.py:248
  141.2 23.3 %collective-permute-start.40 = (bf16[512,384]{1,0:T(8,128)(2,1)S(1)}, bf16[512,384]{1,0:T(8,128)(2,1)S(1)}, u32[]{:S(2)}, u32[]{:S(2)}) collective-permute-start(bf16[512,384]{1,0:T(8,128)(2,1)S(1)} %broadcast_select_fusion.2), channel_id=1, source_target_pairs={{0,2},{1,3},{6,4},{7,5},{8,10},{9,11},{14,12},{15,13},{16,18},{17,... | collective-permute-start | bytes 1179656 | tf_op jit(solution)/shard_map/scatter_step_1/ppermute | solution.py:248
  164.7 19.2 %collective-permute-start.51 = (bf16[512,384]{1,0:T(8,128)(2,1)S(1)}, bf16[512,384]{1,0:T(8,128)(2,1)S(1)}, u32[]{:S(2)}, u32[]{:S(2)}) collective-permute-start(bf16[512,384]{1,0:T(8,128)(2,1)S(1)} %add_convert_fusion.2), channel_id=1, source_target_pairs={{0,2},{1,3},{2,4},{3,5},{8,10},{9,11},{10,12},{11,13},{16,18},{17,... | collective-permute-start | bytes 1179656 | tf_op jit(solution)/shard_map/scatter_step_2/ppermute | solution.py:248
  169.1 15.7 %collective-permute-start.53 = (bf16[512,384]{1,0:T(8,128)(2,1)S(1)}, bf16[512,384]{1,0:T(8,128)(2,1)S(1)}, u32[]{:S(2)}, u32[]{:S(2)}) collective-permute-start(bf16[512,384]{1,0:T(8,128)(2,1)S(1)} %add_convert_fusion.2), channel_id=1, source_target_pairs={{4,2},{5,3},{6,4},{7,5},{12,10},{13,11},{14,12},{15,13},{20,18},{2... | collective-permute-start | bytes 1179656 | tf_op jit(solution)/shard_map/scatter_step_2/ppermute | solution.py:248
  172.5 16.5 %copy-start.1 = (bf16[512,384]{1,0:T(8,128)(2,1)S(1)}, bf16[512,384]{1,0:T(8,128)(2,1)}, u32[]{:S(2)}) copy-start(bf16[512,384]{1,0:T(8,128)(2,1)} %copy-done) | copy-start | bytes 1179652
  172.6 14.9 %collective-permute-start.46 = (bf16[512,384]{1,0:T(8,128)(2,1)S(1)}, bf16[512,384]{1,0:T(8,128)(2,1)S(1)}, u32[]{:S(2)}, u32[]{:S(2)}) collective-permute-start(bf16[512,384]{1,0:T(8,128)(2,1)S(1)} %add_convert_fusion.5), channel_id=1, source_target_pairs={{0,2},{1,3},{2,4},{3,5},{8,10},{9,11},{10,12},{11,13},{16,18},{17,... | collective-permute-start | bytes 1179656 | tf_op jit(solution)/shard_map/scatter_step_2/ppermute | solution.py:248
  178.0 11.2 %collective-permute-start.48 = (bf16[512,384]{1,0:T(8,128)(2,1)S(1)}, bf16[512,384]{1,0:T(8,128)(2,1)S(1)}, u32[]{:S(2)}, u32[]{:S(2)}) collective-permute-start(bf16[512,384]{1,0:T(8,128)(2,1)S(1)} %add_convert_fusion.5), channel_id=1, source_target_pairs={{4,2},{5,3},{6,4},{7,5},{12,10},{13,11},{14,12},{15,13},{20,18},{2... | collective-permute-start | bytes 1179656 | tf_op jit(solution)/shard_map/scatter_step_2/ppermute | solution.py:248
  178.7 15.6 %collective-permute-start.41 = (bf16[512,384]{1,0:T(8,128)(2,1)S(1)}, bf16[512,384]{1,0:T(8,128)(2,1)S(1)}, u32[]{:S(2)}, u32[]{:S(2)}) collective-permute-start(bf16[512,384]{1,0:T(8,128)(2,1)S(1)} %add_convert_fusion.8), channel_id=1, source_target_pairs={{0,2},{1,3},{2,4},{3,5},{8,10},{9,11},{10,12},{11,13},{16,18},{17,... | collective-permute-start | bytes 1179656 | tf_op jit(solution)/shard_map/scatter_step_2/ppermute | solution.py:248
  183.9 16.7 %collective-permute-start.43 = (bf16[512,384]{1,0:T(8,128)(2,1)S(1)}, bf16[512,384]{1,0:T(8,128)(2,1)S(1)}, u32[]{:S(2)}, u32[]{:S(2)}) collective-permute-start(bf16[512,384]{1,0:T(8,128)(2,1)S(1)} %add_convert_fusion.8), channel_id=1, source_target_pairs={{4,2},{5,3},{6,4},{7,5},{12,10},{13,11},{14,12},{15,13},{20,18},{2... | collective-permute-start | bytes 1179656 | tf_op jit(solution)/shard_map/scatter_step_2/ppermute | solution.py:248
  184.8 12.4 %collective-permute-start.38 = (bf16[2,128,1024]{2,1,0:T(8,128)(2,1)S(1)}, bf16[2,128,1024]{2,1,0:T(8,128)(2,1)S(1)}, u32[]{:S(2)}, u32[]{:S(2)}) collective-permute-start(bf16[2,128,1024]{2,1,0:T(8,128)(2,1)S(1)} %pad_maximum_fusion), channel_id=1, source_target_pairs={{0,8},{8,0},{16,24},{24,16},{1,9},{9,1},{17,25},{25,17},{2,10},{10... | collective-permute-start | bytes 1572872 | tf_op jit(solution)/shard_map/back/ppermute | solution.py:253
  187.5 12.1 %collective-permute-start.36 = (bf16[2,128,1024]{2,1,0:T(8,128)(2,1)S(1)}, bf16[2,128,1024]{2,1,0:T(8,128)(2,1)S(1)}, u32[]{:S(2)}, u32[]{:S(2)}) collective-permute-start(bf16[2,128,1024]{2,1,0:T(8,128)(2,1)S(1)} %slice.141), channel_id=1, source_target_pairs={{0,16},{8,24},{16,0},{24,8},{1,17},{9,25},{17,1},{25,9},{2,18},{10... | collective-permute-start | bytes 1572872 | tf_op jit(solution)/shard_map/back/ppermute | solution.py:253
  197.3 14.6 %collective-permute-start.39 = (bf16[128,1024]{1,0:T(8,128)(2,1)S(1)}, bf16[128,1024]{1,0:T(8,128)(2,1)S(1)}, u32[]{:S(2)}, u32[]{:S(2)}) collective-permute-start(bf16[128,1024]{1,0:T(8,128)(2,1)S(1)} %fusion.9), channel_id=1, source_target_pairs={{0,16},{8,24},{16,0},{24,8},{1,17},{9,25},{17,1},{25,9},{2,18},{10... | collective-permute-start | bytes 786440 | tf_op jit(solution)/shard_map/back/ppermute | solution.py:253
  199.8 26.3 %copy-start.18 = (bf16[512,384]{1,0:T(8,128)(2,1)S(1)}, bf16[512,384]{1,0:T(8,128)(2,1)}, u32[]{:S(2)}) copy-start(bf16[512,384]{1,0:T(8,128)(2,1)} %copy-done.17) | copy-start | bytes 1179652
  199.8 13.4 %collective-permute-start.37 = (bf16[128,1024]{1,0:T(8,128)(2,1)S(1)}, bf16[128,1024]{1,0:T(8,128)(2,1)S(1)}, u32[]{:S(2)}, u32[]{:S(2)}) collective-permute-start(bf16[128,1024]{1,0:T(8,128)(2,1)S(1)} %fusion.8), channel_id=1, source_target_pairs={{0,8},{8,0},{16,24},{24,16},{1,9},{9,1},{17,25},{25,17},{2,10},{10... | collective-permute-start | bytes 786440 | tf_op jit(solution)/shard_map/back/ppermute | solution.py:253
  200.7 32.3 %collective-permute-start.52 = (bf16[512,384]{1,0:T(8,128)(2,1)S(1)}, bf16[512,384]{1,0:T(8,128)(2,1)S(1)}, u32[]{:S(2)}, u32[]{:S(2)}) collective-permute-start(bf16[512,384]{1,0:T(8,128)(2,1)S(1)} %add_convert_fusion.1), channel_id=1, source_target_pairs={{0,2},{1,3},{2,4},{3,5},{4,6},{5,7},{8,10},{9,11},{10,12},{11,13},... | collective-permute-start | bytes 1179656 | tf_op jit(solution)/shard_map/scatter_step_3/ppermute | solution.py:248
  205.6 27.4 %collective-permute-start.54 = (bf16[512,384]{1,0:T(8,128)(2,1)S(1)}, bf16[512,384]{1,0:T(8,128)(2,1)S(1)}, u32[]{:S(2)}, u32[]{:S(2)}) collective-permute-start(bf16[512,384]{1,0:T(8,128)(2,1)S(1)} %add_convert_fusion), channel_id=1, source_target_pairs={{2,0},{3,1},{4,2},{5,3},{6,4},{7,5},{10,8},{11,9},{12,10},{13,11},... | collective-permute-start | bytes 1179656 | tf_op jit(solution)/shard_map/scatter_step_3/ppermute | solution.py:248
  206.9 15.1 %collective-permute-start.47 = (bf16[512,384]{1,0:T(8,128)(2,1)S(1)}, bf16[512,384]{1,0:T(8,128)(2,1)S(1)}, u32[]{:S(2)}, u32[]{:S(2)}) collective-permute-start(bf16[512,384]{1,0:T(8,128)(2,1)S(1)} %add_convert_fusion.4), channel_id=1, source_target_pairs={{0,2},{1,3},{2,4},{3,5},{4,6},{5,7},{8,10},{9,11},{10,12},{11,13},... | collective-permute-start | bytes 1179656 | tf_op jit(solution)/shard_map/scatter_step_3/ppermute | solution.py:248
  211.8 14.2 %collective-permute-start.49 = (bf16[512,384]{1,0:T(8,128)(2,1)S(1)}, bf16[512,384]{1,0:T(8,128)(2,1)S(1)}, u32[]{:S(2)}, u32[]{:S(2)}) collective-permute-start(bf16[512,384]{1,0:T(8,128)(2,1)S(1)} %add_convert_fusion.3), channel_id=1, source_target_pairs={{2,0},{3,1},{4,2},{5,3},{6,4},{7,5},{10,8},{11,9},{12,10},{13,11},... | collective-permute-start | bytes 1179656 | tf_op jit(solution)/shard_map/scatter_step_3/ppermute | solution.py:248
  213.3 14.5 %collective-permute-start.42 = (bf16[512,384]{1,0:T(8,128)(2,1)S(1)}, bf16[512,384]{1,0:T(8,128)(2,1)S(1)}, u32[]{:S(2)}, u32[]{:S(2)}) collective-permute-start(bf16[512,384]{1,0:T(8,128)(2,1)S(1)} %add_convert_fusion.7), channel_id=1, source_target_pairs={{0,2},{1,3},{2,4},{3,5},{4,6},{5,7},{8,10},{9,11},{10,12},{11,13},... | collective-permute-start | bytes 1179656 | tf_op jit(solution)/shard_map/scatter_step_3/ppermute | solution.py:248
  222.0 10.7 %collective-permute-start.44 = (bf16[512,384]{1,0:T(8,128)(2,1)S(1)}, bf16[512,384]{1,0:T(8,128)(2,1)S(1)}, u32[]{:S(2)}, u32[]{:S(2)}) collective-permute-start(bf16[512,384]{1,0:T(8,128)(2,1)S(1)} %add_convert_fusion.6), channel_id=1, source_target_pairs={{2,0},{3,1},{4,2},{5,3},{6,4},{7,5},{10,8},{11,9},{12,10},{13,11},... | collective-permute-start | bytes 1179656 | tf_op jit(solution)/shard_map/scatter_step_3/ppermute | solution.py:248
  226.3 8.5 %collective-permute-start.56 = (f32[256,384]{1,0:T(8,128)S(1)}, f32[256,384]{1,0:T(8,128)S(1)}, u32[]{:S(2)}, u32[]{:S(2)}) collective-permute-start(f32[256,384]{1,0:T(8,128)S(1)} %constant_dynamic-slice_fusion.1), channel_id=1, source_target_pairs={{0,1},{1,0},{2,3},{3,2},{4,5},{5,4},{6,7},{7,6},{8,9},{9,8},{10,11... | collective-permute-start | bytes 1179656 | tf_op jit(solution)/shard_map/ppermute | solution.py:245
  232.9 1.8 collective-permute-start.55
  233.2 2.1 collective-permute-start.57
  (18 other events, 80.5 us)

commit v6 on v5

--- a/solution.py
+++ b/solution.py
@@ -280,7 +280,8 @@
 
     with jax.named_scope("rows"):
         t = [tokens, *(after(flip(tokens, bit), *shards) for bit in (1, 2))]
-        g = [graded, *(after(flip(graded, bit), *shards) for bit in (1, 2))]
+        graded = after(graded, *shards)
+        g = [graded, flip(graded, 1), flip(graded, 2)]
         t.append(flip(t[1], 2))
         g.append(flip(g[2], 1))
         t += [twin(a) for a in t]
@@ -293,41 +294,49 @@
         (at, *g),
     )
 
-    def gather(own):
+    def gather(own, before):
         ups, downs = [own], [own]
         for s in range(1, line):
+            up, down = ups[-1], downs[-1]
+            if s == line - 1:
+                up, down = after(up, *before), after(down, *before)
             with jax.named_scope(f"gather_step_{s}"):
-                ups.append(along(ups[-1], [(i, i + 1) for i in range(s - 1, line - 1)]))
-                downs.append(along(downs[-1], [(i, i - 1) for i in range(1, line - s + 1)]))
+                ups.append(along(up, [(i, i + 1) for i in range(s - 1, line - 1)]))
+                downs.append(along(down, [(i, i - 1) for i in range(1, line - s + 1)]))
         return (own, *ups[1:], *downs[1:])
 
-    def scatter(parts, waits):
+    def begin(parts):
         with jax.named_scope("scatter_step_1"):
             a = jnp.where(z == 0, parts[1], parts[line - 1])
-            up = down = along(a, [(0, 1), (line - 1, line - 2)])
-        for s in range(2, line):
-            if s == 2 and line == 4:
-                a = b = add(parts[2], up)
-            elif s == 2:
-                a = add(parts[2], jnp.where(z == 1, up, 0))
-                b = add(parts[line - 2], jnp.where(z == line - 2, down, 0))
-            else:
-                a, b = add(parts[s], up), add(parts[line - s], down)
-            a, b = after(a, *waits[s - 2]), after(b, *waits[s - 2])
-            with jax.named_scope(f"scatter_step_{s}"):
-                up = along(a, [(i, i + 1) for i in range(s)])
-                down = along(b, [(i, i - 1) for i in range(line - s, line)])
-        return parts[0].astype(F32) + up.astype(F32) + down.astype(F32)
-
-    merged, both, parts = [], [], []
+            first = along(a, [(0, 1), (line - 1, line - 2)])
+        return first, first
+
+    def hop(parts, state, s, waits):
+        up, down = state
+        if s == 2 and line == 4:
+            a = b = add(parts[2], up)
+        elif s == 2:
+            a = add(parts[2], jnp.where(z == 1, up, 0))
+            b = add(parts[line - 2], jnp.where(z == line - 2, down, 0))
+        else:
+            a, b = add(parts[s], up), add(parts[line - s], down)
+        a, b = after(a, *waits), after(b, *waits)
+        with jax.named_scope(f"scatter_step_{s}"):
+            up = along(a, [(i, i + 1) for i in range(s)])
+            down = along(b, [(i, i - 1) for i in range(line - s, line)])
+        return up, down
+
+    merged, both, parts, states, tie, before = [], [], [], [], (), (t[experts - 1], g[experts - 1])
     for i in range(chunks):
-        loaded = gather(shards[i])
+        loaded = gather(shards[i], before)
+        if i == 0:
+            before = (loaded[line - 1], loaded[2 * line - 2])
         got = call(
             lambda *r: chunk_kernel(line, len(t), *r),
             [SMEM] + [ANY] * (len(t) + 2 * line),
             [shape((2 * feats, 3 * step), BF16)] * line
             + [shape((count, 2 * step), BF16), shape((width, 2 * step), BF16)],
-            (at, *t, scaled, *loaded),
+            (at, *t, after(scaled, *tie), *loaded),
             (
                 pltpu.VMEM((count, width), BF16),
                 pltpu.VMEM((count, width), BF16),
@@ -342,8 +351,16 @@
         merged.append(got[line])
         both.append(got[line + 1])
         parts.append(got[:line])
+        states.append(begin(got[:line]))
+        if i == 0:
+            before += (merged[0],)
+            tie = states[0]
+        else:
+            tie = states[i - 1]
+            states[i - 1] = hop(parts[i - 1], tie, 2, ())
 
     block = experts * rows
+    merged[-1] = after(merged[-1], *states[-2])
     keep, give = call(
         lambda *r: route_kernel(chunks, *r),
         [VMEM] * (2 * chunks),
@@ -352,7 +369,7 @@
         flops=4 * count * width * step * chunks,
     )
     with jax.named_scope("back"):
-        other = twin(give)
+        other = twin(after(give, *states[-1]))
         ret = keep.astype(F32) + other.astype(F32)
         ret = ret.reshape(experts, rows, width)
         left, right = ret[:, :, : width // 2], ret[:, :, width // 2 :]
@@ -364,7 +381,12 @@
         left = left[0] + near.astype(F32)
         right = right[0] + odd[0].astype(F32) + last.astype(F32)
         grad_input = jnp.concatenate((left, right), axis=1).astype(BF16)
-    sums = [scatter(p, ((other,), *(((odd, far),) * (line - 3)))) for p in parts]
+    states[-1] = hop(parts[-1], states[-1], 2, (other,))
+    sums = []
+    for own, (up, down) in zip(parts, states):
+        for s in range(3, line):
+            up, down = hop(own, (up, down), s, (odd, far))
+        sums.append(own[0].astype(F32) + up.astype(F32) + down.astype(F32))
 
     own = [lax.dynamic_slice_in_dim(s, c * feats, feats, 0) for s in sums]
     other = [twin(lax.dynamic_slice_in_dim(s, (1 - c) * feats, feats, 0)) for s in sums]

time: 240 us -> 228 us (0.950)
  waiting for transfers between devices: 95.3 us -> 65.3 us
  starting transfers between devices: 88.6 us -> 102 us
  local copies, waits for them, and re-layouts: 10.8 us -> 13.7 us
    ppermute x33, waiting for transfers between devices: 78.4 us -> 44.8 us  [along(): lax.ppermute(a, 'wide', [(2 * s + i, 2 * t + i) for s, t in hops for i in...]
    ppermute x33, starting transfers between devices: 72.3 us -> 88.8 us  [along(): lax.ppermute(a, 'wide', [(2 * s + i, 2 * t + i) for s, t in hops for i in...]
    ppermute x10, starting transfers between devices: 13.7 us -> 10.4 us  [flip(): return lax.ppermute(a, 'expert', [(e, e ^ bit) for e in range(experts)])]
    unnamed x55 -> x97, local copies, waits for them, and re-layouts: 8.84 us -> 11.7 us
    convert_element_type x9, other arithmetic: 0.94 us -> 3.72 us  [add(): return (a.astype(F32) + b.astype(F32)).astype(BF16)]
  transfers between devices with their start and end apart: 58 -> 58, of which waited for: 25 -> 18; matrix products, arithmetic and copies ran while one was open for 4% -> 5% of each run, Pallas kernels for 8% -> 15%
where the time goes in v6:
time: 228 us; the launch traced here: 227 us
  starting transfers between devices  102 us (45%)
  waiting for transfers between devices  65.3 us (29%)
  Pallas kernels  33.7 us (15%)
  local copies, waits for them, and re-layouts  13.7 us (6%)
  other arithmetic  10.6 us (5%)
    ppermute x33, starting transfers between devices, along(): lax.ppermute(a, 'wide', [(2 * s + i, 2 * t + i) for s, t in hops for i in...  88.8 us
    ppermute x33, waiting for transfers between devices, along(): lax.ppermute(a, 'wide', [(2 * s + i, 2 * t + i) for s, t in hops for i in...  44.8 us
    pallas_call x7, Pallas kernels, call(): pl.pallas_call(body, out_shape=outs, in_specs=ins, out_specs=[VMEM] * len...  33.7 us
    ppermute x10, waiting for transfers between devices, flip(): return lax.ppermute(a, 'expert', [(e, e ^ bit) for e in range(experts)])  17.7 us
    unnamed x97, local copies, waits for them, and re-layouts  11.7 us
    ppermute x10, starting transfers between devices, flip(): return lax.ppermute(a, 'expert', [(e, e ^ bit) for e in range(experts)])  10.4 us
  transfers between devices with their start and end apart: 58, of which 18 were waited for; matrix products, arithmetic and copies ran while one was open for 5% of the time, Pallas kernels for 15%

profile of v6, /device:TPU:0, one launch (start us, length us, event | category | flops | bytes accessed | tf_op | source)
XLA Modules:
  0.0 226.8 jit_solution(6563956638583338870)
XLA Ops:
  1.1 2.6 %collective-permute-start.4 = (bf16[128,2048]{1,0:T(8,128)(2,1)}, bf16[128,2048]{1,0:T(8,128)(2,1)}, u32[]{:S(2)}, u32[]{:S(2)}) collective-permute-start(bf16[128,2048]{1,0:T(8,128)(2,1)} %r_1_.5), channel_id=1, source_target_pairs={{0,16},{8,24},{16,0},{24,8},{1,17},{9,25},{17,1},{25,9},{2,18},{10... | collective-permute-start | bytes 1572872 | tf_op jit(solution)/shard_map/rows/ppermute | solution.py:253
  3.7 1.5 collective-permute-start
  5.3 1.0 copy-done.10
  6.3 1.0 copy-done.11
  7.3 1.0 copy-done.12
  11.4 1.2 collective-permute-done.3.r_6_
  13.3 1.3 collective-permute-start.20
  14.6 4.6 %collective-permute-start.17 = (bf16[512,384]{1,0:T(8,128)(2,1)S(1)}, bf16[512,384]{1,0:T(8,128)(2,1)S(1)}, u32[]{:S(2)}, u32[]{:S(2)}) collective-permute-start(bf16[512,384]{1,0:T(8,128)(2,1)S(1)} %get-tuple-element.58.r_10_), channel_id=1, source_target_pairs={{0,2},{1,3},{2,4},{3,5},{4,6},{5,7},{8,10},{9,11},{10,12},{11,13},... | collective-permute-start | bytes 1179656 | tf_op jit(solution)/shard_map/gather_step_1/ppermute | solution.py:248
  21.3 1.3 collective-permute-start.27
  22.6 4.6 %collective-permute-start.24 = (bf16[512,384]{1,0:T(8,128)(2,1)S(1)}, bf16[512,384]{1,0:T(8,128)(2,1)S(1)}, u32[]{:S(2)}, u32[]{:S(2)}) collective-permute-start(bf16[512,384]{1,0:T(8,128)(2,1)S(1)} %get-tuple-element.59.r_10_), channel_id=1, source_target_pairs={{0,2},{1,3},{2,4},{3,5},{4,6},{5,7},{8,10},{9,11},{10,12},{11,13},... | collective-permute-start | bytes 1179656 | tf_op jit(solution)/shard_map/gather_step_1/ppermute | solution.py:248
  27.2 1.4 collective-permute-done.17.r_11_
  29.2 5.7 %collective-permute-done.27.r_14_ = bf16[512,384]{1,0:T(8,128)(2,1)} collective-permute-done((bf16[512,384]{1,0:T(8,128)(2,1)S(1)}, bf16[512,384]{1,0:T(8,128)(2,1)}, u32[]{:S(2)}, u32[]{:S(2)}) %collective-permute-start.27) | collective-permute-done | bytes 393248 | tf_op jit(solution)/shard_map/gather_step_1/ppermute | solution.py:248
  34.9 1.3 collective-permute-start.21
  36.9 1.4 collective-permute-start.18
  39.6 3.9 %collective-permute-done.10.r_2_ = bf16[128,2176]{1,0:T(8,128)(2,1)S(1)} collective-permute-done((bf16[128,2176]{1,0:T(8,128)(2,1)S(1)}, bf16[128,2176]{1,0:T(8,128)(2,1)S(1)}, u32[]{:S(2)}, u32[]{:S(2)}) %collective-permute-start.10) | collective-permute-done | bytes 557088 | tf_op jit(solution)/shard_map/rows/ppermute | solution.py:253
  44.3 2.9 %collective-permute-done.21.r_15_ = bf16[512,384]{1,0:T(8,128)(2,1)} collective-permute-done((bf16[512,384]{1,0:T(8,128)(2,1)S(1)}, bf16[512,384]{1,0:T(8,128)(2,1)}, u32[]{:S(2)}, u32[]{:S(2)}) %collective-permute-start.21) | collective-permute-done | bytes 393248 | tf_op jit(solution)/shard_map/gather_step_2/ppermute | solution.py:248
  47.7 6.5 %collective-permute-done.12.r_4_ = bf16[128,2176]{1,0:T(8,128)(2,1)S(1)} collective-permute-done((bf16[128,2176]{1,0:T(8,128)(2,1)S(1)}, bf16[128,2176]{1,0:T(8,128)(2,1)S(1)}, u32[]{:S(2)}, u32[]{:S(2)}) %collective-permute-start.12) | collective-permute-done | bytes 557088 | tf_op jit(solution)/shard_map/rows/ppermute | solution.py:253
  56.0 1.5 collective-permute-start.19
  58.2 1.3 collective-permute-start.22
  60.4 1.3 collective-permute-start.28
  61.7 1.0 copy-done.7
  62.7 1.1 copy-done.9
  63.8 1.3 shard_map.104.r_9_
  65.2 1.4 collective-permute-start.33
  66.6 8.5 %collective-permute-start.30 = (bf16[512,384]{1,0:T(8,128)(2,1)S(1)}, bf16[512,384]{1,0:T(8,128)(2,1)S(1)}, u32[]{:S(2)}, u32[]{:S(2)}) collective-permute-start(bf16[512,384]{1,0:T(8,128)(2,1)S(1)} %copy-done.27), channel_id=1, source_target_pairs={{0,2},{1,3},{2,4},{3,5},{4,6},{5,7},{8,10},{9,11},{10,12},{11,13},... | collective-permute-start | bytes 1179656 | tf_op jit(solution)/shard_map/gather_step_1/ppermute | solution.py:248
  75.9 7.7 %shard_map.105 = (bf16[512,384]{1,0:T(8,128)(2,1)S(1)}, bf16[512,384]{1,0:T(8,128)(2,1)S(1)}, bf16[512,384]{1,0:T(8,128)(2,1)S(1)}, bf16[512,384]{1,0:T(8,128)(2...) custom-call(s32[3]{0:T(128)S(1)} %pad_add_fusion.r_0_, bf16[128,2048]{1,0:T(8,128)(2,1)S(1)} %copy-done.21, ...), custom_call_target="tpu_custom_call" | custom-call | flops 3221225472 | bytes 14286860 | tf_op jit(solution)/shard_map/pallas_call | solution.py:100
  83.7 13.3 %collective-permute-start.23 = (bf16[512,384]{1,0:T(8,128)(2,1)S(1)}, bf16[512,384]{1,0:T(8,128)(2,1)S(1)}, u32[]{:S(2)}, u32[]{:S(2)}) collective-permute-start(bf16[512,384]{1,0:T(8,128)(2,1)S(1)} %broadcast_select_fusion.5), channel_id=1, source_target_pairs={{0,2},{1,3},{6,4},{7,5},{8,10},{9,11},{14,12},{15,13},{16,18},{17,... | collective-permute-start | bytes 1179656 | tf_op jit(solution)/shard_map/scatter_step_1/ppermute | solution.py:248
  97.7 1.3 collective-permute-start.29
  99.0 1.3 collective-permute-start.34
  101.0 3.9 %collective-permute-done.23 = bf16[512,384]{1,0:T(8,128)(2,1)S(1)} collective-permute-done((bf16[512,384]{1,0:T(8,128)(2,1)S(1)}, bf16[512,384]{1,0:T(8,128)(2,1)S(1)}, u32[]{:S(2)}, u32[]{:S(2)}) %collective-permute-start.23) | collective-permute-done | bytes 393248 | tf_op jit(solution)/shard_map/scatter_step_1/ppermute | solution.py:248
  104.9 6.9 %collective-permute-done.29.r_16_ = bf16[512,384]{1,0:T(8,128)(2,1)S(1)} collective-permute-done((bf16[512,384]{1,0:T(8,128)(2,1)}, bf16[512,384]{1,0:T(8,128)(2,1)S(1)}, u32[]{:S(2)}, u32[]{:S(2)}) %collective-permute-start.29) | collective-permute-done | bytes 393248 | tf_op jit(solution)/shard_map/gather_step_3/ppermute | solution.py:248
  111.8 7.9 %shard_map.106 = (bf16[512,384]{1,0:T(8,128)(2,1)S(1)}, bf16[512,384]{1,0:T(8,128)(2,1)S(1)}, bf16[512,384]{1,0:T(8,128)(2,1)S(1)}, bf16[512,384]{1,0:T(8,128)(2...) custom-call(s32[3]{0:T(128)S(1)} %pad_add_fusion.r_0_, bf16[128,2048]{1,0:T(8,128)(2,1)S(1)} %copy-done.21, ...), custom_call_target="tpu_custom_call" | custom-call | flops 3221225472 | bytes 14286860 | tf_op jit(solution)/shard_map/pallas_call | solution.py:100
  120.5 1.6 collective-permute-start.36
  122.9 1.3 collective-permute-start.35
  124.2 3.2 %collective-permute-done.36 = bf16[512,384]{1,0:T(8,128)(2,1)S(1)} collective-permute-done((bf16[512,384]{1,0:T(8,128)(2,1)S(1)}, bf16[512,384]{1,0:T(8,128)(2,1)S(1)}, u32[]{:S(2)}, u32[]{:S(2)}) %collective-permute-start.36) | collective-permute-done | bytes 393248 | tf_op jit(solution)/shard_map/scatter_step_1/ppermute | solution.py:248
  128.2 5.0 %collective-permute-start.37 = (bf16[512,384]{1,0:T(8,128)(2,1)S(1)}, bf16[512,384]{1,0:T(8,128)(2,1)S(1)}, u32[]{:S(2)}, u32[]{:S(2)}) collective-permute-start(bf16[512,384]{1,0:T(8,128)(2,1)S(1)} %add_convert_fusion.8), channel_id=1, source_target_pairs={{0,2},{1,3},{2,4},{3,5},{8,10},{9,11},{10,12},{11,13},{16,18},{17,... | collective-permute-start | bytes 1179656 | tf_op jit(solution)/shard_map/scatter_step_2/ppermute | solution.py:248
  133.3 8.0 %shard_map.107 = (bf16[512,384]{1,0:T(8,128)(2,1)S(1)}, bf16[512,384]{1,0:T(8,128)(2,1)S(1)}, bf16[512,384]{1,0:T(8,128)(2,1)S(1)}, bf16[512,384]{1,0:T(8,128)(2...) custom-call(s32[3]{0:T(128)S(1)} %pad_add_fusion.r_0_, bf16[128,2048]{1,0:T(8,128)(2,1)S(1)} %copy-done.21, ...), custom_call_target="tpu_custom_call" | custom-call | flops 3221225472 | bytes 14286860 | tf_op jit(solution)/shard_map/pallas_call | solution.py:100
  141.4 4.8 %collective-permute-start.39 = (bf16[512,384]{1,0:T(8,128)(2,1)S(1)}, bf16[512,384]{1,0:T(8,128)(2,1)S(1)}, u32[]{:S(2)}, u32[]{:S(2)}) collective-permute-start(bf16[512,384]{1,0:T(8,128)(2,1)S(1)} %broadcast_select_fusion.3), channel_id=1, source_target_pairs={{0,2},{1,3},{6,4},{7,5},{8,10},{9,11},{14,12},{15,13},{16,18},{17,... | collective-permute-start | bytes 1179656 | tf_op jit(solution)/shard_map/scatter_step_1/ppermute | solution.py:248
  146.3 7.4 %shard_map.108 = (bf16[512,2048]{1,0:T(8,128)(2,1)S(1)}, bf16[512,2048]{1,0:T(8,128)(2,1)}) custom-call(bf16[1024,256]{1,0:T(8,128)(2,1)S(1)} %get-tuple-element.66.r_0_, bf16[1024,256]{1,0:T(8,128)(2,1)S(1)} %get-tuple-element.72.r_1_, bf16[1024,256]{1,0:T(8,128)(2,1)S(1)} %get-tuple-element.79.r_2_, bf16[2048,256]{1,0:T(8,128)(2,1)S(1)} %get-tuple-element.80.r_3_, ...), custom_call_target="tpu_custom_call" | custom-call | flops 3221225472 | bytes 8912896 | tf_op jit(solution)/shard_map/pallas_call | solution.py:100
  153.8 0.8 add_convert_fusion.7
  154.7 1.4 collective-permute-start.47
  156.1 2.5 %collective-permute-start.45 = (bf16[512,384]{1,0:T(8,128)(2,1)}, bf16[512,384]{1,0:T(8,128)(2,1)}, u32[]{:S(2)}, u32[]{:S(2)}) collective-permute-start(bf16[512,384]{1,0:T(8,128)(2,1)} %add_convert_fusion.7), channel_id=1, source_target_pairs={{0,2},{1,3},{2,4},{3,5},{8,10},{9,11},{10,12},{11,13},{16,18},{17,... | collective-permute-start | bytes 1179656 | tf_op jit(solution)/shard_map/scatter_step_2/ppermute | solution.py:248
  158.6 1.2 add_convert_fusion.5
  159.8 7.4 %collective-permute-done.45 = bf16[512,384]{1,0:T(8,128)(2,1)} collective-permute-done((bf16[512,384]{1,0:T(8,128)(2,1)}, bf16[512,384]{1,0:T(8,128)(2,1)}, u32[]{:S(2)}, u32[]{:S(2)}) %collective-permute-start.45) | collective-permute-done | bytes 393248 | tf_op jit(solution)/shard_map/scatter_step_2/ppermute | solution.py:248
  167.1 1.1 add_convert_fusion.6
  169.1 2.3 %convert_add_fusion = f32[512,2048]{1,0:T(8,128)S(1)} fusion(bf16[512,2048]{1,0:T(8,128)(2,1)} %collective-permute-done.40, bf16[512,2048]{1,0:T(8,128)(2,1)S(1)} %get-tuple-element.83), kind=kLoop, calls=%fused_computation | loop fusion | flops 3145728 | bytes 8388608 | tf_op jit(solution)/shard_map/back/add | solution.py:373
  171.9 1.6 collective-permute-start.43
  174.3 5.0 %collective-permute-start.51 = (bf16[512,384]{1,0:T(8,128)(2,1)S(1)}, bf16[512,384]{1,0:T(8,128)(2,1)S(1)}, u32[]{:S(2)}, u32[]{:S(2)}) collective-permute-start(bf16[512,384]{1,0:T(8,128)(2,1)S(1)} %add_convert_fusion.2), channel_id=1, source_target_pairs={{0,2},{1,3},{2,4},{3,5},{8,10},{9,11},{10,12},{11,13},{16,18},{17,... | collective-permute-start | bytes 1179656 | tf_op jit(solution)/shard_map/scatter_step_2/ppermute | solution.py:248
  179.4 6.0 %collective-permute-done.43 = bf16[2,128,1024]{2,1,0:T(8,128)(2,1)S(1)} collective-permute-done((bf16[2,128,1024]{2,1,0:T(8,128)(2,1)S(1)}, bf16[2,128,1024]{2,1,0:T(8,128)(2,1)S(1)}, u32[]{:S(2)}, u32[]{:S(2)}) %collective-permute-start.43) | collective-permute-done | bytes 524320 | tf_op jit(solution)/shard_map/back/ppermute | solution.py:253
  186.1 0.8 collective-permute-done.41
  187.1 1.2 collective-permute-start.42
  188.5 5.0 %collective-permute-start.46 = (bf16[512,384]{1,0:T(8,128)(2,1)S(1)}, bf16[512,384]{1,0:T(8,128)(2,1)S(1)}, u32[]{:S(2)}, u32[]{:S(2)}) collective-permute-start(bf16[512,384]{1,0:T(8,128)(2,1)S(1)} %add_convert_fusion.6), channel_id=1, source_target_pairs={{0,2},{1,3},{2,4},{3,5},{4,6},{5,7},{8,10},{9,11},{10,12},{11,13},... | collective-permute-start | bytes 1179656 | tf_op jit(solution)/shard_map/scatter_step_3/ppermute | solution.py:248
  193.5 1.3 collective-permute-start.48
  194.8 5.2 %collective-permute-start.49 = (bf16[512,384]{1,0:T(8,128)(2,1)S(1)}, bf16[512,384]{1,0:T(8,128)(2,1)S(1)}, u32[]{:S(2)}, u32[]{:S(2)}) collective-permute-start(bf16[512,384]{1,0:T(8,128)(2,1)S(1)} %add_convert_fusion.4), channel_id=1, source_target_pairs={{0,2},{1,3},{2,4},{3,5},{4,6},{5,7},{8,10},{9,11},{10,12},{11,13},... | collective-permute-start | bytes 1179656 | tf_op jit(solution)/shard_map/scatter_step_3/ppermute | solution.py:248
  200.1 1.3 collective-permute-start.50
  201.5 4.6 %collective-permute-start.52 = (bf16[512,384]{1,0:T(8,128)(2,1)S(1)}, bf16[512,384]{1,0:T(8,128)(2,1)S(1)}, u32[]{:S(2)}, u32[]{:S(2)}) collective-permute-start(bf16[512,384]{1,0:T(8,128)(2,1)S(1)} %add_convert_fusion.1), channel_id=1, source_target_pairs={{0,2},{1,3},{2,4},{3,5},{4,6},{5,7},{8,10},{9,11},{10,12},{11,13},... | collective-permute-start | bytes 1179656 | tf_op jit(solution)/shard_map/scatter_step_3/ppermute | solution.py:248
  206.1 0.8 pad_maximum_fusion.1
  207.0 1.3 collective-permute-start.54
  208.5 2.9 %collective-permute-done.49 = bf16[512,384]{1,0:T(8,128)(2,1)S(1)} collective-permute-done((bf16[512,384]{1,0:T(8,128)(2,1)S(1)}, bf16[512,384]{1,0:T(8,128)(2,1)S(1)}, u32[]{:S(2)}, u32[]{:S(2)}) %collective-permute-start.49) | collective-permute-done | bytes 393248 | tf_op jit(solution)/shard_map/scatter_step_3/ppermute | solution.py:248
  211.5 5.1 %collective-permute-done.50 = bf16[512,384]{1,0:T(8,128)(2,1)S(1)} collective-permute-done((bf16[512,384]{1,0:T(8,128)(2,1)S(1)}, bf16[512,384]{1,0:T(8,128)(2,1)S(1)}, u32[]{:S(2)}, u32[]{:S(2)}) %collective-permute-start.50) | collective-permute-done | bytes 393248 | tf_op jit(solution)/shard_map/scatter_step_3/ppermute | solution.py:248
  217.4 4.7 %collective-permute-done.54 = bf16[512,384]{1,0:T(8,128)(2,1)S(1)} collective-permute-done((bf16[512,384]{1,0:T(8,128)(2,1)S(1)}, bf16[512,384]{1,0:T(8,128)(2,1)S(1)}, u32[]{:S(2)}, u32[]{:S(2)}) %collective-permute-start.54) | collective-permute-done | bytes 393248 | tf_op jit(solution)/shard_map/scatter_step_3/ppermute | solution.py:248
  222.5 1.6 collective-permute-done.57
  224.5 1.0 broadcast_select_fusion.2
  225.5 1.3 broadcast_select_fusion
  (196 shorter events, 23.3 us)
Async XLA Ops:
  0.6 19.3 %collective-permute-start.6 = (bf16[128,2048]{1,0:T(8,128)(2,1)}, bf16[128,2048]{1,0:T(8,128)(2,1)S(1)}, u32[]{:S(2)}, u32[]{:S(2)}) collective-permute-start(bf16[128,2048]{1,0:T(8,128)(2,1)} %r_1_.5), channel_id=1, source_target_pairs={{0,1},{1,0},{2,3},{3,2},{4,5},{5,4},{6,7},{7,6},{8,9},{9,8},{10,11... | collective-permute-start | bytes 1572872 | tf_op jit(solution)/shard_map/rows/ppermute | solution.py:245
  1.1 20.1 %collective-permute-start.4 = (bf16[128,2048]{1,0:T(8,128)(2,1)}, bf16[128,2048]{1,0:T(8,128)(2,1)}, u32[]{:S(2)}, u32[]{:S(2)}) collective-permute-start(bf16[128,2048]{1,0:T(8,128)(2,1)} %r_1_.5), channel_id=1, source_target_pairs={{0,16},{8,24},{16,0},{24,8},{1,17},{9,25},{17,1},{25,9},{2,18},{10... | collective-permute-start | bytes 1572872 | tf_op jit(solution)/shard_map/rows/ppermute | solution.py:253
  3.7 18.8 %collective-permute-start = (bf16[128,2048]{1,0:T(8,128)(2,1)}, bf16[128,2048]{1,0:T(8,128)(2,1)}, u32[]{:S(2)}, u32[]{:S(2)}) collective-permute-start(bf16[128,2048]{1,0:T(8,128)(2,1)} %r_1_.5), channel_id=1, source_target_pairs={{0,8},{8,0},{16,24},{24,16},{1,9},{9,1},{17,25},{25,17},{2,10},{10... | collective-permute-start | bytes 1572872 | tf_op jit(solution)/shard_map/rows/ppermute | solution.py:253
  9.1 2.1 collective-permute-start.1
  9.1 2.3 collective-permute-start.2
  11.2 1.4 collective-permute-start.3
  13.3 46.3 %copy-start.26 = (bf16[512,384]{1,0:T(8,128)(2,1)}, bf16[512,384]{1,0:T(8,128)(2,1)S(1)}, u32[]{:S(2)}) copy-start(bf16[512,384]{1,0:T(8,128)(2,1)S(1)} %get-tuple-element.60.r_10_) | copy-start | bytes 1179652
  13.3 46.3 %copy-start.28 = (bf16[512,384]{1,0:T(8,128)(2,1)}, bf16[512,384]{1,0:T(8,128)(2,1)S(1)}, u32[]{:S(2)}) copy-start(bf16[512,384]{1,0:T(8,128)(2,1)S(1)} %get-tuple-element.59.r_10_) | copy-start | bytes 1179652
  13.3 13.9 %collective-permute-start.20 = (bf16[512,384]{1,0:T(8,128)(2,1)S(1)}, bf16[512,384]{1,0:T(8,128)(2,1)S(1)}, u32[]{:S(2)}, u32[]{:S(2)}) collective-permute-start(bf16[512,384]{1,0:T(8,128)(2,1)S(1)} %get-tuple-element.58.r_10_), channel_id=1, source_target_pairs={{2,0},{3,1},{4,2},{5,3},{6,4},{7,5},{10,8},{11,9},{12,10},{13,11},... | collective-permute-start | bytes 1179656 | tf_op jit(solution)/shard_map/gather_step_1/ppermute | solution.py:248
  14.6 14.1 %collective-permute-start.17 = (bf16[512,384]{1,0:T(8,128)(2,1)S(1)}, bf16[512,384]{1,0:T(8,128)(2,1)S(1)}, u32[]{:S(2)}, u32[]{:S(2)}) collective-permute-start(bf16[512,384]{1,0:T(8,128)(2,1)S(1)} %get-tuple-element.58.r_10_), channel_id=1, source_target_pairs={{0,2},{1,3},{2,4},{3,5},{4,6},{5,7},{8,10},{9,11},{10,12},{11,13},... | collective-permute-start | bytes 1179656 | tf_op jit(solution)/shard_map/gather_step_1/ppermute | solution.py:248
  20.8 18.3 %collective-permute-start.11 = (bf16[128,2176]{1,0:T(8,128)(2,1)S(1)}, bf16[128,2176]{1,0:T(8,128)(2,1)S(1)}, u32[]{:S(2)}, u32[]{:S(2)}) collective-permute-start(bf16[128,2176]{1,0:T(8,128)(2,1)S(1)} %fusion.1.r_1_), channel_id=1, source_target_pairs={{0,16},{8,24},{16,0},{24,8},{1,17},{9,25},{17,1},{25,9},{2,18},{10... | collective-permute-start | bytes 1671176 | tf_op jit(solution)/shard_map/rows/ppermute | solution.py:253
  21.3 13.6 %collective-permute-start.27 = (bf16[512,384]{1,0:T(8,128)(2,1)S(1)}, bf16[512,384]{1,0:T(8,128)(2,1)}, u32[]{:S(2)}, u32[]{:S(2)}) collective-permute-start(bf16[512,384]{1,0:T(8,128)(2,1)S(1)} %get-tuple-element.59.r_10_), channel_id=1, source_target_pairs={{2,0},{3,1},{4,2},{5,3},{6,4},{7,5},{10,8},{11,9},{12,10},{13,11},... | collective-permute-start | bytes 1179656 | tf_op jit(solution)/shard_map/gather_step_1/ppermute | solution.py:248
  22.6 14.3 %collective-permute-start.24 = (bf16[512,384]{1,0:T(8,128)(2,1)S(1)}, bf16[512,384]{1,0:T(8,128)(2,1)S(1)}, u32[]{:S(2)}, u32[]{:S(2)}) collective-permute-start(bf16[512,384]{1,0:T(8,128)(2,1)S(1)} %get-tuple-element.59.r_10_), channel_id=1, source_target_pairs={{0,2},{1,3},{2,4},{3,5},{4,6},{5,7},{8,10},{9,11},{10,12},{11,13},... | collective-permute-start | bytes 1179656 | tf_op jit(solution)/shard_map/gather_step_1/ppermute | solution.py:248
  27.2 12.5 %collective-permute-start.13 = (bf16[128,2176]{1,0:T(8,128)(2,1)S(1)}, bf16[128,2176]{1,0:T(8,128)(2,1)S(1)}, u32[]{:S(2)}, u32[]{:S(2)}) collective-permute-start(bf16[128,2176]{1,0:T(8,128)(2,1)S(1)} %fusion.1.r_1_), channel_id=1, source_target_pairs={{0,1},{1,0},{2,3},{3,2},{4,5},{5,4},{6,7},{7,6},{8,9},{9,8},{10,11... | collective-permute-start | bytes 1671176 | tf_op jit(solution)/shard_map/rows/ppermute | solution.py:245
  28.6 14.9 %collective-permute-start.10 = (bf16[128,2176]{1,0:T(8,128)(2,1)S(1)}, bf16[128,2176]{1,0:T(8,128)(2,1)S(1)}, u32[]{:S(2)}, u32[]{:S(2)}) collective-permute-start(bf16[128,2176]{1,0:T(8,128)(2,1)S(1)} %fusion.1.r_1_), channel_id=1, source_target_pairs={{0,8},{8,0},{16,24},{24,16},{1,9},{9,1},{17,25},{25,17},{2,10},{10... | collective-permute-start | bytes 1671176 | tf_op jit(solution)/shard_map/rows/ppermute | solution.py:253
  34.9 12.3 %collective-permute-start.21 = (bf16[512,384]{1,0:T(8,128)(2,1)S(1)}, bf16[512,384]{1,0:T(8,128)(2,1)}, u32[]{:S(2)}, u32[]{:S(2)}) collective-permute-start(bf16[512,384]{1,0:T(8,128)(2,1)S(1)} %collective-permute-done.20.r_14_), channel_id=1, source_target_pairs={{2,0},{3,1},{4,2},{5,3},{10,8},{11,9},{12,10},{13,11},{18,16},{19,... | collective-permute-start | bytes 1179656 | tf_op jit(solution)/shard_map/gather_step_2/ppermute | solution.py:248
  36.9 10.3 %collective-permute-start.18 = (bf16[512,384]{1,0:T(8,128)(2,1)S(1)}, bf16[512,384]{1,0:T(8,128)(2,1)}, u32[]{:S(2)}, u32[]{:S(2)}) collective-permute-start(bf16[512,384]{1,0:T(8,128)(2,1)S(1)} %collective-permute-done.17.r_11_), channel_id=1, source_target_pairs={{2,4},{3,5},{4,6},{5,7},{10,12},{11,13},{12,14},{13,15},{18,20},{1... | collective-permute-start | bytes 1179656 | tf_op jit(solution)/shard_map/gather_step_2/ppermute | solution.py:248
  39.1 15.1 %collective-permute-start.12 = (bf16[128,2176]{1,0:T(8,128)(2,1)S(1)}, bf16[128,2176]{1,0:T(8,128)(2,1)S(1)}, u32[]{:S(2)}, u32[]{:S(2)}) collective-permute-start(bf16[128,2176]{1,0:T(8,128)(2,1)S(1)} %collective-permute-done.11.r_3_), channel_id=1, source_target_pairs={{0,8},{8,0},{16,24},{24,16},{1,9},{9,1},{17,25},{25,17},{2,10},{10... | collective-permute-start | bytes 1671176 | tf_op jit(solution)/shard_map/rows/ppermute | solution.py:253
  39.6 14.6 %collective-permute-start.7 = (bf16[128,2048]{1,0:T(8,128)(2,1)}, bf16[128,2048]{1,0:T(8,128)(2,1)S(1)}, u32[]{:S(2)}, u32[]{:S(2)}) collective-permute-start(bf16[128,2048]{1,0:T(8,128)(2,1)} %collective-permute-done.r_2_), channel_id=1, source_target_pairs={{0,1},{1,0},{2,3},{3,2},{4,5},{5,4},{6,7},{7,6},{8,9},{9,8},{10,11... | collective-permute-start | bytes 1572872 | tf_op jit(solution)/shard_map/rows/ppermute | solution.py:245
  43.5 12.5 %collective-permute-start.5 = (bf16[128,2048]{1,0:T(8,128)(2,1)}, bf16[128,2048]{1,0:T(8,128)(2,1)}, u32[]{:S(2)}, u32[]{:S(2)}) collective-permute-start(bf16[128,2048]{1,0:T(8,128)(2,1)} %collective-permute-done.r_2_), channel_id=1, source_target_pairs={{0,16},{8,24},{16,0},{24,8},{1,17},{9,25},{17,1},{25,9},{2,18},{10... | collective-permute-start | bytes 1572872 | tf_op jit(solution)/shard_map/rows/ppermute | solution.py:253
  47.2 8.8 %collective-permute-start.15 = (bf16[128,2176]{1,0:T(8,128)(2,1)S(1)}, bf16[128,2176]{1,0:T(8,128)(2,1)S(1)}, u32[]{:S(2)}, u32[]{:S(2)}) collective-permute-start(bf16[128,2176]{1,0:T(8,128)(2,1)S(1)} %collective-permute-done.11.r_3_), channel_id=1, source_target_pairs={{0,1},{1,0},{2,3},{3,2},{4,5},{5,4},{6,7},{7,6},{8,9},{9,8},{10,11... | collective-permute-start | bytes 1671176 | tf_op jit(solution)/shard_map/rows/ppermute | solution.py:245
  47.2 10.3 %collective-permute-start.14 = (bf16[128,2176]{1,0:T(8,128)(2,1)S(1)}, bf16[128,2176]{1,0:T(8,128)(2,1)S(1)}, u32[]{:S(2)}, u32[]{:S(2)}) collective-permute-start(bf16[128,2176]{1,0:T(8,128)(2,1)S(1)} %collective-permute-done.10.r_2_), channel_id=1, source_target_pairs={{0,1},{1,0},{2,3},{3,2},{4,5},{5,4},{6,7},{7,6},{8,9},{9,8},{10,11... | collective-permute-start | bytes 1671176 | tf_op jit(solution)/shard_map/rows/ppermute | solution.py:245
  54.2 5.3 %collective-permute-start.16 = (bf16[128,2176]{1,0:T(8,128)(2,1)S(1)}, bf16[128,2176]{1,0:T(8,128)(2,1)S(1)}, u32[]{:S(2)}, u32[]{:S(2)}) collective-permute-start(bf16[128,2176]{1,0:T(8,128)(2,1)S(1)} %collective-permute-done.12.r_4_), channel_id=1, source_target_pairs={{0,1},{1,0},{2,3},{3,2},{4,5},{5,4},{6,7},{7,6},{8,9},{9,8},{10,11... | collective-permute-start | bytes 1671176 | tf_op jit(solution)/shard_map/rows/ppermute | solution.py:245
  55.0 10.1 %collective-permute-start.8 = (bf16[128,2048]{1,0:T(8,128)(2,1)}, bf16[128,2048]{1,0:T(8,128)(2,1)}, u32[]{:S(2)}, u32[]{:S(2)}) collective-permute-start(bf16[128,2048]{1,0:T(8,128)(2,1)} %collective-permute-done.4.r_3_), channel_id=1, source_target_pairs={{0,1},{1,0},{2,3},{3,2},{4,5},{5,4},{6,7},{7,6},{8,9},{9,8},{10,11... | collective-permute-start | bytes 1572872 | tf_op jit(solution)/shard_map/rows/ppermute | solution.py:245
  56.0 10.6 %collective-permute-start.9 = (bf16[128,2048]{1,0:T(8,128)(2,1)}, bf16[128,2048]{1,0:T(8,128)(2,1)}, u32[]{:S(2)}, u32[]{:S(2)}) collective-permute-start(bf16[128,2048]{1,0:T(8,128)(2,1)} %collective-permute-done.5.r_4_), channel_id=1, source_target_pairs={{0,1},{1,0},{2,3},{3,2},{4,5},{5,4},{6,7},{7,6},{8,9},{9,8},{10,11... | collective-permute-start | bytes 1572872 | tf_op jit(solution)/shard_map/rows/ppermute | solution.py:245
  56.0 19.2 %collective-permute-start.19 = (bf16[512,384]{1,0:T(8,128)(2,1)}, bf16[512,384]{1,0:T(8,128)(2,1)}, u32[]{:S(2)}, u32[]{:S(2)}) collective-permute-start(bf16[512,384]{1,0:T(8,128)(2,1)} %collective-permute-done.18.r_12_), channel_id=1, source_target_pairs={{4,6},{5,7},{12,14},{13,15},{20,22},{21,23},{28,30},{29,31}} | collective-permute-start | bytes 1179656 | tf_op jit(solution)/shard_map/gather_step_3/ppermute | solution.py:248
  58.2 17.6 %collective-permute-start.22 = (bf16[512,384]{1,0:T(8,128)(2,1)}, bf16[512,384]{1,0:T(8,128)(2,1)}, u32[]{:S(2)}, u32[]{:S(2)}) collective-permute-start(bf16[512,384]{1,0:T(8,128)(2,1)} %collective-permute-done.21.r_15_), channel_id=1, source_target_pairs={{2,0},{3,1},{10,8},{11,9},{18,16},{19,17},{26,24},{27,25}} | collective-permute-start | bytes 1179656 | tf_op jit(solution)/shard_map/gather_step_3/ppermute | solution.py:248
  60.4 23.2 %collective-permute-start.28 = (bf16[512,384]{1,0:T(8,128)(2,1)}, bf16[512,384]{1,0:T(8,128)(2,1)}, u32[]{:S(2)}, u32[]{:S(2)}) collective-permute-start(bf16[512,384]{1,0:T(8,128)(2,1)} %collective-permute-done.27.r_14_), channel_id=1, source_target_pairs={{2,0},{3,1},{4,2},{5,3},{10,8},{11,9},{12,10},{13,11},{18,16},{19,... | collective-permute-start | bytes 1179656 | tf_op jit(solution)/shard_map/gather_step_2/ppermute | solution.py:248
  65.1 46.7 %copy-start.29 = (bf16[512,384]{1,0:T(8,128)(2,1)S(1)}, bf16[512,384]{1,0:T(8,128)(2,1)}, u32[]{:S(2)}) copy-start(bf16[512,384]{1,0:T(8,128)(2,1)} %copy-done.28) | copy-start | bytes 1179652
  65.2 33.8 %collective-permute-start.33 = (bf16[512,384]{1,0:T(8,128)(2,1)S(1)}, bf16[512,384]{1,0:T(8,128)(2,1)S(1)}, u32[]{:S(2)}, u32[]{:S(2)}) collective-permute-start(bf16[512,384]{1,0:T(8,128)(2,1)S(1)} %copy-done.27), channel_id=1, source_target_pairs={{2,0},{3,1},{4,2},{5,3},{6,4},{7,5},{10,8},{11,9},{12,10},{13,11},... | collective-permute-start | bytes 1179656 | tf_op jit(solution)/shard_map/gather_step_1/ppermute | solution.py:248
  66.6 33.6 %collective-permute-start.30 = (bf16[512,384]{1,0:T(8,128)(2,1)S(1)}, bf16[512,384]{1,0:T(8,128)(2,1)S(1)}, u32[]{:S(2)}, u32[]{:S(2)}) collective-permute-start(bf16[512,384]{1,0:T(8,128)(2,1)S(1)} %copy-done.27), channel_id=1, source_target_pairs={{0,2},{1,3},{2,4},{3,5},{4,6},{5,7},{8,10},{9,11},{10,12},{11,13},... | collective-permute-start | bytes 1179656 | tf_op jit(solution)/shard_map/gather_step_1/ppermute | solution.py:248
  75.2 8.5 %collective-permute-start.25 = (bf16[512,384]{1,0:T(8,128)(2,1)S(1)}, bf16[512,384]{1,0:T(8,128)(2,1)S(1)}, u32[]{:S(2)}, u32[]{:S(2)}) collective-permute-start(bf16[512,384]{1,0:T(8,128)(2,1)S(1)} %copy-done.31), channel_id=1, source_target_pairs={{2,4},{3,5},{4,6},{5,7},{10,12},{11,13},{12,14},{13,15},{18,20},{1... | collective-permute-start | bytes 1179656 | tf_op jit(solution)/shard_map/gather_step_2/ppermute | solution.py:248
  83.6 21.3 %copy-start.15 = (bf16[512,384]{1,0:T(8,128)(2,1)}, bf16[512,384]{1,0:T(8,128)(2,1)S(1)}, u32[]{:S(2)}) copy-start(bf16[512,384]{1,0:T(8,128)(2,1)S(1)} %get-tuple-element.88) | copy-start | bytes 1179652
  83.7 21.2 %collective-permute-start.23 = (bf16[512,384]{1,0:T(8,128)(2,1)S(1)}, bf16[512,384]{1,0:T(8,128)(2,1)S(1)}, u32[]{:S(2)}, u32[]{:S(2)}) collective-permute-start(bf16[512,384]{1,0:T(8,128)(2,1)S(1)} %broadcast_select_fusion.5), channel_id=1, source_target_pairs={{0,2},{1,3},{6,4},{7,5},{8,10},{9,11},{14,12},{15,13},{16,18},{17,... | collective-permute-start | bytes 1179656 | tf_op jit(solution)/shard_map/scatter_step_1/ppermute | solution.py:248
  97.0 7.9 %collective-permute-start.26 = (bf16[512,384]{1,0:T(8,128)(2,1)S(1)}, bf16[512,384]{1,0:T(8,128)(2,1)S(1)}, u32[]{:S(2)}, u32[]{:S(2)}) collective-permute-start(bf16[512,384]{1,0:T(8,128)(2,1)S(1)} %collective-permute-done.25.r_12_), channel_id=1, source_target_pairs={{4,6},{5,7},{12,14},{13,15},{20,22},{21,23},{28,30},{29,31}} | collective-permute-start | bytes 1179656 | tf_op jit(solution)/shard_map/gather_step_3/ppermute | solution.py:248
  97.7 14.2 %collective-permute-start.29 = (bf16[512,384]{1,0:T(8,128)(2,1)}, bf16[512,384]{1,0:T(8,128)(2,1)S(1)}, u32[]{:S(2)}, u32[]{:S(2)}) collective-permute-start(bf16[512,384]{1,0:T(8,128)(2,1)} %collective-permute-done.28.r_15_), channel_id=1, source_target_pairs={{2,0},{3,1},{10,8},{11,9},{18,16},{19,17},{26,24},{27,25}} | collective-permute-start | bytes 1179656 | tf_op jit(solution)/shard_map/gather_step_3/ppermute | solution.py:248
  99.0 23.2 %collective-permute-start.34 = (bf16[512,384]{1,0:T(8,128)(2,1)S(1)}, bf16[512,384]{1,0:T(8,128)(2,1)S(1)}, u32[]{:S(2)}, u32[]{:S(2)}) collective-permute-start(bf16[512,384]{1,0:T(8,128)(2,1)S(1)} %collective-permute-done.33.r_14_), channel_id=1, source_target_pairs={{2,0},{3,1},{4,2},{5,3},{10,8},{11,9},{12,10},{13,11},{18,16},{19,... | collective-permute-start | bytes 1179656 | tf_op jit(solution)/shard_map/gather_step_2/ppermute | solution.py:248
  100.3 21.9 %collective-permute-start.31 = (bf16[512,384]{1,0:T(8,128)(2,1)S(1)}, bf16[512,384]{1,0:T(8,128)(2,1)S(1)}, u32[]{:S(2)}, u32[]{:S(2)}) collective-permute-start(bf16[512,384]{1,0:T(8,128)(2,1)S(1)} %collective-permute-done.30.r_11_), channel_id=1, source_target_pairs={{2,4},{3,5},{4,6},{5,7},{10,12},{11,13},{12,14},{13,15},{18,20},{1... | collective-permute-start | bytes 1179656 | tf_op jit(solution)/shard_map/gather_step_2/ppermute | solution.py:248
  120.5 6.9 %collective-permute-start.36 = (bf16[512,384]{1,0:T(8,128)(2,1)S(1)}, bf16[512,384]{1,0:T(8,128)(2,1)S(1)}, u32[]{:S(2)}, u32[]{:S(2)}) collective-permute-start(bf16[512,384]{1,0:T(8,128)(2,1)S(1)} %broadcast_select_fusion.4), channel_id=1, source_target_pairs={{0,2},{1,3},{6,4},{7,5},{8,10},{9,11},{14,12},{15,13},{16,18},{17,... | collective-permute-start | bytes 1179656 | tf_op jit(solution)/shard_map/scatter_step_1/ppermute | solution.py:248
  122.2 11.1 %collective-permute-start.32 = (bf16[512,384]{1,0:T(8,128)(2,1)S(1)}, bf16[512,384]{1,0:T(8,128)(2,1)S(1)}, u32[]{:S(2)}, u32[]{:S(2)}) collective-permute-start(bf16[512,384]{1,0:T(8,128)(2,1)S(1)} %collective-permute-done.31.r_12_), channel_id=1, source_target_pairs={{4,6},{5,7},{12,14},{13,15},{20,22},{21,23},{28,30},{29,31}} | collective-permute-start | bytes 1179656 | tf_op jit(solution)/shard_map/gather_step_3/ppermute | solution.py:248
  122.9 10.4 %collective-permute-start.35 = (bf16[512,384]{1,0:T(8,128)(2,1)S(1)}, bf16[512,384]{1,0:T(8,128)(2,1)S(1)}, u32[]{:S(2)}, u32[]{:S(2)}) collective-permute-start(bf16[512,384]{1,0:T(8,128)(2,1)S(1)} %collective-permute-done.34.r_15_), channel_id=1, source_target_pairs={{2,0},{3,1},{10,8},{11,9},{18,16},{19,17},{26,24},{27,25}} | collective-permute-start | bytes 1179656 | tf_op jit(solution)/shard_map/gather_step_3/ppermute | solution.py:248
  127.5 18.7 %collective-permute-start.38 = (bf16[512,384]{1,0:T(8,128)(2,1)S(1)}, bf16[512,384]{1,0:T(8,128)(2,1)S(1)}, u32[]{:S(2)}, u32[]{:S(2)}) collective-permute-start(bf16[512,384]{1,0:T(8,128)(2,1)S(1)} %add_convert_fusion.8), channel_id=1, source_target_pairs={{4,2},{5,3},{6,4},{7,5},{12,10},{13,11},{14,12},{15,13},{20,18},{2... | collective-permute-start | bytes 1179656 | tf_op jit(solution)/shard_map/scatter_step_2/ppermute | solution.py:248
  128.2 18.0 %collective-permute-start.37 = (bf16[512,384]{1,0:T(8,128)(2,1)S(1)}, bf16[512,384]{1,0:T(8,128)(2,1)S(1)}, u32[]{:S(2)}, u32[]{:S(2)}) collective-permute-start(bf16[512,384]{1,0:T(8,128)(2,1)S(1)} %add_convert_fusion.8), channel_id=1, source_target_pairs={{0,2},{1,3},{2,4},{3,5},{8,10},{9,11},{10,12},{11,13},{16,18},{17,... | collective-permute-start | bytes 1179656 | tf_op jit(solution)/shard_map/scatter_step_2/ppermute | solution.py:248
  141.4 12.3 %collective-permute-start.39 = (bf16[512,384]{1,0:T(8,128)(2,1)S(1)}, bf16[512,384]{1,0:T(8,128)(2,1)S(1)}, u32[]{:S(2)}, u32[]{:S(2)}) collective-permute-start(bf16[512,384]{1,0:T(8,128)(2,1)S(1)} %broadcast_select_fusion.3), channel_id=1, source_target_pairs={{0,2},{1,3},{6,4},{7,5},{8,10},{9,11},{14,12},{15,13},{16,18},{17,... | collective-permute-start | bytes 1179656 | tf_op jit(solution)/shard_map/scatter_step_1/ppermute | solution.py:248
  153.7 14.6 %collective-permute-start.40 = (bf16[512,2048]{1,0:T(8,128)(2,1)}, bf16[512,2048]{1,0:T(8,128)(2,1)}, u32[]{:S(2)}, u32[]{:S(2)}) collective-permute-start(bf16[512,2048]{1,0:T(8,128)(2,1)} %get-tuple-element.87), channel_id=1, source_target_pairs={{0,1},{1,0},{2,3},{3,2},{4,5},{5,4},{6,7},{7,6},{8,9},{9,8},{10,11... | collective-permute-start | bytes 6291464 | tf_op jit(solution)/shard_map/back/ppermute | solution.py:245
  154.7 3.9 %collective-permute-start.47 = (bf16[512,384]{1,0:T(8,128)(2,1)}, bf16[512,384]{1,0:T(8,128)(2,1)}, u32[]{:S(2)}, u32[]{:S(2)}) collective-permute-start(bf16[512,384]{1,0:T(8,128)(2,1)} %add_convert_fusion.7), channel_id=1, source_target_pairs={{4,2},{5,3},{6,4},{7,5},{12,10},{13,11},{14,12},{15,13},{20,18},{2... | collective-permute-start | bytes 1179656 | tf_op jit(solution)/shard_map/scatter_step_2/ppermute | solution.py:248
  156.1 11.0 %collective-permute-start.45 = (bf16[512,384]{1,0:T(8,128)(2,1)}, bf16[512,384]{1,0:T(8,128)(2,1)}, u32[]{:S(2)}, u32[]{:S(2)}) collective-permute-start(bf16[512,384]{1,0:T(8,128)(2,1)} %add_convert_fusion.7), channel_id=1, source_target_pairs={{0,2},{1,3},{2,4},{3,5},{8,10},{9,11},{10,12},{11,13},{16,18},{17,... | collective-permute-start | bytes 1179656 | tf_op jit(solution)/shard_map/scatter_step_2/ppermute | solution.py:248
  168.4 10.9 %collective-permute-start.53 = (bf16[512,384]{1,0:T(8,128)(2,1)S(1)}, bf16[512,384]{1,0:T(8,128)(2,1)S(1)}, u32[]{:S(2)}, u32[]{:S(2)}) collective-permute-start(bf16[512,384]{1,0:T(8,128)(2,1)S(1)} %add_convert_fusion.2), channel_id=1, source_target_pairs={{4,2},{5,3},{6,4},{7,5},{12,10},{13,11},{14,12},{15,13},{20,18},{2... | collective-permute-start | bytes 1179656 | tf_op jit(solution)/shard_map/scatter_step_2/ppermute | solution.py:248
  171.9 13.6 %collective-permute-start.43 = (bf16[2,128,1024]{2,1,0:T(8,128)(2,1)S(1)}, bf16[2,128,1024]{2,1,0:T(8,128)(2,1)S(1)}, u32[]{:S(2)}, u32[]{:S(2)}) collective-permute-start(bf16[2,128,1024]{2,1,0:T(8,128)(2,1)S(1)} %pad_maximum_fusion), channel_id=1, source_target_pairs={{0,8},{8,0},{16,24},{24,16},{1,9},{9,1},{17,25},{25,17},{2,10},{10... | collective-permute-start | bytes 1572872 | tf_op jit(solution)/shard_map/back/ppermute | solution.py:253
  173.6 13.3 %collective-permute-start.41 = (bf16[2,128,1024]{2,1,0:T(8,128)(2,1)S(1)}, bf16[2,128,1024]{2,1,0:T(8,128)(2,1)S(1)}, u32[]{:S(2)}, u32[]{:S(2)}) collective-permute-start(bf16[2,128,1024]{2,1,0:T(8,128)(2,1)S(1)} %slice.141), channel_id=1, source_target_pairs={{0,16},{8,24},{16,0},{24,8},{1,17},{9,25},{17,1},{25,9},{2,18},{10... | collective-permute-start | bytes 1572872 | tf_op jit(solution)/shard_map/back/ppermute | solution.py:253
  174.3 14.1 %collective-permute-start.51 = (bf16[512,384]{1,0:T(8,128)(2,1)S(1)}, bf16[512,384]{1,0:T(8,128)(2,1)S(1)}, u32[]{:S(2)}, u32[]{:S(2)}) collective-permute-start(bf16[512,384]{1,0:T(8,128)(2,1)S(1)} %add_convert_fusion.2), channel_id=1, source_target_pairs={{0,2},{1,3},{2,4},{3,5},{8,10},{9,11},{10,12},{11,13},{16,18},{17,... | collective-permute-start | bytes 1179656 | tf_op jit(solution)/shard_map/scatter_step_2/ppermute | solution.py:248
  185.5 14.5 %collective-permute-start.44 = (bf16[128,1024]{1,0:T(8,128)(2,1)S(1)}, bf16[128,1024]{1,0:T(8,128)(2,1)S(1)}, u32[]{:S(2)}, u32[]{:S(2)}) collective-permute-start(bf16[128,1024]{1,0:T(8,128)(2,1)S(1)} %fusion.9), channel_id=1, source_target_pairs={{0,16},{8,24},{16,0},{24,8},{1,17},{9,25},{17,1},{25,9},{2,18},{10... | collective-permute-start | bytes 786440 | tf_op jit(solution)/shard_map/back/ppermute | solution.py:253
  187.1 21.1 %copy-start.16 = (bf16[512,384]{1,0:T(8,128)(2,1)S(1)}, bf16[512,384]{1,0:T(8,128)(2,1)}, u32[]{:S(2)}) copy-start(bf16[512,384]{1,0:T(8,128)(2,1)} %copy-done.15) | copy-start | bytes 1179652
  187.1 14.3 %collective-permute-start.42 = (bf16[128,1024]{1,0:T(8,128)(2,1)S(1)}, bf16[128,1024]{1,0:T(8,128)(2,1)S(1)}, u32[]{:S(2)}, u32[]{:S(2)}) collective-permute-start(bf16[128,1024]{1,0:T(8,128)(2,1)S(1)} %fusion.8), channel_id=1, source_target_pairs={{0,8},{8,0},{16,24},{24,16},{1,9},{9,1},{17,25},{25,17},{2,10},{10... | collective-permute-start | bytes 786440 | tf_op jit(solution)/shard_map/back/ppermute | solution.py:253
  188.5 18.5 %collective-permute-start.46 = (bf16[512,384]{1,0:T(8,128)(2,1)S(1)}, bf16[512,384]{1,0:T(8,128)(2,1)S(1)}, u32[]{:S(2)}, u32[]{:S(2)}) collective-permute-start(bf16[512,384]{1,0:T(8,128)(2,1)S(1)} %add_convert_fusion.6), channel_id=1, source_target_pairs={{0,2},{1,3},{2,4},{3,5},{4,6},{5,7},{8,10},{9,11},{10,12},{11,13},... | collective-permute-start | bytes 1179656 | tf_op jit(solution)/shard_map/scatter_step_3/ppermute | solution.py:248
  193.5 14.7 %collective-permute-start.48 = (bf16[512,384]{1,0:T(8,128)(2,1)S(1)}, bf16[512,384]{1,0:T(8,128)(2,1)S(1)}, u32[]{:S(2)}, u32[]{:S(2)}) collective-permute-start(bf16[512,384]{1,0:T(8,128)(2,1)S(1)} %add_convert_fusion.5), channel_id=1, source_target_pairs={{2,0},{3,1},{4,2},{5,3},{6,4},{7,5},{10,8},{11,9},{12,10},{13,11},... | collective-permute-start | bytes 1179656 | tf_op jit(solution)/shard_map/scatter_step_3/ppermute | solution.py:248
  194.8 16.7 %collective-permute-start.49 = (bf16[512,384]{1,0:T(8,128)(2,1)S(1)}, bf16[512,384]{1,0:T(8,128)(2,1)S(1)}, u32[]{:S(2)}, u32[]{:S(2)}) collective-permute-start(bf16[512,384]{1,0:T(8,128)(2,1)S(1)} %add_convert_fusion.4), channel_id=1, source_target_pairs={{0,2},{1,3},{2,4},{3,5},{4,6},{5,7},{8,10},{9,11},{10,12},{11,13},... | collective-permute-start | bytes 1179656 | tf_op jit(solution)/shard_map/scatter_step_3/ppermute | solution.py:248
  200.1 16.5 %collective-permute-start.50 = (bf16[512,384]{1,0:T(8,128)(2,1)S(1)}, bf16[512,384]{1,0:T(8,128)(2,1)S(1)}, u32[]{:S(2)}, u32[]{:S(2)}) collective-permute-start(bf16[512,384]{1,0:T(8,128)(2,1)S(1)} %add_convert_fusion.3), channel_id=1, source_target_pairs={{2,0},{3,1},{4,2},{5,3},{6,4},{7,5},{10,8},{11,9},{12,10},{13,11},... | collective-permute-start | bytes 1179656 | tf_op jit(solution)/shard_map/scatter_step_3/ppermute | solution.py:248
  201.5 15.9 %collective-permute-start.52 = (bf16[512,384]{1,0:T(8,128)(2,1)S(1)}, bf16[512,384]{1,0:T(8,128)(2,1)S(1)}, u32[]{:S(2)}, u32[]{:S(2)}) collective-permute-start(bf16[512,384]{1,0:T(8,128)(2,1)S(1)} %add_convert_fusion.1), channel_id=1, source_target_pairs={{0,2},{1,3},{2,4},{3,5},{4,6},{5,7},{8,10},{9,11},{10,12},{11,13},... | collective-permute-start | bytes 1179656 | tf_op jit(solution)/shard_map/scatter_step_3/ppermute | solution.py:248
  207.0 15.1 %collective-permute-start.54 = (bf16[512,384]{1,0:T(8,128)(2,1)S(1)}, bf16[512,384]{1,0:T(8,128)(2,1)S(1)}, u32[]{:S(2)}, u32[]{:S(2)}) collective-permute-start(bf16[512,384]{1,0:T(8,128)(2,1)S(1)} %add_convert_fusion), channel_id=1, source_target_pairs={{2,0},{3,1},{4,2},{5,3},{6,4},{7,5},{10,8},{11,9},{12,10},{13,11},... | collective-permute-start | bytes 1179656 | tf_op jit(solution)/shard_map/scatter_step_3/ppermute | solution.py:248
  208.4 13.7 %copy-start.20 = (bf16[512,384]{1,0:T(8,128)(2,1)S(1)}, bf16[512,384]{1,0:T(8,128)(2,1)}, u32[]{:S(2)}) copy-start(bf16[512,384]{1,0:T(8,128)(2,1)} %copy-done.19) | copy-start | bytes 1179652
  208.5 13.9 %collective-permute-start.55 = (f32[256,384]{1,0:T(8,128)S(1)}, f32[256,384]{1,0:T(8,128)S(1)}, u32[]{:S(2)}, u32[]{:S(2)}) collective-permute-start(f32[256,384]{1,0:T(8,128)S(1)} %constant_dynamic-slice_fusion.2), channel_id=1, source_target_pairs={{0,1},{1,0},{2,3},{3,2},{4,5},{5,4},{6,7},{7,6},{8,9},{9,8},{10,11... | collective-permute-start | bytes 1179656 | tf_op jit(solution)/shard_map/ppermute | solution.py:245
  216.7 5.7 %collective-permute-start.56 = (f32[256,384]{1,0:T(8,128)S(1)}, f32[256,384]{1,0:T(8,128)S(1)}, u32[]{:S(2)}, u32[]{:S(2)}) collective-permute-start(f32[256,384]{1,0:T(8,128)S(1)} %constant_dynamic-slice_fusion.1), channel_id=1, source_target_pairs={{0,1},{1,0},{2,3},{3,2},{4,5},{5,4},{6,7},{7,6},{8,9},{9,8},{10,11... | collective-permute-start | bytes 1179656 | tf_op jit(solution)/shard_map/ppermute | solution.py:245
  222.3 1.8 collective-permute-start.57
  (39 other events, 240.7 us)

commit v7 on v6

--- a/solution.py
+++ b/solution.py
@@ -294,16 +294,27 @@
         (at, *g),
     )
 
-    def gather(own, before):
-        ups, downs = [own], [own]
-        for s in range(1, line):
-            up, down = ups[-1], downs[-1]
-            if s == line - 1:
-                up, down = after(up, *before), after(down, *before)
-            with jax.named_scope(f"gather_step_{s}"):
-                ups.append(along(up, [(i, i + 1) for i in range(s - 1, line - 1)]))
-                downs.append(along(down, [(i, i - 1) for i in range(1, line - s + 1)]))
-        return (own, *ups[1:], *downs[1:])
+    ups = [[a] for a in shards]
+    downs = [[a] for a in shards]
+
+    def forward(i, s, waits):
+        up, down = after(ups[i][-1], *waits), after(downs[i][-1], *waits)
+        with jax.named_scope(f"gather_step_{s}"):
+            ups[i].append(along(up, [(j, j + 1) for j in range(s - 1, line - 1)]))
+            downs[i].append(along(down, [(j, j - 1) for j in range(1, line - s + 1)]))
+        return ups[i][-1], downs[i][-1]
+
+    landed = ()
+    for s in range(1, line - 1):
+        landed = ()
+        for i in range(chunks):
+            hops = forward(i, s, ())
+            if s == 1 or i == chunks - 1:
+                landed += hops
+        if s == 1:
+            firsts = landed
+    last = landed
+    landed = forward(0, line - 1, firsts)
 
     def begin(parts):
         with jax.named_scope("scatter_step_1"):
@@ -326,11 +337,13 @@
             down = along(b, [(i, i - 1) for i in range(line - s, line)])
         return up, down
 
-    merged, both, parts, states, tie, before = [], [], [], [], (), (t[experts - 1], g[experts - 1])
+    merged, both, parts, states, starts, tie = [], [], [], [], [], ()
     for i in range(chunks):
-        loaded = gather(shards[i], before)
-        if i == 0:
-            before = (loaded[line - 1], loaded[2 * line - 2])
+        if i == 1:
+            landed = forward(i, line - 1, landed + last)
+        elif i > 1:
+            landed = forward(i, line - 1, landed + (merged[0],))
+        loaded = (shards[i], *ups[i][1:], *downs[i][1:])
         got = call(
             lambda *r: chunk_kernel(line, len(t), *r),
             [SMEM] + [ANY] * (len(t) + 2 * line),
@@ -352,15 +365,14 @@
         both.append(got[line + 1])
         parts.append(got[:line])
         states.append(begin(got[:line]))
+        starts.append(states[-1])
         if i == 0:
-            before += (merged[0],)
             tie = states[0]
         else:
-            tie = states[i - 1]
-            states[i - 1] = hop(parts[i - 1], tie, 2, ())
+            states[i - 1] = hop(parts[i - 1], states[i - 1], 2, ())
 
     block = experts * rows
-    merged[-1] = after(merged[-1], *states[-2])
+    merged[-1] = after(merged[-1], *states[0], *starts[-2])
     keep, give = call(
         lambda *r: route_kernel(chunks, *r),
         [VMEM] * (2 * chunks),
@@ -383,9 +395,9 @@
         grad_input = jnp.concatenate((left, right), axis=1).astype(BF16)
     states[-1] = hop(parts[-1], states[-1], 2, (other,))
     sums = []
-    for own, (up, down) in zip(parts, states):
+    for i, (own, (up, down)) in enumerate(zip(parts, states)):
         for s in range(3, line):
-            up, down = hop(own, (up, down), s, (odd, far))
+            up, down = hop(own, (up, down), s, (odd, far) if i == chunks - 1 else (other,))
         sums.append(own[0].astype(F32) + up.astype(F32) + down.astype(F32))
 
     own = [lax.dynamic_slice_in_dim(s, c * feats, feats, 0) for s in sums]

time: 228 us -> 235 us (1.031)
  waiting for transfers between devices: 65.3 us -> 83.3 us
  starting transfers between devices: 102 us -> 86.2 us
  local copies, waits for them, and re-layouts: 13.7 us -> 17.7 us
    ppermute x33, waiting for transfers between devices: 44.8 us -> 68.4 us  [along(): lax.ppermute(a, 'wide', [(2 * s + i, 2 * t + i) for s, t in hops for i in...]
    ppermute x33, starting transfers between devices: 88.8 us -> 74.5 us  [along(): lax.ppermute(a, 'wide', [(2 * s + i, 2 * t + i) for s, t in hops for i in...]
    ppermute x10, waiting for transfers between devices: 17.7 us -> 12.7 us  [flip(): return lax.ppermute(a, 'expert', [(e, e ^ bit) for e in range(experts)])]
    unnamed x97 -> x119, local copies, waits for them, and re-layouts: 11.7 us -> 16.5 us
  transfers between devices with their start and end apart: 58 -> 58, of which waited for: 18 -> 22; matrix products, arithmetic and copies ran while one was open for 5% -> 4% of each run, Pallas kernels for 15% -> 15%
where the time goes in v7:
time: 235 us; the launch traced here: 234 us
  starting transfers between devices  86.2 us (37%)
  waiting for transfers between devices  83.3 us (35%)
  Pallas kernels  34.5 us (15%)
  local copies, waits for them, and re-layouts  17.7 us (8%)
  other arithmetic  10.2 us (4%)
    ppermute x33, starting transfers between devices, along(): lax.ppermute(a, 'wide', [(2 * s + i, 2 * t + i) for s, t in hops for i in...  74.5 us
    ppermute x33, waiting for transfers between devices, along(): lax.ppermute(a, 'wide', [(2 * s + i, 2 * t + i) for s, t in hops for i in...  68.4 us
    pallas_call x7, Pallas kernels, call(): pl.pallas_call(body, out_shape=outs, in_specs=ins, out_specs=[VMEM] * len...  34.5 us
    unnamed x119, local copies, waits for them, and re-layouts  16.5 us
    ppermute x10, waiting for transfers between devices, flip(): return lax.ppermute(a, 'expert', [(e, e ^ bit) for e in range(experts)])  12.7 us
    ppermute x10, starting transfers between devices, flip(): return lax.ppermute(a, 'expert', [(e, e ^ bit) for e in range(experts)])  9.34 us
  transfers between devices with their start and end apart: 58, of which 22 were waited for; matrix products, arithmetic and copies ran while one was open for 4% of the time, Pallas kernels for 15%

profile of v7, /device:TPU:0, one launch (start us, length us, event | category | flops | bytes accessed | tf_op | source)
XLA Modules:
  0.0 233.9 jit_solution(11521944402256039412)
XLA Ops:
  0.6 3.0 %collective-permute-start = (bf16[128,2048]{1,0:T(8,128)(2,1)}, bf16[128,2048]{1,0:T(8,128)(2,1)}, u32[]{:S(2)}, u32[]{:S(2)}) collective-permute-start(bf16[128,2048]{1,0:T(8,128)(2,1)} %r_1_.5), channel_id=1, source_target_pairs={{0,8},{8,0},{16,24},{24,16},{1,9},{9,1},{17,25},{25,17},{2,10},{10... | collective-permute-start | bytes 1572872 | tf_op jit(solution)/shard_map/rows/ppermute | solution.py:253
  3.6 1.5 collective-permute-start.4
  5.2 1.0 copy-done.7
  6.2 1.0 copy-done.8
  7.2 1.0 copy-done.9
  11.7 3.5 %collective-permute-start.17 = (bf16[512,384]{1,0:T(8,128)(2,1)S(1)}, bf16[512,384]{1,0:T(8,128)(2,1)S(1)}, u32[]{:S(2)}, u32[]{:S(2)}) collective-permute-start(bf16[512,384]{1,0:T(8,128)(2,1)S(1)} %get-tuple-element.58.r_10_), channel_id=1, source_target_pairs={{0,2},{1,3},{2,4},{3,5},{4,6},{5,7},{8,10},{9,11},{10,12},{11,13},... | collective-permute-start | bytes 1179656 | tf_op jit(solution)/shard_map/gather_step_1/ppermute | solution.py:248
  15.3 1.3 collective-permute-start.19
  17.3 4.6 %collective-permute-start.20 = (bf16[512,384]{1,0:T(8,128)(2,1)S(1)}, bf16[512,384]{1,0:T(8,128)(2,1)S(1)}, u32[]{:S(2)}, u32[]{:S(2)}) collective-permute-start(bf16[512,384]{1,0:T(8,128)(2,1)S(1)} %get-tuple-element.59.r_10_), channel_id=1, source_target_pairs={{0,2},{1,3},{2,4},{3,5},{4,6},{5,7},{8,10},{9,11},{10,12},{11,13},... | collective-permute-start | bytes 1179656 | tf_op jit(solution)/shard_map/gather_step_1/ppermute | solution.py:248
  21.9 1.3 collective-permute-start.21
  24.1 4.6 %collective-permute-start.22 = (bf16[512,384]{1,0:T(8,128)(2,1)S(1)}, bf16[512,384]{1,0:T(8,128)(2,1)S(1)}, u32[]{:S(2)}, u32[]{:S(2)}) collective-permute-start(bf16[512,384]{1,0:T(8,128)(2,1)S(1)} %get-tuple-element.60.r_10_), channel_id=1, source_target_pairs={{0,2},{1,3},{2,4},{3,5},{4,6},{5,7},{8,10},{9,11},{10,12},{11,13},... | collective-permute-start | bytes 1179656 | tf_op jit(solution)/shard_map/gather_step_1/ppermute | solution.py:248
  28.7 1.3 collective-permute-start.23
  31.4 1.6 collective-permute-done.20.r_11_
  33.6 4.1 %collective-permute-done.21.r_14_ = bf16[512,384]{1,0:T(8,128)(2,1)} collective-permute-done((bf16[512,384]{1,0:T(8,128)(2,1)S(1)}, bf16[512,384]{1,0:T(8,128)(2,1)}, u32[]{:S(2)}, u32[]{:S(2)}) %collective-permute-start.21) | collective-permute-done | bytes 393248 | tf_op jit(solution)/shard_map/gather_step_1/ppermute | solution.py:248
  37.7 3.1 %collective-permute-done.22.r_11_ = bf16[512,384]{1,0:T(8,128)(2,1)S(1)} collective-permute-done((bf16[512,384]{1,0:T(8,128)(2,1)S(1)}, bf16[512,384]{1,0:T(8,128)(2,1)S(1)}, u32[]{:S(2)}, u32[]{:S(2)}) %collective-permute-start.22) | collective-permute-done | bytes 393248 | tf_op jit(solution)/shard_map/gather_step_1/ppermute | solution.py:248
  42.2 2.7 %collective-permute-done.23.r_14_ = bf16[512,384]{1,0:T(8,128)(2,1)S(1)} collective-permute-done((bf16[512,384]{1,0:T(8,128)(2,1)S(1)}, bf16[512,384]{1,0:T(8,128)(2,1)S(1)}, u32[]{:S(2)}, u32[]{:S(2)}) %collective-permute-start.23) | collective-permute-done | bytes 393248 | tf_op jit(solution)/shard_map/gather_step_1/ppermute | solution.py:248
  45.0 1.3 collective-permute-start.25
  46.3 1.4 collective-permute-start.28
  47.7 0.8 copy-done.28
  49.9 1.3 collective-permute-start.30
  52.5 5.6 %collective-permute-done.25.r_15_ = bf16[512,384]{1,0:T(8,128)(2,1)S(1)} collective-permute-done((bf16[512,384]{1,0:T(8,128)(2,1)}, bf16[512,384]{1,0:T(8,128)(2,1)S(1)}, u32[]{:S(2)}, u32[]{:S(2)}) %collective-permute-start.25) | collective-permute-done | bytes 393248 | tf_op jit(solution)/shard_map/gather_step_2/ppermute | solution.py:248
  58.1 1.3 collective-permute-start.32
  60.7 8.4 %collective-permute-done.30.r_15_ = bf16[512,384]{1,0:T(8,128)(2,1)} collective-permute-done((bf16[512,384]{1,0:T(8,128)(2,1)S(1)}, bf16[512,384]{1,0:T(8,128)(2,1)}, u32[]{:S(2)}, u32[]{:S(2)}) %collective-permute-start.30) | collective-permute-done | bytes 393248 | tf_op jit(solution)/shard_map/gather_step_2/ppermute | solution.py:248
  69.1 6.1 %collective-permute-done.32.r_15_ = bf16[512,384]{1,0:T(8,128)(2,1)S(1)} collective-permute-done((bf16[512,384]{1,0:T(8,128)(2,1)}, bf16[512,384]{1,0:T(8,128)(2,1)S(1)}, u32[]{:S(2)}, u32[]{:S(2)}) %collective-permute-start.32) | collective-permute-done | bytes 393248 | tf_op jit(solution)/shard_map/gather_step_2/ppermute | solution.py:248
  76.7 1.3 collective-permute-start.26
  79.2 0.8 copy-done.5
  81.3 6.2 %collective-permute-done.26.r_16_ = bf16[512,384]{1,0:T(8,128)(2,1)S(1)} collective-permute-done((bf16[512,384]{1,0:T(8,128)(2,1)S(1)}, bf16[512,384]{1,0:T(8,128)(2,1)S(1)}, u32[]{:S(2)}, u32[]{:S(2)}) %collective-permute-start.26) | collective-permute-done | bytes 393248 | tf_op jit(solution)/shard_map/gather_step_3/ppermute | solution.py:248
  88.9 1.0 copy-done.6
  90.0 2.0 shard_map.104.r_9_
  92.1 1.4 collective-permute-start.33
  93.6 7.9 %shard_map.105 = (bf16[512,384]{1,0:T(8,128)(2,1)S(1)}, bf16[512,384]{1,0:T(8,128)(2,1)S(1)}, bf16[512,384]{1,0:T(8,128)(2,1)S(1)}, bf16[512,384]{1,0:T(8,128)(2...) custom-call(s32[3]{0:T(128)S(1)} %pad_add_fusion.r_0_, bf16[128,2048]{1,0:T(8,128)(2,1)S(1)} %copy-done.19, ...), custom_call_target="tpu_custom_call" | custom-call | flops 3221225472 | bytes 14286860 | tf_op jit(solution)/shard_map/pallas_call | solution.py:100
  102.3 4.7 %collective-permute-start.27 = (bf16[512,384]{1,0:T(8,128)(2,1)S(1)}, bf16[512,384]{1,0:T(8,128)(2,1)S(1)}, u32[]{:S(2)}, u32[]{:S(2)}) collective-permute-start(bf16[512,384]{1,0:T(8,128)(2,1)S(1)} %broadcast_select_fusion.5), channel_id=1, source_target_pairs={{0,2},{1,3},{6,4},{7,5},{8,10},{9,11},{14,12},{15,13},{16,18},{17,... | collective-permute-start | bytes 1179656 | tf_op jit(solution)/shard_map/scatter_step_1/ppermute | solution.py:248
  107.7 1.3 collective-permute-start.35
  109.0 6.7 %collective-permute-done.27 = bf16[512,384]{1,0:T(8,128)(2,1)S(1)} collective-permute-done((bf16[512,384]{1,0:T(8,128)(2,1)S(1)}, bf16[512,384]{1,0:T(8,128)(2,1)S(1)}, u32[]{:S(2)}, u32[]{:S(2)}) %collective-permute-start.27) | collective-permute-done | bytes 393248 | tf_op jit(solution)/shard_map/scatter_step_1/ppermute | solution.py:248
  115.8 4.5 %collective-permute-start.36 = (bf16[512,384]{1,0:T(8,128)(2,1)S(1)}, bf16[512,384]{1,0:T(8,128)(2,1)S(1)}, u32[]{:S(2)}, u32[]{:S(2)}) collective-permute-start(bf16[512,384]{1,0:T(8,128)(2,1)S(1)} %add_convert_fusion.8), channel_id=1, source_target_pairs={{0,2},{1,3},{2,4},{3,5},{8,10},{9,11},{10,12},{11,13},{16,18},{17,... | collective-permute-start | bytes 1179656 | tf_op jit(solution)/shard_map/scatter_step_2/ppermute | solution.py:248
  121.1 8.1 %shard_map.106 = (bf16[512,384]{1,0:T(8,128)(2,1)S(1)}, bf16[512,384]{1,0:T(8,128)(2,1)S(1)}, bf16[512,384]{1,0:T(8,128)(2,1)S(1)}, bf16[512,384]{1,0:T(8,128)(2...) custom-call(s32[3]{0:T(128)S(1)} %pad_add_fusion.r_0_, bf16[128,2048]{1,0:T(8,128)(2,1)S(1)} %copy-done.19, ...), custom_call_target="tpu_custom_call" | custom-call | flops 3221225472 | bytes 14286860 | tf_op jit(solution)/shard_map/pallas_call | solution.py:100
  130.0 3.5 %collective-permute-start.38 = (bf16[512,384]{1,0:T(8,128)(2,1)S(1)}, bf16[512,384]{1,0:T(8,128)(2,1)S(1)}, u32[]{:S(2)}, u32[]{:S(2)}) collective-permute-start(bf16[512,384]{1,0:T(8,128)(2,1)S(1)} %broadcast_select_fusion.4), channel_id=1, source_target_pairs={{0,2},{1,3},{6,4},{7,5},{8,10},{9,11},{14,12},{15,13},{16,18},{17,... | collective-permute-start | bytes 1179656 | tf_op jit(solution)/shard_map/scatter_step_1/ppermute | solution.py:248
  133.6 7.8 %shard_map.107 = (bf16[512,384]{1,0:T(8,128)(2,1)S(1)}, bf16[512,384]{1,0:T(8,128)(2,1)S(1)}, bf16[512,384]{1,0:T(8,128)(2,1)S(1)}, bf16[512,384]{1,0:T(8,128)(2...) custom-call(s32[3]{0:T(128)S(1)} %pad_add_fusion.r_0_, bf16[128,2048]{1,0:T(8,128)(2,1)S(1)} %copy-done.19, ...), custom_call_target="tpu_custom_call" | custom-call | flops 3221225472 | bytes 14286860 | tf_op jit(solution)/shard_map/pallas_call | solution.py:100
  141.5 1.6 collective-permute-start.39
  143.2 7.4 %shard_map.108 = (bf16[512,2048]{1,0:T(8,128)(2,1)S(1)}, bf16[512,2048]{1,0:T(8,128)(2,1)}) custom-call(bf16[1024,256]{1,0:T(8,128)(2,1)S(1)} %get-tuple-element.66.r_0_, bf16[1024,256]{1,0:T(8,128)(2,1)S(1)} %get-tuple-element.72.r_1_, bf16[1024,256]{1,0:T(8,128)(2,1)S(1)} %get-tuple-element.79.r_2_, bf16[2048,256]{1,0:T(8,128)(2,1)S(1)} %get-tuple-element.80.r_3_, ...), custom_call_target="tpu_custom_call" | custom-call | flops 3221225472 | bytes 8912896 | tf_op jit(solution)/shard_map/pallas_call | solution.py:100
  151.4 1.3 add_convert_fusion.5
  152.7 0.8 collective-permute-start.49
  153.5 4.4 %collective-permute-start.47 = (bf16[512,384]{1,0:T(8,128)(2,1)S(1)}, bf16[512,384]{1,0:T(8,128)(2,1)S(1)}, u32[]{:S(2)}, u32[]{:S(2)}) collective-permute-start(bf16[512,384]{1,0:T(8,128)(2,1)S(1)} %add_convert_fusion.5), channel_id=1, source_target_pairs={{0,2},{1,3},{2,4},{3,5},{8,10},{9,11},{10,12},{11,13},{16,18},{17,... | collective-permute-start | bytes 1179656 | tf_op jit(solution)/shard_map/scatter_step_2/ppermute | solution.py:248
  157.9 1.2 add_convert_fusion.6
  159.5 7.4 %collective-permute-done.47 = bf16[512,384]{1,0:T(8,128)(2,1)S(1)} collective-permute-done((bf16[512,384]{1,0:T(8,128)(2,1)S(1)}, bf16[512,384]{1,0:T(8,128)(2,1)S(1)}, u32[]{:S(2)}, u32[]{:S(2)}) %collective-permute-start.47) | collective-permute-done | bytes 393248 | tf_op jit(solution)/shard_map/scatter_step_2/ppermute | solution.py:248
  167.7 5.5 %collective-permute-start.51 = (bf16[512,384]{1,0:T(8,128)(2,1)S(1)}, bf16[512,384]{1,0:T(8,128)(2,1)S(1)}, u32[]{:S(2)}, u32[]{:S(2)}) collective-permute-start(bf16[512,384]{1,0:T(8,128)(2,1)S(1)} %add_convert_fusion.2), channel_id=1, source_target_pairs={{0,2},{1,3},{2,4},{3,5},{8,10},{9,11},{10,12},{11,13},{16,18},{17,... | collective-permute-start | bytes 1179656 | tf_op jit(solution)/shard_map/scatter_step_2/ppermute | solution.py:248
  173.2 1.3 collective-permute-start.46
  174.5 5.6 %collective-permute-start.45 = (bf16[512,384]{1,0:T(8,128)(2,1)S(1)}, bf16[512,384]{1,0:T(8,128)(2,1)S(1)}, u32[]{:S(2)}, u32[]{:S(2)}) collective-permute-start(bf16[512,384]{1,0:T(8,128)(2,1)S(1)} %add_convert_fusion.7), channel_id=1, source_target_pairs={{0,2},{1,3},{2,4},{3,5},{4,6},{5,7},{8,10},{9,11},{10,12},{11,13},... | collective-permute-start | bytes 1179656 | tf_op jit(solution)/shard_map/scatter_step_3/ppermute | solution.py:248
  180.2 2.3 %convert_add_fusion = f32[512,2048]{1,0:T(8,128)S(1)} fusion(bf16[512,2048]{1,0:T(8,128)(2,1)} %collective-permute-done.40, bf16[512,2048]{1,0:T(8,128)(2,1)S(1)} %get-tuple-element.83), kind=kLoop, calls=%fused_computation | loop fusion | flops 3145728 | bytes 8388608 | tf_op jit(solution)/shard_map/back/add | solution.py:385
  183.6 3.3 %collective-permute-done.46 = bf16[512,384]{1,0:T(8,128)(2,1)S(1)} collective-permute-done((bf16[512,384]{1,0:T(8,128)(2,1)S(1)}, bf16[512,384]{1,0:T(8,128)(2,1)S(1)}, u32[]{:S(2)}, u32[]{:S(2)}) %collective-permute-start.46) | collective-permute-done | bytes 393248 | tf_op jit(solution)/shard_map/scatter_step_3/ppermute | solution.py:248
  186.9 1.3 collective-permute-start.50
  188.2 1.6 collective-permute-done.45
  189.8 5.8 %collective-permute-start.48 = (bf16[512,384]{1,0:T(8,128)(2,1)S(1)}, bf16[512,384]{1,0:T(8,128)(2,1)S(1)}, u32[]{:S(2)}, u32[]{:S(2)}) collective-permute-start(bf16[512,384]{1,0:T(8,128)(2,1)S(1)} %add_convert_fusion.4), channel_id=1, source_target_pairs={{0,2},{1,3},{2,4},{3,5},{4,6},{5,7},{8,10},{9,11},{10,12},{11,13},... | collective-permute-start | bytes 1179656 | tf_op jit(solution)/shard_map/scatter_step_3/ppermute | solution.py:248
  195.8 6.3 %collective-permute-done.50 = bf16[512,384]{1,0:T(8,128)(2,1)S(1)} collective-permute-done((bf16[512,384]{1,0:T(8,128)(2,1)S(1)}, bf16[512,384]{1,0:T(8,128)(2,1)S(1)}, u32[]{:S(2)}, u32[]{:S(2)}) %collective-permute-start.50) | collective-permute-done | bytes 393248 | tf_op jit(solution)/shard_map/scatter_step_3/ppermute | solution.py:248
  204.2 0.9 collective-permute-start.44
  205.1 11.8 %collective-permute-done.41 = bf16[2,128,1024]{2,1,0:T(8,128)(2,1)S(1)} collective-permute-done((bf16[2,128,1024]{2,1,0:T(8,128)(2,1)S(1)}, bf16[2,128,1024]{2,1,0:T(8,128)(2,1)S(1)}, u32[]{:S(2)}, u32[]{:S(2)}) %collective-permute-start.41) | collective-permute-done | bytes 524320 | tf_op jit(solution)/shard_map/back/ppermute | solution.py:253
  217.9 1.3 collective-permute-start.54
  219.2 0.8 collective-permute-done.44
  220.0 3.7 %collective-permute-start.52 = (bf16[512,384]{1,0:T(8,128)(2,1)S(1)}, bf16[512,384]{1,0:T(8,128)(2,1)S(1)}, u32[]{:S(2)}, u32[]{:S(2)}) collective-permute-start(bf16[512,384]{1,0:T(8,128)(2,1)S(1)} %add_convert_fusion.1), channel_id=1, source_target_pairs={{0,2},{1,3},{2,4},{3,5},{4,6},{5,7},{8,10},{9,11},{10,12},{11,13},... | collective-permute-start | bytes 1179656 | tf_op jit(solution)/shard_map/scatter_step_3/ppermute | solution.py:248
  224.0 0.8 pad_maximum_fusion.1
  224.8 2.8 %collective-permute-done.54 = bf16[512,384]{1,0:T(8,128)(2,1)S(1)} collective-permute-done((bf16[512,384]{1,0:T(8,128)(2,1)S(1)}, bf16[512,384]{1,0:T(8,128)(2,1)S(1)}, u32[]{:S(2)}, u32[]{:S(2)}) %collective-permute-start.54) | collective-permute-done | bytes 393248 | tf_op jit(solution)/shard_map/scatter_step_3/ppermute | solution.py:248
  227.6 1.7 collective-permute-done.52
  229.6 1.6 collective-permute-done.57
  231.6 1.0 broadcast_select_fusion.2
  232.6 1.3 broadcast_select_fusion
  (218 shorter events, 28.1 us)
Async XLA Ops:
  0.6 21.2 %collective-permute-start = (bf16[128,2048]{1,0:T(8,128)(2,1)}, bf16[128,2048]{1,0:T(8,128)(2,1)}, u32[]{:S(2)}, u32[]{:S(2)}) collective-permute-start(bf16[128,2048]{1,0:T(8,128)(2,1)} %r_1_.5), channel_id=1, source_target_pairs={{0,8},{8,0},{16,24},{24,16},{1,9},{9,1},{17,25},{25,17},{2,10},{10... | collective-permute-start | bytes 1572872 | tf_op jit(solution)/shard_map/rows/ppermute | solution.py:253
  3.6 20.5 %collective-permute-start.4 = (bf16[128,2048]{1,0:T(8,128)(2,1)}, bf16[128,2048]{1,0:T(8,128)(2,1)S(1)}, u32[]{:S(2)}, u32[]{:S(2)}) collective-permute-start(bf16[128,2048]{1,0:T(8,128)(2,1)} %r_1_.5), channel_id=1, source_target_pairs={{0,16},{8,24},{16,0},{24,8},{1,17},{9,25},{17,1},{25,9},{2,18},{10... | collective-permute-start | bytes 1572872 | tf_op jit(solution)/shard_map/rows/ppermute | solution.py:253
  8.2 22.5 %copy-start.48 = (bf16[128,2048]{1,0:T(8,128)(2,1)S(1)}, bf16[128,2048]{1,0:T(8,128)(2,1)}, u32[]{:S(2)}) copy-start(bf16[128,2048]{1,0:T(8,128)(2,1)} %param.8) | copy-start | bytes 1572868
  9.0 1.5 collective-permute-start.1
  9.1 1.7 collective-permute-start.2
  9.6 1.5 collective-permute-start.3
  11.7 17.0 %collective-permute-start.17 = (bf16[512,384]{1,0:T(8,128)(2,1)S(1)}, bf16[512,384]{1,0:T(8,128)(2,1)S(1)}, u32[]{:S(2)}, u32[]{:S(2)}) collective-permute-start(bf16[512,384]{1,0:T(8,128)(2,1)S(1)} %get-tuple-element.58.r_10_), channel_id=1, source_target_pairs={{0,2},{1,3},{2,4},{3,5},{4,6},{5,7},{8,10},{9,11},{10,12},{11,13},... | collective-permute-start | bytes 1179656 | tf_op jit(solution)/shard_map/gather_step_1/ppermute | solution.py:248
  15.3 15.6 %collective-permute-start.19 = (bf16[512,384]{1,0:T(8,128)(2,1)S(1)}, bf16[512,384]{1,0:T(8,128)(2,1)}, u32[]{:S(2)}, u32[]{:S(2)}) collective-permute-start(bf16[512,384]{1,0:T(8,128)(2,1)S(1)} %get-tuple-element.58.r_10_), channel_id=1, source_target_pairs={{2,0},{3,1},{4,2},{5,3},{6,4},{7,5},{10,8},{11,9},{12,10},{13,11},... | collective-permute-start | bytes 1179656 | tf_op jit(solution)/shard_map/gather_step_1/ppermute | solution.py:248
  17.3 15.8 %collective-permute-start.20 = (bf16[512,384]{1,0:T(8,128)(2,1)S(1)}, bf16[512,384]{1,0:T(8,128)(2,1)S(1)}, u32[]{:S(2)}, u32[]{:S(2)}) collective-permute-start(bf16[512,384]{1,0:T(8,128)(2,1)S(1)} %get-tuple-element.59.r_10_), channel_id=1, source_target_pairs={{0,2},{1,3},{2,4},{3,5},{4,6},{5,7},{8,10},{9,11},{10,12},{11,13},... | collective-permute-start | bytes 1179656 | tf_op jit(solution)/shard_map/gather_step_1/ppermute | solution.py:248
  21.9 15.8 %collective-permute-start.21 = (bf16[512,384]{1,0:T(8,128)(2,1)S(1)}, bf16[512,384]{1,0:T(8,128)(2,1)}, u32[]{:S(2)}, u32[]{:S(2)}) collective-permute-start(bf16[512,384]{1,0:T(8,128)(2,1)S(1)} %get-tuple-element.59.r_10_), channel_id=1, source_target_pairs={{2,0},{3,1},{4,2},{5,3},{6,4},{7,5},{10,8},{11,9},{12,10},{13,11},... | collective-permute-start | bytes 1179656 | tf_op jit(solution)/shard_map/gather_step_1/ppermute | solution.py:248
  24.1 16.7 %collective-permute-start.22 = (bf16[512,384]{1,0:T(8,128)(2,1)S(1)}, bf16[512,384]{1,0:T(8,128)(2,1)S(1)}, u32[]{:S(2)}, u32[]{:S(2)}) collective-permute-start(bf16[512,384]{1,0:T(8,128)(2,1)S(1)} %get-tuple-element.60.r_10_), channel_id=1, source_target_pairs={{0,2},{1,3},{2,4},{3,5},{4,6},{5,7},{8,10},{9,11},{10,12},{11,13},... | collective-permute-start | bytes 1179656 | tf_op jit(solution)/shard_map/gather_step_1/ppermute | solution.py:248
  28.7 16.3 %collective-permute-start.23 = (bf16[512,384]{1,0:T(8,128)(2,1)S(1)}, bf16[512,384]{1,0:T(8,128)(2,1)S(1)}, u32[]{:S(2)}, u32[]{:S(2)}) collective-permute-start(bf16[512,384]{1,0:T(8,128)(2,1)S(1)} %get-tuple-element.60.r_10_), channel_id=1, source_target_pairs={{2,0},{3,1},{4,2},{5,3},{6,4},{7,5},{10,8},{11,9},{12,10},{13,11},... | collective-permute-start | bytes 1179656 | tf_op jit(solution)/shard_map/gather_step_1/ppermute | solution.py:248
  30.8 15.4 %collective-permute-start.10 = (bf16[128,2176]{1,0:T(8,128)(2,1)S(1)}, bf16[128,2176]{1,0:T(8,128)(2,1)S(1)}, u32[]{:S(2)}, u32[]{:S(2)}) collective-permute-start(bf16[128,2176]{1,0:T(8,128)(2,1)S(1)} %fusion.1.r_1_), channel_id=1, source_target_pairs={{0,8},{8,0},{16,24},{24,16},{1,9},{9,1},{17,25},{25,17},{2,10},{10... | collective-permute-start | bytes 1671176 | tf_op jit(solution)/shard_map/rows/ppermute | solution.py:253
  33.1 15.4 %collective-permute-start.11 = (bf16[128,2176]{1,0:T(8,128)(2,1)S(1)}, bf16[128,2176]{1,0:T(8,128)(2,1)S(1)}, u32[]{:S(2)}, u32[]{:S(2)}) collective-permute-start(bf16[128,2176]{1,0:T(8,128)(2,1)S(1)} %fusion.1.r_1_), channel_id=1, source_target_pairs={{0,16},{8,24},{16,0},{24,8},{1,17},{9,25},{17,1},{25,9},{2,18},{10... | collective-permute-start | bytes 1671176 | tf_op jit(solution)/shard_map/rows/ppermute | solution.py:253
  37.7 12.3 %collective-permute-start.13 = (bf16[128,2176]{1,0:T(8,128)(2,1)S(1)}, bf16[128,2176]{1,0:T(8,128)(2,1)S(1)}, u32[]{:S(2)}, u32[]{:S(2)}) collective-permute-start(bf16[128,2176]{1,0:T(8,128)(2,1)S(1)} %fusion.1.r_1_), channel_id=1, source_target_pairs={{0,1},{1,0},{2,3},{3,2},{4,5},{5,4},{6,7},{7,6},{8,9},{9,8},{10,11... | collective-permute-start | bytes 1671176 | tf_op jit(solution)/shard_map/rows/ppermute | solution.py:245
  40.8 11.2 %collective-permute-start.18 = (bf16[512,384]{1,0:T(8,128)(2,1)S(1)}, bf16[512,384]{1,0:T(8,128)(2,1)S(1)}, u32[]{:S(2)}, u32[]{:S(2)}) collective-permute-start(bf16[512,384]{1,0:T(8,128)(2,1)S(1)} %collective-permute-done.17.r_11_), channel_id=1, source_target_pairs={{2,4},{3,5},{4,6},{5,7},{10,12},{11,13},{12,14},{13,15},{18,20},{1... | collective-permute-start | bytes 1179656 | tf_op jit(solution)/shard_map/gather_step_2/ppermute | solution.py:248
  45.0 13.1 %collective-permute-start.25 = (bf16[512,384]{1,0:T(8,128)(2,1)}, bf16[512,384]{1,0:T(8,128)(2,1)S(1)}, u32[]{:S(2)}, u32[]{:S(2)}) collective-permute-start(bf16[512,384]{1,0:T(8,128)(2,1)} %collective-permute-done.19.r_14_), channel_id=1, source_target_pairs={{2,0},{3,1},{4,2},{5,3},{10,8},{11,9},{12,10},{13,11},{18,16},{19,... | collective-permute-start | bytes 1179656 | tf_op jit(solution)/shard_map/gather_step_2/ppermute | solution.py:248
  46.3 13.1 %collective-permute-start.28 = (bf16[512,384]{1,0:T(8,128)(2,1)S(1)}, bf16[512,384]{1,0:T(8,128)(2,1)}, u32[]{:S(2)}, u32[]{:S(2)}) collective-permute-start(bf16[512,384]{1,0:T(8,128)(2,1)S(1)} %collective-permute-done.20.r_11_), channel_id=1, source_target_pairs={{2,4},{3,5},{4,6},{5,7},{10,12},{11,13},{12,14},{13,15},{18,20},{1... | collective-permute-start | bytes 1179656 | tf_op jit(solution)/shard_map/gather_step_2/ppermute | solution.py:248
  48.5 11.5 %collective-permute-start.29 = (bf16[512,384]{1,0:T(8,128)(2,1)S(1)}, bf16[512,384]{1,0:T(8,128)(2,1)S(1)}, u32[]{:S(2)}, u32[]{:S(2)}) collective-permute-start(bf16[512,384]{1,0:T(8,128)(2,1)S(1)} %collective-permute-done.22.r_11_), channel_id=1, source_target_pairs={{2,4},{3,5},{4,6},{5,7},{10,12},{11,13},{12,14},{13,15},{18,20},{1... | collective-permute-start | bytes 1179656 | tf_op jit(solution)/shard_map/gather_step_2/ppermute | solution.py:248
  49.9 19.1 %collective-permute-start.30 = (bf16[512,384]{1,0:T(8,128)(2,1)S(1)}, bf16[512,384]{1,0:T(8,128)(2,1)}, u32[]{:S(2)}, u32[]{:S(2)}) collective-permute-start(bf16[512,384]{1,0:T(8,128)(2,1)S(1)} %collective-permute-done.23.r_14_), channel_id=1, source_target_pairs={{2,0},{3,1},{4,2},{5,3},{10,8},{11,9},{12,10},{13,11},{18,16},{19,... | collective-permute-start | bytes 1179656 | tf_op jit(solution)/shard_map/gather_step_2/ppermute | solution.py:248
  52.0 24.7 %collective-permute-start.5 = (bf16[128,2048]{1,0:T(8,128)(2,1)}, bf16[128,2048]{1,0:T(8,128)(2,1)}, u32[]{:S(2)}, u32[]{:S(2)}) collective-permute-start(bf16[128,2048]{1,0:T(8,128)(2,1)} %collective-permute-done.r_2_), channel_id=1, source_target_pairs={{0,16},{8,24},{16,0},{24,8},{1,17},{9,25},{17,1},{25,9},{2,18},{10... | collective-permute-start | bytes 1572872 | tf_op jit(solution)/shard_map/rows/ppermute | solution.py:253
  58.1 17.1 %collective-permute-start.32 = (bf16[512,384]{1,0:T(8,128)(2,1)}, bf16[512,384]{1,0:T(8,128)(2,1)S(1)}, u32[]{:S(2)}, u32[]{:S(2)}) collective-permute-start(bf16[512,384]{1,0:T(8,128)(2,1)} %collective-permute-done.21.r_14_), channel_id=1, source_target_pairs={{2,0},{3,1},{4,2},{5,3},{10,8},{11,9},{12,10},{13,11},{18,16},{19,... | collective-permute-start | bytes 1179656 | tf_op jit(solution)/shard_map/gather_step_2/ppermute | solution.py:248
  59.4 19.3 %collective-permute-start.12 = (bf16[128,2176]{1,0:T(8,128)(2,1)S(1)}, bf16[128,2176]{1,0:T(8,128)(2,1)S(1)}, u32[]{:S(2)}, u32[]{:S(2)}) collective-permute-start(bf16[128,2176]{1,0:T(8,128)(2,1)S(1)} %collective-permute-done.11.r_3_), channel_id=1, source_target_pairs={{0,8},{8,0},{16,24},{24,16},{1,9},{9,1},{17,25},{25,17},{2,10},{10... | collective-permute-start | bytes 1671176 | tf_op jit(solution)/shard_map/rows/ppermute | solution.py:253
  60.0 18.7 %collective-permute-start.14 = (bf16[128,2176]{1,0:T(8,128)(2,1)S(1)}, bf16[128,2176]{1,0:T(8,128)(2,1)S(1)}, u32[]{:S(2)}, u32[]{:S(2)}) collective-permute-start(bf16[128,2176]{1,0:T(8,128)(2,1)S(1)} %collective-permute-done.10.r_2_), channel_id=1, source_target_pairs={{0,1},{1,0},{2,3},{3,2},{4,5},{5,4},{6,7},{7,6},{8,9},{9,8},{10,11... | collective-permute-start | bytes 1671176 | tf_op jit(solution)/shard_map/rows/ppermute | solution.py:245
  69.1 10.1 %collective-permute-start.15 = (bf16[128,2176]{1,0:T(8,128)(2,1)S(1)}, bf16[128,2176]{1,0:T(8,128)(2,1)S(1)}, u32[]{:S(2)}, u32[]{:S(2)}) collective-permute-start(bf16[128,2176]{1,0:T(8,128)(2,1)S(1)} %collective-permute-done.11.r_3_), channel_id=1, source_target_pairs={{0,1},{1,0},{2,3},{3,2},{4,5},{5,4},{6,7},{7,6},{8,9},{9,8},{10,11... | collective-permute-start | bytes 1671176 | tf_op jit(solution)/shard_map/rows/ppermute | solution.py:245
  75.2 4.9 %collective-permute-start.24 = (bf16[512,384]{1,0:T(8,128)(2,1)S(1)}, bf16[512,384]{1,0:T(8,128)(2,1)S(1)}, u32[]{:S(2)}, u32[]{:S(2)}) collective-permute-start(bf16[512,384]{1,0:T(8,128)(2,1)S(1)} %collective-permute-done.18.r_12_), channel_id=1, source_target_pairs={{4,6},{5,7},{12,14},{13,15},{20,22},{21,23},{28,30},{29,31}} | collective-permute-start | bytes 1179656 | tf_op jit(solution)/shard_map/gather_step_3/ppermute | solution.py:248
  76.7 10.8 %collective-permute-start.26 = (bf16[512,384]{1,0:T(8,128)(2,1)S(1)}, bf16[512,384]{1,0:T(8,128)(2,1)S(1)}, u32[]{:S(2)}, u32[]{:S(2)}) collective-permute-start(bf16[512,384]{1,0:T(8,128)(2,1)S(1)} %collective-permute-done.25.r_15_), channel_id=1, source_target_pairs={{2,0},{3,1},{10,8},{11,9},{18,16},{19,17},{26,24},{27,25}} | collective-permute-start | bytes 1179656 | tf_op jit(solution)/shard_map/gather_step_3/ppermute | solution.py:248
  78.7 9.6 %collective-permute-start.16 = (bf16[128,2176]{1,0:T(8,128)(2,1)S(1)}, bf16[128,2176]{1,0:T(8,128)(2,1)}, u32[]{:S(2)}, u32[]{:S(2)}) collective-permute-start(bf16[128,2176]{1,0:T(8,128)(2,1)S(1)} %collective-permute-done.12.r_4_), channel_id=1, source_target_pairs={{0,1},{1,0},{2,3},{3,2},{4,5},{5,4},{6,7},{7,6},{8,9},{9,8},{10,11... | collective-permute-start | bytes 1671176 | tf_op jit(solution)/shard_map/rows/ppermute | solution.py:245
  78.7 13.3 %collective-permute-start.6 = (bf16[128,2048]{1,0:T(8,128)(2,1)}, bf16[128,2048]{1,0:T(8,128)(2,1)}, u32[]{:S(2)}, u32[]{:S(2)}) collective-permute-start(bf16[128,2048]{1,0:T(8,128)(2,1)} %r_1_.5), channel_id=1, source_target_pairs={{0,1},{1,0},{2,3},{3,2},{4,5},{5,4},{6,7},{7,6},{8,9},{9,8},{10,11... | collective-permute-start | bytes 1572872 | tf_op jit(solution)/shard_map/rows/ppermute | solution.py:245
  80.0 13.5 %collective-permute-start.7 = (bf16[128,2048]{1,0:T(8,128)(2,1)}, bf16[128,2048]{1,0:T(8,128)(2,1)}, u32[]{:S(2)}, u32[]{:S(2)}) collective-permute-start(bf16[128,2048]{1,0:T(8,128)(2,1)} %collective-permute-done.r_2_), channel_id=1, source_target_pairs={{0,1},{1,0},{2,3},{3,2},{4,5},{5,4},{6,7},{7,6},{8,9},{9,8},{10,11... | collective-permute-start | bytes 1572872 | tf_op jit(solution)/shard_map/rows/ppermute | solution.py:245
  80.8 12.7 %collective-permute-start.8 = (bf16[128,2048]{1,0:T(8,128)(2,1)}, bf16[128,2048]{1,0:T(8,128)(2,1)}, u32[]{:S(2)}, u32[]{:S(2)}) collective-permute-start(bf16[128,2048]{1,0:T(8,128)(2,1)} %copy-done.20), channel_id=1, source_target_pairs={{0,1},{1,0},{2,3},{3,2},{4,5},{5,4},{6,7},{7,6},{8,9},{9,8},{10,11... | collective-permute-start | bytes 1572872 | tf_op jit(solution)/shard_map/rows/ppermute | solution.py:245
  88.2 5.3 %collective-permute-start.9 = (bf16[128,2048]{1,0:T(8,128)(2,1)}, bf16[128,2048]{1,0:T(8,128)(2,1)}, u32[]{:S(2)}, u32[]{:S(2)}) collective-permute-start(bf16[128,2048]{1,0:T(8,128)(2,1)} %collective-permute-done.5.r_4_), channel_id=1, source_target_pairs={{0,1},{1,0},{2,3},{3,2},{4,5},{5,4},{6,7},{7,6},{8,9},{9,8},{10,11... | collective-permute-start | bytes 1572872 | tf_op jit(solution)/shard_map/rows/ppermute | solution.py:245
  88.2 18.7 %collective-permute-start.31 = (bf16[512,384]{1,0:T(8,128)(2,1)}, bf16[512,384]{1,0:T(8,128)(2,1)S(1)}, u32[]{:S(2)}, u32[]{:S(2)}) collective-permute-start(bf16[512,384]{1,0:T(8,128)(2,1)} %collective-permute-done.28.r_12_), channel_id=1, source_target_pairs={{4,6},{5,7},{12,14},{13,15},{20,22},{21,23},{28,30},{29,31}} | collective-permute-start | bytes 1179656 | tf_op jit(solution)/shard_map/gather_step_3/ppermute | solution.py:248
  92.1 14.9 %collective-permute-start.33 = (bf16[512,384]{1,0:T(8,128)(2,1)S(1)}, bf16[512,384]{1,0:T(8,128)(2,1)S(1)}, u32[]{:S(2)}, u32[]{:S(2)}) collective-permute-start(bf16[512,384]{1,0:T(8,128)(2,1)S(1)} %copy-done.39), channel_id=1, source_target_pairs={{2,0},{3,1},{10,8},{11,9},{18,16},{19,17},{26,24},{27,25}} | collective-permute-start | bytes 1179656 | tf_op jit(solution)/shard_map/gather_step_3/ppermute | solution.py:248
  101.5 18.9 %copy-start.15 = (bf16[512,384]{1,0:T(8,128)(2,1)}, bf16[512,384]{1,0:T(8,128)(2,1)S(1)}, u32[]{:S(2)}) copy-start(bf16[512,384]{1,0:T(8,128)(2,1)S(1)} %get-tuple-element.88) | copy-start | bytes 1179652
  101.5 19.6 %copy-start.25 = (bf16[512,384]{1,0:T(8,128)(2,1)S(1)}, bf16[512,384]{1,0:T(8,128)(2,1)}, u32[]{:S(2)}) copy-start(bf16[512,384]{1,0:T(8,128)(2,1)} %copy-done.24) | copy-start | bytes 1179652
  101.5 19.6 %copy-start.29 = (bf16[512,384]{1,0:T(8,128)(2,1)S(1)}, bf16[512,384]{1,0:T(8,128)(2,1)}, u32[]{:S(2)}) copy-start(bf16[512,384]{1,0:T(8,128)(2,1)} %copy-done.28) | copy-start | bytes 1179652
  102.3 13.4 %collective-permute-start.27 = (bf16[512,384]{1,0:T(8,128)(2,1)S(1)}, bf16[512,384]{1,0:T(8,128)(2,1)S(1)}, u32[]{:S(2)}, u32[]{:S(2)}) collective-permute-start(bf16[512,384]{1,0:T(8,128)(2,1)S(1)} %broadcast_select_fusion.5), channel_id=1, source_target_pairs={{0,2},{1,3},{6,4},{7,5},{8,10},{9,11},{14,12},{15,13},{16,18},{17,... | collective-permute-start | bytes 1179656 | tf_op jit(solution)/shard_map/scatter_step_1/ppermute | solution.py:248
  107.0 26.5 %collective-permute-start.34 = (bf16[512,384]{1,0:T(8,128)(2,1)S(1)}, bf16[512,384]{1,0:T(8,128)(2,1)S(1)}, u32[]{:S(2)}, u32[]{:S(2)}) collective-permute-start(bf16[512,384]{1,0:T(8,128)(2,1)S(1)} %copy-done.37), channel_id=1, source_target_pairs={{4,6},{5,7},{12,14},{13,15},{20,22},{21,23},{28,30},{29,31}} | collective-permute-start | bytes 1179656 | tf_op jit(solution)/shard_map/gather_step_3/ppermute | solution.py:248
  107.7 25.9 %collective-permute-start.35 = (bf16[512,384]{1,0:T(8,128)(2,1)}, bf16[512,384]{1,0:T(8,128)(2,1)S(1)}, u32[]{:S(2)}, u32[]{:S(2)}) collective-permute-start(bf16[512,384]{1,0:T(8,128)(2,1)} %collective-permute-done.30.r_15_), channel_id=1, source_target_pairs={{2,0},{3,1},{10,8},{11,9},{18,16},{19,17},{26,24},{27,25}} | collective-permute-start | bytes 1179656 | tf_op jit(solution)/shard_map/gather_step_3/ppermute | solution.py:248
  115.8 17.8 %copy-start.23 = (bf16[512,384]{1,0:T(8,128)(2,1)S(1)}, bf16[512,384]{1,0:T(8,128)(2,1)}, u32[]{:S(2)}) copy-start(bf16[512,384]{1,0:T(8,128)(2,1)} %copy-done.22) | copy-start | bytes 1179652
  115.8 27.3 %collective-permute-start.36 = (bf16[512,384]{1,0:T(8,128)(2,1)S(1)}, bf16[512,384]{1,0:T(8,128)(2,1)S(1)}, u32[]{:S(2)}, u32[]{:S(2)}) collective-permute-start(bf16[512,384]{1,0:T(8,128)(2,1)S(1)} %add_convert_fusion.8), channel_id=1, source_target_pairs={{0,2},{1,3},{2,4},{3,5},{8,10},{9,11},{10,12},{11,13},{16,18},{17,... | collective-permute-start | bytes 1179656 | tf_op jit(solution)/shard_map/scatter_step_2/ppermute | solution.py:248
  120.4 22.7 %collective-permute-start.37 = (bf16[512,384]{1,0:T(8,128)(2,1)S(1)}, bf16[512,384]{1,0:T(8,128)(2,1)S(1)}, u32[]{:S(2)}, u32[]{:S(2)}) collective-permute-start(bf16[512,384]{1,0:T(8,128)(2,1)S(1)} %add_convert_fusion.8), channel_id=1, source_target_pairs={{4,2},{5,3},{6,4},{7,5},{12,10},{13,11},{14,12},{15,13},{20,18},{2... | collective-permute-start | bytes 1179656 | tf_op jit(solution)/shard_map/scatter_step_2/ppermute | solution.py:248
  130.0 13.2 %collective-permute-start.38 = (bf16[512,384]{1,0:T(8,128)(2,1)S(1)}, bf16[512,384]{1,0:T(8,128)(2,1)S(1)}, u32[]{:S(2)}, u32[]{:S(2)}) collective-permute-start(bf16[512,384]{1,0:T(8,128)(2,1)S(1)} %broadcast_select_fusion.4), channel_id=1, source_target_pairs={{0,2},{1,3},{6,4},{7,5},{8,10},{9,11},{14,12},{15,13},{16,18},{17,... | collective-permute-start | bytes 1179656 | tf_op jit(solution)/shard_map/scatter_step_1/ppermute | solution.py:248
  141.5 9.1 %collective-permute-start.39 = (bf16[512,384]{1,0:T(8,128)(2,1)S(1)}, bf16[512,384]{1,0:T(8,128)(2,1)S(1)}, u32[]{:S(2)}, u32[]{:S(2)}) collective-permute-start(bf16[512,384]{1,0:T(8,128)(2,1)S(1)} %broadcast_select_fusion.3), channel_id=1, source_target_pairs={{0,2},{1,3},{6,4},{7,5},{8,10},{9,11},{14,12},{15,13},{16,18},{17,... | collective-permute-start | bytes 1179656 | tf_op jit(solution)/shard_map/scatter_step_1/ppermute | solution.py:248
  151.4 15.7 %collective-permute-start.40 = (bf16[512,2048]{1,0:T(8,128)(2,1)}, bf16[512,2048]{1,0:T(8,128)(2,1)}, u32[]{:S(2)}, u32[]{:S(2)}) collective-permute-start(bf16[512,2048]{1,0:T(8,128)(2,1)} %get-tuple-element.87), channel_id=1, source_target_pairs={{0,1},{1,0},{2,3},{3,2},{4,5},{5,4},{6,7},{7,6},{8,9},{9,8},{10,11... | collective-permute-start | bytes 6291464 | tf_op jit(solution)/shard_map/back/ppermute | solution.py:245
  152.7 6.7 %collective-permute-start.49 = (bf16[512,384]{1,0:T(8,128)(2,1)S(1)}, bf16[512,384]{1,0:T(8,128)(2,1)S(1)}, u32[]{:S(2)}, u32[]{:S(2)}) collective-permute-start(bf16[512,384]{1,0:T(8,128)(2,1)S(1)} %add_convert_fusion.5), channel_id=1, source_target_pairs={{4,2},{5,3},{6,4},{7,5},{12,10},{13,11},{14,12},{15,13},{20,18},{2... | collective-permute-start | bytes 1179656 | tf_op jit(solution)/shard_map/scatter_step_2/ppermute | solution.py:248
  153.5 13.4 %collective-permute-start.47 = (bf16[512,384]{1,0:T(8,128)(2,1)S(1)}, bf16[512,384]{1,0:T(8,128)(2,1)S(1)}, u32[]{:S(2)}, u32[]{:S(2)}) collective-permute-start(bf16[512,384]{1,0:T(8,128)(2,1)S(1)} %add_convert_fusion.5), channel_id=1, source_target_pairs={{0,2},{1,3},{2,4},{3,5},{8,10},{9,11},{10,12},{11,13},{16,18},{17,... | collective-permute-start | bytes 1179656 | tf_op jit(solution)/shard_map/scatter_step_2/ppermute | solution.py:248
  167.0 36.4 %collective-permute-start.53 = (bf16[512,384]{1,0:T(8,128)(2,1)S(1)}, bf16[512,384]{1,0:T(8,128)(2,1)S(1)}, u32[]{:S(2)}, u32[]{:S(2)}) collective-permute-start(bf16[512,384]{1,0:T(8,128)(2,1)S(1)} %add_convert_fusion.2), channel_id=1, source_target_pairs={{4,2},{5,3},{6,4},{7,5},{12,10},{13,11},{14,12},{15,13},{20,18},{2... | collective-permute-start | bytes 1179656 | tf_op jit(solution)/shard_map/scatter_step_2/ppermute | solution.py:248
  167.7 50.1 %collective-permute-start.51 = (bf16[512,384]{1,0:T(8,128)(2,1)S(1)}, bf16[512,384]{1,0:T(8,128)(2,1)S(1)}, u32[]{:S(2)}, u32[]{:S(2)}) collective-permute-start(bf16[512,384]{1,0:T(8,128)(2,1)S(1)} %add_convert_fusion.2), channel_id=1, source_target_pairs={{0,2},{1,3},{2,4},{3,5},{8,10},{9,11},{10,12},{11,13},{16,18},{17,... | collective-permute-start | bytes 1179656 | tf_op jit(solution)/shard_map/scatter_step_2/ppermute | solution.py:248
  173.2 13.7 %collective-permute-start.46 = (bf16[512,384]{1,0:T(8,128)(2,1)S(1)}, bf16[512,384]{1,0:T(8,128)(2,1)S(1)}, u32[]{:S(2)}, u32[]{:S(2)}) collective-permute-start(bf16[512,384]{1,0:T(8,128)(2,1)S(1)} %add_convert_fusion.6), channel_id=1, source_target_pairs={{2,0},{3,1},{4,2},{5,3},{6,4},{7,5},{10,8},{11,9},{12,10},{13,11},... | collective-permute-start | bytes 1179656 | tf_op jit(solution)/shard_map/scatter_step_3/ppermute | solution.py:248
  174.5 15.3 %collective-permute-start.45 = (bf16[512,384]{1,0:T(8,128)(2,1)S(1)}, bf16[512,384]{1,0:T(8,128)(2,1)S(1)}, u32[]{:S(2)}, u32[]{:S(2)}) collective-permute-start(bf16[512,384]{1,0:T(8,128)(2,1)S(1)} %add_convert_fusion.7), channel_id=1, source_target_pairs={{0,2},{1,3},{2,4},{3,5},{4,6},{5,7},{8,10},{9,11},{10,12},{11,13},... | collective-permute-start | bytes 1179656 | tf_op jit(solution)/shard_map/scatter_step_3/ppermute | solution.py:248
  182.9 20.4 %copy-start.18 = (bf16[512,384]{1,0:T(8,128)(2,1)S(1)}, bf16[512,384]{1,0:T(8,128)(2,1)}, u32[]{:S(2)}) copy-start(bf16[512,384]{1,0:T(8,128)(2,1)} %copy-done.17) | copy-start | bytes 1179652
  183.0 21.2 %collective-permute-start.43 = (bf16[2,128,1024]{2,1,0:T(8,128)(2,1)S(1)}, bf16[2,128,1024]{2,1,0:T(8,128)(2,1)S(1)}, u32[]{:S(2)}, u32[]{:S(2)}) collective-permute-start(bf16[2,128,1024]{2,1,0:T(8,128)(2,1)S(1)} %pad_maximum_fusion), channel_id=1, source_target_pairs={{0,8},{8,0},{16,24},{24,16},{1,9},{9,1},{17,25},{25,17},{2,10},{10... | collective-permute-start | bytes 1572872 | tf_op jit(solution)/shard_map/back/ppermute | solution.py:253
  186.9 15.2 %collective-permute-start.50 = (bf16[512,384]{1,0:T(8,128)(2,1)S(1)}, bf16[512,384]{1,0:T(8,128)(2,1)S(1)}, u32[]{:S(2)}, u32[]{:S(2)}) collective-permute-start(bf16[512,384]{1,0:T(8,128)(2,1)S(1)} %add_convert_fusion.3), channel_id=1, source_target_pairs={{2,0},{3,1},{4,2},{5,3},{6,4},{7,5},{10,8},{11,9},{12,10},{13,11},... | collective-permute-start | bytes 1179656 | tf_op jit(solution)/shard_map/scatter_step_3/ppermute | solution.py:248
  189.8 13.4 %collective-permute-start.48 = (bf16[512,384]{1,0:T(8,128)(2,1)S(1)}, bf16[512,384]{1,0:T(8,128)(2,1)S(1)}, u32[]{:S(2)}, u32[]{:S(2)}) collective-permute-start(bf16[512,384]{1,0:T(8,128)(2,1)S(1)} %add_convert_fusion.4), channel_id=1, source_target_pairs={{0,2},{1,3},{2,4},{3,5},{4,6},{5,7},{8,10},{9,11},{10,12},{11,13},... | collective-permute-start | bytes 1179656 | tf_op jit(solution)/shard_map/scatter_step_3/ppermute | solution.py:248
  202.1 14.9 %collective-permute-start.41 = (bf16[2,128,1024]{2,1,0:T(8,128)(2,1)S(1)}, bf16[2,128,1024]{2,1,0:T(8,128)(2,1)S(1)}, u32[]{:S(2)}, u32[]{:S(2)}) collective-permute-start(bf16[2,128,1024]{2,1,0:T(8,128)(2,1)S(1)} %slice.141), channel_id=1, source_target_pairs={{0,16},{8,24},{16,0},{24,8},{1,17},{9,25},{17,1},{25,9},{2,18},{10... | collective-permute-start | bytes 1572872 | tf_op jit(solution)/shard_map/back/ppermute | solution.py:253
  203.3 26.2 %collective-permute-start.55 = (f32[256,384]{1,0:T(8,128)S(1)}, f32[256,384]{1,0:T(8,128)S(1)}, u32[]{:S(2)}, u32[]{:S(2)}) collective-permute-start(f32[256,384]{1,0:T(8,128)S(1)} %constant_dynamic-slice_fusion.2), channel_id=1, source_target_pairs={{0,1},{1,0},{2,3},{3,2},{4,5},{5,4},{6,7},{7,6},{8,9},{9,8},{10,11... | collective-permute-start | bytes 1179656 | tf_op jit(solution)/shard_map/ppermute | solution.py:245
  203.5 26.1 %collective-permute-start.56 = (f32[256,384]{1,0:T(8,128)S(1)}, f32[256,384]{1,0:T(8,128)S(1)}, u32[]{:S(2)}, u32[]{:S(2)}) collective-permute-start(f32[256,384]{1,0:T(8,128)S(1)} %constant_dynamic-slice_fusion.1), channel_id=1, source_target_pairs={{0,1},{1,0},{2,3},{3,2},{4,5},{5,4},{6,7},{7,6},{8,9},{9,8},{10,11... | collective-permute-start | bytes 1179656 | tf_op jit(solution)/shard_map/ppermute | solution.py:245
  204.2 15.8 %collective-permute-start.44 = (bf16[128,1024]{1,0:T(8,128)(2,1)S(1)}, bf16[128,1024]{1,0:T(8,128)(2,1)S(1)}, u32[]{:S(2)}, u32[]{:S(2)}) collective-permute-start(bf16[128,1024]{1,0:T(8,128)(2,1)S(1)} %fusion.9), channel_id=1, source_target_pairs={{0,16},{8,24},{16,0},{24,8},{1,17},{9,25},{17,1},{25,9},{2,18},{10... | collective-permute-start | bytes 786440 | tf_op jit(solution)/shard_map/back/ppermute | solution.py:253
  217.2 6.7 %collective-permute-start.42 = (bf16[128,1024]{1,0:T(8,128)(2,1)S(1)}, bf16[128,1024]{1,0:T(8,128)(2,1)S(1)}, u32[]{:S(2)}, u32[]{:S(2)}) collective-permute-start(bf16[128,1024]{1,0:T(8,128)(2,1)S(1)} %fusion.8), channel_id=1, source_target_pairs={{0,8},{8,0},{16,24},{24,16},{1,9},{9,1},{17,25},{25,17},{2,10},{10... | collective-permute-start | bytes 786440 | tf_op jit(solution)/shard_map/back/ppermute | solution.py:253
  217.9 9.7 %collective-permute-start.54 = (bf16[512,384]{1,0:T(8,128)(2,1)S(1)}, bf16[512,384]{1,0:T(8,128)(2,1)S(1)}, u32[]{:S(2)}, u32[]{:S(2)}) collective-permute-start(bf16[512,384]{1,0:T(8,128)(2,1)S(1)} %add_convert_fusion), channel_id=1, source_target_pairs={{2,0},{3,1},{4,2},{5,3},{6,4},{7,5},{10,8},{11,9},{12,10},{13,11},... | collective-permute-start | bytes 1179656 | tf_op jit(solution)/shard_map/scatter_step_3/ppermute | solution.py:248
  220.0 9.2 %collective-permute-start.52 = (bf16[512,384]{1,0:T(8,128)(2,1)S(1)}, bf16[512,384]{1,0:T(8,128)(2,1)S(1)}, u32[]{:S(2)}, u32[]{:S(2)}) collective-permute-start(bf16[512,384]{1,0:T(8,128)(2,1)S(1)} %add_convert_fusion.1), channel_id=1, source_target_pairs={{0,2},{1,3},{2,4},{3,5},{4,6},{5,7},{8,10},{9,11},{10,12},{11,13},... | collective-permute-start | bytes 1179656 | tf_op jit(solution)/shard_map/scatter_step_3/ppermute | solution.py:248
  229.4 1.8 collective-permute-start.57
  (50 other events, 250.3 us)

commit v8 on v7

--- a/solution.py
+++ b/solution.py
@@ -381,23 +381,25 @@
         flops=4 * count * width * step * chunks,
     )
     with jax.named_scope("back"):
-        other = twin(after(give, *states[-1]))
+        states[0] = hop(parts[0], states[0], line - 1, ())
+        other = after(twin(after(give, *states[-1], *states[0])), *states[1])
+        states[-1] = hop(parts[-1], states[-1], 2, ())
+        states[1] = hop(parts[1], states[1], line - 1, (other,))
         ret = keep.astype(F32) + other.astype(F32)
         ret = ret.reshape(experts, rows, width)
         left, right = ret[:, :, : width // 2], ret[:, :, width // 2 :]
         far = flip(left[2:].astype(BF16), 2)
         odd = flip(jnp.stack((right[1], right[3])).astype(BF16), 1)
         left = left[:2] + far.astype(F32)
-        near = flip(left[1].astype(BF16), 1)
-        last = flip((right[2] + odd[1].astype(F32)).astype(BF16), 2)
+        busy = (*states[-1], *states[1])
+        near = flip(after(left[1].astype(BF16), *busy), 1)
+        last = flip(after((right[2] + odd[1].astype(F32)).astype(BF16), *busy), 2)
         left = left[0] + near.astype(F32)
         right = right[0] + odd[0].astype(F32) + last.astype(F32)
         grad_input = jnp.concatenate((left, right), axis=1).astype(BF16)
-    states[-1] = hop(parts[-1], states[-1], 2, (other,))
+    states[-1] = hop(parts[-1], states[-1], line - 1, (odd, far))
     sums = []
-    for i, (own, (up, down)) in enumerate(zip(parts, states)):
-        for s in range(3, line):
-            up, down = hop(own, (up, down), s, (odd, far) if i == chunks - 1 else (other,))
+    for own, (up, down) in zip(parts, states):
         sums.append(own[0].astype(F32) + up.astype(F32) + down.astype(F32))
 
     own = [lax.dynamic_slice_in_dim(s, c * feats, feats, 0) for s in sums]

time: 235 us -> 236 us (level)
  waiting for transfers between devices: 83.3 us -> 74.6 us
  local copies, waits for them, and re-layouts: 17.7 us -> 23.1 us
  other arithmetic: 10.2 us -> 12.8 us
    ppermute x10, waiting for transfers between devices: 12.7 us -> 3.26 us  [flip(): return lax.ppermute(a, 'expert', [(e, e ^ bit) for e in range(experts)])]
    unnamed x119 -> x103, local copies, waits for them, and re-layouts: 16.5 us -> 21.9 us
  transfers between devices with their start and end apart: 58 -> 58, of which waited for: 22 -> 20; matrix products, arithmetic and copies ran while one was open for 4% -> 5% of each run, Pallas kernels for 15% -> 14%
where the time goes in v8:
time: 236 us; the launch traced here: 234 us
  starting transfers between devices  88.3 us (37%)
  waiting for transfers between devices  74.6 us (32%)
  Pallas kernels  33.6 us (14%)
  local copies, waits for them, and re-layouts  23.1 us (10%)
  other arithmetic  12.8 us (5%)
    ppermute x33, starting transfers between devices, along(): lax.ppermute(a, 'wide', [(2 * s + i, 2 * t + i) for s, t in hops for i in...  76.5 us
    ppermute x33, waiting for transfers between devices, along(): lax.ppermute(a, 'wide', [(2 * s + i, 2 * t + i) for s, t in hops for i in...  69.8 us
    pallas_call x7, Pallas kernels, call(): pl.pallas_call(body, out_shape=outs, in_specs=ins, out_specs=[VMEM] * len...  33.6 us
    unnamed x103, local copies, waits for them, and re-layouts  21.9 us
    ppermute x10, starting transfers between devices, flip(): return lax.ppermute(a, 'expert', [(e, e ^ bit) for e in range(experts)])  9.91 us
  transfers between devices with their start and end apart: 58, of which 20 were waited for; matrix products, arithmetic and copies ran while one was open for 5% of the time, Pallas kernels for 14%

profile of v8, /device:TPU:0, one launch (start us, length us, event | category | flops | bytes accessed | tf_op | source)
XLA Modules:
  0.0 234.2 jit_solution(16248672933340268323)
XLA Ops:
  0.6 3.0 %collective-permute-start = (bf16[128,2048]{1,0:T(8,128)(2,1)}, bf16[128,2048]{1,0:T(8,128)(2,1)}, u32[]{:S(2)}, u32[]{:S(2)}) collective-permute-start(bf16[128,2048]{1,0:T(8,128)(2,1)} %r_1_.5), channel_id=1, source_target_pairs={{0,8},{8,0},{16,24},{24,16},{1,9},{9,1},{17,25},{25,17},{2,10},{10... | collective-permute-start | bytes 1572872 | tf_op jit(solution)/shard_map/rows/ppermute | solution.py:253
  3.6 1.5 collective-permute-start.4
  5.2 1.0 copy-done.2
  6.2 1.0 copy-done.3
  7.2 1.0 copy-done.4
  11.7 3.5 %collective-permute-start.17 = (bf16[512,384]{1,0:T(8,128)(2,1)S(1)}, bf16[512,384]{1,0:T(8,128)(2,1)S(1)}, u32[]{:S(2)}, u32[]{:S(2)}) collective-permute-start(bf16[512,384]{1,0:T(8,128)(2,1)S(1)} %get-tuple-element.58.r_10_), channel_id=1, source_target_pairs={{0,2},{1,3},{2,4},{3,5},{4,6},{5,7},{8,10},{9,11},{10,12},{11,13},... | collective-permute-start | bytes 1179656 | tf_op jit(solution)/shard_map/gather_step_1/ppermute | solution.py:248
  15.3 1.3 collective-permute-start.19
  17.3 4.6 %collective-permute-start.20 = (bf16[512,384]{1,0:T(8,128)(2,1)S(1)}, bf16[512,384]{1,0:T(8,128)(2,1)S(1)}, u32[]{:S(2)}, u32[]{:S(2)}) collective-permute-start(bf16[512,384]{1,0:T(8,128)(2,1)S(1)} %get-tuple-element.59.r_10_), channel_id=1, source_target_pairs={{0,2},{1,3},{2,4},{3,5},{4,6},{5,7},{8,10},{9,11},{10,12},{11,13},... | collective-permute-start | bytes 1179656 | tf_op jit(solution)/shard_map/gather_step_1/ppermute | solution.py:248
  21.9 1.3 collective-permute-start.21
  24.1 4.6 %collective-permute-start.22 = (bf16[512,384]{1,0:T(8,128)(2,1)S(1)}, bf16[512,384]{1,0:T(8,128)(2,1)S(1)}, u32[]{:S(2)}, u32[]{:S(2)}) collective-permute-start(bf16[512,384]{1,0:T(8,128)(2,1)S(1)} %get-tuple-element.60.r_10_), channel_id=1, source_target_pairs={{0,2},{1,3},{2,4},{3,5},{4,6},{5,7},{8,10},{9,11},{10,12},{11,13},... | collective-permute-start | bytes 1179656 | tf_op jit(solution)/shard_map/gather_step_1/ppermute | solution.py:248
  28.7 1.3 collective-permute-start.23
  31.4 1.6 collective-permute-done.20.r_11_
  33.6 4.1 %collective-permute-done.21.r_14_ = bf16[512,384]{1,0:T(8,128)(2,1)} collective-permute-done((bf16[512,384]{1,0:T(8,128)(2,1)S(1)}, bf16[512,384]{1,0:T(8,128)(2,1)}, u32[]{:S(2)}, u32[]{:S(2)}) %collective-permute-start.21) | collective-permute-done | bytes 393248 | tf_op jit(solution)/shard_map/gather_step_1/ppermute | solution.py:248
  37.7 3.1 %collective-permute-done.22.r_11_ = bf16[512,384]{1,0:T(8,128)(2,1)S(1)} collective-permute-done((bf16[512,384]{1,0:T(8,128)(2,1)S(1)}, bf16[512,384]{1,0:T(8,128)(2,1)S(1)}, u32[]{:S(2)}, u32[]{:S(2)}) %collective-permute-start.22) | collective-permute-done | bytes 393248 | tf_op jit(solution)/shard_map/gather_step_1/ppermute | solution.py:248
  42.2 2.7 %collective-permute-done.23.r_14_ = bf16[512,384]{1,0:T(8,128)(2,1)S(1)} collective-permute-done((bf16[512,384]{1,0:T(8,128)(2,1)S(1)}, bf16[512,384]{1,0:T(8,128)(2,1)S(1)}, u32[]{:S(2)}, u32[]{:S(2)}) %collective-permute-start.23) | collective-permute-done | bytes 393248 | tf_op jit(solution)/shard_map/gather_step_1/ppermute | solution.py:248
  45.0 1.3 collective-permute-start.25
  46.3 1.4 collective-permute-start.28
  50.0 1.3 collective-permute-start.30
  52.5 5.5 %collective-permute-done.25.r_15_ = bf16[512,384]{1,0:T(8,128)(2,1)S(1)} collective-permute-done((bf16[512,384]{1,0:T(8,128)(2,1)}, bf16[512,384]{1,0:T(8,128)(2,1)S(1)}, u32[]{:S(2)}, u32[]{:S(2)}) %collective-permute-start.25) | collective-permute-done | bytes 393248 | tf_op jit(solution)/shard_map/gather_step_2/ppermute | solution.py:248
  58.1 1.3 collective-permute-start.32
  60.7 8.4 %collective-permute-done.30.r_15_ = bf16[512,384]{1,0:T(8,128)(2,1)} collective-permute-done((bf16[512,384]{1,0:T(8,128)(2,1)S(1)}, bf16[512,384]{1,0:T(8,128)(2,1)}, u32[]{:S(2)}, u32[]{:S(2)}) %collective-permute-start.30) | collective-permute-done | bytes 393248 | tf_op jit(solution)/shard_map/gather_step_2/ppermute | solution.py:248
  69.1 6.1 %collective-permute-done.32.r_15_ = bf16[512,384]{1,0:T(8,128)(2,1)S(1)} collective-permute-done((bf16[512,384]{1,0:T(8,128)(2,1)}, bf16[512,384]{1,0:T(8,128)(2,1)S(1)}, u32[]{:S(2)}, u32[]{:S(2)}) %collective-permute-start.32) | collective-permute-done | bytes 393248 | tf_op jit(solution)/shard_map/gather_step_2/ppermute | solution.py:248
  76.6 1.3 collective-permute-start.26
  81.3 6.2 %collective-permute-done.26.r_16_ = bf16[512,384]{1,0:T(8,128)(2,1)S(1)} collective-permute-done((bf16[512,384]{1,0:T(8,128)(2,1)S(1)}, bf16[512,384]{1,0:T(8,128)(2,1)S(1)}, u32[]{:S(2)}, u32[]{:S(2)}) %collective-permute-start.26) | collective-permute-done | bytes 393248 | tf_op jit(solution)/shard_map/gather_step_3/ppermute | solution.py:248
  88.9 1.0 copy-done.1
  90.0 2.0 shard_map.104.r_9_
  92.1 1.4 collective-permute-start.33
  93.6 7.9 %shard_map.105 = (bf16[512,384]{1,0:T(8,128)(2,1)S(1)}, bf16[512,384]{1,0:T(8,128)(2,1)S(1)}, bf16[512,384]{1,0:T(8,128)(2,1)S(1)}, bf16[512,384]{1,0:T(8,128)(2...) custom-call(s32[3]{0:T(128)S(1)} %pad_add_fusion.r_0_, bf16[128,2048]{1,0:T(8,128)(2,1)S(1)} %copy-done.5, ...), custom_call_target="tpu_custom_call" | custom-call | flops 3221225472 | bytes 14286860 | tf_op jit(solution)/shard_map/pallas_call | solution.py:100
  101.6 4.8 %collective-permute-start.27 = (bf16[512,384]{1,0:T(8,128)(2,1)S(1)}, bf16[512,384]{1,0:T(8,128)(2,1)S(1)}, u32[]{:S(2)}, u32[]{:S(2)}) collective-permute-start(bf16[512,384]{1,0:T(8,128)(2,1)S(1)} %broadcast_select_fusion.5), channel_id=1, source_target_pairs={{0,2},{1,3},{6,4},{7,5},{8,10},{9,11},{14,12},{15,13},{16,18},{17,... | collective-permute-start | bytes 1179656 | tf_op jit(solution)/shard_map/scatter_step_1/ppermute | solution.py:248
  107.1 1.3 collective-permute-start.35
  108.4 6.7 %collective-permute-done.27 = bf16[512,384]{1,0:T(8,128)(2,1)S(1)} collective-permute-done((bf16[512,384]{1,0:T(8,128)(2,1)S(1)}, bf16[512,384]{1,0:T(8,128)(2,1)S(1)}, u32[]{:S(2)}, u32[]{:S(2)}) %collective-permute-start.27) | collective-permute-done | bytes 393248 | tf_op jit(solution)/shard_map/scatter_step_1/ppermute | solution.py:248
  115.3 4.5 %collective-permute-start.36 = (bf16[512,384]{1,0:T(8,128)(2,1)S(1)}, bf16[512,384]{1,0:T(8,128)(2,1)S(1)}, u32[]{:S(2)}, u32[]{:S(2)}) collective-permute-start(bf16[512,384]{1,0:T(8,128)(2,1)S(1)} %add_convert_fusion.8), channel_id=1, source_target_pairs={{0,2},{1,3},{2,4},{3,5},{8,10},{9,11},{10,12},{11,13},{16,18},{17,... | collective-permute-start | bytes 1179656 | tf_op jit(solution)/shard_map/scatter_step_2/ppermute | solution.py:248
  120.5 8.1 %shard_map.106 = (bf16[512,384]{1,0:T(8,128)(2,1)S(1)}, bf16[512,384]{1,0:T(8,128)(2,1)S(1)}, bf16[512,384]{1,0:T(8,128)(2,1)S(1)}, bf16[512,384]{1,0:T(8,128)(2...) custom-call(s32[3]{0:T(128)S(1)} %pad_add_fusion.r_0_, bf16[128,2048]{1,0:T(8,128)(2,1)S(1)} %copy-done.5, ...), custom_call_target="tpu_custom_call" | custom-call | flops 3221225472 | bytes 14286860 | tf_op jit(solution)/shard_map/pallas_call | solution.py:100
  130.3 4.3 %collective-permute-start.38 = (bf16[512,384]{1,0:T(8,128)(2,1)}, bf16[512,384]{1,0:T(8,128)(2,1)}, u32[]{:S(2)}, u32[]{:S(2)}) collective-permute-start(bf16[512,384]{1,0:T(8,128)(2,1)} %broadcast_select_fusion.4), channel_id=1, source_target_pairs={{0,2},{1,3},{6,4},{7,5},{8,10},{9,11},{14,12},{15,13},{16,18},{17,... | collective-permute-start | bytes 1179656 | tf_op jit(solution)/shard_map/scatter_step_1/ppermute | solution.py:248
  134.7 7.8 %shard_map.107 = (bf16[512,384]{1,0:T(8,128)(2,1)S(1)}, bf16[512,384]{1,0:T(8,128)(2,1)S(1)}, bf16[512,384]{1,0:T(8,128)(2,1)S(1)}, bf16[512,384]{1,0:T(8,128)(2...) custom-call(s32[3]{0:T(128)S(1)} %pad_add_fusion.r_0_, bf16[128,2048]{1,0:T(8,128)(2,1)S(1)} %copy-done.5, ...), custom_call_target="tpu_custom_call" | custom-call | flops 3221225472 | bytes 14286860 | tf_op jit(solution)/shard_map/pallas_call | solution.py:100
  142.5 0.9 broadcast_select_fusion.3
  143.4 2.1 collective-permute-start.39
  146.4 2.0 collective-permute-start.40
  149.3 1.5 collective-permute-start.41
  150.8 1.2 copy-done.35
  152.0 1.2 copy-done.37
  153.3 1.2 copy-done.39
  154.5 1.0 copy-done.41
  155.5 1.0 copy-done.43
  156.6 1.0 copy-done.45
  157.6 6.5 %shard_map.108 = (bf16[512,2048]{1,0:T(8,128)(2,1)S(1)}, bf16[512,2048]{1,0:T(8,128)(2,1)S(1)}) custom-call(bf16[1024,256]{1,0:T(8,128)(2,1)S(1)} %copy-done.41, bf16[1024,256]{1,0:T(8,128)(2,1)S(1)} %copy-done.43, bf16[1024,256]{1,0:T(8,128)(2,1)S(1)} %copy-done.45, bf16[2048,256]{1,0:T(8,128)(2,1)S(1)} %copy-done.35, bf16[2048,256]{1,0:T(8,128)(2,1)S(1)} %copy-done.37, ...), custom_call_target="tpu_custom_call" | custom-call | flops 3221225472 | bytes 8912896 | tf_op jit(solution)/shard_map/pallas_call | solution.py:100
  164.2 1.1 add_convert_fusion.5
  165.3 4.6 %collective-permute-start.43 = (bf16[512,384]{1,0:T(8,128)(2,1)S(1)}, bf16[512,384]{1,0:T(8,128)(2,1)S(1)}, u32[]{:S(2)}, u32[]{:S(2)}) collective-permute-start(bf16[512,384]{1,0:T(8,128)(2,1)S(1)} %add_convert_fusion.5), channel_id=1, source_target_pairs={{0,2},{1,3},{2,4},{3,5},{8,10},{9,11},{10,12},{11,13},{16,18},{17,... | collective-permute-start | bytes 1179656 | tf_op jit(solution)/shard_map/scatter_step_2/ppermute | solution.py:248
  170.6 1.1 add_convert_fusion.4
  171.7 5.0 %collective-permute-start.46 = (bf16[512,384]{1,0:T(8,128)(2,1)S(1)}, bf16[512,384]{1,0:T(8,128)(2,1)S(1)}, u32[]{:S(2)}, u32[]{:S(2)}) collective-permute-start(bf16[512,384]{1,0:T(8,128)(2,1)S(1)} %add_convert_fusion.4), channel_id=1, source_target_pairs={{0,2},{1,3},{2,4},{3,5},{8,10},{9,11},{10,12},{11,13},{16,18},{17,... | collective-permute-start | bytes 1179656 | tf_op jit(solution)/shard_map/back/scatter_step_2/ppermute | solution.py:248
  177.4 1.3 convert_add_fusion.3
  179.6 7.7 %collective-permute-done.46 = bf16[512,384]{1,0:T(8,128)(2,1)S(1)} collective-permute-done((bf16[512,384]{1,0:T(8,128)(2,1)S(1)}, bf16[512,384]{1,0:T(8,128)(2,1)S(1)}, u32[]{:S(2)}, u32[]{:S(2)}) %collective-permute-start.46) | collective-permute-done | bytes 393248 | tf_op jit(solution)/shard_map/back/scatter_step_2/ppermute | solution.py:248
  187.5 8.7 %collective-permute-start.48 = (bf16[512,384]{1,0:T(8,128)(2,1)S(1)}, bf16[512,384]{1,0:T(8,128)(2,1)S(1)}, u32[]{:S(2)}, u32[]{:S(2)}) collective-permute-start(bf16[512,384]{1,0:T(8,128)(2,1)S(1)} %add_convert_fusion.3), channel_id=1, source_target_pairs={{0,2},{1,3},{2,4},{3,5},{4,6},{5,7},{8,10},{9,11},{10,12},{11,13},... | collective-permute-start | bytes 1179656 | tf_op jit(solution)/shard_map/back/scatter_step_3/ppermute | solution.py:248
  196.2 1.3 collective-permute-start.49
  199.9 4.2 %collective-permute-done.48 = bf16[512,384]{1,0:T(8,128)(2,1)S(1)} collective-permute-done((bf16[512,384]{1,0:T(8,128)(2,1)S(1)}, bf16[512,384]{1,0:T(8,128)(2,1)S(1)}, u32[]{:S(2)}, u32[]{:S(2)}) %collective-permute-start.48) | collective-permute-done | bytes 393248 | tf_op jit(solution)/shard_map/back/scatter_step_3/ppermute | solution.py:248
  204.1 4.1 %collective-permute-done.49 = bf16[512,384]{1,0:T(8,128)(2,1)S(1)} collective-permute-done((bf16[512,384]{1,0:T(8,128)(2,1)S(1)}, bf16[512,384]{1,0:T(8,128)(2,1)S(1)}, u32[]{:S(2)}, u32[]{:S(2)}) %collective-permute-start.49) | collective-permute-done | bytes 393248 | tf_op jit(solution)/shard_map/back/scatter_step_3/ppermute | solution.py:248
  208.4 3.2 %collective-permute-done.45 = bf16[2,128,1024]{2,1,0:T(8,128)(2,1)S(1)} collective-permute-done((bf16[2,128,1024]{2,1,0:T(8,128)(2,1)S(1)}, bf16[2,128,1024]{2,1,0:T(8,128)(2,1)S(1)}, u32[]{:S(2)}, u32[]{:S(2)}) %collective-permute-start.45) | collective-permute-done | bytes 524320 | tf_op jit(solution)/shard_map/back/ppermute | solution.py:253
  212.5 1.4 collective-permute-start.52
  214.0 1.3 collective-permute-start.54
  215.3 5.2 %collective-permute-start.53 = (bf16[512,384]{1,0:T(8,128)(2,1)S(1)}, bf16[512,384]{1,0:T(8,128)(2,1)S(1)}, u32[]{:S(2)}, u32[]{:S(2)}) collective-permute-start(bf16[512,384]{1,0:T(8,128)(2,1)S(1)} %add_convert_fusion.1), channel_id=1, source_target_pairs={{0,2},{1,3},{2,4},{3,5},{4,6},{5,7},{8,10},{9,11},{10,12},{11,13},... | collective-permute-start | bytes 1179656 | tf_op jit(solution)/shard_map/scatter_step_3/ppermute | solution.py:248
  220.7 7.6 %collective-permute-done.54 = bf16[512,384]{1,0:T(8,128)(2,1)S(1)} collective-permute-done((bf16[512,384]{1,0:T(8,128)(2,1)S(1)}, bf16[512,384]{1,0:T(8,128)(2,1)S(1)}, u32[]{:S(2)}, u32[]{:S(2)}) %collective-permute-start.54) | collective-permute-done | bytes 393248 | tf_op jit(solution)/shard_map/scatter_step_3/ppermute | solution.py:248
  228.3 1.2 collective-permute-done.53
  231.9 1.0 broadcast_select_fusion.2
  232.9 1.3 broadcast_select_fusion
  (202 shorter events, 33.1 us)
Async XLA Ops:
  0.6 21.2 %collective-permute-start = (bf16[128,2048]{1,0:T(8,128)(2,1)}, bf16[128,2048]{1,0:T(8,128)(2,1)}, u32[]{:S(2)}, u32[]{:S(2)}) collective-permute-start(bf16[128,2048]{1,0:T(8,128)(2,1)} %r_1_.5), channel_id=1, source_target_pairs={{0,8},{8,0},{16,24},{24,16},{1,9},{9,1},{17,25},{25,17},{2,10},{10... | collective-permute-start | bytes 1572872 | tf_op jit(solution)/shard_map/rows/ppermute | solution.py:253
  3.6 20.5 %collective-permute-start.4 = (bf16[128,2048]{1,0:T(8,128)(2,1)}, bf16[128,2048]{1,0:T(8,128)(2,1)S(1)}, u32[]{:S(2)}, u32[]{:S(2)}) collective-permute-start(bf16[128,2048]{1,0:T(8,128)(2,1)} %r_1_.5), channel_id=1, source_target_pairs={{0,16},{8,24},{16,0},{24,8},{1,17},{9,25},{17,1},{25,9},{2,18},{10... | collective-permute-start | bytes 1572872 | tf_op jit(solution)/shard_map/rows/ppermute | solution.py:253
  8.2 22.5 %copy-start.46 = (bf16[128,2048]{1,0:T(8,128)(2,1)S(1)}, bf16[128,2048]{1,0:T(8,128)(2,1)}, u32[]{:S(2)}) copy-start(bf16[128,2048]{1,0:T(8,128)(2,1)} %param.8) | copy-start | bytes 1572868
  9.0 1.5 collective-permute-start.1
  9.1 1.7 collective-permute-start.2
  9.6 1.5 collective-permute-start.3
  11.7 17.0 %collective-permute-start.17 = (bf16[512,384]{1,0:T(8,128)(2,1)S(1)}, bf16[512,384]{1,0:T(8,128)(2,1)S(1)}, u32[]{:S(2)}, u32[]{:S(2)}) collective-permute-start(bf16[512,384]{1,0:T(8,128)(2,1)S(1)} %get-tuple-element.58.r_10_), channel_id=1, source_target_pairs={{0,2},{1,3},{2,4},{3,5},{4,6},{5,7},{8,10},{9,11},{10,12},{11,13},... | collective-permute-start | bytes 1179656 | tf_op jit(solution)/shard_map/gather_step_1/ppermute | solution.py:248
  15.3 15.6 %collective-permute-start.19 = (bf16[512,384]{1,0:T(8,128)(2,1)S(1)}, bf16[512,384]{1,0:T(8,128)(2,1)}, u32[]{:S(2)}, u32[]{:S(2)}) collective-permute-start(bf16[512,384]{1,0:T(8,128)(2,1)S(1)} %get-tuple-element.58.r_10_), channel_id=1, source_target_pairs={{2,0},{3,1},{4,2},{5,3},{6,4},{7,5},{10,8},{11,9},{12,10},{13,11},... | collective-permute-start | bytes 1179656 | tf_op jit(solution)/shard_map/gather_step_1/ppermute | solution.py:248
  17.3 15.8 %collective-permute-start.20 = (bf16[512,384]{1,0:T(8,128)(2,1)S(1)}, bf16[512,384]{1,0:T(8,128)(2,1)S(1)}, u32[]{:S(2)}, u32[]{:S(2)}) collective-permute-start(bf16[512,384]{1,0:T(8,128)(2,1)S(1)} %get-tuple-element.59.r_10_), channel_id=1, source_target_pairs={{0,2},{1,3},{2,4},{3,5},{4,6},{5,7},{8,10},{9,11},{10,12},{11,13},... | collective-permute-start | bytes 1179656 | tf_op jit(solution)/shard_map/gather_step_1/ppermute | solution.py:248
  21.9 15.8 %collective-permute-start.21 = (bf16[512,384]{1,0:T(8,128)(2,1)S(1)}, bf16[512,384]{1,0:T(8,128)(2,1)}, u32[]{:S(2)}, u32[]{:S(2)}) collective-permute-start(bf16[512,384]{1,0:T(8,128)(2,1)S(1)} %get-tuple-element.59.r_10_), channel_id=1, source_target_pairs={{2,0},{3,1},{4,2},{5,3},{6,4},{7,5},{10,8},{11,9},{12,10},{13,11},... | collective-permute-start | bytes 1179656 | tf_op jit(solution)/shard_map/gather_step_1/ppermute | solution.py:248
  24.1 16.7 %collective-permute-start.22 = (bf16[512,384]{1,0:T(8,128)(2,1)S(1)}, bf16[512,384]{1,0:T(8,128)(2,1)S(1)}, u32[]{:S(2)}, u32[]{:S(2)}) collective-permute-start(bf16[512,384]{1,0:T(8,128)(2,1)S(1)} %get-tuple-element.60.r_10_), channel_id=1, source_target_pairs={{0,2},{1,3},{2,4},{3,5},{4,6},{5,7},{8,10},{9,11},{10,12},{11,13},... | collective-permute-start | bytes 1179656 | tf_op jit(solution)/shard_map/gather_step_1/ppermute | solution.py:248
  28.7 16.3 %collective-permute-start.23 = (bf16[512,384]{1,0:T(8,128)(2,1)S(1)}, bf16[512,384]{1,0:T(8,128)(2,1)S(1)}, u32[]{:S(2)}, u32[]{:S(2)}) collective-permute-start(bf16[512,384]{1,0:T(8,128)(2,1)S(1)} %get-tuple-element.60.r_10_), channel_id=1, source_target_pairs={{2,0},{3,1},{4,2},{5,3},{6,4},{7,5},{10,8},{11,9},{12,10},{13,11},... | collective-permute-start | bytes 1179656 | tf_op jit(solution)/shard_map/gather_step_1/ppermute | solution.py:248
  30.8 15.4 %collective-permute-start.10 = (bf16[128,2176]{1,0:T(8,128)(2,1)S(1)}, bf16[128,2176]{1,0:T(8,128)(2,1)S(1)}, u32[]{:S(2)}, u32[]{:S(2)}) collective-permute-start(bf16[128,2176]{1,0:T(8,128)(2,1)S(1)} %fusion.1.r_1_), channel_id=1, source_target_pairs={{0,8},{8,0},{16,24},{24,16},{1,9},{9,1},{17,25},{25,17},{2,10},{10... | collective-permute-start | bytes 1671176 | tf_op jit(solution)/shard_map/rows/ppermute | solution.py:253
  33.1 15.4 %collective-permute-start.11 = (bf16[128,2176]{1,0:T(8,128)(2,1)S(1)}, bf16[128,2176]{1,0:T(8,128)(2,1)S(1)}, u32[]{:S(2)}, u32[]{:S(2)}) collective-permute-start(bf16[128,2176]{1,0:T(8,128)(2,1)S(1)} %fusion.1.r_1_), channel_id=1, source_target_pairs={{0,16},{8,24},{16,0},{24,8},{1,17},{9,25},{17,1},{25,9},{2,18},{10... | collective-permute-start | bytes 1671176 | tf_op jit(solution)/shard_map/rows/ppermute | solution.py:253
  37.7 12.3 %collective-permute-start.13 = (bf16[128,2176]{1,0:T(8,128)(2,1)S(1)}, bf16[128,2176]{1,0:T(8,128)(2,1)S(1)}, u32[]{:S(2)}, u32[]{:S(2)}) collective-permute-start(bf16[128,2176]{1,0:T(8,128)(2,1)S(1)} %fusion.1.r_1_), channel_id=1, source_target_pairs={{0,1},{1,0},{2,3},{3,2},{4,5},{5,4},{6,7},{7,6},{8,9},{9,8},{10,11... | collective-permute-start | bytes 1671176 | tf_op jit(solution)/shard_map/rows/ppermute | solution.py:245
  40.8 11.2 %collective-permute-start.18 = (bf16[512,384]{1,0:T(8,128)(2,1)S(1)}, bf16[512,384]{1,0:T(8,128)(2,1)S(1)}, u32[]{:S(2)}, u32[]{:S(2)}) collective-permute-start(bf16[512,384]{1,0:T(8,128)(2,1)S(1)} %collective-permute-done.17.r_11_), channel_id=1, source_target_pairs={{2,4},{3,5},{4,6},{5,7},{10,12},{11,13},{12,14},{13,15},{18,20},{1... | collective-permute-start | bytes 1179656 | tf_op jit(solution)/shard_map/gather_step_2/ppermute | solution.py:248
  45.0 13.1 %collective-permute-start.25 = (bf16[512,384]{1,0:T(8,128)(2,1)}, bf16[512,384]{1,0:T(8,128)(2,1)S(1)}, u32[]{:S(2)}, u32[]{:S(2)}) collective-permute-start(bf16[512,384]{1,0:T(8,128)(2,1)} %collective-permute-done.19.r_14_), channel_id=1, source_target_pairs={{2,0},{3,1},{4,2},{5,3},{10,8},{11,9},{12,10},{13,11},{18,16},{19,... | collective-permute-start | bytes 1179656 | tf_op jit(solution)/shard_map/gather_step_2/ppermute | solution.py:248
  46.3 13.1 %collective-permute-start.28 = (bf16[512,384]{1,0:T(8,128)(2,1)S(1)}, bf16[512,384]{1,0:T(8,128)(2,1)}, u32[]{:S(2)}, u32[]{:S(2)}) collective-permute-start(bf16[512,384]{1,0:T(8,128)(2,1)S(1)} %collective-permute-done.20.r_11_), channel_id=1, source_target_pairs={{2,4},{3,5},{4,6},{5,7},{10,12},{11,13},{12,14},{13,15},{18,20},{1... | collective-permute-start | bytes 1179656 | tf_op jit(solution)/shard_map/gather_step_2/ppermute | solution.py:248
  48.5 11.4 %collective-permute-start.29 = (bf16[512,384]{1,0:T(8,128)(2,1)S(1)}, bf16[512,384]{1,0:T(8,128)(2,1)S(1)}, u32[]{:S(2)}, u32[]{:S(2)}) collective-permute-start(bf16[512,384]{1,0:T(8,128)(2,1)S(1)} %collective-permute-done.22.r_11_), channel_id=1, source_target_pairs={{2,4},{3,5},{4,6},{5,7},{10,12},{11,13},{12,14},{13,15},{18,20},{1... | collective-permute-start | bytes 1179656 | tf_op jit(solution)/shard_map/gather_step_2/ppermute | solution.py:248
  50.0 19.1 %collective-permute-start.30 = (bf16[512,384]{1,0:T(8,128)(2,1)S(1)}, bf16[512,384]{1,0:T(8,128)(2,1)}, u32[]{:S(2)}, u32[]{:S(2)}) collective-permute-start(bf16[512,384]{1,0:T(8,128)(2,1)S(1)} %collective-permute-done.23.r_14_), channel_id=1, source_target_pairs={{2,0},{3,1},{4,2},{5,3},{10,8},{11,9},{12,10},{13,11},{18,16},{19,... | collective-permute-start | bytes 1179656 | tf_op jit(solution)/shard_map/gather_step_2/ppermute | solution.py:248
  52.0 24.6 %collective-permute-start.5 = (bf16[128,2048]{1,0:T(8,128)(2,1)}, bf16[128,2048]{1,0:T(8,128)(2,1)}, u32[]{:S(2)}, u32[]{:S(2)}) collective-permute-start(bf16[128,2048]{1,0:T(8,128)(2,1)} %collective-permute-done.r_2_), channel_id=1, source_target_pairs={{0,16},{8,24},{16,0},{24,8},{1,17},{9,25},{17,1},{25,9},{2,18},{10... | collective-permute-start | bytes 1572872 | tf_op jit(solution)/shard_map/rows/ppermute | solution.py:253
  58.1 17.2 %collective-permute-start.32 = (bf16[512,384]{1,0:T(8,128)(2,1)}, bf16[512,384]{1,0:T(8,128)(2,1)S(1)}, u32[]{:S(2)}, u32[]{:S(2)}) collective-permute-start(bf16[512,384]{1,0:T(8,128)(2,1)} %collective-permute-done.21.r_14_), channel_id=1, source_target_pairs={{2,0},{3,1},{4,2},{5,3},{10,8},{11,9},{12,10},{13,11},{18,16},{19,... | collective-permute-start | bytes 1179656 | tf_op jit(solution)/shard_map/gather_step_2/ppermute | solution.py:248
  59.4 19.3 %collective-permute-start.12 = (bf16[128,2176]{1,0:T(8,128)(2,1)S(1)}, bf16[128,2176]{1,0:T(8,128)(2,1)S(1)}, u32[]{:S(2)}, u32[]{:S(2)}) collective-permute-start(bf16[128,2176]{1,0:T(8,128)(2,1)S(1)} %collective-permute-done.11.r_3_), channel_id=1, source_target_pairs={{0,8},{8,0},{16,24},{24,16},{1,9},{9,1},{17,25},{25,17},{2,10},{10... | collective-permute-start | bytes 1671176 | tf_op jit(solution)/shard_map/rows/ppermute | solution.py:253
  60.0 18.7 %collective-permute-start.14 = (bf16[128,2176]{1,0:T(8,128)(2,1)S(1)}, bf16[128,2176]{1,0:T(8,128)(2,1)S(1)}, u32[]{:S(2)}, u32[]{:S(2)}) collective-permute-start(bf16[128,2176]{1,0:T(8,128)(2,1)S(1)} %collective-permute-done.10.r_2_), channel_id=1, source_target_pairs={{0,1},{1,0},{2,3},{3,2},{4,5},{5,4},{6,7},{7,6},{8,9},{9,8},{10,11... | collective-permute-start | bytes 1671176 | tf_op jit(solution)/shard_map/rows/ppermute | solution.py:245
  69.1 10.1 %collective-permute-start.15 = (bf16[128,2176]{1,0:T(8,128)(2,1)S(1)}, bf16[128,2176]{1,0:T(8,128)(2,1)S(1)}, u32[]{:S(2)}, u32[]{:S(2)}) collective-permute-start(bf16[128,2176]{1,0:T(8,128)(2,1)S(1)} %collective-permute-done.11.r_3_), channel_id=1, source_target_pairs={{0,1},{1,0},{2,3},{3,2},{4,5},{5,4},{6,7},{7,6},{8,9},{9,8},{10,11... | collective-permute-start | bytes 1671176 | tf_op jit(solution)/shard_map/rows/ppermute | solution.py:245
  75.2 4.9 %collective-permute-start.24 = (bf16[512,384]{1,0:T(8,128)(2,1)S(1)}, bf16[512,384]{1,0:T(8,128)(2,1)S(1)}, u32[]{:S(2)}, u32[]{:S(2)}) collective-permute-start(bf16[512,384]{1,0:T(8,128)(2,1)S(1)} %collective-permute-done.18.r_12_), channel_id=1, source_target_pairs={{4,6},{5,7},{12,14},{13,15},{20,22},{21,23},{28,30},{29,31}} | collective-permute-start | bytes 1179656 | tf_op jit(solution)/shard_map/gather_step_3/ppermute | solution.py:248
  76.6 10.8 %collective-permute-start.26 = (bf16[512,384]{1,0:T(8,128)(2,1)S(1)}, bf16[512,384]{1,0:T(8,128)(2,1)S(1)}, u32[]{:S(2)}, u32[]{:S(2)}) collective-permute-start(bf16[512,384]{1,0:T(8,128)(2,1)S(1)} %collective-permute-done.25.r_15_), channel_id=1, source_target_pairs={{2,0},{3,1},{10,8},{11,9},{18,16},{19,17},{26,24},{27,25}} | collective-permute-start | bytes 1179656 | tf_op jit(solution)/shard_map/gather_step_3/ppermute | solution.py:248
  78.7 9.6 %collective-permute-start.16 = (bf16[128,2176]{1,0:T(8,128)(2,1)S(1)}, bf16[128,2176]{1,0:T(8,128)(2,1)}, u32[]{:S(2)}, u32[]{:S(2)}) collective-permute-start(bf16[128,2176]{1,0:T(8,128)(2,1)S(1)} %collective-permute-done.12.r_4_), channel_id=1, source_target_pairs={{0,1},{1,0},{2,3},{3,2},{4,5},{5,4},{6,7},{7,6},{8,9},{9,8},{10,11... | collective-permute-start | bytes 1671176 | tf_op jit(solution)/shard_map/rows/ppermute | solution.py:245
  78.7 13.3 %collective-permute-start.6 = (bf16[128,2048]{1,0:T(8,128)(2,1)}, bf16[128,2048]{1,0:T(8,128)(2,1)}, u32[]{:S(2)}, u32[]{:S(2)}) collective-permute-start(bf16[128,2048]{1,0:T(8,128)(2,1)} %r_1_.5), channel_id=1, source_target_pairs={{0,1},{1,0},{2,3},{3,2},{4,5},{5,4},{6,7},{7,6},{8,9},{9,8},{10,11... | collective-permute-start | bytes 1572872 | tf_op jit(solution)/shard_map/rows/ppermute | solution.py:245
  80.0 13.5 %collective-permute-start.7 = (bf16[128,2048]{1,0:T(8,128)(2,1)}, bf16[128,2048]{1,0:T(8,128)(2,1)}, u32[]{:S(2)}, u32[]{:S(2)}) collective-permute-start(bf16[128,2048]{1,0:T(8,128)(2,1)} %collective-permute-done.r_2_), channel_id=1, source_target_pairs={{0,1},{1,0},{2,3},{3,2},{4,5},{5,4},{6,7},{7,6},{8,9},{9,8},{10,11... | collective-permute-start | bytes 1572872 | tf_op jit(solution)/shard_map/rows/ppermute | solution.py:245
  80.9 12.6 %collective-permute-start.8 = (bf16[128,2048]{1,0:T(8,128)(2,1)}, bf16[128,2048]{1,0:T(8,128)(2,1)}, u32[]{:S(2)}, u32[]{:S(2)}) collective-permute-start(bf16[128,2048]{1,0:T(8,128)(2,1)} %copy-done.6), channel_id=1, source_target_pairs={{0,1},{1,0},{2,3},{3,2},{4,5},{5,4},{6,7},{7,6},{8,9},{9,8},{10,11... | collective-permute-start | bytes 1572872 | tf_op jit(solution)/shard_map/rows/ppermute | solution.py:245
  88.2 5.3 %collective-permute-start.9 = (bf16[128,2048]{1,0:T(8,128)(2,1)}, bf16[128,2048]{1,0:T(8,128)(2,1)}, u32[]{:S(2)}, u32[]{:S(2)}) collective-permute-start(bf16[128,2048]{1,0:T(8,128)(2,1)} %collective-permute-done.5.r_4_), channel_id=1, source_target_pairs={{0,1},{1,0},{2,3},{3,2},{4,5},{5,4},{6,7},{7,6},{8,9},{9,8},{10,11... | collective-permute-start | bytes 1572872 | tf_op jit(solution)/shard_map/rows/ppermute | solution.py:245
  88.2 18.2 %collective-permute-start.31 = (bf16[512,384]{1,0:T(8,128)(2,1)}, bf16[512,384]{1,0:T(8,128)(2,1)S(1)}, u32[]{:S(2)}, u32[]{:S(2)}) collective-permute-start(bf16[512,384]{1,0:T(8,128)(2,1)} %collective-permute-done.28.r_12_), channel_id=1, source_target_pairs={{4,6},{5,7},{12,14},{13,15},{20,22},{21,23},{28,30},{29,31}} | collective-permute-start | bytes 1179656 | tf_op jit(solution)/shard_map/gather_step_3/ppermute | solution.py:248
  92.1 14.4 %collective-permute-start.33 = (bf16[512,384]{1,0:T(8,128)(2,1)S(1)}, bf16[512,384]{1,0:T(8,128)(2,1)S(1)}, u32[]{:S(2)}, u32[]{:S(2)}) collective-permute-start(bf16[512,384]{1,0:T(8,128)(2,1)S(1)} %copy-done.25), channel_id=1, source_target_pairs={{2,0},{3,1},{10,8},{11,9},{18,16},{19,17},{26,24},{27,25}} | collective-permute-start | bytes 1179656 | tf_op jit(solution)/shard_map/gather_step_3/ppermute | solution.py:248
  101.5 19.0 %copy-start.11 = (bf16[512,384]{1,0:T(8,128)(2,1)S(1)}, bf16[512,384]{1,0:T(8,128)(2,1)}, u32[]{:S(2)}) copy-start(bf16[512,384]{1,0:T(8,128)(2,1)} %copy-done.10) | copy-start | bytes 1179652
  101.5 19.0 %copy-start.15 = (bf16[512,384]{1,0:T(8,128)(2,1)S(1)}, bf16[512,384]{1,0:T(8,128)(2,1)}, u32[]{:S(2)}) copy-start(bf16[512,384]{1,0:T(8,128)(2,1)} %copy-done.14) | copy-start | bytes 1179652
  101.6 13.5 %collective-permute-start.27 = (bf16[512,384]{1,0:T(8,128)(2,1)S(1)}, bf16[512,384]{1,0:T(8,128)(2,1)S(1)}, u32[]{:S(2)}, u32[]{:S(2)}) collective-permute-start(bf16[512,384]{1,0:T(8,128)(2,1)S(1)} %broadcast_select_fusion.5), channel_id=1, source_target_pairs={{0,2},{1,3},{6,4},{7,5},{8,10},{9,11},{14,12},{15,13},{16,18},{17,... | collective-permute-start | bytes 1179656 | tf_op jit(solution)/shard_map/scatter_step_1/ppermute | solution.py:248
  106.4 28.2 %collective-permute-start.34 = (bf16[512,384]{1,0:T(8,128)(2,1)S(1)}, bf16[512,384]{1,0:T(8,128)(2,1)S(1)}, u32[]{:S(2)}, u32[]{:S(2)}) collective-permute-start(bf16[512,384]{1,0:T(8,128)(2,1)S(1)} %copy-done.23), channel_id=1, source_target_pairs={{4,6},{5,7},{12,14},{13,15},{20,22},{21,23},{28,30},{29,31}} | collective-permute-start | bytes 1179656 | tf_op jit(solution)/shard_map/gather_step_3/ppermute | solution.py:248
  107.1 27.5 %collective-permute-start.35 = (bf16[512,384]{1,0:T(8,128)(2,1)}, bf16[512,384]{1,0:T(8,128)(2,1)S(1)}, u32[]{:S(2)}, u32[]{:S(2)}) collective-permute-start(bf16[512,384]{1,0:T(8,128)(2,1)} %collective-permute-done.30.r_15_), channel_id=1, source_target_pairs={{2,0},{3,1},{10,8},{11,9},{18,16},{19,17},{26,24},{27,25}} | collective-permute-start | bytes 1179656 | tf_op jit(solution)/shard_map/gather_step_3/ppermute | solution.py:248
  115.2 19.4 %copy-start.9 = (bf16[512,384]{1,0:T(8,128)(2,1)S(1)}, bf16[512,384]{1,0:T(8,128)(2,1)}, u32[]{:S(2)}) copy-start(bf16[512,384]{1,0:T(8,128)(2,1)} %copy-done.8) | copy-start | bytes 1179652
  115.2 19.4 %copy-start.13 = (bf16[512,384]{1,0:T(8,128)(2,1)S(1)}, bf16[512,384]{1,0:T(8,128)(2,1)}, u32[]{:S(2)}) copy-start(bf16[512,384]{1,0:T(8,128)(2,1)} %copy-done.12) | copy-start | bytes 1179652
  115.3 19.4 %copy-start.17 = (bf16[512,384]{1,0:T(8,128)(2,1)S(1)}, bf16[512,384]{1,0:T(8,128)(2,1)}, u32[]{:S(2)}) copy-start(bf16[512,384]{1,0:T(8,128)(2,1)} %copy-done.16) | copy-start | bytes 1179652
  115.3 30.2 %collective-permute-start.36 = (bf16[512,384]{1,0:T(8,128)(2,1)S(1)}, bf16[512,384]{1,0:T(8,128)(2,1)S(1)}, u32[]{:S(2)}, u32[]{:S(2)}) collective-permute-start(bf16[512,384]{1,0:T(8,128)(2,1)S(1)} %add_convert_fusion.8), channel_id=1, source_target_pairs={{0,2},{1,3},{2,4},{3,5},{8,10},{9,11},{10,12},{11,13},{16,18},{17,... | collective-permute-start | bytes 1179656 | tf_op jit(solution)/shard_map/scatter_step_2/ppermute | solution.py:248
  119.8 28.6 %collective-permute-start.37 = (bf16[512,384]{1,0:T(8,128)(2,1)S(1)}, bf16[512,384]{1,0:T(8,128)(2,1)S(1)}, u32[]{:S(2)}, u32[]{:S(2)}) collective-permute-start(bf16[512,384]{1,0:T(8,128)(2,1)S(1)} %add_convert_fusion.8), channel_id=1, source_target_pairs={{4,2},{5,3},{6,4},{7,5},{12,10},{13,11},{14,12},{15,13},{20,18},{2... | collective-permute-start | bytes 1179656 | tf_op jit(solution)/shard_map/scatter_step_2/ppermute | solution.py:248
  130.3 20.5 %collective-permute-start.38 = (bf16[512,384]{1,0:T(8,128)(2,1)}, bf16[512,384]{1,0:T(8,128)(2,1)}, u32[]{:S(2)}, u32[]{:S(2)}) collective-permute-start(bf16[512,384]{1,0:T(8,128)(2,1)} %broadcast_select_fusion.4), channel_id=1, source_target_pairs={{0,2},{1,3},{6,4},{7,5},{8,10},{9,11},{14,12},{15,13},{16,18},{17,... | collective-permute-start | bytes 1179656 | tf_op jit(solution)/shard_map/scatter_step_1/ppermute | solution.py:248
  143.4 20.6 %collective-permute-start.39 = (bf16[512,384]{1,0:T(8,128)(2,1)}, bf16[512,384]{1,0:T(8,128)(2,1)}, u32[]{:S(2)}, u32[]{:S(2)}) collective-permute-start(bf16[512,384]{1,0:T(8,128)(2,1)} %broadcast_select_fusion.3), channel_id=1, source_target_pairs={{0,2},{1,3},{6,4},{7,5},{8,10},{9,11},{14,12},{15,13},{16,18},{17,... | collective-permute-start | bytes 1179656 | tf_op jit(solution)/shard_map/scatter_step_1/ppermute | solution.py:248
  146.4 17.7 %collective-permute-start.40 = (bf16[512,384]{1,0:T(8,128)(2,1)}, bf16[512,384]{1,0:T(8,128)(2,1)}, u32[]{:S(2)}, u32[]{:S(2)}) collective-permute-start(bf16[512,384]{1,0:T(8,128)(2,1)} %add_convert_fusion.7), channel_id=1, source_target_pairs={{0,2},{1,3},{2,4},{3,5},{4,6},{5,7},{8,10},{9,11},{10,12},{11,13},... | collective-permute-start | bytes 1179656 | tf_op jit(solution)/shard_map/back/scatter_step_3/ppermute | solution.py:248
  149.3 14.8 %collective-permute-start.41 = (bf16[512,384]{1,0:T(8,128)(2,1)}, bf16[512,384]{1,0:T(8,128)(2,1)}, u32[]{:S(2)}, u32[]{:S(2)}) collective-permute-start(bf16[512,384]{1,0:T(8,128)(2,1)} %add_convert_fusion.6), channel_id=1, source_target_pairs={{2,0},{3,1},{4,2},{5,3},{6,4},{7,5},{10,8},{11,9},{12,10},{13,11},... | collective-permute-start | bytes 1179656 | tf_op jit(solution)/shard_map/back/scatter_step_3/ppermute | solution.py:248
  164.1 23.4 %collective-permute-start.42 = (bf16[512,2048]{1,0:T(8,128)(2,1)S(1)}, bf16[512,2048]{1,0:T(8,128)(2,1)S(1)}, u32[]{:S(2)}, u32[]{:S(2)}) collective-permute-start(bf16[512,2048]{1,0:T(8,128)(2,1)S(1)} %get-tuple-element.87), channel_id=1, source_target_pairs={{0,1},{1,0},{2,3},{3,2},{4,5},{5,4},{6,7},{7,6},{8,9},{9,8},{10,11... | collective-permute-start | bytes 6291464 | tf_op jit(solution)/shard_map/back/ppermute | solution.py:245
  165.3 14.0 %collective-permute-start.43 = (bf16[512,384]{1,0:T(8,128)(2,1)S(1)}, bf16[512,384]{1,0:T(8,128)(2,1)S(1)}, u32[]{:S(2)}, u32[]{:S(2)}) collective-permute-start(bf16[512,384]{1,0:T(8,128)(2,1)S(1)} %add_convert_fusion.5), channel_id=1, source_target_pairs={{0,2},{1,3},{2,4},{3,5},{8,10},{9,11},{10,12},{11,13},{16,18},{17,... | collective-permute-start | bytes 1179656 | tf_op jit(solution)/shard_map/scatter_step_2/ppermute | solution.py:248
  169.9 9.5 %collective-permute-start.44 = (bf16[512,384]{1,0:T(8,128)(2,1)S(1)}, bf16[512,384]{1,0:T(8,128)(2,1)S(1)}, u32[]{:S(2)}, u32[]{:S(2)}) collective-permute-start(bf16[512,384]{1,0:T(8,128)(2,1)S(1)} %add_convert_fusion.5), channel_id=1, source_target_pairs={{4,2},{5,3},{6,4},{7,5},{12,10},{13,11},{14,12},{15,13},{20,18},{2... | collective-permute-start | bytes 1179656 | tf_op jit(solution)/shard_map/scatter_step_2/ppermute | solution.py:248
  171.7 15.6 %collective-permute-start.46 = (bf16[512,384]{1,0:T(8,128)(2,1)S(1)}, bf16[512,384]{1,0:T(8,128)(2,1)S(1)}, u32[]{:S(2)}, u32[]{:S(2)}) collective-permute-start(bf16[512,384]{1,0:T(8,128)(2,1)S(1)} %add_convert_fusion.4), channel_id=1, source_target_pairs={{0,2},{1,3},{2,4},{3,5},{8,10},{9,11},{10,12},{11,13},{16,18},{17,... | collective-permute-start | bytes 1179656 | tf_op jit(solution)/shard_map/back/scatter_step_2/ppermute | solution.py:248
  176.7 2.8 %collective-permute-start.47 = (bf16[512,384]{1,0:T(8,128)(2,1)S(1)}, bf16[512,384]{1,0:T(8,128)(2,1)S(1)}, u32[]{:S(2)}, u32[]{:S(2)}) collective-permute-start(bf16[512,384]{1,0:T(8,128)(2,1)S(1)} %add_convert_fusion.4), channel_id=1, source_target_pairs={{4,2},{5,3},{6,4},{7,5},{12,10},{13,11},{14,12},{15,13},{20,18},{2... | collective-permute-start | bytes 1179656 | tf_op jit(solution)/shard_map/back/scatter_step_2/ppermute | solution.py:248
  179.3 8.1 %collective-permute-start.55 = (f32[256,384]{1,0:T(8,128)S(1)}, f32[256,384]{1,0:T(8,128)S(1)}, u32[]{:S(2)}, u32[]{:S(2)}) collective-permute-start(f32[256,384]{1,0:T(8,128)S(1)} %constant_dynamic-slice_fusion.2), channel_id=1, source_target_pairs={{0,1},{1,0},{2,3},{3,2},{4,5},{5,4},{6,7},{7,6},{8,9},{9,8},{10,11... | collective-permute-start | bytes 1179656 | tf_op jit(solution)/shard_map/ppermute | solution.py:245
  187.5 16.6 %collective-permute-start.48 = (bf16[512,384]{1,0:T(8,128)(2,1)S(1)}, bf16[512,384]{1,0:T(8,128)(2,1)S(1)}, u32[]{:S(2)}, u32[]{:S(2)}) collective-permute-start(bf16[512,384]{1,0:T(8,128)(2,1)S(1)} %add_convert_fusion.3), channel_id=1, source_target_pairs={{0,2},{1,3},{2,4},{3,5},{4,6},{5,7},{8,10},{9,11},{10,12},{11,13},... | collective-permute-start | bytes 1179656 | tf_op jit(solution)/shard_map/back/scatter_step_3/ppermute | solution.py:248
  196.2 12.0 %collective-permute-start.49 = (bf16[512,384]{1,0:T(8,128)(2,1)S(1)}, bf16[512,384]{1,0:T(8,128)(2,1)S(1)}, u32[]{:S(2)}, u32[]{:S(2)}) collective-permute-start(bf16[512,384]{1,0:T(8,128)(2,1)S(1)} %add_convert_fusion.2), channel_id=1, source_target_pairs={{2,0},{3,1},{4,2},{5,3},{6,4},{7,5},{10,8},{11,9},{12,10},{13,11},... | collective-permute-start | bytes 1179656 | tf_op jit(solution)/shard_map/back/scatter_step_3/ppermute | solution.py:248
  198.6 13.0 %collective-permute-start.45 = (bf16[2,128,1024]{2,1,0:T(8,128)(2,1)S(1)}, bf16[2,128,1024]{2,1,0:T(8,128)(2,1)S(1)}, u32[]{:S(2)}, u32[]{:S(2)}) collective-permute-start(bf16[2,128,1024]{2,1,0:T(8,128)(2,1)S(1)} %slice.141), channel_id=1, source_target_pairs={{0,16},{8,24},{16,0},{24,8},{1,17},{9,25},{17,1},{25,9},{2,18},{10... | collective-permute-start | bytes 1572872 | tf_op jit(solution)/shard_map/back/ppermute | solution.py:253
  199.3 13.2 %collective-permute-start.51 = (bf16[2,128,1024]{2,1,0:T(8,128)(2,1)S(1)}, bf16[2,128,1024]{2,1,0:T(8,128)(2,1)S(1)}, u32[]{:S(2)}, u32[]{:S(2)}) collective-permute-start(bf16[2,128,1024]{2,1,0:T(8,128)(2,1)S(1)} %pad_maximum_fusion), channel_id=1, source_target_pairs={{0,8},{8,0},{16,24},{24,16},{1,9},{9,1},{17,25},{25,17},{2,10},{10... | collective-permute-start | bytes 1572872 | tf_op jit(solution)/shard_map/back/ppermute | solution.py:253
  211.8 8.7 %collective-permute-start.50 = (bf16[128,1024]{1,0:T(8,128)(2,1)S(1)}, bf16[128,1024]{1,0:T(8,128)(2,1)S(1)}, u32[]{:S(2)}, u32[]{:S(2)}) collective-permute-start(bf16[128,1024]{1,0:T(8,128)(2,1)S(1)} %fusion.8), channel_id=1, source_target_pairs={{0,8},{8,0},{16,24},{24,16},{1,9},{9,1},{17,25},{25,17},{2,10},{10... | collective-permute-start | bytes 786440 | tf_op jit(solution)/shard_map/back/ppermute | solution.py:253
  212.5 8.1 %collective-permute-start.52 = (bf16[128,1024]{1,0:T(8,128)(2,1)S(1)}, bf16[128,1024]{1,0:T(8,128)(2,1)S(1)}, u32[]{:S(2)}, u32[]{:S(2)}) collective-permute-start(bf16[128,1024]{1,0:T(8,128)(2,1)S(1)} %fusion.9), channel_id=1, source_target_pairs={{0,16},{8,24},{16,0},{24,8},{1,17},{9,25},{17,1},{25,9},{2,18},{10... | collective-permute-start | bytes 786440 | tf_op jit(solution)/shard_map/back/ppermute | solution.py:253
  213.9 16.7 %collective-permute-start.56 = (f32[256,384]{1,0:T(8,128)S(1)}, f32[256,384]{1,0:T(8,128)S(1)}, u32[]{:S(2)}, u32[]{:S(2)}) collective-permute-start(f32[256,384]{1,0:T(8,128)S(1)} %constant_dynamic-slice_fusion.1), channel_id=1, source_target_pairs={{0,1},{1,0},{2,3},{3,2},{4,5},{5,4},{6,7},{7,6},{8,9},{9,8},{10,11... | collective-permute-start | bytes 1179656 | tf_op jit(solution)/shard_map/ppermute | solution.py:245
  214.0 14.3 %collective-permute-start.54 = (bf16[512,384]{1,0:T(8,128)(2,1)S(1)}, bf16[512,384]{1,0:T(8,128)(2,1)S(1)}, u32[]{:S(2)}, u32[]{:S(2)}) collective-permute-start(bf16[512,384]{1,0:T(8,128)(2,1)S(1)} %add_convert_fusion), channel_id=1, source_target_pairs={{2,0},{3,1},{4,2},{5,3},{6,4},{7,5},{10,8},{11,9},{12,10},{13,11},... | collective-permute-start | bytes 1179656 | tf_op jit(solution)/shard_map/scatter_step_3/ppermute | solution.py:248
  215.3 14.2 %collective-permute-start.53 = (bf16[512,384]{1,0:T(8,128)(2,1)S(1)}, bf16[512,384]{1,0:T(8,128)(2,1)S(1)}, u32[]{:S(2)}, u32[]{:S(2)}) collective-permute-start(bf16[512,384]{1,0:T(8,128)(2,1)S(1)} %add_convert_fusion.1), channel_id=1, source_target_pairs={{0,2},{1,3},{2,4},{3,5},{4,6},{5,7},{8,10},{9,11},{10,12},{11,13},... | collective-permute-start | bytes 1179656 | tf_op jit(solution)/shard_map/scatter_step_3/ppermute | solution.py:248
  229.7 1.8 collective-permute-start.57
  (42 other events, 145.1 us)

commit v9 on v6

--- a/solution.py
+++ b/solution.py
@@ -294,16 +294,24 @@
         (at, *g),
     )
 
-    def gather(own, before):
-        ups, downs = [own], [own]
-        for s in range(1, line):
-            up, down = ups[-1], downs[-1]
+    def forward(up, down, s):
+        with jax.named_scope(f"gather_step_{s}"):
+            return (
+                along(up, [(i, i + 1) for i in range(s - 1, line - 1)]),
+                along(down, [(i, i - 1) for i in range(1, line - s + 1)]),
+            )
+
+    firsts = [forward(a, a, 1) for a in shards]
+
+    def gather(i, before):
+        hops = [firsts[i]]
+        for s in range(2, line):
+            up, down = hops[-1]
+            waits = firsts[-1] if s == 2 and 0 < i < chunks - 1 else ()
             if s == line - 1:
-                up, down = after(up, *before), after(down, *before)
-            with jax.named_scope(f"gather_step_{s}"):
-                ups.append(along(up, [(i, i + 1) for i in range(s - 1, line - 1)]))
-                downs.append(along(down, [(i, i - 1) for i in range(1, line - s + 1)]))
-        return (own, *ups[1:], *downs[1:])
+                waits += before
+            hops.append(forward(after(up, *waits), after(down, *waits), s))
+        return (shards[i], *(h[0] for h in hops), *(h[1] for h in hops))
 
     def begin(parts):
         with jax.named_scope("scatter_step_1"):
@@ -328,7 +336,7 @@
 
     merged, both, parts, states, tie, before = [], [], [], [], (), (t[experts - 1], g[experts - 1])
     for i in range(chunks):
-        loaded = gather(shards[i], before)
+        loaded = gather(i, before)
         if i == 0:
             before = (loaded[line - 1], loaded[2 * line - 2])
         got = call(
@@ -369,23 +377,23 @@
         flops=4 * count * width * step * chunks,
     )
     with jax.named_scope("back"):
-        other = twin(after(give, *states[-1]))
+        states[0] = hop(parts[0], states[0], line - 1, ())
+        other = after(twin(after(give, *states[-1])), *states[0])
+        states[1] = hop(parts[1], states[1], line - 1, (other,))
         ret = keep.astype(F32) + other.astype(F32)
         ret = ret.reshape(experts, rows, width)
         left, right = ret[:, :, : width // 2], ret[:, :, width // 2 :]
         far = flip(left[2:].astype(BF16), 2)
         odd = flip(jnp.stack((right[1], right[3])).astype(BF16), 1)
         left = left[:2] + far.astype(F32)
-        near = flip(left[1].astype(BF16), 1)
-        last = flip((right[2] + odd[1].astype(F32)).astype(BF16), 2)
+        near = flip(after(left[1].astype(BF16), *states[1]), 1)
+        last = flip(after((right[2] + odd[1].astype(F32)).astype(BF16), *states[1]), 2)
         left = left[0] + near.astype(F32)
         right = right[0] + odd[0].astype(F32) + last.astype(F32)
         grad_input = jnp.concatenate((left, right), axis=1).astype(BF16)
-    states[-1] = hop(parts[-1], states[-1], 2, (other,))
+    states[-1] = hop(parts[-1], hop(parts[-1], states[-1], 2, (other,)), line - 1, (odd, far))
     sums = []
     for own, (up, down) in zip(parts, states):
-        for s in range(3, line):
-            up, down = hop(own, (up, down), s, (odd, far))
         sums.append(own[0].astype(F32) + up.astype(F32) + down.astype(F32))
 
     own = [lax.dynamic_slice_in_dim(s, c * feats, feats, 0) for s in sums]

time: 228 us -> 239 us (1.048)
  waiting for transfers between devices: 65.3 us -> 74 us
  starting transfers between devices: 102 us -> 105 us
    ppermute x33, waiting for transfers between devices: 44.8 us -> 53.1 us  [along(): lax.ppermute(a, 'wide', [(2 * s + i, 2 * t + i) for s, t in hops for i in...]
    ppermute x10, starting transfers between devices: 10.4 us -> 15.3 us  [flip(): return lax.ppermute(a, 'expert', [(e, e ^ bit) for e in range(experts)])]
    unnamed x97 -> x99, local copies, waits for them, and re-layouts: 11.7 us -> 10.3 us
  transfers between devices with their start and end apart: 58 -> 58, of which waited for: 18 -> 21; matrix products, arithmetic and copies ran while one was open for 5% -> 5% of each run, Pallas kernels for 15% -> 14%
where the time goes in v9:
time: 239 us; the launch traced here: 237 us
  starting transfers between devices  105 us (44%)
  waiting for transfers between devices  74 us (31%)
  Pallas kernels  32.8 us (14%)
  local copies, waits for them, and re-layouts  12.2 us (5%)
  other arithmetic  11.7 us (5%)
    ppermute x33, starting transfers between devices, along(): lax.ppermute(a, 'wide', [(2 * s + i, 2 * t + i) for s, t in hops for i in...  87.5 us
    ppermute x33, waiting for transfers between devices, along(): lax.ppermute(a, 'wide', [(2 * s + i, 2 * t + i) for s, t in hops for i in...  53.1 us
    pallas_call x7, Pallas kernels, call(): pl.pallas_call(body, out_shape=outs, in_specs=ins, out_specs=[VMEM] * len...  32.8 us
    ppermute x10, waiting for transfers between devices, flip(): return lax.ppermute(a, 'expert', [(e, e ^ bit) for e in range(experts)])  18.6 us
    ppermute x10, starting transfers between devices, flip(): return lax.ppermute(a, 'expert', [(e, e ^ bit) for e in range(experts)])  15.3 us
    unnamed x99, local copies, waits for them, and re-layouts  10.3 us
  transfers between devices with their start and end apart: 58, of which 21 were waited for; matrix products, arithmetic and copies ran while one was open for 5% of the time, Pallas kernels for 14%

profile of v9, /device:TPU:0, one launch (start us, length us, event | category | flops | bytes accessed | tf_op | source)
XLA Modules:
  0.0 237.5 jit_solution(16366358064528655287)
XLA Ops:
  0.6 3.0 %collective-permute-start = (bf16[128,2048]{1,0:T(8,128)(2,1)}, bf16[128,2048]{1,0:T(8,128)(2,1)S(1)}, u32[]{:S(2)}, u32[]{:S(2)}) collective-permute-start(bf16[128,2048]{1,0:T(8,128)(2,1)} %r_1_.5), channel_id=1, source_target_pairs={{0,8},{8,0},{16,24},{24,16},{1,9},{9,1},{17,25},{25,17},{2,10},{10... | collective-permute-start | bytes 1572872 | tf_op jit(solution)/shard_map/rows/ppermute | solution.py:253
  3.6 1.5 collective-permute-start.4
  12.5 1.3 collective-permute-start.20
  14.4 1.3 collective-permute-done.r_2_
  15.8 3.7 %collective-permute-start.17 = (bf16[512,384]{1,0:T(8,128)(2,1)S(1)}, bf16[512,384]{1,0:T(8,128)(2,1)S(1)}, u32[]{:S(2)}, u32[]{:S(2)}) collective-permute-start(bf16[512,384]{1,0:T(8,128)(2,1)S(1)} %get-tuple-element.61.r_10_), channel_id=1, source_target_pairs={{0,2},{1,3},{2,4},{3,5},{4,6},{5,7},{8,10},{9,11},{10,12},{11,13},... | collective-permute-start | bytes 1179656 | tf_op jit(solution)/shard_map/gather_step_1/ppermute | solution.py:248
  20.3 1.3 collective-permute-start.26
  22.4 4.6 %collective-permute-start.25 = (bf16[512,384]{1,0:T(8,128)(2,1)S(1)}, bf16[512,384]{1,0:T(8,128)(2,1)S(1)}, u32[]{:S(2)}, u32[]{:S(2)}) collective-permute-start(bf16[512,384]{1,0:T(8,128)(2,1)S(1)} %get-tuple-element.63.r_10_), channel_id=1, source_target_pairs={{0,2},{1,3},{2,4},{3,5},{4,6},{5,7},{8,10},{9,11},{10,12},{11,13},... | collective-permute-start | bytes 1179656 | tf_op jit(solution)/shard_map/gather_step_1/ppermute | solution.py:248
  27.0 1.3 collective-permute-start.29
  28.6 1.5 collective-permute-start.10
  30.1 4.7 %collective-permute-done.26.r_14_ = bf16[512,384]{1,0:T(8,128)(2,1)S(1)} collective-permute-done((bf16[512,384]{1,0:T(8,128)(2,1)S(1)}, bf16[512,384]{1,0:T(8,128)(2,1)S(1)}, u32[]{:S(2)}, u32[]{:S(2)}) %collective-permute-start.26) | collective-permute-done | bytes 393248 | tf_op jit(solution)/shard_map/gather_step_1/ppermute | solution.py:248
  35.8 4.1 %collective-permute-start.24 = (bf16[512,384]{1,0:T(8,128)(2,1)S(1)}, bf16[512,384]{1,0:T(8,128)(2,1)S(1)}, u32[]{:S(2)}, u32[]{:S(2)}) collective-permute-start(bf16[512,384]{1,0:T(8,128)(2,1)S(1)} %get-tuple-element.62.r_10_), channel_id=1, source_target_pairs={{0,2},{1,3},{2,4},{3,5},{4,6},{5,7},{8,10},{9,11},{10,12},{11,13},... | collective-permute-start | bytes 1179656 | tf_op jit(solution)/shard_map/gather_step_1/ppermute | solution.py:248
  39.9 2.4 %collective-permute-done.29.r_14_ = bf16[512,384]{1,0:T(8,128)(2,1)S(1)} collective-permute-done((bf16[512,384]{1,0:T(8,128)(2,1)S(1)}, bf16[512,384]{1,0:T(8,128)(2,1)S(1)}, u32[]{:S(2)}, u32[]{:S(2)}) %collective-permute-start.29) | collective-permute-done | bytes 393248 | tf_op jit(solution)/shard_map/gather_step_1/ppermute | solution.py:248
  42.3 1.3 collective-permute-start.21
  44.4 3.6 %collective-permute-done.24.r_11_ = bf16[512,384]{1,0:T(8,128)(2,1)S(1)} collective-permute-done((bf16[512,384]{1,0:T(8,128)(2,1)S(1)}, bf16[512,384]{1,0:T(8,128)(2,1)S(1)}, u32[]{:S(2)}, u32[]{:S(2)}) %collective-permute-start.24) | collective-permute-done | bytes 393248 | tf_op jit(solution)/shard_map/gather_step_1/ppermute | solution.py:248
  48.0 1.5 collective-permute-start.5
  49.5 3.6 %collective-permute-done.12.r_4_ = bf16[128,2176]{1,0:T(8,128)(2,1)S(1)} collective-permute-done((bf16[128,2176]{1,0:T(8,128)(2,1)S(1)}, bf16[128,2176]{1,0:T(8,128)(2,1)S(1)}, u32[]{:S(2)}, u32[]{:S(2)}) %collective-permute-start.12) | collective-permute-done | bytes 557088 | tf_op jit(solution)/shard_map/rows/ppermute | solution.py:253
  53.1 1.5 collective-permute-done.21.r_15_
  54.6 1.4 collective-permute-start.18
  56.8 3.9 %collective-permute-done.5.r_4_ = bf16[128,2048]{1,0:T(8,128)(2,1)} collective-permute-done((bf16[128,2048]{1,0:T(8,128)(2,1)}, bf16[128,2048]{1,0:T(8,128)(2,1)}, u32[]{:S(2)}, u32[]{:S(2)}) %collective-permute-start.5) | collective-permute-done | bytes 524320 | tf_op jit(solution)/shard_map/rows/ppermute | solution.py:253
  62.0 1.3 collective-permute-start.22
  64.2 1.4 collective-permute-start.19
  65.6 1.1 copy-done.3
  66.7 1.1 copy-done.5
  67.8 1.3 shard_map.104.r_9_
  69.2 1.4 collective-permute-start.34
  71.3 1.3 collective-permute-start.30
  72.6 7.9 %collective-permute-done.22.r_16_ = bf16[512,384]{1,0:T(8,128)(2,1)} collective-permute-done((bf16[512,384]{1,0:T(8,128)(2,1)}, bf16[512,384]{1,0:T(8,128)(2,1)}, u32[]{:S(2)}, u32[]{:S(2)}) %collective-permute-start.22) | collective-permute-done | bytes 393248 | tf_op jit(solution)/shard_map/gather_step_3/ppermute | solution.py:248
  81.3 7.4 %shard_map.105 = (bf16[512,384]{1,0:T(8,128)(2,1)S(1)}, bf16[512,384]{1,0:T(8,128)(2,1)S(1)}, bf16[512,384]{1,0:T(8,128)(2,1)S(1)}, bf16[512,384]{1,0:T(8,128)(2...) custom-call(s32[3]{0:T(128)S(1)} %pad_add_fusion.r_0_, bf16[128,2048]{1,0:T(8,128)(2,1)S(1)} %copy-done.15, ...), custom_call_target="tpu_custom_call" | custom-call | flops 3221225472 | bytes 14286860 | tf_op jit(solution)/shard_map/pallas_call | solution.py:100
  88.9 12.1 %collective-permute-start.23 = (bf16[512,384]{1,0:T(8,128)(2,1)S(1)}, bf16[512,384]{1,0:T(8,128)(2,1)S(1)}, u32[]{:S(2)}, u32[]{:S(2)}) collective-permute-start(bf16[512,384]{1,0:T(8,128)(2,1)S(1)} %broadcast_select_fusion.5), channel_id=1, source_target_pairs={{0,2},{1,3},{6,4},{7,5},{8,10},{9,11},{14,12},{15,13},{16,18},{17,... | collective-permute-start | bytes 1179656 | tf_op jit(solution)/shard_map/scatter_step_1/ppermute | solution.py:248
  101.0 1.4 collective-permute-start.31
  103.2 1.3 collective-permute-start.35
  105.2 3.6 %collective-permute-done.23 = bf16[512,384]{1,0:T(8,128)(2,1)S(1)} collective-permute-done((bf16[512,384]{1,0:T(8,128)(2,1)S(1)}, bf16[512,384]{1,0:T(8,128)(2,1)S(1)}, u32[]{:S(2)}, u32[]{:S(2)}) %collective-permute-start.23) | collective-permute-done | bytes 393248 | tf_op jit(solution)/shard_map/scatter_step_1/ppermute | solution.py:248
  108.8 6.3 %collective-permute-done.31.r_16_ = bf16[512,384]{1,0:T(8,128)(2,1)S(1)} collective-permute-done((bf16[512,384]{1,0:T(8,128)(2,1)S(1)}, bf16[512,384]{1,0:T(8,128)(2,1)S(1)}, u32[]{:S(2)}, u32[]{:S(2)}) %collective-permute-start.31) | collective-permute-done | bytes 393248 | tf_op jit(solution)/shard_map/gather_step_3/ppermute | solution.py:248
  115.1 7.7 %shard_map.106 = (bf16[512,384]{1,0:T(8,128)(2,1)S(1)}, bf16[512,384]{1,0:T(8,128)(2,1)S(1)}, bf16[512,384]{1,0:T(8,128)(2,1)S(1)}, bf16[512,384]{1,0:T(8,128)(2...) custom-call(s32[3]{0:T(128)S(1)} %pad_add_fusion.r_0_, bf16[128,2048]{1,0:T(8,128)(2,1)S(1)} %copy-done.15, ...), custom_call_target="tpu_custom_call" | custom-call | flops 3221225472 | bytes 14286860 | tf_op jit(solution)/shard_map/pallas_call | solution.py:100
  122.9 1.5 collective-permute-start.36
  124.5 7.5 %shard_map.107 = (bf16[512,384]{1,0:T(8,128)(2,1)S(1)}, bf16[512,384]{1,0:T(8,128)(2,1)S(1)}, bf16[512,384]{1,0:T(8,128)(2,1)S(1)}, bf16[512,384]{1,0:T(8,128)(2...) custom-call(s32[3]{0:T(128)S(1)} %pad_add_fusion.r_0_, bf16[128,2048]{1,0:T(8,128)(2,1)S(1)} %copy-done.15, ...), custom_call_target="tpu_custom_call" | custom-call | flops 3221225472 | bytes 14286860 | tf_op jit(solution)/shard_map/pallas_call | solution.py:100
  132.2 2.0 collective-permute-start.37
  135.0 6.2 %collective-permute-start.39 = (bf16[512,384]{1,0:T(8,128)(2,1)S(1)}, bf16[512,384]{1,0:T(8,128)(2,1)S(1)}, u32[]{:S(2)}, u32[]{:S(2)}) collective-permute-start(bf16[512,384]{1,0:T(8,128)(2,1)S(1)} %broadcast_select_fusion.3), channel_id=1, source_target_pairs={{0,2},{1,3},{6,4},{7,5},{8,10},{9,11},{14,12},{15,13},{16,18},{17,... | collective-permute-start | bytes 1179656 | tf_op jit(solution)/shard_map/scatter_step_1/ppermute | solution.py:248
  142.0 2.1 collective-permute-start.41
  144.2 7.4 %shard_map.108 = (bf16[512,2048]{1,0:T(8,128)(2,1)S(1)}, bf16[512,2048]{1,0:T(8,128)(2,1)}) custom-call(bf16[1024,256]{1,0:T(8,128)(2,1)S(1)} %copy-done.39, bf16[1024,256]{1,0:T(8,128)(2,1)S(1)} %get-tuple-element.77.r_1_, bf16[1024,256]{1,0:T(8,128)(2,1)S(1)} %get-tuple-element.84.r_2_, bf16[2048,256]{1,0:T(8,128)(2,1)S(1)} %get-tuple-element.85.r_3_, ...), custom_call_target="tpu_custom_call" | custom-call | flops 3221225472 | bytes 8912896 | tf_op jit(solution)/shard_map/pallas_call | solution.py:100
  152.5 1.3 collective-permute-start.44
  153.8 2.5 %collective-permute-done.41 = bf16[512,384]{1,0:T(8,128)(2,1)S(1)} collective-permute-done((bf16[512,384]{1,0:T(8,128)(2,1)S(1)}, bf16[512,384]{1,0:T(8,128)(2,1)S(1)}, u32[]{:S(2)}, u32[]{:S(2)}) %collective-permute-start.41) | collective-permute-done | bytes 393248 | tf_op jit(solution)/shard_map/scatter_step_2/ppermute | solution.py:248
  157.2 8.0 %collective-permute-start.42 = (bf16[512,384]{1,0:T(8,128)(2,1)}, bf16[512,384]{1,0:T(8,128)(2,1)}, u32[]{:S(2)}, u32[]{:S(2)}) collective-permute-start(bf16[512,384]{1,0:T(8,128)(2,1)} %add_convert_fusion.6), channel_id=1, source_target_pairs={{0,2},{1,3},{2,4},{3,5},{4,6},{5,7},{8,10},{9,11},{10,12},{11,13},... | collective-permute-start | bytes 1179656 | tf_op jit(solution)/shard_map/back/scatter_step_3/ppermute | solution.py:248
  165.2 1.3 add_convert_fusion.2
  166.5 5.2 %collective-permute-done.44 = bf16[512,384]{1,0:T(8,128)(2,1)} collective-permute-done((bf16[512,384]{1,0:T(8,128)(2,1)}, bf16[512,384]{1,0:T(8,128)(2,1)}, u32[]{:S(2)}, u32[]{:S(2)}) %collective-permute-start.44) | collective-permute-done | bytes 393248 | tf_op jit(solution)/shard_map/back/scatter_step_3/ppermute | solution.py:248
  171.7 2.0 collective-permute-done.42
  173.7 1.4 convert_add_fusion.3
  175.5 1.5 collective-permute-done.55
  177.0 4.4 %collective-permute-start.51 = (bf16[512,384]{1,0:T(8,128)(2,1)S(1)}, bf16[512,384]{1,0:T(8,128)(2,1)S(1)}, u32[]{:S(2)}, u32[]{:S(2)}) collective-permute-start(bf16[512,384]{1,0:T(8,128)(2,1)S(1)} %add_convert_fusion.2), channel_id=1, source_target_pairs={{0,2},{1,3},{2,4},{3,5},{8,10},{9,11},{10,12},{11,13},{16,18},{17,... | collective-permute-start | bytes 1179656 | tf_op jit(solution)/shard_map/scatter_step_2/ppermute | solution.py:248
  182.1 1.3 collective-permute-start.47
  183.4 4.9 %collective-permute-start.46 = (bf16[512,384]{1,0:T(8,128)(2,1)S(1)}, bf16[512,384]{1,0:T(8,128)(2,1)S(1)}, u32[]{:S(2)}, u32[]{:S(2)}) collective-permute-start(bf16[512,384]{1,0:T(8,128)(2,1)S(1)} %add_convert_fusion.4), channel_id=1, source_target_pairs={{0,2},{1,3},{2,4},{3,5},{4,6},{5,7},{8,10},{9,11},{10,12},{11,13},... | collective-permute-start | bytes 1179656 | tf_op jit(solution)/shard_map/back/scatter_step_3/ppermute | solution.py:248
  188.3 2.3 convert_add_fusion
  191.1 1.6 collective-permute-start.49
  192.7 2.8 %collective-permute-done.47 = bf16[512,384]{1,0:T(8,128)(2,1)S(1)} collective-permute-done((bf16[512,384]{1,0:T(8,128)(2,1)S(1)}, bf16[512,384]{1,0:T(8,128)(2,1)S(1)}, u32[]{:S(2)}, u32[]{:S(2)}) %collective-permute-start.47) | collective-permute-done | bytes 393248 | tf_op jit(solution)/shard_map/back/scatter_step_3/ppermute | solution.py:248
  195.5 1.5 collective-permute-start.45
  197.0 1.5 collective-permute-done.46
  198.8 9.7 %collective-permute-done.45 = bf16[2,128,1024]{2,1,0:T(8,128)(2,1)S(1)} collective-permute-done((bf16[2,128,1024]{2,1,0:T(8,128)(2,1)S(1)}, bf16[2,128,1024]{2,1,0:T(8,128)(2,1)S(1)}, u32[]{:S(2)}, u32[]{:S(2)}) %collective-permute-start.45) | collective-permute-done | bytes 524320 | tf_op jit(solution)/shard_map/back/ppermute | solution.py:253
  208.8 1.6 collective-permute-start.48
  210.5 1.6 collective-permute-start.50
  212.1 10.5 %collective-permute-start.52 = (bf16[512,384]{1,0:T(8,128)(2,1)S(1)}, bf16[512,384]{1,0:T(8,128)(2,1)S(1)}, u32[]{:S(2)}, u32[]{:S(2)}) collective-permute-start(bf16[512,384]{1,0:T(8,128)(2,1)S(1)} %add_convert_fusion.1), channel_id=1, source_target_pairs={{0,2},{1,3},{2,4},{3,5},{4,6},{5,7},{8,10},{9,11},{10,12},{11,13},... | collective-permute-start | bytes 1179656 | tf_op jit(solution)/shard_map/scatter_step_3/ppermute | solution.py:248
  222.6 1.3 collective-permute-start.54
  224.1 4.5 %collective-permute-done.52 = bf16[512,384]{1,0:T(8,128)(2,1)S(1)} collective-permute-done((bf16[512,384]{1,0:T(8,128)(2,1)S(1)}, bf16[512,384]{1,0:T(8,128)(2,1)S(1)}, u32[]{:S(2)}, u32[]{:S(2)}) %collective-permute-start.52) | collective-permute-done | bytes 393248 | tf_op jit(solution)/shard_map/scatter_step_3/ppermute | solution.py:248
  228.6 4.1 %collective-permute-done.54 = bf16[512,384]{1,0:T(8,128)(2,1)S(1)} collective-permute-done((bf16[512,384]{1,0:T(8,128)(2,1)S(1)}, bf16[512,384]{1,0:T(8,128)(2,1)S(1)}, u32[]{:S(2)}, u32[]{:S(2)}) %collective-permute-start.54) | collective-permute-done | bytes 393248 | tf_op jit(solution)/shard_map/scatter_step_3/ppermute | solution.py:248
  236.1 1.3 broadcast_select_fusion
  (198 shorter events, 26.5 us)
Async XLA Ops:
  0.6 15.1 %collective-permute-start = (bf16[128,2048]{1,0:T(8,128)(2,1)}, bf16[128,2048]{1,0:T(8,128)(2,1)S(1)}, u32[]{:S(2)}, u32[]{:S(2)}) collective-permute-start(bf16[128,2048]{1,0:T(8,128)(2,1)} %r_1_.5), channel_id=1, source_target_pairs={{0,8},{8,0},{16,24},{24,16},{1,9},{9,1},{17,25},{25,17},{2,10},{10... | collective-permute-start | bytes 1572872 | tf_op jit(solution)/shard_map/rows/ppermute | solution.py:253
  3.6 16.7 %collective-permute-start.4 = (bf16[128,2048]{1,0:T(8,128)(2,1)}, bf16[128,2048]{1,0:T(8,128)(2,1)}, u32[]{:S(2)}, u32[]{:S(2)}) collective-permute-start(bf16[128,2048]{1,0:T(8,128)(2,1)} %r_1_.5), channel_id=1, source_target_pairs={{0,16},{8,24},{16,0},{24,8},{1,17},{9,25},{17,1},{25,9},{2,18},{10... | collective-permute-start | bytes 1572872 | tf_op jit(solution)/shard_map/rows/ppermute | solution.py:253
  9.0 2.3 collective-permute-start.1
  9.1 2.8 %collective-permute-start.2 = (bf16[256,384]{1,0:T(8,128)(2,1)S(1)}, bf16[256,384]{1,0:T(8,128)(2,1)S(1)}, u32[]{:S(2)}, u32[]{:S(2)}) collective-permute-start(bf16[256,384]{1,0:T(8,128)(2,1)S(1)} %get-tuple-element.59), channel_id=1, source_target_pairs={{0,1},{1,0},{2,3},{3,2},{4,5},{5,4},{6,7},{7,6},{8,9},{9,8},{10,11... | collective-permute-start | bytes 589832 | tf_op jit(solution)/shard_map/ppermute | solution.py:245
  9.6 2.3 collective-permute-start.3
  11.3 10.3 %collective-permute-start.6 = (bf16[128,2048]{1,0:T(8,128)(2,1)}, bf16[128,2048]{1,0:T(8,128)(2,1)S(1)}, u32[]{:S(2)}, u32[]{:S(2)}) collective-permute-start(bf16[128,2048]{1,0:T(8,128)(2,1)} %r_1_.5), channel_id=1, source_target_pairs={{0,1},{1,0},{2,3},{3,2},{4,5},{5,4},{6,7},{7,6},{8,9},{9,8},{10,11... | collective-permute-start | bytes 1572872 | tf_op jit(solution)/shard_map/rows/ppermute | solution.py:245
  12.5 50.9 %copy-start.20 = (bf16[512,384]{1,0:T(8,128)(2,1)}, bf16[512,384]{1,0:T(8,128)(2,1)S(1)}, u32[]{:S(2)}) copy-start(bf16[512,384]{1,0:T(8,128)(2,1)S(1)} %get-tuple-element.63.r_10_) | copy-start | bytes 1179652
  12.5 50.9 %copy-start.22 = (bf16[512,384]{1,0:T(8,128)(2,1)}, bf16[512,384]{1,0:T(8,128)(2,1)S(1)}, u32[]{:S(2)}) copy-start(bf16[512,384]{1,0:T(8,128)(2,1)S(1)} %get-tuple-element.62.r_10_) | copy-start | bytes 1179652
  12.5 14.5 %collective-permute-start.20 = (bf16[512,384]{1,0:T(8,128)(2,1)S(1)}, bf16[512,384]{1,0:T(8,128)(2,1)S(1)}, u32[]{:S(2)}, u32[]{:S(2)}) collective-permute-start(bf16[512,384]{1,0:T(8,128)(2,1)S(1)} %get-tuple-element.61.r_10_), channel_id=1, source_target_pairs={{2,0},{3,1},{4,2},{5,3},{6,4},{7,5},{10,8},{11,9},{12,10},{13,11},... | collective-permute-start | bytes 1179656 | tf_op jit(solution)/shard_map/gather_step_1/ppermute | solution.py:248
  13.9 20.9 %collective-permute-start.11 = (bf16[128,2176]{1,0:T(8,128)(2,1)S(1)}, bf16[128,2176]{1,0:T(8,128)(2,1)S(1)}, u32[]{:S(2)}, u32[]{:S(2)}) collective-permute-start(bf16[128,2176]{1,0:T(8,128)(2,1)S(1)} %fusion.1.r_1_), channel_id=1, source_target_pairs={{0,16},{8,24},{16,0},{24,8},{1,17},{9,25},{17,1},{25,9},{2,18},{10... | collective-permute-start | bytes 1671176 | tf_op jit(solution)/shard_map/rows/ppermute | solution.py:253
  15.8 12.8 %collective-permute-start.17 = (bf16[512,384]{1,0:T(8,128)(2,1)S(1)}, bf16[512,384]{1,0:T(8,128)(2,1)S(1)}, u32[]{:S(2)}, u32[]{:S(2)}) collective-permute-start(bf16[512,384]{1,0:T(8,128)(2,1)S(1)} %get-tuple-element.61.r_10_), channel_id=1, source_target_pairs={{0,2},{1,3},{2,4},{3,5},{4,6},{5,7},{8,10},{9,11},{10,12},{11,13},... | collective-permute-start | bytes 1179656 | tf_op jit(solution)/shard_map/gather_step_1/ppermute | solution.py:248
  20.3 14.5 %collective-permute-start.26 = (bf16[512,384]{1,0:T(8,128)(2,1)S(1)}, bf16[512,384]{1,0:T(8,128)(2,1)S(1)}, u32[]{:S(2)}, u32[]{:S(2)}) collective-permute-start(bf16[512,384]{1,0:T(8,128)(2,1)S(1)} %get-tuple-element.63.r_10_), channel_id=1, source_target_pairs={{2,0},{3,1},{4,2},{5,3},{6,4},{7,5},{10,8},{11,9},{12,10},{13,11},... | collective-permute-start | bytes 1179656 | tf_op jit(solution)/shard_map/gather_step_1/ppermute | solution.py:248
  22.4 13.4 %collective-permute-start.25 = (bf16[512,384]{1,0:T(8,128)(2,1)S(1)}, bf16[512,384]{1,0:T(8,128)(2,1)S(1)}, u32[]{:S(2)}, u32[]{:S(2)}) collective-permute-start(bf16[512,384]{1,0:T(8,128)(2,1)S(1)} %get-tuple-element.63.r_10_), channel_id=1, source_target_pairs={{0,2},{1,3},{2,4},{3,5},{4,6},{5,7},{8,10},{9,11},{10,12},{11,13},... | collective-permute-start | bytes 1179656 | tf_op jit(solution)/shard_map/gather_step_1/ppermute | solution.py:248
  27.0 15.4 %collective-permute-start.29 = (bf16[512,384]{1,0:T(8,128)(2,1)S(1)}, bf16[512,384]{1,0:T(8,128)(2,1)S(1)}, u32[]{:S(2)}, u32[]{:S(2)}) collective-permute-start(bf16[512,384]{1,0:T(8,128)(2,1)S(1)} %get-tuple-element.62.r_10_), channel_id=1, source_target_pairs={{2,0},{3,1},{4,2},{5,3},{6,4},{7,5},{10,8},{11,9},{12,10},{13,11},... | collective-permute-start | bytes 1179656 | tf_op jit(solution)/shard_map/gather_step_1/ppermute | solution.py:248
  28.6 15.8 %collective-permute-start.10 = (bf16[128,2176]{1,0:T(8,128)(2,1)S(1)}, bf16[128,2176]{1,0:T(8,128)(2,1)S(1)}, u32[]{:S(2)}, u32[]{:S(2)}) collective-permute-start(bf16[128,2176]{1,0:T(8,128)(2,1)S(1)} %fusion.1.r_1_), channel_id=1, source_target_pairs={{0,8},{8,0},{16,24},{24,16},{1,9},{9,1},{17,25},{25,17},{2,10},{10... | collective-permute-start | bytes 1671176 | tf_op jit(solution)/shard_map/rows/ppermute | solution.py:253
  34.8 28.6 %copy-start.24 = (bf16[512,384]{1,0:T(8,128)(2,1)}, bf16[512,384]{1,0:T(8,128)(2,1)S(1)}, u32[]{:S(2)}) copy-start(bf16[512,384]{1,0:T(8,128)(2,1)S(1)} %collective-permute-done.26.r_14_) | copy-start | bytes 1179652
  34.8 14.7 %collective-permute-start.13 = (bf16[128,2176]{1,0:T(8,128)(2,1)S(1)}, bf16[128,2176]{1,0:T(8,128)(2,1)S(1)}, u32[]{:S(2)}, u32[]{:S(2)}) collective-permute-start(bf16[128,2176]{1,0:T(8,128)(2,1)S(1)} %fusion.1.r_1_), channel_id=1, source_target_pairs={{0,1},{1,0},{2,3},{3,2},{4,5},{5,4},{6,7},{7,6},{8,9},{9,8},{10,11... | collective-permute-start | bytes 1671176 | tf_op jit(solution)/shard_map/rows/ppermute | solution.py:245
  34.8 18.3 %collective-permute-start.12 = (bf16[128,2176]{1,0:T(8,128)(2,1)S(1)}, bf16[128,2176]{1,0:T(8,128)(2,1)S(1)}, u32[]{:S(2)}, u32[]{:S(2)}) collective-permute-start(bf16[128,2176]{1,0:T(8,128)(2,1)S(1)} %collective-permute-done.11.r_3_), channel_id=1, source_target_pairs={{0,8},{8,0},{16,24},{24,16},{1,9},{9,1},{17,25},{25,17},{2,10},{10... | collective-permute-start | bytes 1671176 | tf_op jit(solution)/shard_map/rows/ppermute | solution.py:253
  35.8 27.6 %copy-start.26 = (bf16[512,384]{1,0:T(8,128)(2,1)}, bf16[512,384]{1,0:T(8,128)(2,1)S(1)}, u32[]{:S(2)}) copy-start(bf16[512,384]{1,0:T(8,128)(2,1)S(1)} %collective-permute-done.25.r_11_) | copy-start | bytes 1179652
  35.8 12.1 %collective-permute-start.24 = (bf16[512,384]{1,0:T(8,128)(2,1)S(1)}, bf16[512,384]{1,0:T(8,128)(2,1)S(1)}, u32[]{:S(2)}, u32[]{:S(2)}) collective-permute-start(bf16[512,384]{1,0:T(8,128)(2,1)S(1)} %get-tuple-element.62.r_10_), channel_id=1, source_target_pairs={{0,2},{1,3},{2,4},{3,5},{4,6},{5,7},{8,10},{9,11},{10,12},{11,13},... | collective-permute-start | bytes 1179656 | tf_op jit(solution)/shard_map/gather_step_1/ppermute | solution.py:248
  42.3 12.2 %collective-permute-start.21 = (bf16[512,384]{1,0:T(8,128)(2,1)S(1)}, bf16[512,384]{1,0:T(8,128)(2,1)}, u32[]{:S(2)}, u32[]{:S(2)}) collective-permute-start(bf16[512,384]{1,0:T(8,128)(2,1)S(1)} %collective-permute-done.20.r_14_), channel_id=1, source_target_pairs={{2,0},{3,1},{4,2},{5,3},{10,8},{11,9},{12,10},{13,11},{18,16},{19,... | collective-permute-start | bytes 1179656 | tf_op jit(solution)/shard_map/gather_step_2/ppermute | solution.py:248
  44.4 16.3 %collective-permute-start.14 = (bf16[128,2176]{1,0:T(8,128)(2,1)S(1)}, bf16[128,2176]{1,0:T(8,128)(2,1)S(1)}, u32[]{:S(2)}, u32[]{:S(2)}) collective-permute-start(bf16[128,2176]{1,0:T(8,128)(2,1)S(1)} %collective-permute-done.10.r_2_), channel_id=1, source_target_pairs={{0,1},{1,0},{2,3},{3,2},{4,5},{5,4},{6,7},{7,6},{8,9},{9,8},{10,11... | collective-permute-start | bytes 1671176 | tf_op jit(solution)/shard_map/rows/ppermute | solution.py:245
  48.0 12.8 %collective-permute-start.5 = (bf16[128,2048]{1,0:T(8,128)(2,1)}, bf16[128,2048]{1,0:T(8,128)(2,1)}, u32[]{:S(2)}, u32[]{:S(2)}) collective-permute-start(bf16[128,2048]{1,0:T(8,128)(2,1)} %copy-done.16), channel_id=1, source_target_pairs={{0,16},{8,24},{16,0},{24,8},{1,17},{9,25},{17,1},{25,9},{2,18},{10... | collective-permute-start | bytes 1572872 | tf_op jit(solution)/shard_map/rows/ppermute | solution.py:253
  49.5 11.8 %collective-permute-start.15 = (bf16[128,2176]{1,0:T(8,128)(2,1)S(1)}, bf16[128,2176]{1,0:T(8,128)(2,1)S(1)}, u32[]{:S(2)}, u32[]{:S(2)}) collective-permute-start(bf16[128,2176]{1,0:T(8,128)(2,1)S(1)} %collective-permute-done.11.r_3_), channel_id=1, source_target_pairs={{0,1},{1,0},{2,3},{3,2},{4,5},{5,4},{6,7},{7,6},{8,9},{9,8},{10,11... | collective-permute-start | bytes 1671176 | tf_op jit(solution)/shard_map/rows/ppermute | solution.py:245
  53.1 10.3 %collective-permute-start.16 = (bf16[128,2176]{1,0:T(8,128)(2,1)S(1)}, bf16[128,2176]{1,0:T(8,128)(2,1)S(1)}, u32[]{:S(2)}, u32[]{:S(2)}) collective-permute-start(bf16[128,2176]{1,0:T(8,128)(2,1)S(1)} %collective-permute-done.12.r_4_), channel_id=1, source_target_pairs={{0,1},{1,0},{2,3},{3,2},{4,5},{5,4},{6,7},{7,6},{8,9},{9,8},{10,11... | collective-permute-start | bytes 1671176 | tf_op jit(solution)/shard_map/rows/ppermute | solution.py:245
  54.6 2.2 collective-permute-start.18
  56.8 12.3 %collective-permute-start.8 = (bf16[128,2048]{1,0:T(8,128)(2,1)}, bf16[128,2048]{1,0:T(8,128)(2,1)}, u32[]{:S(2)}, u32[]{:S(2)}) collective-permute-start(bf16[128,2048]{1,0:T(8,128)(2,1)} %collective-permute-done.4.r_3_), channel_id=1, source_target_pairs={{0,1},{1,0},{2,3},{3,2},{4,5},{5,4},{6,7},{7,6},{8,9},{9,8},{10,11... | collective-permute-start | bytes 1572872 | tf_op jit(solution)/shard_map/rows/ppermute | solution.py:245
  60.7 9.9 %collective-permute-start.7 = (bf16[128,2048]{1,0:T(8,128)(2,1)}, bf16[128,2048]{1,0:T(8,128)(2,1)}, u32[]{:S(2)}, u32[]{:S(2)}) collective-permute-start(bf16[128,2048]{1,0:T(8,128)(2,1)} %copy-done.16), channel_id=1, source_target_pairs={{0,1},{1,0},{2,3},{3,2},{4,5},{5,4},{6,7},{7,6},{8,9},{9,8},{10,11... | collective-permute-start | bytes 1572872 | tf_op jit(solution)/shard_map/rows/ppermute | solution.py:245
  60.7 10.6 %collective-permute-start.9 = (bf16[128,2048]{1,0:T(8,128)(2,1)}, bf16[128,2048]{1,0:T(8,128)(2,1)}, u32[]{:S(2)}, u32[]{:S(2)}) collective-permute-start(bf16[128,2048]{1,0:T(8,128)(2,1)} %collective-permute-done.5.r_4_), channel_id=1, source_target_pairs={{0,1},{1,0},{2,3},{3,2},{4,5},{5,4},{6,7},{7,6},{8,9},{9,8},{10,11... | collective-permute-start | bytes 1572872 | tf_op jit(solution)/shard_map/rows/ppermute | solution.py:245
  62.0 18.6 %collective-permute-start.22 = (bf16[512,384]{1,0:T(8,128)(2,1)}, bf16[512,384]{1,0:T(8,128)(2,1)}, u32[]{:S(2)}, u32[]{:S(2)}) collective-permute-start(bf16[512,384]{1,0:T(8,128)(2,1)} %collective-permute-done.21.r_15_), channel_id=1, source_target_pairs={{2,0},{3,1},{10,8},{11,9},{18,16},{19,17},{26,24},{27,25}} | collective-permute-start | bytes 1179656 | tf_op jit(solution)/shard_map/gather_step_3/ppermute | solution.py:248
  64.2 17.1 %collective-permute-start.19 = (bf16[512,384]{1,0:T(8,128)(2,1)}, bf16[512,384]{1,0:T(8,128)(2,1)}, u32[]{:S(2)}, u32[]{:S(2)}) collective-permute-start(bf16[512,384]{1,0:T(8,128)(2,1)} %collective-permute-done.18.r_12_), channel_id=1, source_target_pairs={{4,6},{5,7},{12,14},{13,15},{20,22},{21,23},{28,30},{29,31}} | collective-permute-start | bytes 1179656 | tf_op jit(solution)/shard_map/gather_step_3/ppermute | solution.py:248
  69.1 46.0 %copy-start.23 = (bf16[512,384]{1,0:T(8,128)(2,1)S(1)}, bf16[512,384]{1,0:T(8,128)(2,1)}, u32[]{:S(2)}) copy-start(bf16[512,384]{1,0:T(8,128)(2,1)} %copy-done.22) | copy-start | bytes 1179652
  69.2 34.0 %collective-permute-start.34 = (bf16[512,384]{1,0:T(8,128)(2,1)S(1)}, bf16[512,384]{1,0:T(8,128)(2,1)S(1)}, u32[]{:S(2)}, u32[]{:S(2)}) collective-permute-start(bf16[512,384]{1,0:T(8,128)(2,1)S(1)} %copy-done.25), channel_id=1, source_target_pairs={{2,0},{3,1},{4,2},{5,3},{10,8},{11,9},{12,10},{13,11},{18,16},{19,... | collective-permute-start | bytes 1179656 | tf_op jit(solution)/shard_map/gather_step_2/ppermute | solution.py:248
  70.6 33.9 %collective-permute-start.32 = (bf16[512,384]{1,0:T(8,128)(2,1)S(1)}, bf16[512,384]{1,0:T(8,128)(2,1)S(1)}, u32[]{:S(2)}, u32[]{:S(2)}) collective-permute-start(bf16[512,384]{1,0:T(8,128)(2,1)S(1)} %copy-done.27), channel_id=1, source_target_pairs={{2,4},{3,5},{4,6},{5,7},{10,12},{11,13},{12,14},{13,15},{18,20},{1... | collective-permute-start | bytes 1179656 | tf_op jit(solution)/shard_map/gather_step_2/ppermute | solution.py:248
  71.3 29.7 %collective-permute-start.30 = (bf16[512,384]{1,0:T(8,128)(2,1)S(1)}, bf16[512,384]{1,0:T(8,128)(2,1)S(1)}, u32[]{:S(2)}, u32[]{:S(2)}) collective-permute-start(bf16[512,384]{1,0:T(8,128)(2,1)S(1)} %copy-done.29), channel_id=1, source_target_pairs={{2,0},{3,1},{4,2},{5,3},{10,8},{11,9},{12,10},{13,11},{18,16},{19,... | collective-permute-start | bytes 1179656 | tf_op jit(solution)/shard_map/gather_step_2/ppermute | solution.py:248
  80.6 21.9 %collective-permute-start.27 = (bf16[512,384]{1,0:T(8,128)(2,1)S(1)}, bf16[512,384]{1,0:T(8,128)(2,1)S(1)}, u32[]{:S(2)}, u32[]{:S(2)}) collective-permute-start(bf16[512,384]{1,0:T(8,128)(2,1)S(1)} %copy-done.35), channel_id=1, source_target_pairs={{2,4},{3,5},{4,6},{5,7},{10,12},{11,13},{12,14},{13,15},{18,20},{1... | collective-permute-start | bytes 1179656 | tf_op jit(solution)/shard_map/gather_step_2/ppermute | solution.py:248
  88.8 26.3 %copy-start.14 = (bf16[512,384]{1,0:T(8,128)(2,1)}, bf16[512,384]{1,0:T(8,128)(2,1)S(1)}, u32[]{:S(2)}) copy-start(bf16[512,384]{1,0:T(8,128)(2,1)S(1)} %get-tuple-element.99) | copy-start | bytes 1179652
  88.9 19.9 %collective-permute-start.23 = (bf16[512,384]{1,0:T(8,128)(2,1)S(1)}, bf16[512,384]{1,0:T(8,128)(2,1)S(1)}, u32[]{:S(2)}, u32[]{:S(2)}) collective-permute-start(bf16[512,384]{1,0:T(8,128)(2,1)S(1)} %broadcast_select_fusion.5), channel_id=1, source_target_pairs={{0,2},{1,3},{6,4},{7,5},{8,10},{9,11},{14,12},{15,13},{16,18},{17,... | collective-permute-start | bytes 1179656 | tf_op jit(solution)/shard_map/scatter_step_1/ppermute | solution.py:248
  101.0 14.1 %collective-permute-start.31 = (bf16[512,384]{1,0:T(8,128)(2,1)S(1)}, bf16[512,384]{1,0:T(8,128)(2,1)S(1)}, u32[]{:S(2)}, u32[]{:S(2)}) collective-permute-start(bf16[512,384]{1,0:T(8,128)(2,1)S(1)} %collective-permute-done.30.r_15_), channel_id=1, source_target_pairs={{2,0},{3,1},{10,8},{11,9},{18,16},{19,17},{26,24},{27,25}} | collective-permute-start | bytes 1179656 | tf_op jit(solution)/shard_map/gather_step_3/ppermute | solution.py:248
  102.5 12.6 %collective-permute-start.28 = (bf16[512,384]{1,0:T(8,128)(2,1)S(1)}, bf16[512,384]{1,0:T(8,128)(2,1)S(1)}, u32[]{:S(2)}, u32[]{:S(2)}) collective-permute-start(bf16[512,384]{1,0:T(8,128)(2,1)S(1)} %collective-permute-done.27.r_12_), channel_id=1, source_target_pairs={{4,6},{5,7},{12,14},{13,15},{20,22},{21,23},{28,30},{29,31}} | collective-permute-start | bytes 1179656 | tf_op jit(solution)/shard_map/gather_step_3/ppermute | solution.py:248
  103.2 21.3 %collective-permute-start.35 = (bf16[512,384]{1,0:T(8,128)(2,1)S(1)}, bf16[512,384]{1,0:T(8,128)(2,1)S(1)}, u32[]{:S(2)}, u32[]{:S(2)}) collective-permute-start(bf16[512,384]{1,0:T(8,128)(2,1)S(1)} %collective-permute-done.34.r_15_), channel_id=1, source_target_pairs={{2,0},{3,1},{10,8},{11,9},{18,16},{19,17},{26,24},{27,25}} | collective-permute-start | bytes 1179656 | tf_op jit(solution)/shard_map/gather_step_3/ppermute | solution.py:248
  104.5 20.0 %collective-permute-start.33 = (bf16[512,384]{1,0:T(8,128)(2,1)S(1)}, bf16[512,384]{1,0:T(8,128)(2,1)S(1)}, u32[]{:S(2)}, u32[]{:S(2)}) collective-permute-start(bf16[512,384]{1,0:T(8,128)(2,1)S(1)} %collective-permute-done.32.r_12_), channel_id=1, source_target_pairs={{4,6},{5,7},{12,14},{13,15},{20,22},{21,23},{28,30},{29,31}} | collective-permute-start | bytes 1179656 | tf_op jit(solution)/shard_map/gather_step_3/ppermute | solution.py:248
  122.9 9.2 %collective-permute-start.36 = (bf16[512,384]{1,0:T(8,128)(2,1)S(1)}, bf16[512,384]{1,0:T(8,128)(2,1)S(1)}, u32[]{:S(2)}, u32[]{:S(2)}) collective-permute-start(bf16[512,384]{1,0:T(8,128)(2,1)S(1)} %broadcast_select_fusion.4), channel_id=1, source_target_pairs={{0,2},{1,3},{6,4},{7,5},{8,10},{9,11},{14,12},{15,13},{16,18},{17,... | collective-permute-start | bytes 1179656 | tf_op jit(solution)/shard_map/scatter_step_1/ppermute | solution.py:248
  132.2 11.9 %collective-permute-start.37 = (bf16[512,384]{1,0:T(8,128)(2,1)S(1)}, bf16[512,384]{1,0:T(8,128)(2,1)S(1)}, u32[]{:S(2)}, u32[]{:S(2)}) collective-permute-start(bf16[512,384]{1,0:T(8,128)(2,1)S(1)} %add_convert_fusion.8), channel_id=1, source_target_pairs={{0,2},{1,3},{2,4},{3,5},{8,10},{9,11},{10,12},{11,13},{16,18},{17,... | collective-permute-start | bytes 1179656 | tf_op jit(solution)/shard_map/scatter_step_2/ppermute | solution.py:248
  134.2 9.9 %collective-permute-start.38 = (bf16[512,384]{1,0:T(8,128)(2,1)S(1)}, bf16[512,384]{1,0:T(8,128)(2,1)S(1)}, u32[]{:S(2)}, u32[]{:S(2)}) collective-permute-start(bf16[512,384]{1,0:T(8,128)(2,1)S(1)} %add_convert_fusion.8), channel_id=1, source_target_pairs={{4,2},{5,3},{6,4},{7,5},{12,10},{13,11},{14,12},{15,13},{20,18},{2... | collective-permute-start | bytes 1179656 | tf_op jit(solution)/shard_map/scatter_step_2/ppermute | solution.py:248
  135.0 16.6 %collective-permute-start.39 = (bf16[512,384]{1,0:T(8,128)(2,1)S(1)}, bf16[512,384]{1,0:T(8,128)(2,1)S(1)}, u32[]{:S(2)}, u32[]{:S(2)}) collective-permute-start(bf16[512,384]{1,0:T(8,128)(2,1)S(1)} %broadcast_select_fusion.3), channel_id=1, source_target_pairs={{0,2},{1,3},{6,4},{7,5},{8,10},{9,11},{14,12},{15,13},{16,18},{17,... | collective-permute-start | bytes 1179656 | tf_op jit(solution)/shard_map/scatter_step_1/ppermute | solution.py:248
  141.3 10.4 %collective-permute-start.43 = (bf16[512,384]{1,0:T(8,128)(2,1)S(1)}, bf16[512,384]{1,0:T(8,128)(2,1)S(1)}, u32[]{:S(2)}, u32[]{:S(2)}) collective-permute-start(bf16[512,384]{1,0:T(8,128)(2,1)S(1)} %add_convert_fusion.7), channel_id=1, source_target_pairs={{4,2},{5,3},{6,4},{7,5},{12,10},{13,11},{14,12},{15,13},{20,18},{2... | collective-permute-start | bytes 1179656 | tf_op jit(solution)/shard_map/scatter_step_2/ppermute | solution.py:248
  142.0 14.4 %collective-permute-start.41 = (bf16[512,384]{1,0:T(8,128)(2,1)S(1)}, bf16[512,384]{1,0:T(8,128)(2,1)S(1)}, u32[]{:S(2)}, u32[]{:S(2)}) collective-permute-start(bf16[512,384]{1,0:T(8,128)(2,1)S(1)} %add_convert_fusion.7), channel_id=1, source_target_pairs={{0,2},{1,3},{2,4},{3,5},{8,10},{9,11},{10,12},{11,13},{16,18},{17,... | collective-permute-start | bytes 1179656 | tf_op jit(solution)/shard_map/scatter_step_2/ppermute | solution.py:248
  151.6 25.4 %collective-permute-start.40 = (bf16[512,2048]{1,0:T(8,128)(2,1)}, bf16[512,2048]{1,0:T(8,128)(2,1)}, u32[]{:S(2)}, u32[]{:S(2)}) collective-permute-start(bf16[512,2048]{1,0:T(8,128)(2,1)} %get-tuple-element.92), channel_id=1, source_target_pairs={{0,1},{1,0},{2,3},{3,2},{4,5},{5,4},{6,7},{7,6},{8,9},{9,8},{10,11... | collective-permute-start | bytes 6291464 | tf_op jit(solution)/shard_map/back/ppermute | solution.py:245
  152.5 19.2 %collective-permute-start.44 = (bf16[512,384]{1,0:T(8,128)(2,1)}, bf16[512,384]{1,0:T(8,128)(2,1)}, u32[]{:S(2)}, u32[]{:S(2)}) collective-permute-start(bf16[512,384]{1,0:T(8,128)(2,1)} %add_convert_fusion.5), channel_id=1, source_target_pairs={{2,0},{3,1},{4,2},{5,3},{6,4},{7,5},{10,8},{11,9},{12,10},{13,11},... | collective-permute-start | bytes 1179656 | tf_op jit(solution)/shard_map/back/scatter_step_3/ppermute | solution.py:248
  157.2 16.6 %collective-permute-start.42 = (bf16[512,384]{1,0:T(8,128)(2,1)}, bf16[512,384]{1,0:T(8,128)(2,1)}, u32[]{:S(2)}, u32[]{:S(2)}) collective-permute-start(bf16[512,384]{1,0:T(8,128)(2,1)} %add_convert_fusion.6), channel_id=1, source_target_pairs={{0,2},{1,3},{2,4},{3,5},{4,6},{5,7},{8,10},{9,11},{10,12},{11,13},... | collective-permute-start | bytes 1179656 | tf_op jit(solution)/shard_map/back/scatter_step_3/ppermute | solution.py:248
  175.2 1.8 collective-permute-start.55
  177.0 21.7 %collective-permute-start.51 = (bf16[512,384]{1,0:T(8,128)(2,1)S(1)}, bf16[512,384]{1,0:T(8,128)(2,1)S(1)}, u32[]{:S(2)}, u32[]{:S(2)}) collective-permute-start(bf16[512,384]{1,0:T(8,128)(2,1)S(1)} %add_convert_fusion.2), channel_id=1, source_target_pairs={{0,2},{1,3},{2,4},{3,5},{8,10},{9,11},{10,12},{11,13},{16,18},{17,... | collective-permute-start | bytes 1179656 | tf_op jit(solution)/shard_map/scatter_step_2/ppermute | solution.py:248
  181.4 30.6 %collective-permute-start.53 = (bf16[512,384]{1,0:T(8,128)(2,1)S(1)}, bf16[512,384]{1,0:T(8,128)(2,1)S(1)}, u32[]{:S(2)}, u32[]{:S(2)}) collective-permute-start(bf16[512,384]{1,0:T(8,128)(2,1)S(1)} %add_convert_fusion.2), channel_id=1, source_target_pairs={{4,2},{5,3},{6,4},{7,5},{12,10},{13,11},{14,12},{15,13},{20,18},{2... | collective-permute-start | bytes 1179656 | tf_op jit(solution)/shard_map/scatter_step_2/ppermute | solution.py:248
  182.1 13.4 %collective-permute-start.47 = (bf16[512,384]{1,0:T(8,128)(2,1)S(1)}, bf16[512,384]{1,0:T(8,128)(2,1)S(1)}, u32[]{:S(2)}, u32[]{:S(2)}) collective-permute-start(bf16[512,384]{1,0:T(8,128)(2,1)S(1)} %add_convert_fusion.3), channel_id=1, source_target_pairs={{2,0},{3,1},{4,2},{5,3},{6,4},{7,5},{10,8},{11,9},{12,10},{13,11},... | collective-permute-start | bytes 1179656 | tf_op jit(solution)/shard_map/back/scatter_step_3/ppermute | solution.py:248
  183.4 15.1 %collective-permute-start.46 = (bf16[512,384]{1,0:T(8,128)(2,1)S(1)}, bf16[512,384]{1,0:T(8,128)(2,1)S(1)}, u32[]{:S(2)}, u32[]{:S(2)}) collective-permute-start(bf16[512,384]{1,0:T(8,128)(2,1)S(1)} %add_convert_fusion.4), channel_id=1, source_target_pairs={{0,2},{1,3},{2,4},{3,5},{4,6},{5,7},{8,10},{9,11},{10,12},{11,13},... | collective-permute-start | bytes 1179656 | tf_op jit(solution)/shard_map/back/scatter_step_3/ppermute | solution.py:248
  191.1 19.3 %collective-permute-start.49 = (bf16[2,128,1024]{2,1,0:T(8,128)(2,1)S(1)}, bf16[2,128,1024]{2,1,0:T(8,128)(2,1)S(1)}, u32[]{:S(2)}, u32[]{:S(2)}) collective-permute-start(bf16[2,128,1024]{2,1,0:T(8,128)(2,1)S(1)} %pad_maximum_fusion), channel_id=1, source_target_pairs={{0,8},{8,0},{16,24},{24,16},{1,9},{9,1},{17,25},{25,17},{2,10},{10... | collective-permute-start | bytes 1572872 | tf_op jit(solution)/shard_map/back/ppermute | solution.py:253
  195.5 13.1 %collective-permute-start.45 = (bf16[2,128,1024]{2,1,0:T(8,128)(2,1)S(1)}, bf16[2,128,1024]{2,1,0:T(8,128)(2,1)S(1)}, u32[]{:S(2)}, u32[]{:S(2)}) collective-permute-start(bf16[2,128,1024]{2,1,0:T(8,128)(2,1)S(1)} %slice.141), channel_id=1, source_target_pairs={{0,16},{8,24},{16,0},{24,8},{1,17},{9,25},{17,1},{25,9},{2,18},{10... | collective-permute-start | bytes 1572872 | tf_op jit(solution)/shard_map/back/ppermute | solution.py:253
  198.6 35.2 %collective-permute-start.56 = (f32[256,384]{1,0:T(8,128)S(1)}, f32[256,384]{1,0:T(8,128)S(1)}, u32[]{:S(2)}, u32[]{:S(2)}) collective-permute-start(f32[256,384]{1,0:T(8,128)S(1)} %constant_dynamic-slice_fusion.1), channel_id=1, source_target_pairs={{0,1},{1,0},{2,3},{3,2},{4,5},{5,4},{6,7},{7,6},{8,9},{9,8},{10,11... | collective-permute-start | bytes 1179656 | tf_op jit(solution)/shard_map/ppermute | solution.py:245
  208.8 15.1 %collective-permute-start.48 = (bf16[128,1024]{1,0:T(8,128)(2,1)S(1)}, bf16[128,1024]{1,0:T(8,128)(2,1)S(1)}, u32[]{:S(2)}, u32[]{:S(2)}) collective-permute-start(bf16[128,1024]{1,0:T(8,128)(2,1)S(1)} %fusion.8), channel_id=1, source_target_pairs={{0,8},{8,0},{16,24},{24,16},{1,9},{9,1},{17,25},{25,17},{2,10},{10... | collective-permute-start | bytes 786440 | tf_op jit(solution)/shard_map/back/ppermute | solution.py:253
  210.5 13.5 %collective-permute-start.50 = (bf16[128,1024]{1,0:T(8,128)(2,1)S(1)}, bf16[128,1024]{1,0:T(8,128)(2,1)S(1)}, u32[]{:S(2)}, u32[]{:S(2)}) collective-permute-start(bf16[128,1024]{1,0:T(8,128)(2,1)S(1)} %fusion.9), channel_id=1, source_target_pairs={{0,16},{8,24},{16,0},{24,8},{1,17},{9,25},{17,1},{25,9},{2,18},{10... | collective-permute-start | bytes 786440 | tf_op jit(solution)/shard_map/back/ppermute | solution.py:253
  212.1 16.5 %collective-permute-start.52 = (bf16[512,384]{1,0:T(8,128)(2,1)S(1)}, bf16[512,384]{1,0:T(8,128)(2,1)S(1)}, u32[]{:S(2)}, u32[]{:S(2)}) collective-permute-start(bf16[512,384]{1,0:T(8,128)(2,1)S(1)} %add_convert_fusion.1), channel_id=1, source_target_pairs={{0,2},{1,3},{2,4},{3,5},{4,6},{5,7},{8,10},{9,11},{10,12},{11,13},... | collective-permute-start | bytes 1179656 | tf_op jit(solution)/shard_map/scatter_step_3/ppermute | solution.py:248
  222.6 10.1 %collective-permute-start.54 = (bf16[512,384]{1,0:T(8,128)(2,1)S(1)}, bf16[512,384]{1,0:T(8,128)(2,1)S(1)}, u32[]{:S(2)}, u32[]{:S(2)}) collective-permute-start(bf16[512,384]{1,0:T(8,128)(2,1)S(1)} %add_convert_fusion), channel_id=1, source_target_pairs={{2,0},{3,1},{4,2},{5,3},{6,4},{7,5},{10,8},{11,9},{12,10},{13,11},... | collective-permute-start | bytes 1179656 | tf_op jit(solution)/shard_map/scatter_step_3/ppermute | solution.py:248
  232.9 1.8 collective-permute-start.57
  (40 other events, 344.6 us)

commit v10 on v6

--- a/solution.py
+++ b/solution.py
@@ -375,16 +375,18 @@
         left, right = ret[:, :, : width // 2], ret[:, :, width // 2 :]
         far = flip(left[2:].astype(BF16), 2)
         odd = flip(jnp.stack((right[1], right[3])).astype(BF16), 1)
+        for s in range(3, line):
+            states[0] = hop(parts[0], states[0], s, ())
         left = left[:2] + far.astype(F32)
-        near = flip(left[1].astype(BF16), 1)
-        last = flip((right[2] + odd[1].astype(F32)).astype(BF16), 2)
+        near = flip(after(left[1].astype(BF16), *states[0]), 1)
+        last = flip(after((right[2] + odd[1].astype(F32)).astype(BF16), *states[0]), 2)
         left = left[0] + near.astype(F32)
         right = right[0] + odd[0].astype(F32) + last.astype(F32)
         grad_input = jnp.concatenate((left, right), axis=1).astype(BF16)
     states[-1] = hop(parts[-1], states[-1], 2, (other,))
     sums = []
-    for own, (up, down) in zip(parts, states):
-        for s in range(3, line):
+    for i, (own, (up, down)) in enumerate(zip(parts, states)):
+        for s in range(3 if i else line, line):
             up, down = hop(own, (up, down), s, (odd, far))
         sums.append(own[0].astype(F32) + up.astype(F32) + down.astype(F32))
 

time: 228 us -> 225 us (0.987)
  starting transfers between devices: 102 us -> 80.6 us
  waiting for transfers between devices: 65.3 us -> 84.7 us
    ppermute x33, starting transfers between devices: 88.8 us -> 67.2 us  [along(): lax.ppermute(a, 'wide', [(2 * s + i, 2 * t + i) for s, t in hops for i in...]
    ppermute x33, waiting for transfers between devices: 44.8 us -> 63.5 us  [along(): lax.ppermute(a, 'wide', [(2 * s + i, 2 * t + i) for s, t in hops for i in...]
    unnamed x97 -> x99, local copies, waits for them, and re-layouts: 11.7 us -> 10.3 us
  transfers between devices with their start and end apart: 58 -> 58, of which waited for: 18 -> 26; matrix products, arithmetic and copies ran while one was open for 5% -> 5% of each run, Pallas kernels for 15% -> 15%
where the time goes in v10:
time: 225 us; the launch traced here: 224 us
  waiting for transfers between devices  84.7 us (38%)
  starting transfers between devices  80.6 us (36%)
  Pallas kernels  32.7 us (15%)
  local copies, waits for them, and re-layouts  12.2 us (5%)
  other arithmetic  11.8 us (5%)
    ppermute x33, starting transfers between devices, along(): lax.ppermute(a, 'wide', [(2 * s + i, 2 * t + i) for s, t in hops for i in...  67.2 us
    ppermute x33, waiting for transfers between devices, along(): lax.ppermute(a, 'wide', [(2 * s + i, 2 * t + i) for s, t in hops for i in...  63.5 us
    pallas_call x7, Pallas kernels, call(): pl.pallas_call(body, out_shape=outs, in_specs=ins, out_specs=[VMEM] * len...  32.7 us
    ppermute x10, waiting for transfers between devices, flip(): return lax.ppermute(a, 'expert', [(e, e ^ bit) for e in range(experts)])  18.8 us
    ppermute x10, starting transfers between devices, flip(): return lax.ppermute(a, 'expert', [(e, e ^ bit) for e in range(experts)])  11.5 us
    unnamed x99, local copies, waits for them, and re-layouts  10.3 us
  transfers between devices with their start and end apart: 58, of which 26 were waited for; matrix products, arithmetic and copies ran while one was open for 5% of the time, Pallas kernels for 15%

profile of v10, /device:TPU:0, one launch (start us, length us, event | category | flops | bytes accessed | tf_op | source)
XLA Modules:
  0.0 223.8 jit_solution(9797246135060765620)
XLA Ops:
  0.6 3.0 %collective-permute-start = (bf16[128,2048]{1,0:T(8,128)(2,1)}, bf16[128,2048]{1,0:T(8,128)(2,1)S(1)}, u32[]{:S(2)}, u32[]{:S(2)}) collective-permute-start(bf16[128,2048]{1,0:T(8,128)(2,1)} %r_1_.5), channel_id=1, source_target_pairs={{0,8},{8,0},{16,24},{24,16},{1,9},{9,1},{17,25},{25,17},{2,10},{10... | collective-permute-start | bytes 1572872 | tf_op jit(solution)/shard_map/rows/ppermute | solution.py:253
  3.6 1.5 collective-permute-start.4
  5.2 1.0 copy-done.6
  6.2 1.0 copy-done.7
  12.5 3.5 %collective-permute-start.17 = (bf16[512,384]{1,0:T(8,128)(2,1)S(1)}, bf16[512,384]{1,0:T(8,128)(2,1)S(1)}, u32[]{:S(2)}, u32[]{:S(2)}) collective-permute-start(bf16[512,384]{1,0:T(8,128)(2,1)S(1)} %get-tuple-element.58.r_10_), channel_id=1, source_target_pairs={{0,2},{1,3},{2,4},{3,5},{4,6},{5,7},{8,10},{9,11},{10,12},{11,13},... | collective-permute-start | bytes 1179656 | tf_op jit(solution)/shard_map/gather_step_1/ppermute | solution.py:248
  16.6 1.3 collective-permute-start.20
  18.7 4.6 %collective-permute-start.24 = (bf16[512,384]{1,0:T(8,128)(2,1)S(1)}, bf16[512,384]{1,0:T(8,128)(2,1)S(1)}, u32[]{:S(2)}, u32[]{:S(2)}) collective-permute-start(bf16[512,384]{1,0:T(8,128)(2,1)S(1)} %get-tuple-element.59.r_10_), channel_id=1, source_target_pairs={{0,2},{1,3},{2,4},{3,5},{4,6},{5,7},{8,10},{9,11},{10,12},{11,13},... | collective-permute-start | bytes 1179656 | tf_op jit(solution)/shard_map/gather_step_1/ppermute | solution.py:248
  24.1 1.3 collective-permute-start.27
  25.5 4.5 %collective-permute-start.30 = (bf16[512,384]{1,0:T(8,128)(2,1)S(1)}, bf16[512,384]{1,0:T(8,128)(2,1)S(1)}, u32[]{:S(2)}, u32[]{:S(2)}) collective-permute-start(bf16[512,384]{1,0:T(8,128)(2,1)S(1)} %get-tuple-element.60.r_10_), channel_id=1, source_target_pairs={{0,2},{1,3},{2,4},{3,5},{4,6},{5,7},{8,10},{9,11},{10,12},{11,13},... | collective-permute-start | bytes 1179656 | tf_op jit(solution)/shard_map/gather_step_1/ppermute | solution.py:248
  31.1 2.8 %collective-permute-done.24.r_11_ = bf16[512,384]{1,0:T(8,128)(2,1)S(1)} collective-permute-done((bf16[512,384]{1,0:T(8,128)(2,1)S(1)}, bf16[512,384]{1,0:T(8,128)(2,1)S(1)}, u32[]{:S(2)}, u32[]{:S(2)}) %collective-permute-start.24) | collective-permute-done | bytes 393248 | tf_op jit(solution)/shard_map/gather_step_1/ppermute | solution.py:248
  34.5 3.0 %collective-permute-done.27.r_14_ = bf16[512,384]{1,0:T(8,128)(2,1)S(1)} collective-permute-done((bf16[512,384]{1,0:T(8,128)(2,1)S(1)}, bf16[512,384]{1,0:T(8,128)(2,1)S(1)}, u32[]{:S(2)}, u32[]{:S(2)}) %collective-permute-start.27) | collective-permute-done | bytes 393248 | tf_op jit(solution)/shard_map/gather_step_1/ppermute | solution.py:248
  37.5 1.3 collective-permute-start.33
  38.8 2.7 %collective-permute-done.30.r_11_ = bf16[512,384]{1,0:T(8,128)(2,1)S(1)} collective-permute-done((bf16[512,384]{1,0:T(8,128)(2,1)S(1)}, bf16[512,384]{1,0:T(8,128)(2,1)S(1)}, u32[]{:S(2)}, u32[]{:S(2)}) %collective-permute-start.30) | collective-permute-done | bytes 393248 | tf_op jit(solution)/shard_map/gather_step_1/ppermute | solution.py:248
  41.4 1.4 collective-permute-start.18
  43.6 2.5 %collective-permute-done.10.r_2_ = bf16[128,2176]{1,0:T(8,128)(2,1)S(1)} collective-permute-done((bf16[128,2176]{1,0:T(8,128)(2,1)S(1)}, bf16[128,2176]{1,0:T(8,128)(2,1)S(1)}, u32[]{:S(2)}, u32[]{:S(2)}) %collective-permute-start.10) | collective-permute-done | bytes 557088 | tf_op jit(solution)/shard_map/rows/ppermute | solution.py:253
  46.1 2.9 %collective-permute-done.33.r_14_ = bf16[512,384]{1,0:T(8,128)(2,1)S(1)} collective-permute-done((bf16[512,384]{1,0:T(8,128)(2,1)S(1)}, bf16[512,384]{1,0:T(8,128)(2,1)S(1)}, u32[]{:S(2)}, u32[]{:S(2)}) %collective-permute-start.33) | collective-permute-done | bytes 393248 | tf_op jit(solution)/shard_map/gather_step_1/ppermute | solution.py:248
  49.0 1.5 collective-permute-start.5
  50.5 4.4 %collective-permute-done.12.r_4_ = bf16[128,2176]{1,0:T(8,128)(2,1)S(1)} collective-permute-done((bf16[128,2176]{1,0:T(8,128)(2,1)S(1)}, bf16[128,2176]{1,0:T(8,128)(2,1)S(1)}, u32[]{:S(2)}, u32[]{:S(2)}) %collective-permute-start.12) | collective-permute-done | bytes 557088 | tf_op jit(solution)/shard_map/rows/ppermute | solution.py:253
  54.9 1.3 collective-permute-start.21
  57.0 11.4 %collective-permute-done.21.r_15_ = bf16[512,384]{1,0:T(8,128)(2,1)} collective-permute-done((bf16[512,384]{1,0:T(8,128)(2,1)S(1)}, bf16[512,384]{1,0:T(8,128)(2,1)}, u32[]{:S(2)}, u32[]{:S(2)}) %collective-permute-start.21) | collective-permute-done | bytes 393248 | tf_op jit(solution)/shard_map/gather_step_2/ppermute | solution.py:248
  69.8 1.4 collective-permute-start.19
  72.1 1.3 collective-permute-start.22
  73.4 1.0 copy-done.3
  74.5 1.1 copy-done.5
  75.6 1.3 shard_map.104.r_9_
  77.8 1.3 collective-permute-start.28
  79.8 1.3 collective-permute-start.34
  81.1 5.1 %collective-permute-done.22.r_16_ = bf16[512,384]{1,0:T(8,128)(2,1)} collective-permute-done((bf16[512,384]{1,0:T(8,128)(2,1)}, bf16[512,384]{1,0:T(8,128)(2,1)}, u32[]{:S(2)}, u32[]{:S(2)}) %collective-permute-start.22) | collective-permute-done | bytes 393248 | tf_op jit(solution)/shard_map/gather_step_3/ppermute | solution.py:248
  86.3 7.4 %shard_map.105 = (bf16[512,384]{1,0:T(8,128)(2,1)S(1)}, bf16[512,384]{1,0:T(8,128)(2,1)S(1)}, bf16[512,384]{1,0:T(8,128)(2,1)S(1)}, bf16[512,384]{1,0:T(8,128)(2...) custom-call(s32[3]{0:T(128)S(1)} %pad_add_fusion.r_0_, bf16[128,2048]{1,0:T(8,128)(2,1)S(1)} %copy-done.15, ...), custom_call_target="tpu_custom_call" | custom-call | flops 3221225472 | bytes 14286860 | tf_op jit(solution)/shard_map/pallas_call | solution.py:100
  93.8 5.5 %collective-permute-start.23 = (bf16[512,384]{1,0:T(8,128)(2,1)S(1)}, bf16[512,384]{1,0:T(8,128)(2,1)S(1)}, u32[]{:S(2)}, u32[]{:S(2)}) collective-permute-start(bf16[512,384]{1,0:T(8,128)(2,1)S(1)} %broadcast_select_fusion.5), channel_id=1, source_target_pairs={{0,2},{1,3},{6,4},{7,5},{8,10},{9,11},{14,12},{15,13},{16,18},{17,... | collective-permute-start | bytes 1179656 | tf_op jit(solution)/shard_map/scatter_step_1/ppermute | solution.py:248
  100.2 1.3 collective-permute-start.29
  102.5 1.3 collective-permute-start.35
  103.8 3.6 %collective-permute-done.23 = bf16[512,384]{1,0:T(8,128)(2,1)S(1)} collective-permute-done((bf16[512,384]{1,0:T(8,128)(2,1)S(1)}, bf16[512,384]{1,0:T(8,128)(2,1)S(1)}, u32[]{:S(2)}, u32[]{:S(2)}) %collective-permute-start.23) | collective-permute-done | bytes 393248 | tf_op jit(solution)/shard_map/scatter_step_1/ppermute | solution.py:248
  107.5 6.7 %collective-permute-done.29.r_16_ = bf16[512,384]{1,0:T(8,128)(2,1)S(1)} collective-permute-done((bf16[512,384]{1,0:T(8,128)(2,1)S(1)}, bf16[512,384]{1,0:T(8,128)(2,1)S(1)}, u32[]{:S(2)}, u32[]{:S(2)}) %collective-permute-start.29) | collective-permute-done | bytes 393248 | tf_op jit(solution)/shard_map/gather_step_3/ppermute | solution.py:248
  114.2 7.7 %shard_map.106 = (bf16[512,384]{1,0:T(8,128)(2,1)S(1)}, bf16[512,384]{1,0:T(8,128)(2,1)S(1)}, bf16[512,384]{1,0:T(8,128)(2,1)S(1)}, bf16[512,384]{1,0:T(8,128)(2...) custom-call(s32[3]{0:T(128)S(1)} %pad_add_fusion.r_0_, bf16[128,2048]{1,0:T(8,128)(2,1)S(1)} %copy-done.15, ...), custom_call_target="tpu_custom_call" | custom-call | flops 3221225472 | bytes 14286860 | tf_op jit(solution)/shard_map/pallas_call | solution.py:100
  122.0 1.5 collective-permute-start.36
  123.6 7.5 %shard_map.107 = (bf16[512,384]{1,0:T(8,128)(2,1)S(1)}, bf16[512,384]{1,0:T(8,128)(2,1)S(1)}, bf16[512,384]{1,0:T(8,128)(2,1)S(1)}, bf16[512,384]{1,0:T(8,128)(2...) custom-call(s32[3]{0:T(128)S(1)} %pad_add_fusion.r_0_, bf16[128,2048]{1,0:T(8,128)(2,1)S(1)} %copy-done.15, ...), custom_call_target="tpu_custom_call" | custom-call | flops 3221225472 | bytes 14286860 | tf_op jit(solution)/shard_map/pallas_call | solution.py:100
  131.3 2.0 collective-permute-start.37
  134.0 3.7 %collective-permute-start.39 = (bf16[512,384]{1,0:T(8,128)(2,1)S(1)}, bf16[512,384]{1,0:T(8,128)(2,1)S(1)}, u32[]{:S(2)}, u32[]{:S(2)}) collective-permute-start(bf16[512,384]{1,0:T(8,128)(2,1)S(1)} %broadcast_select_fusion.3), channel_id=1, source_target_pairs={{0,2},{1,3},{6,4},{7,5},{8,10},{9,11},{14,12},{15,13},{16,18},{17,... | collective-permute-start | bytes 1179656 | tf_op jit(solution)/shard_map/scatter_step_1/ppermute | solution.py:248
  137.9 1.3 collective-permute-start.42
  140.1 2.7 %collective-permute-done.37 = bf16[512,384]{1,0:T(8,128)(2,1)S(1)} collective-permute-done((bf16[512,384]{1,0:T(8,128)(2,1)S(1)}, bf16[512,384]{1,0:T(8,128)(2,1)S(1)}, u32[]{:S(2)}, u32[]{:S(2)}) %collective-permute-start.37) | collective-permute-done | bytes 393248 | tf_op jit(solution)/shard_map/scatter_step_2/ppermute | solution.py:248
  142.8 7.4 %shard_map.108 = (bf16[512,2048]{1,0:T(8,128)(2,1)S(1)}, bf16[512,2048]{1,0:T(8,128)(2,1)}) custom-call(bf16[1024,256]{1,0:T(8,128)(2,1)S(1)} %copy-done.39, bf16[1024,256]{1,0:T(8,128)(2,1)S(1)} %get-tuple-element.72.r_1_, bf16[1024,256]{1,0:T(8,128)(2,1)S(1)} %get-tuple-element.79.r_2_, bf16[2048,256]{1,0:T(8,128)(2,1)S(1)} %get-tuple-element.80.r_3_, ...), custom_call_target="tpu_custom_call" | custom-call | flops 3221225472 | bytes 8912896 | tf_op jit(solution)/shard_map/pallas_call | solution.py:100
  150.6 4.2 %collective-permute-done.42 = bf16[512,384]{1,0:T(8,128)(2,1)S(1)} collective-permute-done((bf16[512,384]{1,0:T(8,128)(2,1)S(1)}, bf16[512,384]{1,0:T(8,128)(2,1)S(1)}, u32[]{:S(2)}, u32[]{:S(2)}) %collective-permute-start.42) | collective-permute-done | bytes 393248 | tf_op jit(solution)/shard_map/scatter_step_2/ppermute | solution.py:248
  155.6 5.2 %collective-permute-start.43 = (bf16[512,384]{1,0:T(8,128)(2,1)}, bf16[512,384]{1,0:T(8,128)(2,1)}, u32[]{:S(2)}, u32[]{:S(2)}) collective-permute-start(bf16[512,384]{1,0:T(8,128)(2,1)} %add_convert_fusion.6), channel_id=1, source_target_pairs={{0,2},{1,3},{2,4},{3,5},{4,6},{5,7},{8,10},{9,11},{10,12},{11,13},... | collective-permute-start | bytes 1179656 | tf_op jit(solution)/shard_map/back/scatter_step_3/ppermute | solution.py:248
  161.7 1.3 collective-permute-start.45
  163.0 1.3 add_convert_fusion.2
  164.3 2.6 %collective-permute-done.43 = bf16[512,384]{1,0:T(8,128)(2,1)} collective-permute-done((bf16[512,384]{1,0:T(8,128)(2,1)}, bf16[512,384]{1,0:T(8,128)(2,1)}, u32[]{:S(2)}, u32[]{:S(2)}) %collective-permute-start.43) | collective-permute-done | bytes 393248 | tf_op jit(solution)/shard_map/back/scatter_step_3/ppermute | solution.py:248
  166.9 5.7 %collective-permute-done.45 = bf16[512,384]{1,0:T(8,128)(2,1)} collective-permute-done((bf16[512,384]{1,0:T(8,128)(2,1)}, bf16[512,384]{1,0:T(8,128)(2,1)}, u32[]{:S(2)}, u32[]{:S(2)}) %collective-permute-start.45) | collective-permute-done | bytes 393248 | tf_op jit(solution)/shard_map/back/scatter_step_3/ppermute | solution.py:248
  172.6 1.4 convert_add_fusion.3
  174.4 1.5 collective-permute-done.55
  176.6 2.3 %collective-permute-start.51 = (bf16[512,384]{1,0:T(8,128)(2,1)S(1)}, bf16[512,384]{1,0:T(8,128)(2,1)S(1)}, u32[]{:S(2)}, u32[]{:S(2)}) collective-permute-start(bf16[512,384]{1,0:T(8,128)(2,1)S(1)} %add_convert_fusion.2), channel_id=1, source_target_pairs={{0,2},{1,3},{2,4},{3,5},{8,10},{9,11},{10,12},{11,13},{16,18},{17,... | collective-permute-start | bytes 1179656 | tf_op jit(solution)/shard_map/scatter_step_2/ppermute | solution.py:248
  178.8 2.3 %convert_add_fusion = f32[512,2048]{1,0:T(8,128)S(1)} fusion(bf16[512,2048]{1,0:T(8,128)(2,1)} %collective-permute-done.40, bf16[512,2048]{1,0:T(8,128)(2,1)S(1)} %get-tuple-element.83), kind=kLoop, calls=%fused_computation | loop fusion | flops 3145728 | bytes 8388608 | tf_op jit(solution)/shard_map/back/add | solution.py:373
  181.6 1.6 collective-permute-start.41
  184.0 11.3 %collective-permute-done.41 = bf16[2,128,1024]{2,1,0:T(8,128)(2,1)S(1)} collective-permute-done((bf16[2,128,1024]{2,1,0:T(8,128)(2,1)S(1)}, bf16[2,128,1024]{2,1,0:T(8,128)(2,1)S(1)}, u32[]{:S(2)}, u32[]{:S(2)}) %collective-permute-start.41) | collective-permute-done | bytes 524320 | tf_op jit(solution)/shard_map/back/ppermute | solution.py:253
  196.8 1.0 collective-permute-start.48
  197.9 1.3 collective-permute-start.50
  199.2 4.9 %collective-permute-start.49 = (bf16[512,384]{1,0:T(8,128)(2,1)S(1)}, bf16[512,384]{1,0:T(8,128)(2,1)S(1)}, u32[]{:S(2)}, u32[]{:S(2)}) collective-permute-start(bf16[512,384]{1,0:T(8,128)(2,1)S(1)} %add_convert_fusion.4), channel_id=1, source_target_pairs={{0,2},{1,3},{2,4},{3,5},{4,6},{5,7},{8,10},{9,11},{10,12},{11,13},... | collective-permute-start | bytes 1179656 | tf_op jit(solution)/shard_map/scatter_step_3/ppermute | solution.py:248
  204.1 1.3 collective-permute-start.54
  205.4 4.6 %collective-permute-start.52 = (bf16[512,384]{1,0:T(8,128)(2,1)S(1)}, bf16[512,384]{1,0:T(8,128)(2,1)S(1)}, u32[]{:S(2)}, u32[]{:S(2)}) collective-permute-start(bf16[512,384]{1,0:T(8,128)(2,1)S(1)} %add_convert_fusion.1), channel_id=1, source_target_pairs={{0,2},{1,3},{2,4},{3,5},{4,6},{5,7},{8,10},{9,11},{10,12},{11,13},... | collective-permute-start | bytes 1179656 | tf_op jit(solution)/shard_map/scatter_step_3/ppermute | solution.py:248
  210.2 2.0 collective-permute-done.50
  212.2 1.5 collective-permute-done.49
  213.9 4.1 %collective-permute-done.54 = bf16[512,384]{1,0:T(8,128)(2,1)S(1)} collective-permute-done((bf16[512,384]{1,0:T(8,128)(2,1)S(1)}, bf16[512,384]{1,0:T(8,128)(2,1)S(1)}, u32[]{:S(2)}, u32[]{:S(2)}) %collective-permute-start.54) | collective-permute-done | bytes 393248 | tf_op jit(solution)/shard_map/scatter_step_3/ppermute | solution.py:248
  217.9 1.2 collective-permute-done.52
  222.5 1.3 broadcast_select_fusion
  (198 shorter events, 27.9 us)
Async XLA Ops:
  0.6 16.0 %collective-permute-start = (bf16[128,2048]{1,0:T(8,128)(2,1)}, bf16[128,2048]{1,0:T(8,128)(2,1)S(1)}, u32[]{:S(2)}, u32[]{:S(2)}) collective-permute-start(bf16[128,2048]{1,0:T(8,128)(2,1)} %r_1_.5), channel_id=1, source_target_pairs={{0,8},{8,0},{16,24},{24,16},{1,9},{9,1},{17,25},{25,17},{2,10},{10... | collective-permute-start | bytes 1572872 | tf_op jit(solution)/shard_map/rows/ppermute | solution.py:253
  3.6 15.1 %collective-permute-start.4 = (bf16[128,2048]{1,0:T(8,128)(2,1)}, bf16[128,2048]{1,0:T(8,128)(2,1)}, u32[]{:S(2)}, u32[]{:S(2)}) collective-permute-start(bf16[128,2048]{1,0:T(8,128)(2,1)} %r_1_.5), channel_id=1, source_target_pairs={{0,16},{8,24},{16,0},{24,8},{1,17},{9,25},{17,1},{25,9},{2,18},{10... | collective-permute-start | bytes 1572872 | tf_op jit(solution)/shard_map/rows/ppermute | solution.py:253
  9.0 2.3 %collective-permute-start.1 = (bf16[256,384]{1,0:T(8,128)(2,1)S(1)}, bf16[256,384]{1,0:T(8,128)(2,1)S(1)}, u32[]{:S(2)}, u32[]{:S(2)}) collective-permute-start(bf16[256,384]{1,0:T(8,128)(2,1)S(1)} %get-tuple-element.55), channel_id=1, source_target_pairs={{0,1},{1,0},{2,3},{3,2},{4,5},{5,4},{6,7},{7,6},{8,9},{9,8},{10,11... | collective-permute-start | bytes 589832 | tf_op jit(solution)/shard_map/ppermute | solution.py:245
  9.1 2.8 %collective-permute-start.2 = (bf16[256,384]{1,0:T(8,128)(2,1)S(1)}, bf16[256,384]{1,0:T(8,128)(2,1)S(1)}, u32[]{:S(2)}, u32[]{:S(2)}) collective-permute-start(bf16[256,384]{1,0:T(8,128)(2,1)S(1)} %get-tuple-element.56), channel_id=1, source_target_pairs={{0,1},{1,0},{2,3},{3,2},{4,5},{5,4},{6,7},{7,6},{8,9},{9,8},{10,11... | collective-permute-start | bytes 589832 | tf_op jit(solution)/shard_map/ppermute | solution.py:245
  9.6 2.3 %collective-permute-start.3 = (bf16[256,384]{1,0:T(8,128)(2,1)S(1)}, bf16[256,384]{1,0:T(8,128)(2,1)S(1)}, u32[]{:S(2)}, u32[]{:S(2)}) collective-permute-start(bf16[256,384]{1,0:T(8,128)(2,1)S(1)} %get-tuple-element.57), channel_id=1, source_target_pairs={{0,1},{1,0},{2,3},{3,2},{4,5},{5,4},{6,7},{7,6},{8,9},{9,8},{10,11... | collective-permute-start | bytes 589832 | tf_op jit(solution)/shard_map/ppermute | solution.py:245
  11.3 12.0 %collective-permute-start.6 = (bf16[128,2048]{1,0:T(8,128)(2,1)}, bf16[128,2048]{1,0:T(8,128)(2,1)S(1)}, u32[]{:S(2)}, u32[]{:S(2)}) collective-permute-start(bf16[128,2048]{1,0:T(8,128)(2,1)} %r_1_.5), channel_id=1, source_target_pairs={{0,1},{1,0},{2,3},{3,2},{4,5},{5,4},{6,7},{7,6},{8,9},{9,8},{10,11... | collective-permute-start | bytes 1572872 | tf_op jit(solution)/shard_map/rows/ppermute | solution.py:245
  12.5 58.8 %copy-start.20 = (bf16[512,384]{1,0:T(8,128)(2,1)}, bf16[512,384]{1,0:T(8,128)(2,1)S(1)}, u32[]{:S(2)}) copy-start(bf16[512,384]{1,0:T(8,128)(2,1)S(1)} %get-tuple-element.60.r_10_) | copy-start | bytes 1179652
  12.5 58.8 %copy-start.22 = (bf16[512,384]{1,0:T(8,128)(2,1)}, bf16[512,384]{1,0:T(8,128)(2,1)S(1)}, u32[]{:S(2)}) copy-start(bf16[512,384]{1,0:T(8,128)(2,1)S(1)} %get-tuple-element.59.r_10_) | copy-start | bytes 1179652
  12.5 13.0 %collective-permute-start.17 = (bf16[512,384]{1,0:T(8,128)(2,1)S(1)}, bf16[512,384]{1,0:T(8,128)(2,1)S(1)}, u32[]{:S(2)}, u32[]{:S(2)}) collective-permute-start(bf16[512,384]{1,0:T(8,128)(2,1)S(1)} %get-tuple-element.58.r_10_), channel_id=1, source_target_pairs={{0,2},{1,3},{2,4},{3,5},{4,6},{5,7},{8,10},{9,11},{10,12},{11,13},... | collective-permute-start | bytes 1179656 | tf_op jit(solution)/shard_map/gather_step_1/ppermute | solution.py:248
  16.1 17.8 %collective-permute-start.11 = (bf16[128,2176]{1,0:T(8,128)(2,1)S(1)}, bf16[128,2176]{1,0:T(8,128)(2,1)S(1)}, u32[]{:S(2)}, u32[]{:S(2)}) collective-permute-start(bf16[128,2176]{1,0:T(8,128)(2,1)S(1)} %fusion.1.r_1_), channel_id=1, source_target_pairs={{0,16},{8,24},{16,0},{24,8},{1,17},{9,25},{17,1},{25,9},{2,18},{10... | collective-permute-start | bytes 1671176 | tf_op jit(solution)/shard_map/rows/ppermute | solution.py:253
  16.6 13.9 %collective-permute-start.20 = (bf16[512,384]{1,0:T(8,128)(2,1)S(1)}, bf16[512,384]{1,0:T(8,128)(2,1)S(1)}, u32[]{:S(2)}, u32[]{:S(2)}) collective-permute-start(bf16[512,384]{1,0:T(8,128)(2,1)S(1)} %get-tuple-element.58.r_10_), channel_id=1, source_target_pairs={{2,0},{3,1},{4,2},{5,3},{6,4},{7,5},{10,8},{11,9},{12,10},{13,11},... | collective-permute-start | bytes 1179656 | tf_op jit(solution)/shard_map/gather_step_1/ppermute | solution.py:248
  18.7 15.2 %collective-permute-start.24 = (bf16[512,384]{1,0:T(8,128)(2,1)S(1)}, bf16[512,384]{1,0:T(8,128)(2,1)S(1)}, u32[]{:S(2)}, u32[]{:S(2)}) collective-permute-start(bf16[512,384]{1,0:T(8,128)(2,1)S(1)} %get-tuple-element.59.r_10_), channel_id=1, source_target_pairs={{0,2},{1,3},{2,4},{3,5},{4,6},{5,7},{8,10},{9,11},{10,12},{11,13},... | collective-permute-start | bytes 1179656 | tf_op jit(solution)/shard_map/gather_step_1/ppermute | solution.py:248
  24.1 13.4 %collective-permute-start.27 = (bf16[512,384]{1,0:T(8,128)(2,1)S(1)}, bf16[512,384]{1,0:T(8,128)(2,1)S(1)}, u32[]{:S(2)}, u32[]{:S(2)}) collective-permute-start(bf16[512,384]{1,0:T(8,128)(2,1)S(1)} %get-tuple-element.59.r_10_), channel_id=1, source_target_pairs={{2,0},{3,1},{4,2},{5,3},{6,4},{7,5},{10,8},{11,9},{12,10},{13,11},... | collective-permute-start | bytes 1179656 | tf_op jit(solution)/shard_map/gather_step_1/ppermute | solution.py:248
  25.5 16.0 %collective-permute-start.30 = (bf16[512,384]{1,0:T(8,128)(2,1)S(1)}, bf16[512,384]{1,0:T(8,128)(2,1)S(1)}, u32[]{:S(2)}, u32[]{:S(2)}) collective-permute-start(bf16[512,384]{1,0:T(8,128)(2,1)S(1)} %get-tuple-element.60.r_10_), channel_id=1, source_target_pairs={{0,2},{1,3},{2,4},{3,5},{4,6},{5,7},{8,10},{9,11},{10,12},{11,13},... | collective-permute-start | bytes 1179656 | tf_op jit(solution)/shard_map/gather_step_1/ppermute | solution.py:248
  30.6 15.6 %collective-permute-start.10 = (bf16[128,2176]{1,0:T(8,128)(2,1)S(1)}, bf16[128,2176]{1,0:T(8,128)(2,1)S(1)}, u32[]{:S(2)}, u32[]{:S(2)}) collective-permute-start(bf16[128,2176]{1,0:T(8,128)(2,1)S(1)} %fusion.1.r_1_), channel_id=1, source_target_pairs={{0,8},{8,0},{16,24},{24,16},{1,9},{9,1},{17,25},{25,17},{2,10},{10... | collective-permute-start | bytes 1671176 | tf_op jit(solution)/shard_map/rows/ppermute | solution.py:253
  33.9 37.4 %copy-start.26 = (bf16[512,384]{1,0:T(8,128)(2,1)}, bf16[512,384]{1,0:T(8,128)(2,1)S(1)}, u32[]{:S(2)}) copy-start(bf16[512,384]{1,0:T(8,128)(2,1)S(1)} %collective-permute-done.24.r_11_) | copy-start | bytes 1179652
  33.9 16.6 %collective-permute-start.13 = (bf16[128,2176]{1,0:T(8,128)(2,1)S(1)}, bf16[128,2176]{1,0:T(8,128)(2,1)S(1)}, u32[]{:S(2)}, u32[]{:S(2)}) collective-permute-start(bf16[128,2176]{1,0:T(8,128)(2,1)S(1)} %fusion.1.r_1_), channel_id=1, source_target_pairs={{0,1},{1,0},{2,3},{3,2},{4,5},{5,4},{6,7},{7,6},{8,9},{9,8},{10,11... | collective-permute-start | bytes 1671176 | tf_op jit(solution)/shard_map/rows/ppermute | solution.py:245
  33.9 21.0 %collective-permute-start.12 = (bf16[128,2176]{1,0:T(8,128)(2,1)S(1)}, bf16[128,2176]{1,0:T(8,128)(2,1)S(1)}, u32[]{:S(2)}, u32[]{:S(2)}) collective-permute-start(bf16[128,2176]{1,0:T(8,128)(2,1)S(1)} %collective-permute-done.11.r_3_), channel_id=1, source_target_pairs={{0,8},{8,0},{16,24},{24,16},{1,9},{9,1},{17,25},{25,17},{2,10},{10... | collective-permute-start | bytes 1671176 | tf_op jit(solution)/shard_map/rows/ppermute | solution.py:253
  37.5 33.8 %copy-start.28 = (bf16[512,384]{1,0:T(8,128)(2,1)}, bf16[512,384]{1,0:T(8,128)(2,1)S(1)}, u32[]{:S(2)}) copy-start(bf16[512,384]{1,0:T(8,128)(2,1)S(1)} %collective-permute-done.27.r_14_) | copy-start | bytes 1179652
  37.5 11.5 %collective-permute-start.33 = (bf16[512,384]{1,0:T(8,128)(2,1)S(1)}, bf16[512,384]{1,0:T(8,128)(2,1)S(1)}, u32[]{:S(2)}, u32[]{:S(2)}) collective-permute-start(bf16[512,384]{1,0:T(8,128)(2,1)S(1)} %get-tuple-element.60.r_10_), channel_id=1, source_target_pairs={{2,0},{3,1},{4,2},{5,3},{6,4},{7,5},{10,8},{11,9},{12,10},{13,11},... | collective-permute-start | bytes 1179656 | tf_op jit(solution)/shard_map/gather_step_1/ppermute | solution.py:248
  41.4 29.9 %copy-start.24 = (bf16[512,384]{1,0:T(8,128)(2,1)}, bf16[512,384]{1,0:T(8,128)(2,1)S(1)}, u32[]{:S(2)}) copy-start(bf16[512,384]{1,0:T(8,128)(2,1)S(1)} %collective-permute-done.30.r_11_) | copy-start | bytes 1179652
  41.4 13.5 %collective-permute-start.18 = (bf16[512,384]{1,0:T(8,128)(2,1)S(1)}, bf16[512,384]{1,0:T(8,128)(2,1)}, u32[]{:S(2)}, u32[]{:S(2)}) collective-permute-start(bf16[512,384]{1,0:T(8,128)(2,1)S(1)} %collective-permute-done.17.r_11_), channel_id=1, source_target_pairs={{2,4},{3,5},{4,6},{5,7},{10,12},{11,13},{12,14},{13,15},{18,20},{1... | collective-permute-start | bytes 1179656 | tf_op jit(solution)/shard_map/gather_step_2/ppermute | solution.py:248
  46.1 22.8 %collective-permute-start.14 = (bf16[128,2176]{1,0:T(8,128)(2,1)S(1)}, bf16[128,2176]{1,0:T(8,128)(2,1)S(1)}, u32[]{:S(2)}, u32[]{:S(2)}) collective-permute-start(bf16[128,2176]{1,0:T(8,128)(2,1)S(1)} %collective-permute-done.10.r_2_), channel_id=1, source_target_pairs={{0,1},{1,0},{2,3},{3,2},{4,5},{5,4},{6,7},{7,6},{8,9},{9,8},{10,11... | collective-permute-start | bytes 1671176 | tf_op jit(solution)/shard_map/rows/ppermute | solution.py:245
  49.0 19.4 %collective-permute-start.5 = (bf16[128,2048]{1,0:T(8,128)(2,1)}, bf16[128,2048]{1,0:T(8,128)(2,1)}, u32[]{:S(2)}, u32[]{:S(2)}) collective-permute-start(bf16[128,2048]{1,0:T(8,128)(2,1)} %copy-done.16), channel_id=1, source_target_pairs={{0,16},{8,24},{16,0},{24,8},{1,17},{9,25},{17,1},{25,9},{2,18},{10... | collective-permute-start | bytes 1572872 | tf_op jit(solution)/shard_map/rows/ppermute | solution.py:253
  50.5 18.5 %collective-permute-start.15 = (bf16[128,2176]{1,0:T(8,128)(2,1)S(1)}, bf16[128,2176]{1,0:T(8,128)(2,1)S(1)}, u32[]{:S(2)}, u32[]{:S(2)}) collective-permute-start(bf16[128,2176]{1,0:T(8,128)(2,1)S(1)} %collective-permute-done.11.r_3_), channel_id=1, source_target_pairs={{0,1},{1,0},{2,3},{3,2},{4,5},{5,4},{6,7},{7,6},{8,9},{9,8},{10,11... | collective-permute-start | bytes 1671176 | tf_op jit(solution)/shard_map/rows/ppermute | solution.py:245
  54.9 16.4 %collective-permute-start.16 = (bf16[128,2176]{1,0:T(8,128)(2,1)S(1)}, bf16[128,2176]{1,0:T(8,128)(2,1)S(1)}, u32[]{:S(2)}, u32[]{:S(2)}) collective-permute-start(bf16[128,2176]{1,0:T(8,128)(2,1)S(1)} %collective-permute-done.12.r_4_), channel_id=1, source_target_pairs={{0,1},{1,0},{2,3},{3,2},{4,5},{5,4},{6,7},{7,6},{8,9},{9,8},{10,11... | collective-permute-start | bytes 1671176 | tf_op jit(solution)/shard_map/rows/ppermute | solution.py:245
  54.9 13.5 %collective-permute-start.21 = (bf16[512,384]{1,0:T(8,128)(2,1)S(1)}, bf16[512,384]{1,0:T(8,128)(2,1)}, u32[]{:S(2)}, u32[]{:S(2)}) collective-permute-start(bf16[512,384]{1,0:T(8,128)(2,1)S(1)} %collective-permute-done.20.r_14_), channel_id=1, source_target_pairs={{2,0},{3,1},{4,2},{5,3},{10,8},{11,9},{12,10},{13,11},{18,16},{19,... | collective-permute-start | bytes 1179656 | tf_op jit(solution)/shard_map/gather_step_2/ppermute | solution.py:248
  68.4 8.5 %collective-permute-start.7 = (bf16[128,2048]{1,0:T(8,128)(2,1)}, bf16[128,2048]{1,0:T(8,128)(2,1)}, u32[]{:S(2)}, u32[]{:S(2)}) collective-permute-start(bf16[128,2048]{1,0:T(8,128)(2,1)} %copy-done.16), channel_id=1, source_target_pairs={{0,1},{1,0},{2,3},{3,2},{4,5},{5,4},{6,7},{7,6},{8,9},{9,8},{10,11... | collective-permute-start | bytes 1572872 | tf_op jit(solution)/shard_map/rows/ppermute | solution.py:245
  68.4 9.3 %collective-permute-start.8 = (bf16[128,2048]{1,0:T(8,128)(2,1)}, bf16[128,2048]{1,0:T(8,128)(2,1)}, u32[]{:S(2)}, u32[]{:S(2)}) collective-permute-start(bf16[128,2048]{1,0:T(8,128)(2,1)} %collective-permute-done.4.r_3_), channel_id=1, source_target_pairs={{0,1},{1,0},{2,3},{3,2},{4,5},{5,4},{6,7},{7,6},{8,9},{9,8},{10,11... | collective-permute-start | bytes 1572872 | tf_op jit(solution)/shard_map/rows/ppermute | solution.py:245
  69.0 10.2 %collective-permute-start.9 = (bf16[128,2048]{1,0:T(8,128)(2,1)}, bf16[128,2048]{1,0:T(8,128)(2,1)}, u32[]{:S(2)}, u32[]{:S(2)}) collective-permute-start(bf16[128,2048]{1,0:T(8,128)(2,1)} %collective-permute-done.5.r_4_), channel_id=1, source_target_pairs={{0,1},{1,0},{2,3},{3,2},{4,5},{5,4},{6,7},{7,6},{8,9},{9,8},{10,11... | collective-permute-start | bytes 1572872 | tf_op jit(solution)/shard_map/rows/ppermute | solution.py:245
  69.8 10.0 %collective-permute-start.19 = (bf16[512,384]{1,0:T(8,128)(2,1)}, bf16[512,384]{1,0:T(8,128)(2,1)}, u32[]{:S(2)}, u32[]{:S(2)}) collective-permute-start(bf16[512,384]{1,0:T(8,128)(2,1)} %collective-permute-done.18.r_12_), channel_id=1, source_target_pairs={{4,6},{5,7},{12,14},{13,15},{20,22},{21,23},{28,30},{29,31}} | collective-permute-start | bytes 1179656 | tf_op jit(solution)/shard_map/gather_step_3/ppermute | solution.py:248
  72.1 14.1 %collective-permute-start.22 = (bf16[512,384]{1,0:T(8,128)(2,1)}, bf16[512,384]{1,0:T(8,128)(2,1)}, u32[]{:S(2)}, u32[]{:S(2)}) collective-permute-start(bf16[512,384]{1,0:T(8,128)(2,1)} %collective-permute-done.21.r_15_), channel_id=1, source_target_pairs={{2,0},{3,1},{10,8},{11,9},{18,16},{19,17},{26,24},{27,25}} | collective-permute-start | bytes 1179656 | tf_op jit(solution)/shard_map/gather_step_3/ppermute | solution.py:248
  76.9 37.2 %copy-start.23 = (bf16[512,384]{1,0:T(8,128)(2,1)S(1)}, bf16[512,384]{1,0:T(8,128)(2,1)}, u32[]{:S(2)}) copy-start(bf16[512,384]{1,0:T(8,128)(2,1)} %copy-done.22) | copy-start | bytes 1179652
  77.0 22.4 %collective-permute-start.25 = (bf16[512,384]{1,0:T(8,128)(2,1)S(1)}, bf16[512,384]{1,0:T(8,128)(2,1)S(1)}, u32[]{:S(2)}, u32[]{:S(2)}) collective-permute-start(bf16[512,384]{1,0:T(8,128)(2,1)S(1)} %copy-done.27), channel_id=1, source_target_pairs={{2,4},{3,5},{4,6},{5,7},{10,12},{11,13},{12,14},{13,15},{18,20},{1... | collective-permute-start | bytes 1179656 | tf_op jit(solution)/shard_map/gather_step_2/ppermute | solution.py:248
  77.8 22.4 %collective-permute-start.28 = (bf16[512,384]{1,0:T(8,128)(2,1)S(1)}, bf16[512,384]{1,0:T(8,128)(2,1)S(1)}, u32[]{:S(2)}, u32[]{:S(2)}) collective-permute-start(bf16[512,384]{1,0:T(8,128)(2,1)S(1)} %copy-done.29), channel_id=1, source_target_pairs={{2,0},{3,1},{4,2},{5,3},{10,8},{11,9},{12,10},{13,11},{18,16},{19,... | collective-permute-start | bytes 1179656 | tf_op jit(solution)/shard_map/gather_step_2/ppermute | solution.py:248
  79.1 22.4 %collective-permute-start.31 = (bf16[512,384]{1,0:T(8,128)(2,1)S(1)}, bf16[512,384]{1,0:T(8,128)(2,1)S(1)}, u32[]{:S(2)}, u32[]{:S(2)}) collective-permute-start(bf16[512,384]{1,0:T(8,128)(2,1)S(1)} %copy-done.25), channel_id=1, source_target_pairs={{2,4},{3,5},{4,6},{5,7},{10,12},{11,13},{12,14},{13,15},{18,20},{1... | collective-permute-start | bytes 1179656 | tf_op jit(solution)/shard_map/gather_step_2/ppermute | solution.py:248
  79.8 22.7 %collective-permute-start.34 = (bf16[512,384]{1,0:T(8,128)(2,1)S(1)}, bf16[512,384]{1,0:T(8,128)(2,1)S(1)}, u32[]{:S(2)}, u32[]{:S(2)}) collective-permute-start(bf16[512,384]{1,0:T(8,128)(2,1)S(1)} %copy-done.31), channel_id=1, source_target_pairs={{2,0},{3,1},{4,2},{5,3},{10,8},{11,9},{12,10},{13,11},{18,16},{19,... | collective-permute-start | bytes 1179656 | tf_op jit(solution)/shard_map/gather_step_2/ppermute | solution.py:248
  93.8 13.6 %collective-permute-start.23 = (bf16[512,384]{1,0:T(8,128)(2,1)S(1)}, bf16[512,384]{1,0:T(8,128)(2,1)S(1)}, u32[]{:S(2)}, u32[]{:S(2)}) collective-permute-start(bf16[512,384]{1,0:T(8,128)(2,1)S(1)} %broadcast_select_fusion.5), channel_id=1, source_target_pairs={{0,2},{1,3},{6,4},{7,5},{8,10},{9,11},{14,12},{15,13},{16,18},{17,... | collective-permute-start | bytes 1179656 | tf_op jit(solution)/shard_map/scatter_step_1/ppermute | solution.py:248
  99.4 8.1 %collective-permute-start.26 = (bf16[512,384]{1,0:T(8,128)(2,1)S(1)}, bf16[512,384]{1,0:T(8,128)(2,1)S(1)}, u32[]{:S(2)}, u32[]{:S(2)}) collective-permute-start(bf16[512,384]{1,0:T(8,128)(2,1)S(1)} %collective-permute-done.25.r_12_), channel_id=1, source_target_pairs={{4,6},{5,7},{12,14},{13,15},{20,22},{21,23},{28,30},{29,31}} | collective-permute-start | bytes 1179656 | tf_op jit(solution)/shard_map/gather_step_3/ppermute | solution.py:248
  100.2 13.9 %collective-permute-start.29 = (bf16[512,384]{1,0:T(8,128)(2,1)S(1)}, bf16[512,384]{1,0:T(8,128)(2,1)S(1)}, u32[]{:S(2)}, u32[]{:S(2)}) collective-permute-start(bf16[512,384]{1,0:T(8,128)(2,1)S(1)} %collective-permute-done.28.r_15_), channel_id=1, source_target_pairs={{2,0},{3,1},{10,8},{11,9},{18,16},{19,17},{26,24},{27,25}} | collective-permute-start | bytes 1179656 | tf_op jit(solution)/shard_map/gather_step_3/ppermute | solution.py:248
  101.5 22.0 %collective-permute-start.32 = (bf16[512,384]{1,0:T(8,128)(2,1)S(1)}, bf16[512,384]{1,0:T(8,128)(2,1)S(1)}, u32[]{:S(2)}, u32[]{:S(2)}) collective-permute-start(bf16[512,384]{1,0:T(8,128)(2,1)S(1)} %collective-permute-done.31.r_12_), channel_id=1, source_target_pairs={{4,6},{5,7},{12,14},{13,15},{20,22},{21,23},{28,30},{29,31}} | collective-permute-start | bytes 1179656 | tf_op jit(solution)/shard_map/gather_step_3/ppermute | solution.py:248
  102.5 21.0 %collective-permute-start.35 = (bf16[512,384]{1,0:T(8,128)(2,1)S(1)}, bf16[512,384]{1,0:T(8,128)(2,1)S(1)}, u32[]{:S(2)}, u32[]{:S(2)}) collective-permute-start(bf16[512,384]{1,0:T(8,128)(2,1)S(1)} %collective-permute-done.34.r_15_), channel_id=1, source_target_pairs={{2,0},{3,1},{10,8},{11,9},{18,16},{19,17},{26,24},{27,25}} | collective-permute-start | bytes 1179656 | tf_op jit(solution)/shard_map/gather_step_3/ppermute | solution.py:248
  122.0 9.2 %collective-permute-start.36 = (bf16[512,384]{1,0:T(8,128)(2,1)S(1)}, bf16[512,384]{1,0:T(8,128)(2,1)S(1)}, u32[]{:S(2)}, u32[]{:S(2)}) collective-permute-start(bf16[512,384]{1,0:T(8,128)(2,1)S(1)} %broadcast_select_fusion.4), channel_id=1, source_target_pairs={{0,2},{1,3},{6,4},{7,5},{8,10},{9,11},{14,12},{15,13},{16,18},{17,... | collective-permute-start | bytes 1179656 | tf_op jit(solution)/shard_map/scatter_step_1/ppermute | solution.py:248
  131.3 11.6 %collective-permute-start.37 = (bf16[512,384]{1,0:T(8,128)(2,1)S(1)}, bf16[512,384]{1,0:T(8,128)(2,1)S(1)}, u32[]{:S(2)}, u32[]{:S(2)}) collective-permute-start(bf16[512,384]{1,0:T(8,128)(2,1)S(1)} %add_convert_fusion.8), channel_id=1, source_target_pairs={{0,2},{1,3},{2,4},{3,5},{8,10},{9,11},{10,12},{11,13},{16,18},{17,... | collective-permute-start | bytes 1179656 | tf_op jit(solution)/shard_map/scatter_step_2/ppermute | solution.py:248
  133.3 9.5 %collective-permute-start.38 = (bf16[512,384]{1,0:T(8,128)(2,1)S(1)}, bf16[512,384]{1,0:T(8,128)(2,1)S(1)}, u32[]{:S(2)}, u32[]{:S(2)}) collective-permute-start(bf16[512,384]{1,0:T(8,128)(2,1)S(1)} %add_convert_fusion.8), channel_id=1, source_target_pairs={{4,2},{5,3},{6,4},{7,5},{12,10},{13,11},{14,12},{15,13},{20,18},{2... | collective-permute-start | bytes 1179656 | tf_op jit(solution)/shard_map/scatter_step_2/ppermute | solution.py:248
  134.0 16.5 %collective-permute-start.39 = (bf16[512,384]{1,0:T(8,128)(2,1)S(1)}, bf16[512,384]{1,0:T(8,128)(2,1)S(1)}, u32[]{:S(2)}, u32[]{:S(2)}) collective-permute-start(bf16[512,384]{1,0:T(8,128)(2,1)S(1)} %broadcast_select_fusion.3), channel_id=1, source_target_pairs={{0,2},{1,3},{6,4},{7,5},{8,10},{9,11},{14,12},{15,13},{16,18},{17,... | collective-permute-start | bytes 1179656 | tf_op jit(solution)/shard_map/scatter_step_1/ppermute | solution.py:248
  137.9 16.9 %collective-permute-start.42 = (bf16[512,384]{1,0:T(8,128)(2,1)S(1)}, bf16[512,384]{1,0:T(8,128)(2,1)S(1)}, u32[]{:S(2)}, u32[]{:S(2)}) collective-permute-start(bf16[512,384]{1,0:T(8,128)(2,1)S(1)} %add_convert_fusion.7), channel_id=1, source_target_pairs={{0,2},{1,3},{2,4},{3,5},{8,10},{9,11},{10,12},{11,13},{16,18},{17,... | collective-permute-start | bytes 1179656 | tf_op jit(solution)/shard_map/scatter_step_2/ppermute | solution.py:248
  139.2 21.6 %collective-permute-start.44 = (bf16[512,384]{1,0:T(8,128)(2,1)S(1)}, bf16[512,384]{1,0:T(8,128)(2,1)S(1)}, u32[]{:S(2)}, u32[]{:S(2)}) collective-permute-start(bf16[512,384]{1,0:T(8,128)(2,1)S(1)} %add_convert_fusion.7), channel_id=1, source_target_pairs={{4,2},{5,3},{6,4},{7,5},{12,10},{13,11},{14,12},{15,13},{20,18},{2... | collective-permute-start | bytes 1179656 | tf_op jit(solution)/shard_map/scatter_step_2/ppermute | solution.py:248
  150.6 25.3 %collective-permute-start.40 = (bf16[512,2048]{1,0:T(8,128)(2,1)}, bf16[512,2048]{1,0:T(8,128)(2,1)}, u32[]{:S(2)}, u32[]{:S(2)}) collective-permute-start(bf16[512,2048]{1,0:T(8,128)(2,1)} %get-tuple-element.87), channel_id=1, source_target_pairs={{0,1},{1,0},{2,3},{3,2},{4,5},{5,4},{6,7},{7,6},{8,9},{9,8},{10,11... | collective-permute-start | bytes 6291464 | tf_op jit(solution)/shard_map/back/ppermute | solution.py:245
  155.6 11.2 %collective-permute-start.43 = (bf16[512,384]{1,0:T(8,128)(2,1)}, bf16[512,384]{1,0:T(8,128)(2,1)}, u32[]{:S(2)}, u32[]{:S(2)}) collective-permute-start(bf16[512,384]{1,0:T(8,128)(2,1)} %add_convert_fusion.6), channel_id=1, source_target_pairs={{0,2},{1,3},{2,4},{3,5},{4,6},{5,7},{8,10},{9,11},{10,12},{11,13},... | collective-permute-start | bytes 1179656 | tf_op jit(solution)/shard_map/back/scatter_step_3/ppermute | solution.py:248
  161.7 11.0 %collective-permute-start.45 = (bf16[512,384]{1,0:T(8,128)(2,1)}, bf16[512,384]{1,0:T(8,128)(2,1)}, u32[]{:S(2)}, u32[]{:S(2)}) collective-permute-start(bf16[512,384]{1,0:T(8,128)(2,1)} %add_convert_fusion.5), channel_id=1, source_target_pairs={{2,0},{3,1},{4,2},{5,3},{6,4},{7,5},{10,8},{11,9},{12,10},{13,11},... | collective-permute-start | bytes 1179656 | tf_op jit(solution)/shard_map/back/scatter_step_3/ppermute | solution.py:248
  174.0 1.8 collective-permute-start.55
  175.9 8.0 %collective-permute-start.53 = (bf16[512,384]{1,0:T(8,128)(2,1)S(1)}, bf16[512,384]{1,0:T(8,128)(2,1)S(1)}, u32[]{:S(2)}, u32[]{:S(2)}) collective-permute-start(bf16[512,384]{1,0:T(8,128)(2,1)S(1)} %add_convert_fusion.2), channel_id=1, source_target_pairs={{4,2},{5,3},{6,4},{7,5},{12,10},{13,11},{14,12},{15,13},{20,18},{2... | collective-permute-start | bytes 1179656 | tf_op jit(solution)/shard_map/scatter_step_2/ppermute | solution.py:248
  176.6 21.2 %collective-permute-start.51 = (bf16[512,384]{1,0:T(8,128)(2,1)S(1)}, bf16[512,384]{1,0:T(8,128)(2,1)S(1)}, u32[]{:S(2)}, u32[]{:S(2)}) collective-permute-start(bf16[512,384]{1,0:T(8,128)(2,1)S(1)} %add_convert_fusion.2), channel_id=1, source_target_pairs={{0,2},{1,3},{2,4},{3,5},{8,10},{9,11},{10,12},{11,13},{16,18},{17,... | collective-permute-start | bytes 1179656 | tf_op jit(solution)/shard_map/scatter_step_2/ppermute | solution.py:248
  181.6 13.8 %collective-permute-start.41 = (bf16[2,128,1024]{2,1,0:T(8,128)(2,1)S(1)}, bf16[2,128,1024]{2,1,0:T(8,128)(2,1)S(1)}, u32[]{:S(2)}, u32[]{:S(2)}) collective-permute-start(bf16[2,128,1024]{2,1,0:T(8,128)(2,1)S(1)} %slice.141), channel_id=1, source_target_pairs={{0,16},{8,24},{16,0},{24,8},{1,17},{9,25},{17,1},{25,9},{2,18},{10... | collective-permute-start | bytes 1572872 | tf_op jit(solution)/shard_map/back/ppermute | solution.py:253
  183.2 13.5 %collective-permute-start.47 = (bf16[2,128,1024]{2,1,0:T(8,128)(2,1)S(1)}, bf16[2,128,1024]{2,1,0:T(8,128)(2,1)S(1)}, u32[]{:S(2)}, u32[]{:S(2)}) collective-permute-start(bf16[2,128,1024]{2,1,0:T(8,128)(2,1)S(1)} %pad_maximum_fusion), channel_id=1, source_target_pairs={{0,8},{8,0},{16,24},{24,16},{1,9},{9,1},{17,25},{25,17},{2,10},{10... | collective-permute-start | bytes 1572872 | tf_op jit(solution)/shard_map/back/ppermute | solution.py:253
  195.5 9.9 %collective-permute-start.46 = (bf16[128,1024]{1,0:T(8,128)(2,1)S(1)}, bf16[128,1024]{1,0:T(8,128)(2,1)S(1)}, u32[]{:S(2)}, u32[]{:S(2)}) collective-permute-start(bf16[128,1024]{1,0:T(8,128)(2,1)S(1)} %fusion.8), channel_id=1, source_target_pairs={{0,8},{8,0},{16,24},{24,16},{1,9},{9,1},{17,25},{25,17},{2,10},{10... | collective-permute-start | bytes 786440 | tf_op jit(solution)/shard_map/back/ppermute | solution.py:253
  196.8 13.3 %collective-permute-start.48 = (bf16[128,1024]{1,0:T(8,128)(2,1)S(1)}, bf16[128,1024]{1,0:T(8,128)(2,1)S(1)}, u32[]{:S(2)}, u32[]{:S(2)}) collective-permute-start(bf16[128,1024]{1,0:T(8,128)(2,1)S(1)} %fusion.9), channel_id=1, source_target_pairs={{0,16},{8,24},{16,0},{24,8},{1,17},{9,25},{17,1},{25,9},{2,18},{10... | collective-permute-start | bytes 786440 | tf_op jit(solution)/shard_map/back/ppermute | solution.py:253
  197.9 14.3 %collective-permute-start.50 = (bf16[512,384]{1,0:T(8,128)(2,1)S(1)}, bf16[512,384]{1,0:T(8,128)(2,1)S(1)}, u32[]{:S(2)}, u32[]{:S(2)}) collective-permute-start(bf16[512,384]{1,0:T(8,128)(2,1)S(1)} %add_convert_fusion.3), channel_id=1, source_target_pairs={{2,0},{3,1},{4,2},{5,3},{6,4},{7,5},{10,8},{11,9},{12,10},{13,11},... | collective-permute-start | bytes 1179656 | tf_op jit(solution)/shard_map/scatter_step_3/ppermute | solution.py:248
  199.2 14.4 %collective-permute-start.49 = (bf16[512,384]{1,0:T(8,128)(2,1)S(1)}, bf16[512,384]{1,0:T(8,128)(2,1)S(1)}, u32[]{:S(2)}, u32[]{:S(2)}) collective-permute-start(bf16[512,384]{1,0:T(8,128)(2,1)S(1)} %add_convert_fusion.4), channel_id=1, source_target_pairs={{0,2},{1,3},{2,4},{3,5},{4,6},{5,7},{8,10},{9,11},{10,12},{11,13},... | collective-permute-start | bytes 1179656 | tf_op jit(solution)/shard_map/scatter_step_3/ppermute | solution.py:248
  204.1 13.8 %collective-permute-start.54 = (bf16[512,384]{1,0:T(8,128)(2,1)S(1)}, bf16[512,384]{1,0:T(8,128)(2,1)S(1)}, u32[]{:S(2)}, u32[]{:S(2)}) collective-permute-start(bf16[512,384]{1,0:T(8,128)(2,1)S(1)} %add_convert_fusion), channel_id=1, source_target_pairs={{2,0},{3,1},{4,2},{5,3},{6,4},{7,5},{10,8},{11,9},{12,10},{13,11},... | collective-permute-start | bytes 1179656 | tf_op jit(solution)/shard_map/scatter_step_3/ppermute | solution.py:248
  205.4 13.7 %collective-permute-start.52 = (bf16[512,384]{1,0:T(8,128)(2,1)S(1)}, bf16[512,384]{1,0:T(8,128)(2,1)S(1)}, u32[]{:S(2)}, u32[]{:S(2)}) collective-permute-start(bf16[512,384]{1,0:T(8,128)(2,1)S(1)} %add_convert_fusion.1), channel_id=1, source_target_pairs={{0,2},{1,3},{2,4},{3,5},{4,6},{5,7},{8,10},{9,11},{10,12},{11,13},... | collective-permute-start | bytes 1179656 | tf_op jit(solution)/shard_map/scatter_step_3/ppermute | solution.py:248
  213.8 6.4 %collective-permute-start.56 = (f32[256,384]{1,0:T(8,128)S(1)}, f32[256,384]{1,0:T(8,128)S(1)}, u32[]{:S(2)}, u32[]{:S(2)}) collective-permute-start(f32[256,384]{1,0:T(8,128)S(1)} %constant_dynamic-slice_fusion.1), channel_id=1, source_target_pairs={{0,1},{1,0},{2,3},{3,2},{4,5},{5,4},{6,7},{7,6},{8,9},{9,8},{10,11... | collective-permute-start | bytes 1179656 | tf_op jit(solution)/shard_map/ppermute | solution.py:245
  219.3 1.8 collective-permute-start.57
  (40 other events, 318.5 us)
